TPU v7x, 512 devices: a whole 4x8x8 slice. The times are simulated.
512 devices in a mesh: row: 16 (over y, x_hi), col: 2 (over core), depth: 16 (over z, x_lo).
Axes of the slice: x: 4 (x_hi: 2, x_lo: 2; x = x_hi * 2 + x_lo), y: 8, z: 8, core: 2. Of those that a mesh axis runs over, the one named last changes fastest.
Arguments:
- y_blocks: float32 [4096, 4096], P('row', 'col'), may hold values from -6 to 6
- z_blocks: float32 [4096, 4096], P('row', 'col'), may hold values from -0.125 to 0.125
- h_blocks: float32 [4096, 4096], P('row', 'col'), may hold values from -0.125 to 0.125
- s_pattern: int32 [16, 16], replicated, may hold values 0 or 1
- h_pattern: int32 [16, 16], replicated, may hold values 0 or 1
- keep_mask: int32 [16, 16], replicated, may hold values 0 or 1
Outputs:
- z_next: float32 [4096, 4096], P('row', 'col')
- h_times_z: float32 [4096, 4096], P('row', 'col')
All inputs are finite; a program needn't handle non-finite values.
Results may differ from a plain program's by a relative error of at most 0.00013.
Values sent between devices are 32-bit elements; how exact they have to be, the bound alone decides.
No kernel may reach another device: no remote copies, remote signals or barrier semaphores. Data moves between devices by JAX's collectives and lax.ppermute only.
A program may use at most 128 MiB of HBM per device.

v0:
```python
import jax
import jax.numpy as jnp
from jax import lax
from jax.sharding import PartitionSpec as P

BLK = 256


def from_root(array, axis, root):
    mine = lax.axis_index(axis) == root
    return lax.psum(jnp.where(mine, array, jnp.zeros_like(array)), axis)


def expand(pattern):
    values = pattern.astype(jnp.float32)
    return jnp.repeat(jnp.repeat(values, BLK, axis=0), BLK, axis=1)


def product(left, right):
    return jnp.dot(left, right, preferred_element_type=jnp.float32, precision=lax.Precision.HIGHEST)


def local(y_blocks, z_blocks, h_blocks, s_pattern, h_pattern, keep_mask):
    nblocks = s_pattern.shape[0]
    row_blocks = y_blocks.shape[0] // BLK
    col_blocks = y_blocks.shape[1] // BLK
    row_at = lax.axis_index("row")
    col_at = lax.axis_index("col")
    layer_at = lax.axis_index("depth")

    def local_tile(pattern):
        return expand(
            lax.dynamic_slice(
                pattern, (row_at * row_blocks, col_at * col_blocks), (row_blocks, col_blocks)
            )
        )

    s_local = local_tile(s_pattern)
    keep_local = local_tile(keep_mask)
    masked_y = y_blocks * s_local
    masked_z = z_blocks * s_local
    masked_h = h_blocks * local_tile(h_pattern)

    def multiply(left, right):
        layers = lax.axis_size("depth")
        inner = nblocks // layers
        lowest = layer_at * inner
        step_width = min(inner, col_blocks, row_blocks)
        inner_at = lowest + 0
        piece_a = lax.dynamic_slice_in_dim(left, inner_at % col_blocks * BLK, step_width * BLK, 1)
        part_a = from_root(piece_a, "col", inner_at // col_blocks)
        part_b = from_root(right, "row", inner_at // row_blocks)
        summed = product(part_a, part_b)
        return summed

    def filter_part(values, row_offset, col_offset):
        keep_part = lax.dynamic_slice(keep_local, (row_offset, col_offset), values.shape)
        return keep_part * values

    def shift_part(values, row_offset, col_offset):
        filtered = filter_part(values, row_offset, col_offset)
        global_rows = (
            row_at * (row_blocks * BLK) + row_offset + jnp.arange(values.shape[0], dtype=jnp.int32)
        )
        global_cols = (
            col_at * (col_blocks * BLK) + col_offset + jnp.arange(values.shape[1], dtype=jnp.int32)
        )
        diagonal_ones = global_rows[:, None] == global_cols[None, :]
        return jnp.where(diagonal_ones, 1.5, 0.0).astype(jnp.float32) - 0.5 * filtered

    def combine_depth(partial_sum, finish):
        share = lax.psum_scatter(partial_sum, "depth", scatter_dimension=0, tiled=True)
        finished = finish(share, layer_at * share.shape[0], 0)
        return lax.all_gather(finished, "depth", axis=0, tiled=True)

    q_matrix = combine_depth(multiply(masked_z, masked_y), shift_part)
    z_next = combine_depth(multiply(q_matrix, masked_z), filter_part)
    h_times_z = combine_depth(multiply(masked_h, z_next), filter_part)
    return (z_next, h_times_z)


def solution(mesh):
    in_specs = (P("row", "col"), P("row", "col"), P("row", "col"), P(), P(), P())
    out_specs = (P("row", "col"), P("row", "col"))
    return jax.shard_map(local, mesh=mesh, in_specs=in_specs, out_specs=out_specs, check_vma=False)
```

profile of v0, /device:TPU:56, one launch (start us, length us, event | category | flops | bytes accessed | tf_op | source)
XLA Modules:
  0.0 970.3 jit_solution(15851494755314473935)
XLA Ops:
  7.2 0.0 all-reduce.7.cloned.1.call-start
  7.2 0.8 convert_bitcast_fusion.1
  8.0 0.1 broadcast_bitcast_fusion.1
  8.1 5.1 broadcast_select_fusion.1
  13.2 0.7 dynamic-slice_select_fusion.1
  13.9 0.0 all-reduce.7.cloned.1.call-update
  13.9 0.0 all-reduce.11.cloned.1.call-start
  14.0 0.7 all-reduce.11.cloned.1.call-update
  14.7 0.0 reduce-scatter.4.cloned.1.call-start
  14.7 38.0 %all-reduce.7.cloned.1.call-done = f32[256,256]{1,0:T(8,128)} async-done(((f32[256,256]{1,0:T(8,128)}), f32[256,256]{1,0:T(8,128)}) %all-reduce.7.cloned.1.call-update) | async-done | bytes 262160 | tf_op jit(solution)/shard_map/psum | solution.py:11
  52.7 217.4 %all-reduce.11.cloned.1.call-done = (f32[256,2048]{1,0:T(8,128)}, f32[256,2048]{1,0:T(8,128)}) async-done(((f32[256,2048]{1,0:T(8,128)}, f32[256,2048]{1,0:T(8,128)}), (f32[256,2048]{1,0:T(8,128)}, f32[256,2048]{1,0:T(8,128)})) %all-reduce.11.cloned.1.call-update) | async-done | bytes 4194320 | tf_op jit(solution)/shard_map/psum | solution.py:11
  270.1 4.9 fusion.1
  275.0 0.0 copy-start.1
  275.0 0.0 reduce-scatter.4.cloned.1.call-update
  275.0 0.0 all-gather.4.cloned.1.call-start
  275.1 0.9 convert_bitcast_fusion
  276.0 0.1 broadcast_bitcast_fusion.2
  276.1 77.6 %reduce-scatter.4.cloned.1.call-done = f32[16,2048]{1,0:T(8,128)} async-done(((f32[256,2048]{1,0:T(8,128)}), f32[16,2048]{1,0:T(8,128)}) %reduce-scatter.4.cloned.1.call-update) | async-done | bytes 131088 | tf_op jit(solution)/shard_map/reduce_scatter | solution.py:72
  353.6 1.6 multiply_subtract_fusion
  355.3 0.0 all-gather.4.cloned.1.call-update
  355.3 0.0 all-reduce.13.cloned.1.call-start
  355.3 0.1 broadcast_bitcast_fusion
  355.4 0.1 dynamic-slice.1
  355.5 1.7 fusion
  357.2 74.2 %all-gather.4.cloned.1.call-done = f32[256,2048]{1,0:T(8,128)} async-done(((f32[16,2048]{1,0:T(8,128)}), f32[256,2048]{1,0:T(8,128)}) %all-gather.4.cloned.1.call-update) | async-done | bytes 2097168 | tf_op jit(solution)/shard_map/all_gather | solution.py:74
  431.4 1.7 dynamic-slice_select_fusion
  433.0 0.0 all-reduce.13.cloned.1.call-update
  433.1 0.0 reduce-scatter.6.cloned.1.call-start
  433.1 34.0 %all-reduce.13.cloned.1.call-done = (f32[256,256]{1,0:T(8,128)}, f32[256,256]{1,0:T(8,128)}) async-done(((f32[256,256]{1,0:T(8,128)}, f32[256,256]{1,0:T(8,128)}), (f32[256,256]{1,0:T(8,128)}, f32[256,256]{1,0:T(8,128)})) %all-reduce.13.cloned.1.call-update) | async-done | bytes 524304 | tf_op jit(solution)/shard_map/psum | solution.py:11
  467.1 0.0 copy-done.1
  467.1 4.2 fusion.2
  471.3 0.0 reduce-scatter.6.cloned.1.call-update
  471.4 0.0 all-gather.6.cloned.1.call-start
  471.4 80.1 %reduce-scatter.6.cloned.1.call-done = f32[16,2048]{1,0:T(8,128)} async-done(((f32[256,2048]{1,0:T(8,128)}), f32[16,2048]{1,0:T(8,128)}) %reduce-scatter.6.cloned.1.call-update) | async-done | bytes 131088 | tf_op jit(solution)/shard_map/reduce_scatter | solution.py:72
  551.5 1.6 broadcast_multiply_fusion.2
  553.1 0.0 all-gather.6.cloned.1.call-update
  553.1 0.0 all-reduce.9.cloned.1.call-start
  553.2 75.6 %all-gather.6.cloned.1.call-done = f32[256,2048]{1,0:T(8,128)} async-done(((f32[16,2048]{1,0:T(8,128)}), f32[256,2048]{1,0:T(8,128)}) %all-gather.6.cloned.1.call-update) | async-done | bytes 2097168 | tf_op jit(solution)/shard_map/all_gather | solution.py:74
  628.8 1.5 broadcast_select_fusion
  630.3 0.0 copy-start.3
  630.3 0.0 all-reduce.9.cloned.1.call-update
  630.3 0.0 reduce-scatter.8.cloned.1.call-start
  630.4 170.8 %all-reduce.9.cloned.1.call-done = f32[256,2048]{1,0:T(8,128)} async-done(((f32[256,2048]{1,0:T(8,128)}), f32[256,2048]{1,0:T(8,128)}) %all-reduce.9.cloned.1.call-update) | async-done | bytes 2097168 | tf_op jit(solution)/shard_map/psum | solution.py:11
  801.2 0.0 copy-done.3
  801.2 4.8 fusion.3
  806.0 0.0 copy-start
  806.0 0.0 reduce-scatter.8.cloned.1.call-update
  806.0 0.0 all-gather.8.cloned.1.call-start
  806.0 76.7 %reduce-scatter.8.cloned.1.call-done = f32[16,2048]{1,0:T(8,128)} async-done(((f32[256,2048]{1,0:T(8,128)}), f32[16,2048]{1,0:T(8,128)}) %reduce-scatter.8.cloned.1.call-update) | async-done | bytes 131088 | tf_op jit(solution)/shard_map/reduce_scatter | solution.py:72
  882.8 1.6 broadcast_multiply_fusion.1
  884.3 0.0 all-gather.8.cloned.1.call-update
  884.4 75.4 %all-gather.8.cloned.1.call-done = f32[256,2048]{1,0:T(8,128)} async-done(((f32[16,2048]{1,0:T(8,128)}), f32[256,2048]{1,0:T(8,128)}) %all-gather.8.cloned.1.call-update) | async-done | bytes 2097168 | tf_op jit(solution)/shard_map/all_gather | solution.py:74
  959.8 0.0 copy-done
  959.8 0.0 copy-start.2
  959.8 1.3 copy.19
  961.1 1.0 copy-done.2
  962.1 1.3 copy.20
  (5 shorter events, 0.0 us)
Async XLA Ops:
  7.2 45.6 %all-reduce.7.cloned.1.call-start = ((), (), s32[]{:S(2)}) async-start(), calls=%async_computation.3 | async-start | bytes 524288 | tf_op jit(solution)/shard_map/psum | solution.py:11
  13.9 256.2 %all-reduce.11.cloned.1.call-start = ((), (), s32[]{:S(2)}) async-start(), calls=%async_computation.11 | async-start | bytes 8388608 | tf_op jit(solution)/shard_map/psum | solution.py:11
  14.7 339.0 %reduce-scatter.4.cloned.1.call-start = ((), (), s32[]{:S(2)}) async-start(), calls=%async_computation.4 | async-start | bytes 2228224 | tf_op jit(solution)/shard_map/reduce_scatter | solution.py:72
  275.0 192.2 %copy-start.1 = (f32[256,2048]{1,0:T(8,128)S(1)}, f32[256,2048]{1,0:T(8,128)}, u32[]{:S(2)}) copy-start(f32[256,2048]{1,0:T(8,128)} %get-tuple-element.3) | copy-start | bytes 6291460
  275.0 156.4 %all-gather.4.cloned.1.call-start = ((), (), s32[]{:S(2)}) async-start(), calls=%async_computation.5 | async-start | bytes 2228224 | tf_op jit(solution)/shard_map/all_gather | solution.py:74
  355.3 111.8 %all-reduce.13.cloned.1.call-start = ((), (), s32[]{:S(2)}) async-start(), calls=%async_computation.12 | async-start | bytes 1048576 | tf_op jit(solution)/shard_map/psum | solution.py:11
  433.1 118.5 %reduce-scatter.6.cloned.1.call-start = ((), (), s32[]{:S(2)}) async-start(), calls=%async_computation.6 | async-start | bytes 2228224 | tf_op jit(solution)/shard_map/reduce_scatter | solution.py:72
  471.4 157.4 %all-gather.6.cloned.1.call-start = ((), (), s32[]{:S(2)}) async-start(), calls=%async_computation.7 | async-start | bytes 2228224 | tf_op jit(solution)/shard_map/all_gather | solution.py:74
  553.1 248.0 %all-reduce.9.cloned.1.call-start = ((), (), s32[]{:S(2)}) async-start(), calls=%async_computation.8 | async-start | bytes 4194304 | tf_op jit(solution)/shard_map/psum | solution.py:11
  630.3 170.9 %copy-start.3 = (f32[256,256]{1,0:T(8,128)S(1)}, f32[256,256]{1,0:T(8,128)}, u32[]{:S(2)}) copy-start(f32[256,256]{1,0:T(8,128)} %get-tuple-element.5) | copy-start | bytes 786436
  630.3 252.4 %reduce-scatter.8.cloned.1.call-start = ((), (), s32[]{:S(2)}) async-start(), calls=%async_computation.9 | async-start | bytes 2228224 | tf_op jit(solution)/shard_map/reduce_scatter | solution.py:72
  806.0 153.8 %copy-start = (f32[256,2048]{1,0:T(8,128)S(1)}, f32[256,2048]{1,0:T(8,128)}, u32[]{:S(2)}) copy-start(f32[256,2048]{1,0:T(8,128)} %all-gather.6.cloned.1.call-done) | copy-start | bytes 6291460
  806.0 153.8 %all-gather.8.cloned.1.call-start = ((), (), s32[]{:S(2)}) async-start(), calls=%async_computation.10 | async-start | bytes 2228224 | tf_op jit(solution)/shard_map/all_gather | solution.py:74
  959.8 2.3 copy-start.2
Sparse Core Ops, SparseCore 0:
  14.0 38.6 all-reduce.6
  56.6 213.4 all-reduce.10
  275.1 78.4 reduce-scatter.3
  356.4 74.9 all-gather.3
  435.0 32.1 all-reduce.12
  471.5 80.0 reduce-scatter.5
  554.2 74.5 all-gather.5
  632.3 168.8 all-reduce.8
  806.1 76.6 reduce-scatter.7
  885.3 74.4 all-gather.7
where the time goes:
time: 971 us; the launch traced here: 970 us
  waiting for transfers between devices  921 us (95%)
  other arithmetic  17.1 us (2%)
  between operations  14.2 us (1%)
  matrix products  13.9 us (1%)
    psum x4, waiting for transfers between devices, from_root(): return lax.psum(jnp.where(mine, array, jnp.zeros_like(array)), axis)  460 us
    reduce_scatter x3, waiting for transfers between devices, combine_depth(): lax.psum_scatter(partial_sum, 'depth', scatter_dimension=0, tiled=True)  234 us
    all_gather x3, waiting for transfers between devices, combine_depth(): return lax.all_gather(finished, 'depth', axis=0, tiled=True)  225 us
  transfers between devices with their start and end apart: 10, of which 10 were waited for; matrix products, arithmetic and copies ran while one was open for 0% of the time, Pallas kernels for 0%

commit v1 on v0

v1 whole, which is shorter than its diff:
```python
import jax
import jax.numpy as jnp
from jax import lax
from jax.sharding import Mesh
from jax.sharding import PartitionSpec as P

X = ("xh", "xl")
ROW = ("y", "xh")
DEPTH = ("z", "xl")
HIGH = lax.Precision.HIGH


def spread(piece, axis, n):
    copies = jnp.broadcast_to(piece[None], (n,) + piece.shape)
    return lax.all_to_all(copies, axis, split_axis=0, concat_axis=0, tiled=True)


def swap_core(array):
    return lax.ppermute(array, "core", [(0, 1), (1, 0)])


def local(y_blocks, z_blocks, h_blocks, s_pattern, h_pattern, keep_mask):
    blk, width = y_blocks.shape
    half = blk // 2
    per_core = width // blk
    ny, nz = lax.axis_size("y"), lax.axis_size("z")
    y = lax.axis_index("y")
    xh = lax.axis_index("xh")
    core = lax.axis_index("core")
    z = lax.axis_index("z")
    xl = lax.axis_index("xl")
    row = 2 * y + xh
    panel = z ^ core
    column = per_core * core + panel
    keep = keep_mask.astype(jnp.float32)
    fill = s_pattern.astype(jnp.float32)

    def masked(values, pattern):
        mine = lax.dynamic_slice(pattern.astype(jnp.float32), (row, per_core * core), (1, per_core))
        return values * jnp.repeat(mine, blk, axis=1)

    def left(values):
        parts = values.reshape(blk, per_core // 2, 2, 2, half)

        def pick(a, b):
            part = lax.dynamic_slice(
                parts, (0, 0, a, b, 0), (blk, per_core // 2, 1, 1, half)
            )
            return part.reshape(blk, width // 4)

        own = pick(xh, xl)
        other = lax.ppermute(pick(1 - xh, 1 - xl), X, [(0, 3), (3, 0), (1, 2), (2, 1)])
        upper = jnp.where(xh == 0, own, other)
        lower = jnp.where(xh == 0, other, own)
        mine = jnp.concatenate([upper, lower], axis=0)
        return mine, swap_core(mine)

    def multiply(a, b):
        mine, theirs = a
        inner = mine.shape[1]
        b_mine = lax.dynamic_slice_in_dim(b, core * inner, inner, 0)
        b_theirs = lax.dynamic_slice_in_dim(b, (1 - core) * inner, inner, 0)
        return jnp.dot(mine, b_mine, precision=HIGH) + jnp.dot(theirs, b_theirs, precision=HIGH)

    def piece(values):
        return lax.dynamic_slice(values, (xl * half, panel * blk), (half, blk))

    def sum_x(parts):
        return jnp.sum(lax.all_to_all(parts, X, split_axis=0, concat_axis=0, tiled=True), axis=0)

    def finish(partial):
        return sum_x(partial.reshape(4, half, blk)) * keep[row, column]

    def gathered(all_parts):
        parts = all_parts.reshape(nz // 2, 2, 2, half, blk)
        parts = jnp.where(core == 0, parts, parts[:, ::-1])
        return parts.transpose(2, 3, 0, 1, 4).reshape(blk, width)

    masked_z = masked(z_blocks, fill)
    y_panel = spread(piece(y_blocks) * fill[row, column], "y", ny).reshape(ny * half, blk)
    z_left = left(masked_z)
    z_panel = lax.all_gather(piece(masked_z), "y", axis=0)
    t_part = multiply(z_left, y_panel)
    mine = lax.dynamic_slice_in_dim(t_part, core * blk, blk, 0)
    theirs = swap_core(lax.dynamic_slice_in_dim(t_part, (1 - core) * blk, blk, 0))
    even = (panel % 2) == 0
    blocks = jnp.stack([jnp.where(even, mine, theirs), jnp.where(even, theirs, mine)])
    blocks = blocks.reshape(2, blk, 2, half).transpose(0, 2, 1, 3).reshape(4, blk, half)
    t_share = sum_x(blocks)
    t_row = 2 * y + core
    source = (z ^ xh) & 1
    t_col = per_core * source + (z ^ source)
    at_row = t_row * blk + lax.broadcasted_iota(jnp.int32, (blk, half), 0)
    at_col = t_col * blk + xl * half + lax.broadcasted_iota(jnp.int32, (blk, half), 1)
    q_share = jnp.where(at_row == at_col, 1.5, 0.0) - 0.5 * (keep[t_row, t_col] * t_share)
    q_mine = spread(q_share, "z", nz)
    q_theirs = swap_core(q_mine)
    ordered = z_panel.reshape(2, ny // 2, half, blk).transpose(1, 0, 2, 3)
    ordered = jnp.where(xh == 0, ordered, ordered[:, ::-1]).reshape(ny * half, blk)

    def rows_of(q):
        q = q.transpose(1, 0, 2).reshape(blk, nz * half)
        return jnp.dot(q, ordered, precision=HIGH)

    z_mine, z_theirs = rows_of(q_mine), rows_of(q_theirs)
    first = core == 0
    z_share = finish(
        jnp.stack([jnp.where(first, z_mine, z_theirs), jnp.where(first, z_theirs, z_mine)])
    )
    z_next_panel = spread(z_share, "y", ny).reshape(ny * half, blk)
    z_next = gathered(lax.all_gather(z_share, DEPTH, axis=0))
    h_left = left(masked(h_blocks, h_pattern))
    h_share = finish(multiply(h_left, z_next_panel))
    h_times_z = gathered(spread(h_share, DEPTH, 2 * nz))
    return (z_next, h_times_z)


def solution(mesh):
    parts = Mesh(mesh.devices.reshape(8, 2, 2, 8, 2), ("y", "xh", "core", "z", "xl"))
    spec = P(ROW, "core")
    return jax.shard_map(
        local,
        mesh=parts,
        in_specs=(spec, spec, spec, P(), P(), P()),
        out_specs=(spec, spec),
        check_vma=False,
    )
```

time: 971 us -> 324 us (0.33)
  waiting for transfers between devices: 921 us -> 180 us
  starting transfers between devices: 0.41 us -> 59.8 us
  local copies, waits for them, and re-layouts: 3.99 us -> 36.8 us
    psum x4 -> x0, waiting for transfers between devices: 460 us -> none  [from_root(): return lax.psum(jnp.where(mine, array, jnp.zeros_like(array)), axis)]
    reduce_scatter x3 -> x0, waiting for transfers between devices: 234 us -> none  [combine_depth(): lax.psum_scatter(partial_sum, 'depth', scatter_dimension=0, tiled=True)]
    all_gather x3 -> x2, waiting for transfers between devices: 225 us -> 97.5 us  [the longest x1 85.6 us: local(): z_next = gathered(lax.all_gather(z_share, DEPTH, axis=0))]
    all_to_all x0 -> x7, waiting for transfers between devices: none -> 72.5 us  [the longest x4 52.7 us: spread(): return lax.all_to_all(copies, axis, split_axis=0, concat_axis=0, tiled=True)]
    all_to_all x0 -> x7, starting transfers between devices: none -> 42.2 us  [the longest x4 30.5 us: spread(): return lax.all_to_all(copies, axis, split_axis=0, concat_axis=0, tiled=True)]
    ppermute x0 -> x6, starting transfers between devices: none -> 17.6 us  [the longest x2 9.93 us: left(): lax.ppermute(pick(1 - xh, 1 - xl), X, [(0, 3), (3, 0), (1, 2), (2, 1)])]
    reshape x0 -> x4, local copies, waits for them, and re-layouts: none -> 13.4 us  [the longest x2 6.79 us: left(): parts = values.reshape(blk, per_core // 2, 2, 2, half)]
    dynamic_slice x1 -> x6, local copies, waits for them, and re-layouts: 0.07 us -> 11.4 us  [the longest x1 9.33 us: pick(): lax.dynamic_slice(parts, (0, 0, a, b, 0), (blk, per_core // 2, 1, 1, half))]
  transfers between devices with their start and end apart: 10 -> 15, of which waited for: 10 -> 12; matrix products, arithmetic and copies ran while one was open for 0% -> 8% of each run, Pallas kernels for 0% -> 0%
where the time goes in v1:
time: 324 us; the launch traced here: 318 us
  waiting for transfers between devices  180 us (56%)
  starting transfers between devices  59.8 us (18%)
  local copies, waits for them, and re-layouts  36.8 us (11%)
  other arithmetic  20 us (6%)
  between operations  14.4 us (4%)
  matrix products  7.58 us (2%)
    all_gather x1, waiting for transfers between devices, local(): z_next = gathered(lax.all_gather(z_share, DEPTH, axis=0))  85.6 us
    all_to_all x4, waiting for transfers between devices, spread(): return lax.all_to_all(copies, axis, split_axis=0, concat_axis=0, tiled=True)  52.7 us
    all_to_all x4, starting transfers between devices, spread(): return lax.all_to_all(copies, axis, split_axis=0, concat_axis=0, tiled=True)  30.5 us
    all_to_all x3, waiting for transfers between devices, sum_x(): lax.all_to_all(parts, X, split_axis=0, concat_axis=0, tiled=True)  19.8 us
    all_gather x1, waiting for transfers between devices, local(): z_panel = lax.all_gather(piece(masked_z), 'y', axis=0)  11.9 us
    all_to_all x3, starting transfers between devices, sum_x(): lax.all_to_all(parts, X, split_axis=0, concat_axis=0, tiled=True)  11.7 us
    ppermute x2, starting transfers between devices, left(): lax.ppermute(pick(1 - xh, 1 - xl), X, [(0, 3), (3, 0), (1, 2), (2, 1)])  9.93 us
    dynamic_slice x1, local copies, waits for them, and re-layouts, pick(): lax.dynamic_slice(parts, (0, 0, a, b, 0), (blk, per_core // 2, 1, 1, half))  9.33 us
  transfers between devices with their start and end apart: 15, of which 12 were waited for; matrix products, arithmetic and copies ran while one was open for 8% of the time, Pallas kernels for 0%

profile of v1, /device:TPU:56, one launch (start us, length us, event | category | flops | bytes accessed | tf_op | source)
XLA Modules:
  0.0 318.4 jit_solution(8793874008769537520)
XLA Ops:
  7.2 0.8 fusion.14
  8.0 0.7 convert_element_type.10
  8.9 1.8 broadcast_multiply_fusion.1
  10.7 2.8 reshape.114
  13.5 3.2 %broadcast_multiply_fusion = f32[256,2048]{1,0:T(8,128)} fusion(f32[256,2048]{1,0:T(8,128)} %param.8, f32[2048]{0:T(1024)S(1)} %bitcast.78), kind=kLoop, calls=%fused_computation.9 | loop fusion | flops 524288 | bytes 4202496 | tf_op jit(solution)/shard_map/mul | solution.py:40
  16.7 4.0 %reshape.126 = f32[256,4,2,2,128]{4,3,2,1,0:T(2,128)} reshape(f32[256,2048]{1,0:T(8,128)} %broadcast_multiply_fusion) | data formatting | bytes 4194304 | tf_op jit(solution)/shard_map/reshape | solution.py:43
  20.7 9.3 %dynamic-slice_reduce_fusion.1 = (f32[256,4,128]{2,1,0:T(4,128)}, f32[256,4,128]{2,1,0:T(4,128)}, f32[256,4,128]{2,1,0:T(4,128)S(1)}, f32[256,4,128]{2,1,0:T(4,128)}) fusion(f32[256,4,2,2,128]{4,3,2,1,0:T(2,128)} %reshape.126, s32[]{:T(128)S(6)} %select_n.147, s32[]{:T(128)S(6)} %select_n.148, s32[]{:T(128)S(6)} %select_n.149, s32[]{:T(128)S(6)} %select_n.150, ...), kind=kLoop, calls=%fused_computation.26 | loop fusion | bytes 4194320 | tf_op jit(solution)/shard_map/dynamic_slice | solution.py:46
  30.1 4.7 %collective-permute-start = (f32[256,512]{1,0:T(8,128)S(1)}, f32[256,512]{1,0:T(8,128)S(1)}, u32[]{:S(2)}, u32[]{:S(2)}) collective-permute-start(f32[256,512]{1,0:T(8,128)S(1)} %bitcast.77), channel_id=1, source_target_pairs={{0,33},{33,0},{1,32},{32,1},{2,35},{35,2},{3,34},{34,3},{4,37},{37... | collective-permute-start | bytes 1572872 | tf_op jit(solution)/shard_map/ppermute | solution.py:52
  34.8 0.6 dynamic_slice.62
  35.4 1.6 dynamic-slice_multiply_fusion
  36.9 1.1 broadcast_in_dim.46
  38.0 6.9 %all-to-all-start = ((f32[8,128,256]{2,1,0:T(8,128)}), f32[8,128,256]{2,1,0:T(8,128)}, u32[]{:S(2)}, u32[]{:S(2)}) async-start(f32[8,128,256]{2,1,0:T(8,128)} %broadcast_in_dim.46), calls=%async_computation | async-start | bytes 2097152 | tf_op jit(solution)/shard_map/all_to_all | solution.py:15
  44.9 2.0 collective-permute-done
  46.9 0.8 copy-done.4
  47.7 1.3 bitcast_select_fusion.3
  49.0 1.0 pad_maximum_fusion
  50.0 1.9 collective-permute-start.1
  51.9 3.0 collective-permute-done.1
  54.9 14.0 %all-to-all-done = f32[8,128,256]{2,1,0:T(8,128)} async-done(((f32[8,128,256]{2,1,0:T(8,128)}), f32[8,128,256]{2,1,0:T(8,128)}, u32[]{:S(2)}, u32[]{:S(2)}) %all-to-all-start) | async-done | bytes 1048608 | tf_op jit(solution)/shard_map/all_to_all | solution.py:15
  68.9 2.0 fusion.6
  70.8 1.6 convolution_add_fusion.1
  72.5 0.8 copy-done
  73.3 1.9 collective-permute-start.2
  75.3 1.5 collective-permute-done.2
  76.7 1.0 select_bitcast_fusion.3
  77.7 0.8 fusion.2
  78.6 3.5 %all-to-all-start.1 = ((f32[4,256,128]{2,1,0:T(8,128)}), f32[4,256,128]{2,1,0:T(8,128)S(1)}, u32[]{:S(2)}, u32[]{:S(2)}) async-start(f32[4,256,128]{2,1,0:T(8,128)} %bitcast.6), calls=%async_computation.1 | async-start | bytes 1048576 | tf_op jit(solution)/shard_map/all_to_all | solution.py:69
  82.1 0.7 fusion.15
  82.8 9.3 %all-to-all-done.1 = f32[4,256,128]{2,1,0:T(8,128)S(1)} async-done(((f32[4,256,128]{2,1,0:T(8,128)}), f32[4,256,128]{2,1,0:T(8,128)S(1)}, u32[]{:S(2)}, u32[]{:S(2)}) %all-to-all-start.1) | async-done | bytes 524320 | tf_op jit(solution)/shard_map/all_to_all | solution.py:69
  92.1 0.7 multiply_subtract_fusion
  93.0 1.1 broadcast_in_dim.47
  94.0 10.3 %all-to-all-start.2 = ((f32[8,256,128]{1,2,0:T(8,128)}), f32[8,256,128]{1,2,0:T(8,128)S(1)}, u32[]{:S(2)}, u32[]{:S(2)}) async-start(f32[8,256,128]{1,2,0:T(8,128)} %broadcast_in_dim.47), calls=%async_computation.2 | async-start | bytes 2097152 | tf_op jit(solution)/shard_map/all_to_all | solution.py:15
  104.4 0.7 dynamic_slice.67
  105.1 27.5 %all-to-all-done.2 = f32[8,256,128]{1,2,0:T(8,128)S(1)} async-done(((f32[8,256,128]{1,2,0:T(8,128)}), f32[8,256,128]{1,2,0:T(8,128)S(1)}, u32[]{:S(2)}, u32[]{:S(2)}) %all-to-all-start.2) | async-done | bytes 1048608 | tf_op jit(solution)/shard_map/all_to_all | solution.py:15
  132.5 1.9 collective-permute-start.3
  134.5 11.9 %all-gather.5.cloned.1.call-done = f32[1024,256]{1,0:T(8,128)} async-done(((f32[128,256]{1,0:T(8,128)}), f32[1024,256]{1,0:T(8,128)}) %all-gather.5.cloned.1.call-update) | async-done | bytes 1048592 | tf_op jit(solution)/shard_map/all_gather | solution.py:82
  146.3 1.8 reverse_select_fusion.2
  148.2 1.0 fusion.16
  149.2 1.0 select_bitcast_fusion.1
  150.2 0.8 pad_maximum_fusion.3
  151.1 4.1 %all-to-all-start.3 = ((f32[4,128,256]{2,1,0:T(8,128)}), f32[4,128,256]{2,1,0:T(8,128)S(1)}, u32[]{:S(2)}, u32[]{:S(2)}) async-start(f32[4,128,256]{2,1,0:T(8,128)} %bitcast.17), calls=%async_computation.3 | async-start | bytes 1048576 | tf_op jit(solution)/shard_map/all_to_all | solution.py:69
  155.1 0.8 copy.27
  155.9 5.3 %collective-permute-start.4 = (f32[256,512]{1,0:T(8,128)}, f32[256,512]{1,0:T(8,128)S(1)}, u32[]{:S(2)}, u32[]{:S(2)}) collective-permute-start(f32[256,512]{1,0:T(8,128)} %bitcast.62), channel_id=1, source_target_pairs={{0,33},{33,0},{1,32},{32,1},{2,35},{35,2},{3,34},{34,3},{4,37},{37... | collective-permute-start | bytes 1572872 | tf_op jit(solution)/shard_map/ppermute | solution.py:52
  161.2 3.2 all-to-all-done.3
  164.4 0.7 broadcast_multiply_fusion.3
  165.1 1.1 broadcast_in_dim.50
  166.2 6.1 %all-to-all-start.4 = ((f32[8,128,256]{2,1,0:T(8,128)}), f32[8,128,256]{2,1,0:T(8,128)S(1)}, u32[]{:S(2)}, u32[]{:S(2)}) async-start(f32[8,128,256]{2,1,0:T(8,128)} %broadcast_in_dim.50), calls=%async_computation.4 | async-start | bytes 2097152 | tf_op jit(solution)/shard_map/all_to_all | solution.py:15
  172.5 1.9 collective-permute-start.5
  174.4 2.6 collective-permute-done.5
  177.0 11.3 %all-to-all-done.4 = f32[8,128,256]{2,1,0:T(8,128)S(1)} async-done(((f32[8,128,256]{2,1,0:T(8,128)}), f32[8,128,256]{2,1,0:T(8,128)S(1)}, u32[]{:S(2)}, u32[]{:S(2)}) %all-to-all-start.4) | async-done | bytes 1048608 | tf_op jit(solution)/shard_map/all_to_all | solution.py:15
  188.3 0.6 fusion.3
  188.9 1.4 convolution_add_fusion
  190.3 4.2 %all-to-all-start.5 = ((f32[4,128,256]{2,1,0:T(8,128)}), f32[4,128,256]{2,1,0:T(8,128)S(1)}, u32[]{:S(2)}, u32[]{:S(2)}) async-start(f32[4,128,256]{2,1,0:T(8,128)} %bitcast.23), calls=%async_computation.5 | async-start | bytes 1048576 | tf_op jit(solution)/shard_map/all_to_all | solution.py:69
  194.4 0.7 all-gather.7.cloned.1.call-update
  195.2 7.3 %all-to-all-done.5 = f32[4,128,256]{2,1,0:T(8,128)S(1)} async-done(((f32[4,128,256]{2,1,0:T(8,128)}), f32[4,128,256]{2,1,0:T(8,128)S(1)}, u32[]{:S(2)}, u32[]{:S(2)}) %all-to-all-start.5) | async-done | bytes 524320 | tf_op jit(solution)/shard_map/all_to_all | solution.py:69
  202.6 0.7 broadcast_multiply_fusion.2
  203.3 1.5 broadcast_in_dim.51
  204.8 7.2 %all-to-all-start.6 = ((f32[16,128,256]{2,1,0:T(8,128)}), f32[16,128,256]{2,1,0:T(8,128)S(1)}, u32[]{:S(2)}, u32[]{:S(2)}) async-start(f32[16,128,256]{2,1,0:T(8,128)} %broadcast_in_dim.51), calls=%async_computation.6 | async-start | bytes 4194304 | tf_op jit(solution)/shard_map/all_to_all | solution.py:15
  212.1 85.6 %all-gather.7.cloned.1.call-done = f32[2048,256]{1,0:T(8,128)} async-done(((f32[128,256]{1,0:T(8,128)}), f32[2048,256]{1,0:T(8,128)}) %all-gather.7.cloned.1.call-update) | async-done | bytes 2097168 | tf_op jit(solution)/shard_map/all_gather | solution.py:111
  297.7 2.5 fusion
  300.2 2.9 copy.13
  303.2 3.9 %reshape.125 = f32[256,2048]{1,0:T(8,128)} reshape(f32[2,128,4,2,256]{4,3,2,1,0:T(2,128)} %copy.13) | data formatting | bytes 4194304 | tf_op jit(solution)/shard_map/reshape | solution.py:77
  307.2 1.6 copy.14
  308.9 2.7 reshape.132
  (35 shorter events, 1.1 us)
Async XLA Ops:
  30.1 16.8 %collective-permute-start = (f32[256,512]{1,0:T(8,128)S(1)}, f32[256,512]{1,0:T(8,128)S(1)}, u32[]{:S(2)}, u32[]{:S(2)}) collective-permute-start(f32[256,512]{1,0:T(8,128)S(1)} %bitcast.77), channel_id=1, source_target_pairs={{0,33},{33,0},{1,32},{32,1},{2,35},{35,2},{3,34},{34,3},{4,37},{37... | collective-permute-start | bytes 1572872 | tf_op jit(solution)/shard_map/ppermute | solution.py:52
  38.0 30.9 %all-to-all-start = ((f32[8,128,256]{2,1,0:T(8,128)}), f32[8,128,256]{2,1,0:T(8,128)}, u32[]{:S(2)}, u32[]{:S(2)}) async-start(f32[8,128,256]{2,1,0:T(8,128)} %broadcast_in_dim.46), calls=%async_computation | async-start | bytes 2097152 | tf_op jit(solution)/shard_map/all_to_all | solution.py:15
  46.8 0.8 copy-start.4
  50.0 4.9 %collective-permute-start.1 = (f32[512,512]{1,0:T(8,128)}, f32[512,512]{1,0:T(8,128)}, u32[]{:S(2)}, u32[]{:S(2)}) collective-permute-start(f32[512,512]{1,0:T(8,128)} %pad_maximum_fusion), channel_id=1, source_target_pairs={{0,16},{16,0},{1,17},{17,1},{2,18},{18,2},{3,19},{19,3},{4,20},{20... | collective-permute-start | bytes 3145736 | tf_op jit(solution)/shard_map/ppermute | solution.py:19
  72.5 0.8 copy-start
  73.3 3.4 %collective-permute-start.2 = (f32[256,256]{1,0:T(8,128)S(1)}, f32[256,256]{1,0:T(8,128)S(1)}, u32[]{:S(2)}, u32[]{:S(2)}) collective-permute-start(f32[256,256]{1,0:T(8,128)S(1)} %constant_dynamic-slice_fusion), channel_id=1, source_target_pairs={{0,16},{16,0},{1,17},{17,1},{2,18},{18,2},{3,19},{19,3},{4,20},{20... | collective-permute-start | bytes 786440 | tf_op jit(solution)/shard_map/ppermute | solution.py:19
  75.2 6.8 %copy-start.5 = (s32[16,16]{1,0:T(8,128)S(1)}, s32[16,16]{1,0:T(8,128)}, u32[]{:S(2)}) copy-start(s32[16,16]{1,0:T(8,128)} %param.11) | copy-start | bytes 3076
  78.6 13.5 %all-to-all-start.1 = ((f32[4,256,128]{2,1,0:T(8,128)}), f32[4,256,128]{2,1,0:T(8,128)S(1)}, u32[]{:S(2)}, u32[]{:S(2)}) async-start(f32[4,256,128]{2,1,0:T(8,128)} %bitcast.6), calls=%async_computation.1 | async-start | bytes 1048576 | tf_op jit(solution)/shard_map/all_to_all | solution.py:69
  94.0 38.5 %all-to-all-start.2 = ((f32[8,256,128]{1,2,0:T(8,128)}), f32[8,256,128]{1,2,0:T(8,128)S(1)}, u32[]{:S(2)}, u32[]{:S(2)}) async-start(f32[8,256,128]{1,2,0:T(8,128)} %broadcast_in_dim.47), calls=%async_computation.2 | async-start | bytes 2097152 | tf_op jit(solution)/shard_map/all_to_all | solution.py:15
  104.3 42.0 %all-gather.5.cloned.1.call-start = ((), (), s32[]{:S(2)}) async-start(), calls=%async_computation.7 | async-start | bytes 1179648 | tf_op jit(solution)/shard_map/all_gather | solution.py:82
  132.5 16.7 %collective-permute-start.3 = (f32[8,256,128]{1,2,0:T(8,128)S(1)}, f32[8,256,128]{1,2,0:T(8,128)S(1)}, u32[]{:S(2)}, u32[]{:S(2)}) collective-permute-start(f32[8,256,128]{1,2,0:T(8,128)S(1)} %all-to-all-done.2), channel_id=1, source_target_pairs={{0,16},{16,0},{1,17},{17,1},{2,18},{18,2},{3,19},{19,3},{4,20},{20... | collective-permute-start | bytes 3145736 | tf_op jit(solution)/shard_map/ppermute | solution.py:19
  149.2 5.9 %copy-start.2 = (f32[256,4,128]{2,1,0:T(4,128)S(1)}, f32[256,4,128]{2,1,0:T(4,128)}, u32[]{:S(2)}) copy-start(f32[256,4,128]{2,1,0:T(4,128)} %get-tuple-element.3) | copy-start | bytes 1572868
  151.1 13.3 %all-to-all-start.3 = ((f32[4,128,256]{2,1,0:T(8,128)}), f32[4,128,256]{2,1,0:T(8,128)S(1)}, u32[]{:S(2)}, u32[]{:S(2)}) async-start(f32[4,128,256]{2,1,0:T(8,128)} %bitcast.17), calls=%async_computation.3 | async-start | bytes 1048576 | tf_op jit(solution)/shard_map/all_to_all | solution.py:69
  155.9 16.3 %copy-start.1 = (f32[256,4,128]{2,1,0:T(4,128)S(1)}, f32[256,4,128]{2,1,0:T(4,128)}, u32[]{:S(2)}) copy-start(f32[256,4,128]{2,1,0:T(4,128)} %get-tuple-element.2) | copy-start | bytes 1572868
  155.9 16.3 %collective-permute-start.4 = (f32[256,512]{1,0:T(8,128)}, f32[256,512]{1,0:T(8,128)S(1)}, u32[]{:S(2)}, u32[]{:S(2)}) collective-permute-start(f32[256,512]{1,0:T(8,128)} %bitcast.62), channel_id=1, source_target_pairs={{0,33},{33,0},{1,32},{32,1},{2,35},{35,2},{3,34},{34,3},{4,37},{37... | collective-permute-start | bytes 1572872 | tf_op jit(solution)/shard_map/ppermute | solution.py:52
  165.1 7.3 %copy-start.3 = (f32[128,256]{1,0:T(8,128)}, f32[128,256]{1,0:T(8,128)S(1)}, u32[]{:S(2)}) copy-start(f32[128,256]{1,0:T(8,128)S(1)} %broadcast_multiply_fusion.3) | copy-start | bytes 393220
  166.2 22.1 %all-to-all-start.4 = ((f32[8,128,256]{2,1,0:T(8,128)}), f32[8,128,256]{2,1,0:T(8,128)S(1)}, u32[]{:S(2)}, u32[]{:S(2)}) async-start(f32[8,128,256]{2,1,0:T(8,128)} %broadcast_in_dim.50), calls=%async_computation.4 | async-start | bytes 2097152 | tf_op jit(solution)/shard_map/all_to_all | solution.py:15
  172.5 4.6 %collective-permute-start.5 = (f32[512,512]{1,0:T(8,128)S(1)}, f32[512,512]{1,0:T(8,128)S(1)}, u32[]{:S(2)}, u32[]{:S(2)}) collective-permute-start(f32[512,512]{1,0:T(8,128)S(1)} %pad_maximum_fusion.1), channel_id=1, source_target_pairs={{0,16},{16,0},{1,17},{17,1},{2,18},{18,2},{3,19},{19,3},{4,20},{20... | collective-permute-start | bytes 3145736 | tf_op jit(solution)/shard_map/ppermute | solution.py:19
  190.3 12.2 %all-to-all-start.5 = ((f32[4,128,256]{2,1,0:T(8,128)}), f32[4,128,256]{2,1,0:T(8,128)S(1)}, u32[]{:S(2)}, u32[]{:S(2)}) async-start(f32[4,128,256]{2,1,0:T(8,128)} %bitcast.23), calls=%async_computation.5 | async-start | bytes 1048576 | tf_op jit(solution)/shard_map/all_to_all | solution.py:69
  194.4 103.2 %all-gather.7.cloned.1.call-start = ((), (), s32[]{:S(2)}) async-start(), calls=%async_computation.8 | async-start | bytes 2228224 | tf_op jit(solution)/shard_map/all_gather | solution.py:111
  204.8 102.2 %all-to-all-start.6 = ((f32[16,128,256]{2,1,0:T(8,128)}), f32[16,128,256]{2,1,0:T(8,128)S(1)}, u32[]{:S(2)}, u32[]{:S(2)}) async-start(f32[16,128,256]{2,1,0:T(8,128)} %broadcast_in_dim.51), calls=%async_computation.6 | async-start | bytes 4194304 | tf_op jit(solution)/shard_map/all_to_all | solution.py:15
Sparse Core Ops, SparseCore 0:
  107.8 38.4 all-gather.4
  197.3 100.2 all-gather.6

commit v2 on v1

v2 whole, which is shorter than its diff:
```python
import jax
import jax.numpy as jnp
from jax import lax
from jax.experimental import pallas as pl
from jax.experimental.pallas import tpu as pltpu
from jax.sharding import Mesh
from jax.sharding import PartitionSpec as P

X = ("xh", "xl")
ROW = ("y", "xh")
HIGH = lax.Precision.HIGH


def spread(piece, axis, n):
    copies = jnp.broadcast_to(piece[None], (n,) + piece.shape)
    return lax.all_to_all(copies, axis, split_axis=0, concat_axis=0, tiled=True)


def swap(array, axis):
    return lax.ppermute(array, axis, [(0, 1), (1, 0)])


def place(own, other, blk):
    layers = own[0].shape[0]
    rows = own[0].shape[1]
    n = len(own)

    def kernel(*refs):
        out, sem = refs[2 * n], refs[2 * n + 1]
        xl = lax.axis_index("xl")
        core = lax.axis_index("core")
        copies = []
        for k in range(2 * n):
            mine = xl if k < n else 1 - xl
            at = pl.multiple_of(mine * (n * rows) + (k % n) * rows, rows)
            for layer in range(layers):
                to = pl.multiple_of((layer ^ core) * blk, blk)
                copies.append(
                    pltpu.make_async_copy(
                        refs[k].at[layer],
                        out.at[pl.ds(at, rows), pl.ds(to, blk)],
                        sem.at[k * layers + layer],
                    )
                )
        for copy in copies:
            copy.start()
        for copy in copies:
            copy.wait()

    return pl.pallas_call(
        kernel,
        out_shape=jax.ShapeDtypeStruct((2 * n * rows, layers * blk), own[0].dtype),
        in_specs=[pl.BlockSpec(memory_space=pl.ANY)] * (2 * n),
        out_specs=pl.BlockSpec(memory_space=pl.ANY),
        scratch_shapes=[pltpu.SemaphoreType.DMA((2 * n * layers,))],
    )(*own, *other)


def local(y_blocks, z_blocks, h_blocks, s_pattern, h_pattern, keep_mask):
    blk, width = y_blocks.shape
    half = blk // 2
    per_core = width // blk
    ny, nz = lax.axis_size("y"), lax.axis_size("z")
    y = lax.axis_index("y")
    xh = lax.axis_index("xh")
    core = lax.axis_index("core")
    z = lax.axis_index("z")
    xl = lax.axis_index("xl")
    row = 2 * y + xh
    panel = z ^ core
    column = per_core * core + panel
    keep = keep_mask.astype(jnp.float32)
    fill = s_pattern.astype(jnp.float32)

    def left(values, pattern):
        def pick(a, b):
            return jnp.concatenate(
                [
                    lax.dynamic_slice(values, (0, (2 * m + a) * blk + b * half), (blk, half))
                    * pattern[row, per_core * core + 2 * m + a]
                    for m in range(per_core // 2)
                ],
                axis=1,
            )

        own = pick(xh, xl)
        other = lax.ppermute(pick(1 - xh, 1 - xl), X, [(0, 3), (3, 0), (1, 2), (2, 1)])
        return own, other

    def multiply(mine, theirs, b):
        inner = mine.shape[1]
        b_mine = lax.dynamic_slice_in_dim(b, core * inner, inner, 0)
        b_theirs = lax.dynamic_slice_in_dim(b, (1 - core) * inner, inner, 0)
        return jnp.dot(mine, b_mine, precision=HIGH) + jnp.dot(theirs, b_theirs, precision=HIGH)

    def piece(values):
        return lax.dynamic_slice(values, (xl * half, panel * blk), (half, blk)) * fill[row, column]

    def sum_x(parts):
        return jnp.sum(lax.all_to_all(parts, X, split_axis=0, concat_axis=0, tiled=True), axis=0)

    def finish(partial):
        return sum_x(partial.reshape(4, half, blk)) * keep[row, column]

    y_copies = jnp.broadcast_to(piece(y_blocks)[None], (ny, half, blk))
    y_copies, z_blocks, h_blocks = lax.optimization_barrier((y_copies, z_blocks, h_blocks))
    y_panel = lax.all_to_all(y_copies, "y", split_axis=0, concat_axis=0, tiled=True)
    y_panel = y_panel.reshape(ny * half, blk)
    z_panel = lax.all_gather(piece(z_blocks), "y", axis=0)
    z_left = jnp.concatenate(left(z_blocks, fill), axis=0)
    t_part = multiply(z_left, swap(z_left, "core"), y_panel)
    at = (core ^ xh) * blk
    mine = lax.dynamic_slice_in_dim(t_part, at, blk, 0)
    theirs = swap(lax.dynamic_slice_in_dim(t_part, blk - at, blk, 0), "core")
    even = (panel % 2) == 0
    blocks = jnp.stack([jnp.where(even, mine, theirs), jnp.where(even, theirs, mine)])
    blocks = blocks.reshape(2, blk, 2, half).transpose(0, 2, 1, 3).reshape(4, blk, half)
    blocks, z_panel = lax.optimization_barrier((blocks, z_panel))
    t_share = sum_x(blocks)
    t_row = 2 * y + core
    source = (z ^ xh) & 1
    t_col = per_core * source + (z ^ source)
    at_row = t_row * blk + lax.broadcasted_iota(jnp.int32, (blk, half), 0)
    at_col = t_col * blk + xl * half + lax.broadcasted_iota(jnp.int32, (blk, half), 1)
    q_share = jnp.where(at_row == at_col, 1.5, 0.0) - 0.5 * (keep[t_row, t_col] * t_share)
    q_mine = spread(q_share, "z", nz)
    q_theirs = swap(q_mine, "core")
    ordered = z_panel.reshape(2, ny // 2, half, blk).transpose(1, 0, 2, 3)
    ordered = jnp.where(xh == 0, ordered, ordered[:, ::-1]).reshape(ny * half, blk)

    def rows_of(q):
        q = q.transpose(1, 0, 2).reshape(blk, nz * half)
        return jnp.dot(q, ordered, precision=HIGH)

    z_mine, z_theirs = rows_of(q_mine), rows_of(q_theirs)
    first = core == 0
    z_share = finish(
        jnp.stack([jnp.where(first, z_mine, z_theirs), jnp.where(first, z_theirs, z_mine)])
    )
    z_next_panel = spread(z_share, "y", ny).reshape(ny * half, blk)
    z_own = lax.all_gather(z_share, "z", axis=0)
    own, other = left(h_blocks, h_pattern.astype(jnp.float32))
    own, other = jnp.where(xh == 0, own, other), jnp.where(xh == 0, other, own)
    h_left = jnp.concatenate([own, other], axis=0)
    h_partial = multiply(h_left, swap(h_left, "core"), z_next_panel)
    h_share = finish(h_partial)
    h_share, z_own = lax.optimization_barrier((h_share, z_own))
    z_next = place([z_own], [swap(z_own, "xl")], blk)
    h_own = [spread(h_share[k * half // 2 : (k + 1) * half // 2], "z", nz) for k in range(2)]
    h_times_z = place(h_own, [swap(part, "xl") for part in h_own], blk)
    return (z_next, h_times_z)


def solution(mesh):
    parts = Mesh(mesh.devices.reshape(8, 2, 2, 8, 2), ("y", "xh", "core", "z", "xl"))
    spec = P(ROW, "core")
    return jax.shard_map(
        local,
        mesh=parts,
        in_specs=(spec, spec, spec, P(), P(), P()),
        out_specs=(spec, spec),
        check_vma=False,
    )
```

time: 324 us -> 395 us (1.22)
  Pallas kernels: 0 us -> 130 us
  waiting for transfers between devices: 180 us -> 108 us
  blocking collectives: 0 us -> 57.9 us
  local copies, waits for them, and re-layouts: 36.8 us -> 7.03 us
  starting transfers between devices: 59.8 us -> 50.7 us
    pallas_call x0 -> x2, Pallas kernels: none -> 130 us  [place(): pl.pallas_call(kernel, out_shape=jax.ShapeDtypeStruct((2 * n * rows, laye...]
    all_to_all x0 -> x3, blocking collectives: none -> 57.9 us  [the longest x2 47.5 us: spread(): return lax.all_to_all(copies, axis, split_axis=0, concat_axis=0, tiled=True)]
    all_gather x2, waiting for transfers between devices: 97.5 us -> 46 us  [the longest x1 37.8 us: local(): z_panel = lax.all_gather(piece(z_blocks), 'y', axis=0)]
    all_to_all x4 -> x2, waiting for transfers between devices: 52.7 us -> 20.7 us  [spread(): return lax.all_to_all(copies, axis, split_axis=0, concat_axis=0, tiled=True)]
    all_to_all x4 -> x2, starting transfers between devices: 30.5 us -> 9.1 us  [spread(): return lax.all_to_all(copies, axis, split_axis=0, concat_axis=0, tiled=True)]
    ppermute x2, waiting for transfers between devices: 1.99 us -> 16.2 us  [left(): lax.ppermute(pick(1 - xh, 1 - xl), X, [(0, 3), (3, 0), (1, 2), (2, 1)])]
    reshape x4 -> x0, local copies, waits for them, and re-layouts: 13.4 us -> none  [the longest x2 6.79 us: left(): parts = values.reshape(blk, per_core // 2, 2, 2, half)]
    all_to_all x3 -> x2, waiting for transfers between devices: 19.8 us -> 8.07 us  [sum_x(): lax.all_to_all(parts, X, split_axis=0, concat_axis=0, tiled=True)]
  transfers between devices with their start and end apart: 15 -> 16, of which waited for: 12 -> 12; matrix products, arithmetic and copies ran while one was open for 8% -> 5% of each run, Pallas kernels for 0% -> 16%
where the time goes in v2:
time: 395 us; the launch traced here: 393 us
  Pallas kernels  130 us (33%)
  waiting for transfers between devices  108 us (27%)
  blocking collectives  57.9 us (15%)
  starting transfers between devices  50.7 us (13%)
  other arithmetic  20.8 us (5%)
  between operations  14.6 us (4%)
  local copies, waits for them, and re-layouts  7.03 us (2%)
  matrix products  4.37 us (1%)
    pallas_call x2, Pallas kernels, place(): pl.pallas_call(kernel, out_shape=jax.ShapeDtypeStruct((2 * n * rows, laye...  130 us
    all_to_all x2, blocking collectives, spread(): return lax.all_to_all(copies, axis, split_axis=0, concat_axis=0, tiled=True)  47.5 us
    all_gather x1, waiting for transfers between devices, local(): z_panel = lax.all_gather(piece(z_blocks), 'y', axis=0)  37.8 us
    all_to_all x2, waiting for transfers between devices, spread(): return lax.all_to_all(copies, axis, split_axis=0, concat_axis=0, tiled=True)  20.7 us
    ppermute x7, starting transfers between devices, swap(): return lax.ppermute(array, axis, [(0, 1), (1, 0)])  17.2 us
    ppermute x7, waiting for transfers between devices, swap(): return lax.ppermute(array, axis, [(0, 1), (1, 0)])  17.1 us
    ppermute x2, waiting for transfers between devices, left(): lax.ppermute(pick(1 - xh, 1 - xl), X, [(0, 3), (3, 0), (1, 2), (2, 1)])  16.2 us
    all_to_all x1, blocking collectives, sum_x(): lax.all_to_all(parts, X, split_axis=0, concat_axis=0, tiled=True)  10.5 us
  transfers between devices with their start and end apart: 16, of which 12 were waited for; matrix products, arithmetic and copies ran while one was open for 5% of the time, Pallas kernels for 16%

profile of v2, /device:TPU:56, one launch (start us, length us, event | category | flops | bytes accessed | tf_op | source)
XLA Modules:
  0.0 393.1 jit_solution(7135067433414498904)
XLA Ops:
  7.2 0.8 convert_element_type.11
  8.1 0.7 convert_element_type.9
  8.8 0.7 fusion.15
  9.4 1.6 dynamic-slice_multiply_fusion.17
  11.0 1.1 broadcast_in_dim.18
  12.1 8.6 %all-to-all-start = ((f32[8,128,256]{2,1,0:T(8,128)}), f32[8,128,256]{2,1,0:T(8,128)S(1)}, u32[]{:S(2)}, u32[]{:S(2)}) async-start(f32[8,128,256]{2,1,0:T(8,128)} %broadcast_in_dim.18), calls=%async_computation | async-start | bytes 2097152 | tf_op jit(solution)/shard_map/all_to_all | solution.py:107
  20.7 5.1 %dynamic-slice_multiply_fusion.8 = (f32[256,128]{1,0:T(8,128)S(1)}, f32[256,128]{1,0:T(8,128)S(1)}, f32[256,128]{1,0:T(8,128)S(1)}, f32[256,128]{1,0:T(8,128)S(1...) fusion(f32[256,2048]{1,0:T(8,128)S(1)} %copy-done.6, ...), kind=kLoop, calls=%fused_computation.35 | loop fusion | flops 262144 | bytes 2097216 | tf_op jit(solution)/shard_map/mul | solution.py:79
  25.9 2.9 collective-permute-start.1
  28.8 11.5 %collective-permute-done.1 = f32[256,512]{1,0:T(8,128)S(1)} collective-permute-done((f32[256,512]{1,0:T(8,128)S(1)}, f32[256,512]{1,0:T(8,128)S(1)}, u32[]{:S(2)}, u32[]{:S(2)}) %collective-permute-start.1) | collective-permute-done | bytes 524320 | tf_op jit(solution)/shard_map/ppermute | solution.py:87
  40.3 0.8 copy-done.10
  41.1 0.1 pad_maximum_fusion.1
  41.2 1.9 collective-permute-start.2
  43.1 2.2 dynamic-slice_multiply_fusion
  45.4 0.3 collective-permute-done.2
  45.7 0.6 fusion.4
  46.3 0.3 copy-done.8
  46.6 0.2 copy-done.11
  46.8 0.6 convolution_add_fusion.1
  47.5 2.1 collective-permute-start.3
  49.6 1.3 collective-permute-done.3
  51.0 0.8 fusion
  51.8 37.8 %all-gather.5.cloned.1.call-done = f32[1024,256]{1,0:T(8,128)} async-done(((f32[128,256]{1,0:T(8,128)}), f32[1024,256]{1,0:T(8,128)}) %all-gather.5.cloned.1.call-update) | async-done | bytes 1048592 | tf_op jit(solution)/shard_map/all_gather | solution.py:109
  89.6 4.3 %all-to-all-start.1 = ((f32[4,256,128]{2,1,0:T(8,128)}), f32[4,256,128]{2,1,0:T(8,128)S(1)}, u32[]{:S(2)}, u32[]{:S(2)}) async-start(f32[4,256,128]{2,1,0:T(8,128)} %bitcast.21), calls=%async_computation.1 | async-start | bytes 1048576 | tf_op jit(solution)/shard_map/all_to_all | solution.py:100
  94.0 8.1 %all-to-all-done.1 = f32[4,256,128]{2,1,0:T(8,128)S(1)} async-done(((f32[4,256,128]{2,1,0:T(8,128)}), f32[4,256,128]{2,1,0:T(8,128)S(1)}, u32[]{:S(2)}, u32[]{:S(2)}) %all-to-all-start.1) | async-done | bytes 524320 | tf_op jit(solution)/shard_map/all_to_all | solution.py:100
  102.1 0.7 multiply_subtract_fusion
  102.8 0.1 copy.9
  102.9 0.1 broadcast_in_dim.21
  103.0 30.3 %all_to_all.40 = f32[8,256,128]{1,2,0:T(8,128)S(1)} all-to-all(f32[8,256,128]{1,2,0:T(8,128)S(1)} %broadcast_in_dim.21), channel_id=1, replica_groups=mesh['y'=8,'xh'=2,'core'=2,'z'=8,'xl'=2] {'z'}, dimensions={0} | all-to-all | bytes 2097152 | tf_op jit(solution)/shard_map/all_to_all | solution.py:16
  133.3 1.9 collective-permute-start.4
  135.3 0.1 reverse_select_fusion
  135.4 0.1 copy.10
  135.5 1.0 fusion.18
  136.5 1.4 collective-permute-done.4
  137.9 1.0 select_bitcast_fusion.1
  138.9 0.8 pad_maximum_fusion.6
  139.7 3.5 all-to-all-start.3
  143.2 0.7 fusion.17
  143.9 5.1 %dynamic-slice_multiply_fusion.16 = (f32[256,128]{1,0:T(8,128)S(1)}, f32[256,128]{1,0:T(8,128)S(1)}, f32[256,128]{1,0:T(8,128)S(1)}, f32[256,128]{1,0:T(8,128)S(...) fusion(f32[256,2048]{1,0:T(8,128)S(1)} %copy-done.9, ...), kind=kLoop, calls=%fused_computation.43 | loop fusion | flops 262144 | bytes 2097216 | tf_op jit(solution)/shard_map/mul | solution.py:79
  149.1 5.1 %collective-permute-start = (f32[256,512]{1,0:T(8,128)S(1)}, f32[256,512]{1,0:T(8,128)S(1)}, u32[]{:S(2)}, u32[]{:S(2)}) collective-permute-start(f32[256,512]{1,0:T(8,128)S(1)} %pad_maximum_fusion.4), channel_id=1, source_target_pairs={{0,33},{33,0},{1,32},{32,1},{2,35},{35,2},{3,34},{34,3},{4,37},{37... | collective-permute-start | bytes 1572872 | tf_op jit(solution)/shard_map/ppermute | solution.py:87
  154.2 0.6 broadcast_multiply_fusion.1
  154.9 1.1 broadcast_in_dim.22
  155.9 5.6 %all-to-all-start.4 = ((f32[8,128,256]{2,1,0:T(8,128)}), f32[8,128,256]{2,1,0:T(8,128)S(1)}, u32[]{:S(2)}, u32[]{:S(2)}) async-start(f32[8,128,256]{2,1,0:T(8,128)} %broadcast_in_dim.22), calls=%async_computation.4 | async-start | bytes 2097152 | tf_op jit(solution)/shard_map/all_to_all | solution.py:16
  161.5 4.6 %collective-permute-done = f32[256,512]{1,0:T(8,128)S(1)} collective-permute-done((f32[256,512]{1,0:T(8,128)S(1)}, f32[256,512]{1,0:T(8,128)S(1)}, u32[]{:S(2)}, u32[]{:S(2)}) %collective-permute-start) | collective-permute-done | bytes 524320 | tf_op jit(solution)/shard_map/ppermute | solution.py:87
  166.2 0.1 fusion.8
  166.3 1.0 pad_maximum_fusion
  167.3 1.9 collective-permute-start.5
  169.3 2.8 collective-permute-done.5
  172.1 13.3 %all-to-all-done.4 = f32[8,128,256]{2,1,0:T(8,128)S(1)} async-done(((f32[8,128,256]{2,1,0:T(8,128)}), f32[8,128,256]{2,1,0:T(8,128)S(1)}, u32[]{:S(2)}, u32[]{:S(2)}) %all-to-all-start.4) | async-done | bytes 1048608 | tf_op jit(solution)/shard_map/all_to_all | solution.py:16
  185.4 0.6 fusion.1
  186.0 0.6 convolution_add_fusion
  186.6 10.5 %all_to_all.41 = f32[4,128,256]{2,1,0:T(8,128)S(1)} all-to-all(f32[4,128,256]{2,1,0:T(8,128)S(1)} %bitcast.57), channel_id=1, replica_groups=mesh['y'=8,'xh'=2,'core'=2,'z'=8,'xl'=2] {'xh','xl'}, dimensions={0} | all-to-all | bytes 1048576 | tf_op jit(solution)/shard_map/all_to_all | solution.py:100
  197.2 0.6 broadcast_multiply_fusion
  197.8 8.2 %all-gather.7.cloned.1.call-done = f32[1024,256]{1,0:T(8,128)} async-done(((f32[128,256]{1,0:T(8,128)}), f32[1024,256]{1,0:T(8,128)}) %all-gather.7.cloned.1.call-update) | async-done | bytes 1048592 | tf_op jit(solution)/shard_map/all_gather | solution.py:141
  206.0 17.1 %all_to_all.42.refs_0_ = f32[8,64,256]{2,1,0:T(8,128)S(1)} all-to-all(f32[8,64,256]{2,1,0:T(8,128)S(1)} %broadcast_in_dim.23), channel_id=1, replica_groups=mesh['y'=8,'xh'=2,'core'=2,'z'=8,'xl'=2] {'z'}, dimensions={0} | all-to-all | bytes 1048576 | tf_op jit(solution)/shard_map/all_to_all | solution.py:16
  223.2 0.9 broadcast_in_dim.44
  224.1 3.5 all-to-all-start.7
  227.6 3.5 collective-permute-start.6
  231.1 2.3 collective-permute-start.7
  233.4 7.3 %all-to-all-done.7.refs_1_ = f32[8,64,256]{2,1,0:T(8,128)S(1)} async-done(((f32[8,64,256]{2,1,0:T(8,128)}), f32[8,64,256]{2,1,0:T(8,128)S(1)}, u32[]{:S(2)}, u32[]{:S(2)}) %all-to-all-start.7) | async-done | bytes 524320 | tf_op jit(solution)/shard_map/all_to_all | solution.py:16
  240.8 3.5 collective-permute-start.8
  244.3 11.2 %collective-permute-done.6.refs_1_ = f32[8,128,256]{2,1,0:T(8,128)S(1)} collective-permute-done((f32[8,128,256]{2,1,0:T(8,128)S(1)}, f32[8,128,256]{2,1,0:T(8,128)S(1)}, u32[]{:S(2)}, u32[]{:S(2)}) %collective-permute-start.6) | collective-permute-done | bytes 1048608 | tf_op jit(solution)/shard_map/ppermute | solution.py:20
  255.6 1.0 copy-done.5
  256.5 64.8 %shard_map.77 = f32[256,2048]{1,0:T(8,128)} custom-call(f32[8,128,256]{2,1,0:T(8,128)} %bitcast.60, f32[8,128,256]{2,1,0:T(8,128)} %copy-done.5), custom_call_target="tpu_custom_call" | custom-call | tf_op jit(solution)/shard_map/pallas_call | solution.py:50
  321.4 64.9 %shard_map.78 = f32[256,2048]{1,0:T(8,128)} custom-call(f32[8,64,256]{2,1,0:T(8,128)} %copy-done, f32[8,64,256]{2,1,0:T(8,128)} %copy-done.1, f32[8,64,256]{2,1,0:T(8,128)} %collective-permute-done.7.refs_2_, f32[8,64,256]{2,1,0:T(8,128)} %collective-permute-done.8.refs_3_), custom_call_target="tpu_custom_call" | custom-call | tf_op jit(solution)/shard_map/pallas_call | solution.py:50
  (43 shorter events, 0.4 us)
Async XLA Ops:
  7.2 13.6 %copy-start.6 = (f32[256,2048]{1,0:T(8,128)S(1)}, f32[256,2048]{1,0:T(8,128)}, u32[]{:S(2)}) copy-start(f32[256,2048]{1,0:T(8,128)} %param.7) | copy-start | bytes 6291460
  12.1 33.6 %all-to-all-start = ((f32[8,128,256]{2,1,0:T(8,128)}), f32[8,128,256]{2,1,0:T(8,128)S(1)}, u32[]{:S(2)}, u32[]{:S(2)}) async-start(f32[8,128,256]{2,1,0:T(8,128)} %broadcast_in_dim.18), calls=%async_computation | async-start | bytes 2097152 | tf_op jit(solution)/shard_map/all_to_all | solution.py:107
  20.7 68.9 %all-gather.5.cloned.1.call-start = ((), (), s32[]{:S(2)}) async-start(), calls=%async_computation.8 | async-start | bytes 1179648 | tf_op jit(solution)/shard_map/all_gather | solution.py:109
  25.8 17.3 %copy-start.7 = (f32[256,128]{1,0:T(8,128)}, f32[256,128]{1,0:T(8,128)S(1)}, u32[]{:S(2)}) copy-start(f32[256,128]{1,0:T(8,128)S(1)} %get-tuple-element.23) | copy-start | bytes 393220
  25.9 14.4 %collective-permute-start.1 = (f32[256,512]{1,0:T(8,128)S(1)}, f32[256,512]{1,0:T(8,128)S(1)}, u32[]{:S(2)}, u32[]{:S(2)}) collective-permute-start(f32[256,512]{1,0:T(8,128)S(1)} %pad_maximum_fusion.5), channel_id=1, source_target_pairs={{0,33},{33,0},{1,32},{32,1},{2,35},{35,2},{3,34},{34,3},{4,37},{37... | collective-permute-start | bytes 1572872 | tf_op jit(solution)/shard_map/ppermute | solution.py:87
  40.3 0.8 copy-start.10
  41.2 4.6 %collective-permute-start.2 = (f32[512,512]{1,0:T(8,128)S(1)}, f32[512,512]{1,0:T(8,128)S(1)}, u32[]{:S(2)}, u32[]{:S(2)}) collective-permute-start(f32[512,512]{1,0:T(8,128)S(1)} %pad_maximum_fusion.1), channel_id=1, source_target_pairs={{0,16},{16,0},{1,17},{17,1},{2,18},{18,2},{3,19},{19,3},{4,20},{20... | collective-permute-start | bytes 3145736 | tf_op jit(solution)/shard_map/ppermute | solution.py:20
  45.7 0.9 copy-start.8
  45.7 1.1 copy-start.11
  47.5 3.4 collective-permute-start.3
  89.6 12.4 %all-to-all-start.1 = ((f32[4,256,128]{2,1,0:T(8,128)}), f32[4,256,128]{2,1,0:T(8,128)S(1)}, u32[]{:S(2)}, u32[]{:S(2)}) async-start(f32[4,256,128]{2,1,0:T(8,128)} %bitcast.21), calls=%async_computation.1 | async-start | bytes 1048576 | tf_op jit(solution)/shard_map/all_to_all | solution.py:100
  94.0 41.3 %copy-start.3 = (f32[1024,256]{1,0:T(8,128)S(1)}, f32[1024,256]{1,0:T(8,128)}, u32[]{:S(2)}) copy-start(f32[1024,256]{1,0:T(8,128)} %all-gather.5.cloned.1.call-done) | copy-start | bytes 3145732
  133.3 4.5 %collective-permute-start.4 = (f32[8,256,128]{1,2,0:T(8,128)S(1)}, f32[8,256,128]{1,2,0:T(8,128)S(1)}, u32[]{:S(2)}, u32[]{:S(2)}) collective-permute-start(f32[8,256,128]{1,2,0:T(8,128)S(1)} %all_to_all.40), channel_id=1, source_target_pairs={{0,16},{16,0},{1,17},{17,1},{2,18},{18,2},{3,19},{19,3},{4,20},{20... | collective-permute-start | bytes 3145736 | tf_op jit(solution)/shard_map/ppermute | solution.py:20
  137.9 5.3 %copy-start.12 = (s32[16,16]{1,0:T(8,128)S(1)}, s32[16,16]{1,0:T(8,128)}, u32[]{:S(2)}) copy-start(s32[16,16]{1,0:T(8,128)} %param.10) | copy-start | bytes 3076
  138.9 5.0 %copy-start.9 = (f32[256,2048]{1,0:T(8,128)S(1)}, f32[256,2048]{1,0:T(8,128)}, u32[]{:S(2)}) copy-start(f32[256,2048]{1,0:T(8,128)} %param.8) | copy-start | bytes 6291460
  139.7 14.4 %all-to-all-start.3 = ((f32[4,128,256]{2,1,0:T(8,128)}), f32[4,128,256]{2,1,0:T(8,128)S(1)}, u32[]{:S(2)}, u32[]{:S(2)}) async-start(f32[4,128,256]{2,1,0:T(8,128)} %bitcast.33), calls=%async_computation.3 | async-start | bytes 1048576 | tf_op jit(solution)/shard_map/all_to_all | solution.py:100
  149.1 17.1 %collective-permute-start = (f32[256,512]{1,0:T(8,128)S(1)}, f32[256,512]{1,0:T(8,128)S(1)}, u32[]{:S(2)}, u32[]{:S(2)}) collective-permute-start(f32[256,512]{1,0:T(8,128)S(1)} %pad_maximum_fusion.4), channel_id=1, source_target_pairs={{0,33},{33,0},{1,32},{32,1},{2,35},{35,2},{3,34},{34,3},{4,37},{37... | collective-permute-start | bytes 1572872 | tf_op jit(solution)/shard_map/ppermute | solution.py:87
  154.8 11.4 %copy-start.2 = (f32[128,256]{1,0:T(8,128)}, f32[128,256]{1,0:T(8,128)S(1)}, u32[]{:S(2)}) copy-start(f32[128,256]{1,0:T(8,128)S(1)} %broadcast_multiply_fusion.1) | copy-start | bytes 393220
  155.9 29.5 %all-to-all-start.4 = ((f32[8,128,256]{2,1,0:T(8,128)}), f32[8,128,256]{2,1,0:T(8,128)S(1)}, u32[]{:S(2)}, u32[]{:S(2)}) async-start(f32[8,128,256]{2,1,0:T(8,128)} %broadcast_in_dim.22), calls=%async_computation.4 | async-start | bytes 2097152 | tf_op jit(solution)/shard_map/all_to_all | solution.py:16
  161.5 44.4 %all-gather.7.cloned.1.call-start = ((), (), s32[]{:S(2)}) async-start(), calls=%async_computation.9 | async-start | bytes 1179648 | tf_op jit(solution)/shard_map/all_gather | solution.py:141
  167.3 4.8 %collective-permute-start.5 = (f32[512,512]{1,0:T(8,128)}, f32[512,512]{1,0:T(8,128)S(1)}, u32[]{:S(2)}, u32[]{:S(2)}) collective-permute-start(f32[512,512]{1,0:T(8,128)} %pad_maximum_fusion), channel_id=1, source_target_pairs={{0,16},{16,0},{1,17},{17,1},{2,18},{18,2},{3,19},{19,3},{4,20},{20... | collective-permute-start | bytes 3145736 | tf_op jit(solution)/shard_map/ppermute | solution.py:20
  206.0 21.6 %copy-start.4 = (f32[1024,256]{1,0:T(8,128)S(1)}, f32[1024,256]{1,0:T(8,128)}, u32[]{:S(2)}) copy-start(f32[1024,256]{1,0:T(8,128)} %all-gather.7.cloned.1.call-done) | copy-start | bytes 3145732
  223.2 98.1 %copy-start = (f32[8,64,256]{2,1,0:T(8,128)}, f32[8,64,256]{2,1,0:T(8,128)S(1)}, u32[]{:S(2)}) copy-start(f32[8,64,256]{2,1,0:T(8,128)S(1)} %all_to_all.42.refs_0_) | copy-start | bytes 1572868
  224.1 16.7 %all-to-all-start.7 = ((f32[8,64,256]{2,1,0:T(8,128)}), f32[8,64,256]{2,1,0:T(8,128)S(1)}, u32[]{:S(2)}, u32[]{:S(2)}) async-start(f32[8,64,256]{2,1,0:T(8,128)} %broadcast_in_dim.44), calls=%async_computation.7 | async-start | bytes 1048576 | tf_op jit(solution)/shard_map/all_to_all | solution.py:16
  227.6 28.0 %collective-permute-start.6 = (f32[8,128,256]{2,1,0:T(8,128)S(1)}, f32[8,128,256]{2,1,0:T(8,128)S(1)}, u32[]{:S(2)}, u32[]{:S(2)}) collective-permute-start(f32[8,128,256]{2,1,0:T(8,128)S(1)} %bitcast.61), channel_id=1, source_target_pairs={{0,1},{1,0},{2,3},{3,2},{4,5},{5,4},{6,7},{7,6},{8,9},{9,8},{10,11... | collective-permute-start | bytes 3145736 | tf_op jit(solution)/shard_map/ppermute | solution.py:20
  231.1 90.2 %collective-permute-start.7 = (f32[8,64,256]{2,1,0:T(8,128)S(1)}, f32[8,64,256]{2,1,0:T(8,128)}, u32[]{:S(2)}, u32[]{:S(2)}) collective-permute-start(f32[8,64,256]{2,1,0:T(8,128)S(1)} %all_to_all.42.refs_0_), channel_id=1, source_target_pairs={{0,1},{1,0},{2,3},{3,2},{4,5},{5,4},{6,7},{7,6},{8,9},{9,8},{10,11... | collective-permute-start | bytes 1572872 | tf_op jit(solution)/shard_map/ppermute | solution.py:20
  240.8 80.6 %copy-start.1 = (f32[8,64,256]{2,1,0:T(8,128)}, f32[8,64,256]{2,1,0:T(8,128)S(1)}, u32[]{:S(2)}) copy-start(f32[8,64,256]{2,1,0:T(8,128)S(1)} %all-to-all-done.7.refs_1_) | copy-start | bytes 1572868
  240.8 80.6 %collective-permute-start.8 = (f32[8,64,256]{2,1,0:T(8,128)S(1)}, f32[8,64,256]{2,1,0:T(8,128)}, u32[]{:S(2)}, u32[]{:S(2)}) collective-permute-start(f32[8,64,256]{2,1,0:T(8,128)S(1)} %all-to-all-done.7.refs_1_), channel_id=1, source_target_pairs={{0,1},{1,0},{2,3},{3,2},{4,5},{5,4},{6,7},{7,6},{8,9},{9,8},{10,11... | collective-permute-start | bytes 1572872 | tf_op jit(solution)/shard_map/ppermute | solution.py:20
  255.6 1.0 copy-start.5
Sparse Core Ops, SparseCore 0:
  45.5 44.0 all-gather.4
  169.4 36.5 all-gather.6

commit v3 on v2

--- a/solution.py
+++ b/solution.py
@@ -26,33 +26,22 @@
     n = len(own)
 
     def kernel(*refs):
-        out, sem = refs[2 * n], refs[2 * n + 1]
+        out = refs[2 * n]
         xl = lax.axis_index("xl")
         core = lax.axis_index("core")
-        copies = []
         for k in range(2 * n):
             mine = xl if k < n else 1 - xl
             at = pl.multiple_of(mine * (n * rows) + (k % n) * rows, rows)
             for layer in range(layers):
                 to = pl.multiple_of((layer ^ core) * blk, blk)
-                copies.append(
-                    pltpu.make_async_copy(
-                        refs[k].at[layer],
-                        out.at[pl.ds(at, rows), pl.ds(to, blk)],
-                        sem.at[k * layers + layer],
-                    )
-                )
-        for copy in copies:
-            copy.start()
-        for copy in copies:
-            copy.wait()
+                out[pl.ds(at, rows), pl.ds(to, blk)] = refs[k][layer]
 
     return pl.pallas_call(
         kernel,
         out_shape=jax.ShapeDtypeStruct((2 * n * rows, layers * blk), own[0].dtype),
-        in_specs=[pl.BlockSpec(memory_space=pl.ANY)] * (2 * n),
-        out_specs=pl.BlockSpec(memory_space=pl.ANY),
-        scratch_shapes=[pltpu.SemaphoreType.DMA((2 * n * layers,))],
+        in_specs=[pl.BlockSpec(memory_space=pltpu.VMEM)] * (2 * n),
+        out_specs=pl.BlockSpec(memory_space=pltpu.VMEM),
+        compiler_params=pltpu.CompilerParams(vmem_limit_bytes=24 * 1024 * 1024),
     )(*own, *other)
 
 
@@ -115,7 +104,6 @@
     even = (panel % 2) == 0
     blocks = jnp.stack([jnp.where(even, mine, theirs), jnp.where(even, theirs, mine)])
     blocks = blocks.reshape(2, blk, 2, half).transpose(0, 2, 1, 3).reshape(4, blk, half)
-    blocks, z_panel = lax.optimization_barrier((blocks, z_panel))
     t_share = sum_x(blocks)
     t_row = 2 * y + core
     source = (z ^ xh) & 1
@@ -123,6 +111,7 @@
     at_row = t_row * blk + lax.broadcasted_iota(jnp.int32, (blk, half), 0)
     at_col = t_col * blk + xl * half + lax.broadcasted_iota(jnp.int32, (blk, half), 1)
     q_share = jnp.where(at_row == at_col, 1.5, 0.0) - 0.5 * (keep[t_row, t_col] * t_share)
+    q_share, z_panel = lax.optimization_barrier((q_share, z_panel))
     q_mine = spread(q_share, "z", nz)
     q_theirs = swap(q_mine, "core")
     ordered = z_panel.reshape(2, ny // 2, half, blk).transpose(1, 0, 2, 3)

time: 395 us -> 271 us (0.69)
  Pallas kernels: 130 us -> 3.99 us
    pallas_call x2, Pallas kernels: 130 us -> 3.99 us  [place(): pl.pallas_call(kernel, out_shape=jax.ShapeDtypeStruct((2 * n * rows, laye...]
    all_gather x1, waiting for transfers between devices: 37.8 us -> 23.1 us  [local(): z_panel = lax.all_gather(piece(z_blocks), 'y', axis=0)]
    ppermute x7, waiting for transfers between devices: 17.1 us -> 31 us  [swap(): return lax.ppermute(array, axis, [(0, 1), (1, 0)])]
  transfers between devices with their start and end apart: 16 -> 16, of which waited for: 12 -> 14; matrix products, arithmetic and copies ran while one was open for 5% -> 8% of each run, Pallas kernels for 16% -> 1%
where the time goes in v3:
time: 271 us; the launch traced here: 269 us
  waiting for transfers between devices  109 us (40%)
  blocking collectives  59.8 us (22%)
  starting transfers between devices  51 us (19%)
  other arithmetic  20.8 us (8%)
  between operations  14.5 us (5%)
  local copies, waits for them, and re-layouts  6.01 us (2%)
  matrix products  4.38 us (2%)
  Pallas kernels  3.99 us (1%)
    all_to_all x2, blocking collectives, spread(): return lax.all_to_all(copies, axis, split_axis=0, concat_axis=0, tiled=True)  49.3 us
    ppermute x7, waiting for transfers between devices, swap(): return lax.ppermute(array, axis, [(0, 1), (1, 0)])  31 us
    all_gather x1, waiting for transfers between devices, local(): z_panel = lax.all_gather(piece(z_blocks), 'y', axis=0)  23.1 us
    all_to_all x2, waiting for transfers between devices, spread(): return lax.all_to_all(copies, axis, split_axis=0, concat_axis=0, tiled=True)  20.9 us
    ppermute x7, starting transfers between devices, swap(): return lax.ppermute(array, axis, [(0, 1), (1, 0)])  17 us
    ppermute x2, waiting for transfers between devices, left(): lax.ppermute(pick(1 - xh, 1 - xl), X, [(0, 3), (3, 0), (1, 2), (2, 1)])  15.8 us
    all_to_all x1, blocking collectives, sum_x(): lax.all_to_all(parts, X, split_axis=0, concat_axis=0, tiled=True)  10.5 us
    mul x2, other arithmetic, pick(): lax.dynamic_slice(values, (0, (2 * m + a) * blk + b * half), (blk, half))  10.2 us
  transfers between devices with their start and end apart: 16, of which 14 were waited for; matrix products, arithmetic and copies ran while one was open for 8% of the time, Pallas kernels for 1%

profile of v3, /device:TPU:56, one launch (start us, length us, event | category | flops | bytes accessed | tf_op | source)
XLA Modules:
  0.0 269.1 jit_solution(9664333051074283047)
XLA Ops:
  7.2 0.8 convert_element_type.11
  8.1 0.7 convert_element_type.9
  8.8 0.7 fusion.15
  9.4 1.5 dynamic-slice_multiply_fusion.17
  11.0 1.1 broadcast_in_dim.18
  12.0 8.6 %all-to-all-start = ((f32[8,128,256]{2,1,0:T(8,128)}), f32[8,128,256]{2,1,0:T(8,128)S(1)}, u32[]{:S(2)}, u32[]{:S(2)}) async-start(f32[8,128,256]{2,1,0:T(8,128)} %broadcast_in_dim.18), calls=%async_computation | async-start | bytes 2097152 | tf_op jit(solution)/shard_map/all_to_all | solution.py:96
  20.7 5.1 %dynamic-slice_multiply_fusion.8 = (f32[256,128]{1,0:T(8,128)S(1)}, f32[256,128]{1,0:T(8,128)S(1)}, f32[256,128]{1,0:T(8,128)S(1)}, f32[256,128]{1,0:T(8,128)S(1...) fusion(f32[256,2048]{1,0:T(8,128)S(1)} %copy-done.3, ...), kind=kLoop, calls=%fused_computation.35 | loop fusion | flops 262144 | bytes 2097216 | tf_op jit(solution)/shard_map/mul | solution.py:68
  25.9 2.9 %collective-permute-start.1 = (f32[256,512]{1,0:T(8,128)S(1)}, f32[256,512]{1,0:T(8,128)S(1)}, u32[]{:S(2)}, u32[]{:S(2)}) collective-permute-start(f32[256,512]{1,0:T(8,128)S(1)} %pad_maximum_fusion.5), channel_id=1, source_target_pairs={{0,33},{33,0},{1,32},{32,1},{2,35},{35,2},{3,34},{34,3},{4,37},{37... | collective-permute-start | bytes 1572872 | tf_op jit(solution)/shard_map/ppermute | solution.py:76
  28.8 11.5 %collective-permute-done.1 = f32[256,512]{1,0:T(8,128)S(1)} collective-permute-done((f32[256,512]{1,0:T(8,128)S(1)}, f32[256,512]{1,0:T(8,128)S(1)}, u32[]{:S(2)}, u32[]{:S(2)}) %collective-permute-start.1) | collective-permute-done | bytes 524320 | tf_op jit(solution)/shard_map/ppermute | solution.py:76
  40.3 0.8 copy-done.7
  41.2 1.9 collective-permute-start.2
  43.1 2.2 dynamic-slice_multiply_fusion
  45.3 0.4 collective-permute-done.2
  45.7 0.6 fusion.4
  46.3 0.3 copy-done.5
  46.6 0.2 copy-done.8
  46.9 0.6 convolution_add_fusion.1
  47.5 2.0 collective-permute-start.3
  49.6 1.4 collective-permute-done.3
  51.0 0.8 fusion
  51.8 4.0 %all-to-all-start.1 = ((f32[4,256,128]{2,1,0:T(8,128)}), f32[4,256,128]{2,1,0:T(8,128)S(1)}, u32[]{:S(2)}, u32[]{:S(2)}) async-start(f32[4,256,128]{2,1,0:T(8,128)} %bitcast.21), calls=%async_computation.1 | async-start | bytes 1048576 | tf_op jit(solution)/shard_map/all_to_all | solution.py:89
  55.9 9.8 %all-to-all-done.1 = f32[4,256,128]{2,1,0:T(8,128)S(1)} async-done(((f32[4,256,128]{2,1,0:T(8,128)}), f32[4,256,128]{2,1,0:T(8,128)S(1)}, u32[]{:S(2)}, u32[]{:S(2)}) %all-to-all-start.1) | async-done | bytes 524320 | tf_op jit(solution)/shard_map/all_to_all | solution.py:89
  65.7 0.8 multiply_subtract_fusion
  66.4 23.1 %all-gather.5.cloned.1.call-done = f32[1024,256]{1,0:T(8,128)} async-done(((f32[128,256]{1,0:T(8,128)}), f32[1024,256]{1,0:T(8,128)}) %all-gather.5.cloned.1.call-update) | async-done | bytes 1048592 | tf_op jit(solution)/shard_map/all_gather | solution.py:98
  89.6 0.1 copy.9
  89.7 0.1 broadcast_in_dim.21
  89.8 32.0 %all_to_all.40 = f32[8,256,128]{1,2,0:T(8,128)S(1)} all-to-all(f32[8,256,128]{1,2,0:T(8,128)S(1)} %broadcast_in_dim.21), channel_id=1, replica_groups=mesh['y'=8,'xh'=2,'core'=2,'z'=8,'xl'=2] {'z'}, dimensions={0} | all-to-all | bytes 2097152 | tf_op jit(solution)/shard_map/all_to_all | solution.py:16
  121.8 1.9 collective-permute-start.4
  123.7 0.1 reverse_select_fusion
  123.8 0.1 copy.10
  123.9 1.0 fusion.18
  124.9 1.4 collective-permute-done.4
  126.3 1.0 select_bitcast_fusion.1
  127.3 0.8 pad_maximum_fusion.6
  128.2 4.2 %all-to-all-start.3 = ((f32[4,128,256]{2,1,0:T(8,128)}), f32[4,128,256]{2,1,0:T(8,128)S(1)}, u32[]{:S(2)}, u32[]{:S(2)}) async-start(f32[4,128,256]{2,1,0:T(8,128)} %bitcast.33), calls=%async_computation.3 | async-start | bytes 1048576 | tf_op jit(solution)/shard_map/all_to_all | solution.py:89
  132.4 0.7 fusion.17
  133.1 5.1 %dynamic-slice_multiply_fusion.16 = (f32[256,128]{1,0:T(8,128)S(1)}, f32[256,128]{1,0:T(8,128)S(1)}, f32[256,128]{1,0:T(8,128)S(1)}, f32[256,128]{1,0:T(8,128)S(...) fusion(f32[256,2048]{1,0:T(8,128)S(1)} %copy-done.6, ...), kind=kLoop, calls=%fused_computation.43 | loop fusion | flops 262144 | bytes 2097216 | tf_op jit(solution)/shard_map/mul | solution.py:68
  138.3 5.1 %collective-permute-start = (f32[256,512]{1,0:T(8,128)S(1)}, f32[256,512]{1,0:T(8,128)S(1)}, u32[]{:S(2)}, u32[]{:S(2)}) collective-permute-start(f32[256,512]{1,0:T(8,128)S(1)} %pad_maximum_fusion.4), channel_id=1, source_target_pairs={{0,33},{33,0},{1,32},{32,1},{2,35},{35,2},{3,34},{34,3},{4,37},{37... | collective-permute-start | bytes 1572872 | tf_op jit(solution)/shard_map/ppermute | solution.py:76
  143.4 0.6 broadcast_multiply_fusion.1
  144.1 1.1 broadcast_in_dim.22
  145.1 5.6 %all-to-all-start.4 = ((f32[8,128,256]{2,1,0:T(8,128)}), f32[8,128,256]{2,1,0:T(8,128)S(1)}, u32[]{:S(2)}, u32[]{:S(2)}) async-start(f32[8,128,256]{2,1,0:T(8,128)} %broadcast_in_dim.22), calls=%async_computation.4 | async-start | bytes 2097152 | tf_op jit(solution)/shard_map/all_to_all | solution.py:16
  150.8 4.3 %collective-permute-done = f32[256,512]{1,0:T(8,128)S(1)} collective-permute-done((f32[256,512]{1,0:T(8,128)S(1)}, f32[256,512]{1,0:T(8,128)S(1)}, u32[]{:S(2)}, u32[]{:S(2)}) %collective-permute-start) | collective-permute-done | bytes 524320 | tf_op jit(solution)/shard_map/ppermute | solution.py:76
  155.0 0.1 fusion.8
  155.2 1.0 pad_maximum_fusion
  156.2 1.9 collective-permute-start.5
  158.2 2.8 %collective-permute-done.5 = f32[512,512]{1,0:T(8,128)S(1)} collective-permute-done((f32[512,512]{1,0:T(8,128)}, f32[512,512]{1,0:T(8,128)S(1)}, u32[]{:S(2)}, u32[]{:S(2)}) %collective-permute-start.5) | collective-permute-done | bytes 1048608 | tf_op jit(solution)/shard_map/ppermute | solution.py:20
  161.0 13.6 %all-to-all-done.4 = f32[8,128,256]{2,1,0:T(8,128)S(1)} async-done(((f32[8,128,256]{2,1,0:T(8,128)}), f32[8,128,256]{2,1,0:T(8,128)S(1)}, u32[]{:S(2)}, u32[]{:S(2)}) %all-to-all-start.4) | async-done | bytes 1048608 | tf_op jit(solution)/shard_map/all_to_all | solution.py:16
  174.6 0.6 fusion.1
  175.2 0.6 convolution_add_fusion
  175.8 10.5 %all_to_all.41 = f32[4,128,256]{2,1,0:T(8,128)S(1)} all-to-all(f32[4,128,256]{2,1,0:T(8,128)S(1)} %bitcast.59), channel_id=1, replica_groups=mesh['y'=8,'xh'=2,'core'=2,'z'=8,'xl'=2] {'xh','xl'}, dimensions={0} | all-to-all | bytes 1048576 | tf_op jit(solution)/shard_map/all_to_all | solution.py:89
  186.3 0.6 broadcast_multiply_fusion
  186.9 8.0 %all-gather.7.cloned.1.call-done = f32[1024,256]{1,0:T(8,128)} async-done(((f32[128,256]{1,0:T(8,128)}), f32[1024,256]{1,0:T(8,128)}) %all-gather.7.cloned.1.call-update) | async-done | bytes 1048592 | tf_op jit(solution)/shard_map/all_gather | solution.py:130
  195.0 17.3 %all_to_all.42.refs_0_ = f32[8,64,256]{2,1,0:T(8,128)S(1)} all-to-all(f32[8,64,256]{2,1,0:T(8,128)S(1)} %broadcast_in_dim.23), channel_id=1, replica_groups=mesh['y'=8,'xh'=2,'core'=2,'z'=8,'xl'=2] {'z'}, dimensions={0} | all-to-all | bytes 1048576 | tf_op jit(solution)/shard_map/all_to_all | solution.py:16
  212.3 0.8 broadcast_in_dim.44
  213.1 3.5 %all-to-all-start.7 = ((f32[8,64,256]{2,1,0:T(8,128)}), f32[8,64,256]{2,1,0:T(8,128)S(1)}, u32[]{:S(2)}, u32[]{:S(2)}) async-start(f32[8,64,256]{2,1,0:T(8,128)} %broadcast_in_dim.44), calls=%async_computation.7 | async-start | bytes 1048576 | tf_op jit(solution)/shard_map/all_to_all | solution.py:16
  216.6 3.4 %collective-permute-start.6 = (f32[8,128,256]{2,1,0:T(8,128)S(1)}, f32[8,128,256]{2,1,0:T(8,128)S(1)}, u32[]{:S(2)}, u32[]{:S(2)}) collective-permute-start(f32[8,128,256]{2,1,0:T(8,128)S(1)} %bitcast.50), channel_id=1, source_target_pairs={{0,1},{1,0},{2,3},{3,2},{4,5},{5,4},{6,7},{7,6},{8,9},{9,8},{10,11... | collective-permute-start | bytes 3145736 | tf_op jit(solution)/shard_map/ppermute | solution.py:20
  220.0 2.5 collective-permute-start.7
  222.5 7.3 %all-to-all-done.7.refs_1_ = f32[8,64,256]{2,1,0:T(8,128)S(1)} async-done(((f32[8,64,256]{2,1,0:T(8,128)}), f32[8,64,256]{2,1,0:T(8,128)S(1)}, u32[]{:S(2)}, u32[]{:S(2)}) %all-to-all-start.7) | async-done | bytes 524320 | tf_op jit(solution)/shard_map/all_to_all | solution.py:16
  229.8 3.4 %collective-permute-start.8 = (f32[8,64,256]{2,1,0:T(8,128)S(1)}, f32[8,64,256]{2,1,0:T(8,128)S(1)}, u32[]{:S(2)}, u32[]{:S(2)}) collective-permute-start(f32[8,64,256]{2,1,0:T(8,128)S(1)} %all-to-all-done.7.refs_1_), channel_id=1, source_target_pairs={{0,1},{1,0},{2,3},{3,2},{4,5},{5,4},{6,7},{7,6},{8,9},{9,8},{10,11... | collective-permute-start | bytes 1572872 | tf_op jit(solution)/shard_map/ppermute | solution.py:20
  233.2 11.4 %collective-permute-done.6.refs_1_ = f32[8,128,256]{2,1,0:T(8,128)S(1)} collective-permute-done((f32[8,128,256]{2,1,0:T(8,128)S(1)}, f32[8,128,256]{2,1,0:T(8,128)S(1)}, u32[]{:S(2)}, u32[]{:S(2)}) %collective-permute-start.6) | collective-permute-done | bytes 1048608 | tf_op jit(solution)/shard_map/ppermute | solution.py:20
  244.6 1.5 shard_map.77
  246.1 8.1 %collective-permute-done.7.refs_2_ = f32[8,64,256]{2,1,0:T(8,128)} collective-permute-done((f32[8,64,256]{2,1,0:T(8,128)S(1)}, f32[8,64,256]{2,1,0:T(8,128)}, u32[]{:S(2)}, u32[]{:S(2)}) %collective-permute-start.7) | collective-permute-done | bytes 524320 | tf_op jit(solution)/shard_map/ppermute | solution.py:20
  254.3 5.5 %collective-permute-done.8.refs_3_ = f32[8,64,256]{2,1,0:T(8,128)S(1)} collective-permute-done((f32[8,64,256]{2,1,0:T(8,128)S(1)}, f32[8,64,256]{2,1,0:T(8,128)S(1)}, u32[]{:S(2)}, u32[]{:S(2)}) %collective-permute-start.8) | collective-permute-done | bytes 524320 | tf_op jit(solution)/shard_map/ppermute | solution.py:20
  259.8 2.5 shard_map.78
  (37 shorter events, 0.5 us)
Async XLA Ops:
  7.2 13.5 %copy-start.3 = (f32[256,2048]{1,0:T(8,128)S(1)}, f32[256,2048]{1,0:T(8,128)}, u32[]{:S(2)}) copy-start(f32[256,2048]{1,0:T(8,128)} %param.7) | copy-start | bytes 6291460
  12.0 33.7 %all-to-all-start = ((f32[8,128,256]{2,1,0:T(8,128)}), f32[8,128,256]{2,1,0:T(8,128)S(1)}, u32[]{:S(2)}, u32[]{:S(2)}) async-start(f32[8,128,256]{2,1,0:T(8,128)} %broadcast_in_dim.18), calls=%async_computation | async-start | bytes 2097152 | tf_op jit(solution)/shard_map/all_to_all | solution.py:96
  20.7 68.9 %all-gather.5.cloned.1.call-start = ((), (), s32[]{:S(2)}) async-start(), calls=%async_computation.8 | async-start | bytes 1179648 | tf_op jit(solution)/shard_map/all_gather | solution.py:98
  25.8 17.3 %copy-start.4 = (f32[256,128]{1,0:T(8,128)}, f32[256,128]{1,0:T(8,128)S(1)}, u32[]{:S(2)}) copy-start(f32[256,128]{1,0:T(8,128)S(1)} %get-tuple-element.23) | copy-start | bytes 393220
  25.9 14.4 %collective-permute-start.1 = (f32[256,512]{1,0:T(8,128)S(1)}, f32[256,512]{1,0:T(8,128)S(1)}, u32[]{:S(2)}, u32[]{:S(2)}) collective-permute-start(f32[256,512]{1,0:T(8,128)S(1)} %pad_maximum_fusion.5), channel_id=1, source_target_pairs={{0,33},{33,0},{1,32},{32,1},{2,35},{35,2},{3,34},{34,3},{4,37},{37... | collective-permute-start | bytes 1572872 | tf_op jit(solution)/shard_map/ppermute | solution.py:76
  40.3 0.8 copy-start.7
  41.2 4.6 %collective-permute-start.2 = (f32[512,512]{1,0:T(8,128)S(1)}, f32[512,512]{1,0:T(8,128)S(1)}, u32[]{:S(2)}, u32[]{:S(2)}) collective-permute-start(f32[512,512]{1,0:T(8,128)S(1)} %pad_maximum_fusion.1), channel_id=1, source_target_pairs={{0,16},{16,0},{1,17},{17,1},{2,18},{18,2},{3,19},{19,3},{4,20},{20... | collective-permute-start | bytes 3145736 | tf_op jit(solution)/shard_map/ppermute | solution.py:20
  45.7 0.9 copy-start.5
  45.7 1.1 copy-start.8
  47.5 3.4 %collective-permute-start.3 = (f32[256,256]{1,0:T(8,128)S(1)}, f32[256,256]{1,0:T(8,128)S(1)}, u32[]{:S(2)}, u32[]{:S(2)}) collective-permute-start(f32[256,256]{1,0:T(8,128)S(1)} %constant_dynamic-slice_fusion), channel_id=1, source_target_pairs={{0,16},{16,0},{1,17},{17,1},{2,18},{18,2},{3,19},{19,3},{4,20},{20... | collective-permute-start | bytes 786440 | tf_op jit(solution)/shard_map/ppermute | solution.py:20
  51.8 13.8 %all-to-all-start.1 = ((f32[4,256,128]{2,1,0:T(8,128)}), f32[4,256,128]{2,1,0:T(8,128)S(1)}, u32[]{:S(2)}, u32[]{:S(2)}) async-start(f32[4,256,128]{2,1,0:T(8,128)} %bitcast.21), calls=%async_computation.1 | async-start | bytes 1048576 | tf_op jit(solution)/shard_map/all_to_all | solution.py:89
  89.6 34.1 %copy-start.2 = (f32[1024,256]{1,0:T(8,128)S(1)}, f32[1024,256]{1,0:T(8,128)}, u32[]{:S(2)}) copy-start(f32[1024,256]{1,0:T(8,128)} %all-gather.5.cloned.1.call-done) | copy-start | bytes 3145732
  121.8 4.5 %collective-permute-start.4 = (f32[8,256,128]{1,2,0:T(8,128)S(1)}, f32[8,256,128]{1,2,0:T(8,128)S(1)}, u32[]{:S(2)}, u32[]{:S(2)}) collective-permute-start(f32[8,256,128]{1,2,0:T(8,128)S(1)} %all_to_all.40), channel_id=1, source_target_pairs={{0,16},{16,0},{1,17},{17,1},{2,18},{18,2},{3,19},{19,3},{4,20},{20... | collective-permute-start | bytes 3145736 | tf_op jit(solution)/shard_map/ppermute | solution.py:20
  126.3 6.1 %copy-start.9 = (s32[16,16]{1,0:T(8,128)S(1)}, s32[16,16]{1,0:T(8,128)}, u32[]{:S(2)}) copy-start(s32[16,16]{1,0:T(8,128)} %param.10) | copy-start | bytes 3076
  127.3 5.8 %copy-start.6 = (f32[256,2048]{1,0:T(8,128)S(1)}, f32[256,2048]{1,0:T(8,128)}, u32[]{:S(2)}) copy-start(f32[256,2048]{1,0:T(8,128)} %param.8) | copy-start | bytes 6291460
  128.2 15.2 %all-to-all-start.3 = ((f32[4,128,256]{2,1,0:T(8,128)}), f32[4,128,256]{2,1,0:T(8,128)S(1)}, u32[]{:S(2)}, u32[]{:S(2)}) async-start(f32[4,128,256]{2,1,0:T(8,128)} %bitcast.33), calls=%async_computation.3 | async-start | bytes 1048576 | tf_op jit(solution)/shard_map/all_to_all | solution.py:89
  138.3 16.8 %collective-permute-start = (f32[256,512]{1,0:T(8,128)S(1)}, f32[256,512]{1,0:T(8,128)S(1)}, u32[]{:S(2)}, u32[]{:S(2)}) collective-permute-start(f32[256,512]{1,0:T(8,128)S(1)} %pad_maximum_fusion.4), channel_id=1, source_target_pairs={{0,33},{33,0},{1,32},{32,1},{2,35},{35,2},{3,34},{34,3},{4,37},{37... | collective-permute-start | bytes 1572872 | tf_op jit(solution)/shard_map/ppermute | solution.py:76
  144.1 11.1 %copy-start.1 = (f32[128,256]{1,0:T(8,128)}, f32[128,256]{1,0:T(8,128)S(1)}, u32[]{:S(2)}) copy-start(f32[128,256]{1,0:T(8,128)S(1)} %broadcast_multiply_fusion.1) | copy-start | bytes 393220
  145.1 29.4 %all-to-all-start.4 = ((f32[8,128,256]{2,1,0:T(8,128)}), f32[8,128,256]{2,1,0:T(8,128)S(1)}, u32[]{:S(2)}, u32[]{:S(2)}) async-start(f32[8,128,256]{2,1,0:T(8,128)} %broadcast_in_dim.22), calls=%async_computation.4 | async-start | bytes 2097152 | tf_op jit(solution)/shard_map/all_to_all | solution.py:16
  150.8 44.2 %all-gather.7.cloned.1.call-start = ((), (), s32[]{:S(2)}) async-start(), calls=%async_computation.9 | async-start | bytes 1179648 | tf_op jit(solution)/shard_map/all_gather | solution.py:130
  156.2 4.8 %collective-permute-start.5 = (f32[512,512]{1,0:T(8,128)}, f32[512,512]{1,0:T(8,128)S(1)}, u32[]{:S(2)}, u32[]{:S(2)}) collective-permute-start(f32[512,512]{1,0:T(8,128)} %pad_maximum_fusion), channel_id=1, source_target_pairs={{0,16},{16,0},{1,17},{17,1},{2,18},{18,2},{3,19},{19,3},{4,20},{20... | collective-permute-start | bytes 3145736 | tf_op jit(solution)/shard_map/ppermute | solution.py:20
  194.9 21.7 %copy-start = (f32[1024,256]{1,0:T(8,128)S(1)}, f32[1024,256]{1,0:T(8,128)}, u32[]{:S(2)}) copy-start(f32[1024,256]{1,0:T(8,128)} %all-gather.7.cloned.1.call-done) | copy-start | bytes 3145732
  213.1 16.7 %all-to-all-start.7 = ((f32[8,64,256]{2,1,0:T(8,128)}), f32[8,64,256]{2,1,0:T(8,128)S(1)}, u32[]{:S(2)}, u32[]{:S(2)}) async-start(f32[8,64,256]{2,1,0:T(8,128)} %broadcast_in_dim.44), calls=%async_computation.7 | async-start | bytes 1048576 | tf_op jit(solution)/shard_map/all_to_all | solution.py:16
  216.6 28.0 %collective-permute-start.6 = (f32[8,128,256]{2,1,0:T(8,128)S(1)}, f32[8,128,256]{2,1,0:T(8,128)S(1)}, u32[]{:S(2)}, u32[]{:S(2)}) collective-permute-start(f32[8,128,256]{2,1,0:T(8,128)S(1)} %bitcast.50), channel_id=1, source_target_pairs={{0,1},{1,0},{2,3},{3,2},{4,5},{5,4},{6,7},{7,6},{8,9},{9,8},{10,11... | collective-permute-start | bytes 3145736 | tf_op jit(solution)/shard_map/ppermute | solution.py:20
  220.0 34.2 %collective-permute-start.7 = (f32[8,64,256]{2,1,0:T(8,128)S(1)}, f32[8,64,256]{2,1,0:T(8,128)}, u32[]{:S(2)}, u32[]{:S(2)}) collective-permute-start(f32[8,64,256]{2,1,0:T(8,128)S(1)} %all_to_all.42.refs_0_), channel_id=1, source_target_pairs={{0,1},{1,0},{2,3},{3,2},{4,5},{5,4},{6,7},{7,6},{8,9},{9,8},{10,11... | collective-permute-start | bytes 1572872 | tf_op jit(solution)/shard_map/ppermute | solution.py:20
  229.8 29.9 %collective-permute-start.8 = (f32[8,64,256]{2,1,0:T(8,128)S(1)}, f32[8,64,256]{2,1,0:T(8,128)S(1)}, u32[]{:S(2)}, u32[]{:S(2)}) collective-permute-start(f32[8,64,256]{2,1,0:T(8,128)S(1)} %all-to-all-done.7.refs_1_), channel_id=1, source_target_pairs={{0,1},{1,0},{2,3},{3,2},{4,5},{5,4},{6,7},{7,6},{8,9},{9,8},{10,11... | collective-permute-start | bytes 1572872 | tf_op jit(solution)/shard_map/ppermute | solution.py:20
Sparse Core Ops, SparseCore 0:
  45.4 44.0 all-gather.4
  158.3 36.5 all-gather.6

commit v4 on v3

v4 whole, which is shorter than its diff:
```python
import jax
import jax.numpy as jnp
from jax import lax
from jax.experimental import pallas as pl
from jax.experimental.pallas import tpu as pltpu
from jax.sharding import Mesh
from jax.sharding import PartitionSpec as P

X = ("xh", "xl")
ROW = ("y", "xh")
DEPTH = ("z", "xl")
PLANE = ("xh", "core", "z", "xl")
HIGH = lax.Precision.HIGH
CHUNKS = 2


def copies_of(piece, n):
    return jnp.broadcast_to(piece[None], (n,) + piece.shape)


def spread(copies, axis):
    return lax.all_to_all(copies, axis, split_axis=0, concat_axis=0, tiled=True)


def swap(array, axis):
    return lax.ppermute(array, axis, [(0, 1), (1, 0)])


def after(array, other):
    return lax.optimization_barrier((array, other))[0]


def place(parts, places, shape):
    def kernel(*refs):
        out = refs[-1]
        for part, index, row, column, rows, columns in places():
            out[pl.ds(row, rows), pl.ds(column, columns)] = refs[part][index]

    return pl.pallas_call(
        kernel,
        out_shape=jax.ShapeDtypeStruct(shape, parts[0].dtype),
        in_specs=[pl.BlockSpec(memory_space=pltpu.VMEM)] * len(parts),
        out_specs=pl.BlockSpec(memory_space=pltpu.VMEM),
        compiler_params=pltpu.CompilerParams(vmem_limit_bytes=24 * 1024 * 1024),
    )(*parts)


def local(y_blocks, z_blocks, h_blocks, s_pattern, h_pattern, keep_mask):
    blk, width = y_blocks.shape
    half, quarter = blk // 2, blk // 4
    per_core = width // blk
    ny, nz = lax.axis_size("y"), lax.axis_size("z")
    y = lax.axis_index("y")
    xh = lax.axis_index("xh")
    core = lax.axis_index("core")
    z = lax.axis_index("z")
    xl = lax.axis_index("xl")
    row = 2 * y + xh
    panel = z ^ core
    column = per_core * core + panel
    keep = keep_mask.astype(jnp.float32)
    fill = s_pattern.astype(jnp.float32)


    def left(values, pattern, wait=None):
        def pick(a, b):
            return jnp.concatenate(
                [
                    lax.dynamic_slice(values, (0, (2 * m + a) * blk + b * half), (blk, half))
                    * pattern[row, per_core * core + 2 * m + a]
                    for m in range(per_core // 2)
                ],
                axis=1,
            )

        own = pick(xh, xl)
        other = lax.ppermute(pick(1 - xh, 1 - xl), X, [(0, 3), (3, 0), (1, 2), (2, 1)])
        if wait is not None:
            other = after(other, wait)
        return jnp.concatenate([own, other], axis=0)

    def halves(array):
        inner = array.shape[0] // 2
        return [lax.dynamic_slice_in_dim(array, at * inner, inner, 0) for at in (core, 1 - core)]

    def dot(a, b, dims):
        return lax.dot_general(
            a, b, ((dims[:1], dims[1:]), ((), ())), precision=HIGH, preferred_element_type=jnp.float32
        )

    def sum_x(array, first):
        def share(a, b):
            at = (a ^ first) * blk + b * half
            return lax.dynamic_slice_in_dim(array, at, half, 0)

        total = share(xh, xl)
        for a, b in ((0, 1), (1, 1), (1, 0)):
            pairs = [(i, i ^ (2 * a + b)) for i in range(4)]
            total = total + lax.ppermute(share(xh ^ a, xl ^ b), X, pairs)
        return total * keep[row, column]

    def chunk(array, k):
        return array[:, k * half : (k + 1) * half]

    y_piece = lax.dynamic_slice(y_blocks, (xl * half, panel * blk), (half, blk)) * fill[row, column]
    y_copies = [copies_of(chunk(y_piece, k), ny) for k in range(CHUNKS)]
    y_copies[0], z_blocks, h_blocks = lax.optimization_barrier((y_copies[0], z_blocks, h_blocks))
    y_panels = [spread(y_copies[0], "y")]
    y_panels.append(spread(after(y_copies[1], y_panels[0]), "y"))
    z_piece = jnp.concatenate(
        [
            lax.dynamic_slice(z_blocks, (k * half + xl * quarter, panel * blk), (quarter, blk))
            for k in range(CHUNKS)
        ],
        axis=0,
    )
    z_panel = lax.all_gather(z_piece * fill[row, column], "y", axis=0)
    z_left = left(z_blocks, fill, y_panels[0])
    z_lefts = (z_left, swap(z_left, "core"))
    t_row = 2 * y + core
    source = (z ^ xh) & 1
    t_col = per_core * source + (z ^ source)

    def t_share(y_panel):
        partial = sum(
            dot(b, a, (0, 1)) for a, b in zip(z_lefts, halves(y_panel.reshape(ny * half, half)))
        )
        total = None
        for s in range(4):
            to_xl, to_core = xh ^ (s >> 1), xl ^ (s & 1)
            pairs = []
            for a in range(2):
                for c in range(2):
                    for zz in range(8):
                        for b in range(2):
                            to_xh = (zz ^ c) & 1
                            to = ((to_xh * 2 + (b ^ (s & 1))) * 8 + zz) * 2 + (a ^ (s >> 1))
                            pairs.append((((a * 2 + c) * 8 + zz) * 2 + b, to))
            share = lax.dynamic_slice(
                partial, (to_xl * quarter, (to_core ^ xh) * blk), (quarter, blk)
            )
            got = lax.ppermute(share, PLANE, pairs)
            total = got if total is None else total + got
        return total

    q_mine, q_theirs = [], []
    ordered = z_panel.reshape(2, ny // 2, CHUNKS, quarter, blk).transpose(2, 1, 0, 3, 4)
    ordered = jnp.where(xh == 0, ordered, ordered[:, :, ::-1]).reshape(CHUNKS, ny * quarter, blk)
    last = y_panels[1]
    for k in range(CHUNKS):
        at_col = lax.broadcasted_iota(jnp.int32, (quarter, blk), 0) + k * half + xl * quarter
        at_row = lax.broadcasted_iota(jnp.int32, (quarter, blk), 1)
        diagonal = (t_row == t_col) & (at_row == at_col)
        q_share = jnp.where(diagonal, 1.5, 0.0) - 0.5 * (keep[t_row, t_col] * t_share(y_panels[k]))
        q = spread(after(copies_of(q_share, nz), last), "z")
        last = q
        q_mine.append(q.reshape(nz * quarter, blk))
        q_theirs.append(swap(q, "core").reshape(nz * quarter, blk))
    z_both = jnp.concatenate(
        [sum(dot(q[k], ordered[k], (0, 0)) for k in range(CHUNKS)) for q in (q_mine, q_theirs)], axis=0
    )
    z_shares = [sum_x(chunk(z_both, 0), core)]
    z_copies = copies_of(z_shares[0], ny)
    z_shares.append(sum_x(chunk(after(z_both, z_copies), 1), core))
    z_all = [lax.all_gather(share, DEPTH, axis=0) for share in z_shares]
    panels = [spread(z_copies, "y")]
    panels.append(spread(after(copies_of(z_shares[1], ny), panels[0]), "y"))
    h_left = left(h_blocks, h_pattern.astype(jnp.float32))
    h_lefts = (h_left, swap(h_left, "core"))
    h_own = []
    last = panels[1]
    for k in range(CHUNKS):
        partial = sum(
            dot(a, b, (1, 0)) for a, b in zip(h_lefts, halves(panels[k].reshape(ny * half, half)))
        )
        h_own.append(spread(after(copies_of(sum_x(partial, xh), nz), last), "z"))
        last = (h_own[-1], z_all[0])
    h_other = [swap(part, "xl") for part in h_own]

    def column_of(layer, k):
        return pl.multiple_of((layer ^ lax.axis_index("core")) * blk + k * half, half)

    def z_places():
        return [
            (k, 2 * layer + b, b * half, column_of(layer, k), half, half)
            for k in range(CHUNKS)
            for layer in range(nz)
            for b in range(2)
        ]

    def h_places():
        mine = lax.axis_index("xl")
        return [
            (k + CHUNKS * b, layer, pl.multiple_of((mine ^ b) * half, half), column_of(layer, k), half, half)
            for k in range(CHUNKS)
            for layer in range(nz)
            for b in range(2)
        ]

    return (
        place(z_all, z_places, (blk, width)),
        place(h_own + h_other, h_places, (blk, width)),
    )


def solution(mesh):
    parts = Mesh(mesh.devices.reshape(8, 2, 2, 8, 2), ("y", "xh", "core", "z", "xl"))
    spec = P(ROW, "core")
    return jax.shard_map(
        local,
        mesh=parts,
        in_specs=(spec, spec, spec, P(), P(), P()),
        out_specs=(spec, spec),
        check_vma=False,
    )
```

time: 271 us -> 308 us (1.14)
  starting transfers between devices: 51 us -> 139 us
  blocking collectives: 59.8 us -> 0 us
  waiting for transfers between devices: 109 us -> 102 us
  local copies, waits for them, and re-layouts: 6.01 us -> 11.4 us
  matrix products: 4.38 us -> 9.71 us
  other arithmetic: 20.8 us -> 24.7 us
    ppermute x0 -> x20, starting transfers between devices: none -> 61.1 us  [the longest x12 39.3 us: sum_x(): total = total + lax.ppermute(share(xh ^ a, xl ^ b), X, pairs)]
    all_to_all x3 -> x0, blocking collectives: 59.8 us -> none  [the longest x2 49.3 us: spread(): return lax.all_to_all(copies, axis, split_axis=0, concat_axis=0, tiled=True)]
    all_to_all x2 -> x8, starting transfers between devices: 9.1 us -> 58.9 us  [spread(): return lax.all_to_all(copies, axis, split_axis=0, concat_axis=0, tiled=True)]
    ppermute x7 -> x6, waiting for transfers between devices: 31 us -> 0.02 us  [swap(): return lax.ppermute(array, axis, [(0, 1), (1, 0)])]
    ppermute x0 -> x20, waiting for transfers between devices: none -> 23.7 us  [the longest x12 12.5 us: sum_x(): total = total + lax.ppermute(share(xh ^ a, xl ^ b), X, pairs)]
    all_gather x2 -> x3, waiting for transfers between devices: 31.1 us -> 48.9 us  [the longest x2 48.9 us: local(): z_all = [lax.all_gather(share, DEPTH, axis=0) for share in z_shares]]
    all_to_all x3 -> x0, starting transfers between devices: 16.9 us -> none  [the longest x1 8.64 us: local(): lax.all_to_all(y_copies, 'y', split_axis=0, concat_axis=0, tiled=True)]
    all_to_all x3 -> x0, waiting for transfers between devices: 9.77 us -> none  [the longest x2 9.77 us: sum_x(): lax.all_to_all(parts, X, split_axis=0, concat_axis=0, tiled=True)]
  transfers between devices with their start and end apart: 16 -> 39, of which waited for: 14 -> 12; matrix products, arithmetic and copies ran while one was open for 8% -> 13% of each run, Pallas kernels for 1% -> 1%
where the time goes in v4:
time: 308 us; the launch traced here: 305 us
  starting transfers between devices  139 us (45%)
  waiting for transfers between devices  102 us (33%)
  other arithmetic  24.7 us (8%)
  between operations  14.6 us (5%)
  local copies, waits for them, and re-layouts  11.4 us (4%)
  matrix products  9.71 us (3%)
  Pallas kernels  3.19 us (1%)
    all_to_all x8, starting transfers between devices, spread(): return lax.all_to_all(copies, axis, split_axis=0, concat_axis=0, tiled=True)  58.9 us
    all_gather x2, waiting for transfers between devices, local(): z_all = [lax.all_gather(share, DEPTH, axis=0) for share in z_shares]  48.9 us
    ppermute x12, starting transfers between devices, sum_x(): total = total + lax.ppermute(share(xh ^ a, xl ^ b), X, pairs)  39.3 us
    ppermute x8, starting transfers between devices, t_share(): got = lax.ppermute(share, PLANE, pairs)  21.8 us
    all_to_all x8, waiting for transfers between devices, spread(): return lax.all_to_all(copies, axis, split_axis=0, concat_axis=0, tiled=True)  17.2 us
    ppermute x12, waiting for transfers between devices, sum_x(): total = total + lax.ppermute(share(xh ^ a, xl ^ b), X, pairs)  12.5 us
    ppermute x6, starting transfers between devices, swap(): return lax.ppermute(array, axis, [(0, 1), (1, 0)])  12.3 us
    ppermute x2, waiting for transfers between devices, left(): lax.ppermute(pick(1 - xh, 1 - xl), X, [(0, 3), (3, 0), (1, 2), (2, 1)])  11.5 us
  transfers between devices with their start and end apart: 39, of which 12 were waited for; matrix products, arithmetic and copies ran while one was open for 13% of the time, Pallas kernels for 1%

profile of v4, /device:TPU:56, one launch (start us, length us, event | category | flops | bytes accessed | tf_op | source)
XLA Modules:
  0.0 305.1 jit_solution(13848941596164459814)
XLA Ops:
  7.2 0.8 convert_element_type.10
  8.7 1.5 dynamic-slice_multiply_fusion.16
  10.3 0.8 broadcast_in_dim.28
  11.1 8.6 %all-to-all-start = ((f32[8,128,128]{2,1,0:T(8,128)}), f32[8,128,128]{2,1,0:T(8,128)S(1)}, u32[]{:S(2)}, u32[]{:S(2)}) async-start(f32[8,128,128]{2,1,0:T(8,128)} %broadcast_in_dim.28), calls=%async_computation | async-start | bytes 1048576 | tf_op jit(solution)/shard_map/all_to_all | solution.py:22
  19.7 5.2 %dynamic-slice_multiply_fusion.15 = (f32[256,128]{1,0:T(8,128)S(1)}, f32[256,128]{1,0:T(8,128)S(1)}, f32[256,128]{1,0:T(8,128)S(1)}, f32[256,128]{1,0:T(8,128)S(...) fusion(f32[256,2048]{1,0:T(8,128)S(1)} %copy-done.2, ...), kind=kLoop, calls=%fused_computation.43 | loop fusion | flops 262144 | bytes 2097216 | tf_op jit(solution)/shard_map/mul | solution.py:69
  24.9 3.0 collective-permute-start
  27.9 11.5 %collective-permute-done = f32[256,512]{1,0:T(8,128)S(1)} collective-permute-done((f32[256,512]{1,0:T(8,128)S(1)}, f32[256,512]{1,0:T(8,128)S(1)}, u32[]{:S(2)}, u32[]{:S(2)}) %collective-permute-start) | collective-permute-done | bytes 524320 | tf_op jit(solution)/shard_map/ppermute | solution.py:77
  39.4 1.1 pad_maximum_fusion
  40.5 1.9 collective-permute-start.1
  42.5 0.9 dynamic-slice_bitcast_fusion.1
  44.2 7.2 %all-to-all-start.1 = ((f32[8,128,128]{2,1,0:T(8,128)}), f32[8,128,128]{2,1,0:T(8,128)S(1)}, u32[]{:S(2)}, u32[]{:S(2)}) async-start(f32[8,128,128]{2,1,0:T(8,128)} %broadcast_in_dim.30), calls=%async_computation.1 | async-start | bytes 1048576 | tf_op jit(solution)/shard_map/all_to_all | solution.py:22
  51.4 1.3 maximum_multiply_fusion
  55.0 5.1 %collective-permute-start.3 = (f32[64,256]{1,0:T(8,128)S(1)}, f32[64,256]{1,0:T(8,128)S(1)}, u32[]{:S(2)}, u32[]{:S(2)}) collective-permute-start(f32[64,256]{1,0:T(8,128)S(1)} %get-tuple-element.60), channel_id=1, source_target_pairs={{0,16},{1,0},{2,50},{3,34},{4,20},{5,4},{6,54},{7,38},{8,24},{9,8}... | collective-permute-start | bytes 196616 | tf_op jit(solution)/shard_map/ppermute | solution.py:142
  60.1 1.9 collective-permute-start.4
  62.1 3.4 %collective-permute-start.5 = (f32[64,256]{1,0:T(8,128)S(1)}, f32[64,256]{1,0:T(8,128)S(1)}, u32[]{:S(2)}, u32[]{:S(2)}) collective-permute-start(f32[64,256]{1,0:T(8,128)S(1)} %get-tuple-element.61), channel_id=1, source_target_pairs={{0,17},{1,1},{2,51},{3,35},{4,21},{5,5},{6,55},{7,39},{8,25},{9,9}... | collective-permute-start | bytes 196616 | tf_op jit(solution)/shard_map/ppermute | solution.py:142
  66.3 1.5 collective-permute-done.4
  67.8 4.1 %collective-permute-done.5 = f32[64,256]{1,0:T(8,128)S(1)} collective-permute-done((f32[64,256]{1,0:T(8,128)S(1)}, f32[64,256]{1,0:T(8,128)S(1)}, u32[]{:S(2)}, u32[]{:S(2)}) %collective-permute-start.5) | collective-permute-done | bytes 65568 | tf_op jit(solution)/shard_map/ppermute | solution.py:142
  72.5 0.8 broadcast_in_dim.29
  73.4 10.3 %all-to-all-start.2 = ((f32[8,64,256]{2,1,0:T(8,128)}), f32[8,64,256]{2,1,0:T(8,128)S(1)}, u32[]{:S(2)}, u32[]{:S(2)}) async-start(f32[8,64,256]{2,1,0:T(8,128)} %broadcast_in_dim.29), calls=%async_computation.2 | async-start | bytes 1048576 | tf_op jit(solution)/shard_map/all_to_all | solution.py:22
  85.8 2.8 collective-permute-start.7
  88.6 3.4 %collective-permute-start.8 = (f32[64,256]{1,0:T(8,128)S(1)}, f32[64,256]{1,0:T(8,128)S(1)}, u32[]{:S(2)}, u32[]{:S(2)}) collective-permute-start(f32[64,256]{1,0:T(8,128)S(1)} %get-tuple-element.58), channel_id=1, source_target_pairs={{0,1},{1,17},{2,35},{3,51},{4,5},{5,21},{6,39},{7,55},{8,9},{9,25}... | collective-permute-start | bytes 196616 | tf_op jit(solution)/shard_map/ppermute | solution.py:142
  92.1 3.7 %collective-permute-start.9 = (f32[64,256]{1,0:T(8,128)S(1)}, f32[64,256]{1,0:T(8,128)S(1)}, u32[]{:S(2)}, u32[]{:S(2)}) collective-permute-start(f32[64,256]{1,0:T(8,128)S(1)} %get-tuple-element.57), channel_id=1, source_target_pairs={{0,17},{1,1},{2,51},{3,35},{4,21},{5,5},{6,55},{7,39},{8,25},{9,9}... | collective-permute-start | bytes 196616 | tf_op jit(solution)/shard_map/ppermute | solution.py:142
  96.3 5.1 %collective-permute-done.9 = f32[64,256]{1,0:T(8,128)S(1)} collective-permute-done((f32[64,256]{1,0:T(8,128)S(1)}, f32[64,256]{1,0:T(8,128)S(1)}, u32[]{:S(2)}, u32[]{:S(2)}) %collective-permute-start.9) | collective-permute-done | bytes 65568 | tf_op jit(solution)/shard_map/ppermute | solution.py:142
  102.1 0.8 broadcast_in_dim.31
  102.9 7.9 %all-to-all-start.3 = ((f32[8,64,256]{2,1,0:T(8,128)}), f32[8,64,256]{2,1,0:T(8,128)S(1)}, u32[]{:S(2)}, u32[]{:S(2)}) async-start(f32[8,64,256]{2,1,0:T(8,128)} %broadcast_in_dim.31), calls=%async_computation.3 | async-start | bytes 1048576 | tf_op jit(solution)/shard_map/all_to_all | solution.py:22
  110.9 6.2 %dynamic-slice_multiply_fusion.7 = (f32[256,128]{1,0:T(8,128)S(1)}, f32[256,128]{1,0:T(8,128)S(1)}, f32[256,128]{1,0:T(8,128)S(1)}, f32[256,128]{1,0:T(8,128)S(1...) fusion(f32[256,2048]{1,0:T(8,128)} %param.8, ...), kind=kLoop, calls=%fused_computation.35 | loop fusion | flops 262144 | bytes 2097216 | tf_op jit(solution)/shard_map/mul | solution.py:69
  117.2 4.2 %collective-permute-start.18 = (f32[256,512]{1,0:T(8,128)S(1)}, f32[256,512]{1,0:T(8,128)}, u32[]{:S(2)}, u32[]{:S(2)}) collective-permute-start(f32[256,512]{1,0:T(8,128)S(1)} %pad_maximum_fusion.4), channel_id=1, source_target_pairs={{0,33},{33,0},{1,32},{32,1},{2,35},{35,2},{3,34},{34,3},{4,37},{37... | collective-permute-start | bytes 1572872 | tf_op jit(solution)/shard_map/ppermute | solution.py:77
  121.4 1.8 reverse_select_fusion
  123.2 4.9 %all-to-all-done.3 = f32[8,64,256]{2,1,0:T(8,128)S(1)} async-done(((f32[8,64,256]{2,1,0:T(8,128)}), f32[8,64,256]{2,1,0:T(8,128)S(1)}, u32[]{:S(2)}, u32[]{:S(2)}) %all-to-all-start.3) | async-done | bytes 524320 | tf_op jit(solution)/shard_map/all_to_all | solution.py:22
  128.1 1.9 collective-permute-start.11
  130.2 2.4 collective-permute-start.10
  135.2 1.9 collective-permute-start.12
  137.1 1.9 collective-permute-start.13
  139.0 6.0 %collective-permute-start.14 = (f32[128,128]{1,0:T(8,128)S(1)}, f32[128,128]{1,0:T(8,128)S(1)}, u32[]{:S(2)}, u32[]{:S(2)}) collective-permute-start(f32[128,128]{1,0:T(8,128)S(1)} %get-tuple-element.54), channel_id=1, source_target_pairs={{0,32},{1,33},{32,0},{33,1},{2,34},{3,35},{34,2},{35,3},{4,36},{5,... | collective-permute-start | bytes 196616 | tf_op jit(solution)/shard_map/ppermute | solution.py:99
  145.0 2.1 pad_maximum_fusion.1
  147.1 1.9 collective-permute-start.19
  149.0 1.3 add_multiply_fusion.3
  150.3 1.7 broadcast_in_dim.32
  152.0 7.2 %all-to-all-start.4 = ((f32[8,128,128]{2,1,0:T(8,128)}), f32[8,128,128]{2,1,0:T(8,128)S(1)}, u32[]{:S(2)}, u32[]{:S(2)}) async-start(f32[8,128,128]{2,1,0:T(8,128)} %broadcast_in_dim.32), calls=%async_computation.4 | async-start | bytes 1048576 | tf_op jit(solution)/shard_map/all_to_all | solution.py:22
  159.3 1.9 collective-permute-start.15
  161.2 4.2 %collective-permute-start.16 = (f32[128,128]{1,0:T(8,128)S(1)}, f32[128,128]{1,0:T(8,128)S(1)}, u32[]{:S(2)}, u32[]{:S(2)}) collective-permute-start(f32[128,128]{1,0:T(8,128)S(1)} %get-tuple-element.52), channel_id=1, source_target_pairs={{0,33},{1,32},{32,1},{33,0},{2,35},{3,34},{34,3},{35,2},{4,37},{5,... | collective-permute-start | bytes 196616 | tf_op jit(solution)/shard_map/ppermute | solution.py:99
  165.4 3.7 %collective-permute-start.17 = (f32[128,128]{1,0:T(8,128)S(1)}, f32[128,128]{1,0:T(8,128)S(1)}, u32[]{:S(2)}, u32[]{:S(2)}) collective-permute-start(f32[128,128]{1,0:T(8,128)S(1)} %get-tuple-element.51), channel_id=1, source_target_pairs={{0,32},{1,33},{32,0},{33,1},{2,34},{3,35},{34,2},{35,3},{4,36},{5,... | collective-permute-start | bytes 196616 | tf_op jit(solution)/shard_map/ppermute | solution.py:99
  169.2 4.3 %collective-permute-done.17 = f32[128,128]{1,0:T(8,128)S(1)} collective-permute-done((f32[128,128]{1,0:T(8,128)S(1)}, f32[128,128]{1,0:T(8,128)S(1)}, u32[]{:S(2)}, u32[]{:S(2)}) %collective-permute-start.17) | collective-permute-done | bytes 65568 | tf_op jit(solution)/shard_map/ppermute | solution.py:99
  174.9 7.2 %all-to-all-start.5 = ((f32[8,128,128]{2,1,0:T(8,128)}), f32[8,128,128]{2,1,0:T(8,128)S(1)}, u32[]{:S(2)}, u32[]{:S(2)}) async-start(f32[8,128,128]{2,1,0:T(8,128)} %broadcast_in_dim.34), calls=%async_computation.5 | async-start | bytes 1048576 | tf_op jit(solution)/shard_map/all_to_all | solution.py:22
  182.7 1.6 convolution_add_fusion.3
  184.4 1.9 collective-permute-start.20
  186.3 4.2 %collective-permute-start.21 = (f32[128,128]{1,0:T(8,128)S(1)}, f32[128,128]{1,0:T(8,128)S(1)}, u32[]{:S(2)}, u32[]{:S(2)}) collective-permute-start(f32[128,128]{1,0:T(8,128)S(1)} %get-tuple-element.49), channel_id=1, source_target_pairs={{0,33},{1,32},{32,1},{33,0},{2,35},{3,34},{34,3},{35,2},{4,37},{5,... | collective-permute-start | bytes 196616 | tf_op jit(solution)/shard_map/ppermute | solution.py:99
  190.6 3.7 %collective-permute-start.22 = (f32[128,128]{1,0:T(8,128)S(1)}, f32[128,128]{1,0:T(8,128)S(1)}, u32[]{:S(2)}, u32[]{:S(2)}) collective-permute-start(f32[128,128]{1,0:T(8,128)S(1)} %get-tuple-element.48), channel_id=1, source_target_pairs={{0,32},{1,33},{32,0},{33,1},{2,34},{3,35},{34,2},{35,3},{4,36},{5,... | collective-permute-start | bytes 196616 | tf_op jit(solution)/shard_map/ppermute | solution.py:99
  194.2 4.2 %collective-permute-done.22 = f32[128,128]{1,0:T(8,128)S(1)} collective-permute-done((f32[128,128]{1,0:T(8,128)S(1)}, f32[128,128]{1,0:T(8,128)S(1)}, u32[]{:S(2)}, u32[]{:S(2)}) %collective-permute-start.22) | collective-permute-done | bytes 65568 | tf_op jit(solution)/shard_map/ppermute | solution.py:99
  200.0 3.5 %all-to-all-start.6 = ((f32[8,128,128]{2,1,0:T(8,128)}), f32[8,128,128]{2,1,0:T(8,128)S(1)}, u32[]{:S(2)}, u32[]{:S(2)}) async-start(f32[8,128,128]{2,1,0:T(8,128)} %broadcast_in_dim.33), calls=%async_computation.6 | async-start | bytes 1048576 | tf_op jit(solution)/shard_map/all_to_all | solution.py:22
  204.8 1.6 convolution_add_fusion.2
  206.5 2.8 collective-permute-start.23
  209.3 3.2 %collective-permute-start.24 = (f32[128,128]{1,0:T(8,128)S(1)}, f32[128,128]{1,0:T(8,128)S(1)}, u32[]{:S(2)}, u32[]{:S(2)}) collective-permute-start(f32[128,128]{1,0:T(8,128)S(1)} %get-tuple-element.46), channel_id=1, source_target_pairs={{0,33},{1,32},{32,1},{33,0},{2,35},{3,34},{34,3},{35,2},{4,37},{5,... | collective-permute-start | bytes 196616 | tf_op jit(solution)/shard_map/ppermute | solution.py:99
  212.6 3.8 %collective-permute-start.25 = (f32[128,128]{1,0:T(8,128)S(1)}, f32[128,128]{1,0:T(8,128)S(1)}, u32[]{:S(2)}, u32[]{:S(2)}) collective-permute-start(f32[128,128]{1,0:T(8,128)S(1)} %get-tuple-element.45), channel_id=1, source_target_pairs={{0,32},{1,33},{32,0},{33,1},{2,34},{3,35},{34,2},{35,3},{4,36},{5,... | collective-permute-start | bytes 196616 | tf_op jit(solution)/shard_map/ppermute | solution.py:99
  216.3 1.1 collective-permute-done.24
  217.4 2.9 collective-permute-done.25
  221.8 7.0 %all-to-all-start.7 = ((f32[8,128,128]{2,1,0:T(8,128)}), f32[8,128,128]{2,1,0:T(8,128)S(1)}, u32[]{:S(2)}, u32[]{:S(2)}) async-start(f32[8,128,128]{2,1,0:T(8,128)} %broadcast_in_dim.35), calls=%async_computation.7 | async-start | bytes 1048576 | tf_op jit(solution)/shard_map/all_to_all | solution.py:22
  228.9 2.3 collective-permute-start.26
  231.1 12.2 %all-to-all-done.7.refs_1_ = f32[8,128,128]{2,1,0:T(8,128)S(1)} async-done(((f32[8,128,128]{2,1,0:T(8,128)}), f32[8,128,128]{2,1,0:T(8,128)S(1)}, u32[]{:S(2)}, u32[]{:S(2)}) %all-to-all-start.7) | async-done | bytes 524320 | tf_op jit(solution)/shard_map/all_to_all | solution.py:22
  243.4 1.9 collective-permute-start.27
  245.3 48.8 %all-gather.10.cloned.1.call-done = f32[2048,128]{1,0:T(8,128)} async-done(((f32[128,128]{1,0:T(8,128)}), f32[2048,128]{1,0:T(8,128)}) %all-gather.10.cloned.1.call-update) | async-done | bytes 1048592 | tf_op jit(solution)/shard_map/all_gather | solution.py:165
  294.1 1.2 copy-done.1
  295.3 1.6 shard_map.77
  296.9 1.6 shard_map.78
  (91 shorter events, 17.8 us)
Async XLA Ops:
  7.2 12.5 %copy-start.2 = (f32[256,2048]{1,0:T(8,128)S(1)}, f32[256,2048]{1,0:T(8,128)}, u32[]{:S(2)}) copy-start(f32[256,2048]{1,0:T(8,128)} %param.7) | copy-start | bytes 6291460
  11.1 28.3 %all-to-all-start = ((f32[8,128,128]{2,1,0:T(8,128)}), f32[8,128,128]{2,1,0:T(8,128)S(1)}, u32[]{:S(2)}, u32[]{:S(2)}) async-start(f32[8,128,128]{2,1,0:T(8,128)} %broadcast_in_dim.28), calls=%async_computation | async-start | bytes 1048576 | tf_op jit(solution)/shard_map/all_to_all | solution.py:22
  24.9 14.5 %collective-permute-start = (f32[256,512]{1,0:T(8,128)S(1)}, f32[256,512]{1,0:T(8,128)S(1)}, u32[]{:S(2)}, u32[]{:S(2)}) collective-permute-start(f32[256,512]{1,0:T(8,128)S(1)} %pad_maximum_fusion.3), channel_id=1, source_target_pairs={{0,33},{33,0},{1,32},{32,1},{2,35},{35,2},{3,34},{34,3},{4,37},{37... | collective-permute-start | bytes 1572872 | tf_op jit(solution)/shard_map/ppermute | solution.py:77
  39.4 13.3 %copy-start.4 = (f32[256,512]{1,0:T(8,128)}, f32[256,512]{1,0:T(8,128)S(1)}, u32[]{:S(2)}) copy-start(f32[256,512]{1,0:T(8,128)S(1)} %collective-permute-done) | copy-start | bytes 1572868
  40.5 12.9 %collective-permute-start.1 = (f32[512,512]{1,0:T(8,128)}, f32[512,512]{1,0:T(8,128)S(1)}, u32[]{:S(2)}, u32[]{:S(2)}) collective-permute-start(f32[512,512]{1,0:T(8,128)} %pad_maximum_fusion), channel_id=1, source_target_pairs={{0,16},{16,0},{1,17},{17,1},{2,18},{18,2},{3,19},{19,3},{4,20},{20... | collective-permute-start | bytes 3145736 | tf_op jit(solution)/shard_map/ppermute | solution.py:26
  44.2 28.3 %all-to-all-start.1 = ((f32[8,128,128]{2,1,0:T(8,128)}), f32[8,128,128]{2,1,0:T(8,128)S(1)}, u32[]{:S(2)}, u32[]{:S(2)}) async-start(f32[8,128,128]{2,1,0:T(8,128)} %broadcast_in_dim.30), calls=%async_computation.1 | async-start | bytes 1048576 | tf_op jit(solution)/shard_map/all_to_all | solution.py:22
  51.4 70.0 %all-gather.6.cloned.1.call-start = ((), (), s32[]{:S(2)}) async-start(), calls=%async_computation.8 | async-start | bytes 1179648 | tf_op jit(solution)/shard_map/all_gather | solution.py:117
  52.7 12.8 %copy-start.6 = (s32[16,16]{1,0:T(8,128)S(1)}, s32[16,16]{1,0:T(8,128)}, u32[]{:S(2)}) copy-start(s32[16,16]{1,0:T(8,128)} %param.10) | copy-start | bytes 3076
  52.7 12.8 %copy-start.7 = (s32[16,16]{1,0:T(8,128)S(1)}, s32[16,16]{1,0:T(8,128)}, u32[]{:S(2)}) copy-start(s32[16,16]{1,0:T(8,128)} %param.11) | copy-start | bytes 3076
  54.2 29.5 %copy-start.5 = (f32[256,512]{1,0:T(8,128)S(1)}, f32[256,512]{1,0:T(8,128)}, u32[]{:S(2)}) copy-start(f32[256,512]{1,0:T(8,128)} %copy-done.4) | copy-start | bytes 1572868
  54.2 12.0 %collective-permute-start.2 = (f32[64,256]{1,0:T(8,128)S(1)}, f32[64,256]{1,0:T(8,128)S(1)}, u32[]{:S(2)}, u32[]{:S(2)}) collective-permute-start(f32[64,256]{1,0:T(8,128)S(1)} %get-tuple-element.63), channel_id=1, source_target_pairs={{0,0},{1,16},{2,34},{3,50},{4,4},{5,20},{6,38},{7,54},{8,8},{9,24}... | collective-permute-start | bytes 196616 | tf_op jit(solution)/shard_map/ppermute | solution.py:142
  55.0 11.2 %collective-permute-start.3 = (f32[64,256]{1,0:T(8,128)S(1)}, f32[64,256]{1,0:T(8,128)S(1)}, u32[]{:S(2)}, u32[]{:S(2)}) collective-permute-start(f32[64,256]{1,0:T(8,128)S(1)} %get-tuple-element.60), channel_id=1, source_target_pairs={{0,16},{1,0},{2,50},{3,34},{4,20},{5,4},{6,54},{7,38},{8,24},{9,8}... | collective-permute-start | bytes 196616 | tf_op jit(solution)/shard_map/ppermute | solution.py:142
  60.1 7.7 %collective-permute-start.4 = (f32[64,256]{1,0:T(8,128)S(1)}, f32[64,256]{1,0:T(8,128)S(1)}, u32[]{:S(2)}, u32[]{:S(2)}) collective-permute-start(f32[64,256]{1,0:T(8,128)S(1)} %get-tuple-element.62), channel_id=1, source_target_pairs={{0,1},{1,17},{2,35},{3,51},{4,5},{5,21},{6,39},{7,55},{8,9},{9,25}... | collective-permute-start | bytes 196616 | tf_op jit(solution)/shard_map/ppermute | solution.py:142
  62.1 9.8 %collective-permute-start.5 = (f32[64,256]{1,0:T(8,128)S(1)}, f32[64,256]{1,0:T(8,128)S(1)}, u32[]{:S(2)}, u32[]{:S(2)}) collective-permute-start(f32[64,256]{1,0:T(8,128)S(1)} %get-tuple-element.61), channel_id=1, source_target_pairs={{0,17},{1,1},{2,51},{3,35},{4,21},{5,5},{6,55},{7,39},{8,25},{9,9}... | collective-permute-start | bytes 196616 | tf_op jit(solution)/shard_map/ppermute | solution.py:142
  73.4 28.7 %all-to-all-start.2 = ((f32[8,64,256]{2,1,0:T(8,128)}), f32[8,64,256]{2,1,0:T(8,128)S(1)}, u32[]{:S(2)}, u32[]{:S(2)}) async-start(f32[8,64,256]{2,1,0:T(8,128)} %broadcast_in_dim.29), calls=%async_computation.2 | async-start | bytes 1048576 | tf_op jit(solution)/shard_map/all_to_all | solution.py:22
  85.1 10.6 %collective-permute-start.6 = (f32[64,256]{1,0:T(8,128)S(1)}, f32[64,256]{1,0:T(8,128)S(1)}, u32[]{:S(2)}, u32[]{:S(2)}) collective-permute-start(f32[64,256]{1,0:T(8,128)S(1)} %get-tuple-element.59), channel_id=1, source_target_pairs={{0,0},{1,16},{2,34},{3,50},{4,4},{5,20},{6,38},{7,54},{8,8},{9,24}... | collective-permute-start | bytes 196616 | tf_op jit(solution)/shard_map/ppermute | solution.py:142
  85.8 10.0 %collective-permute-start.7 = (f32[64,256]{1,0:T(8,128)S(1)}, f32[64,256]{1,0:T(8,128)S(1)}, u32[]{:S(2)}, u32[]{:S(2)}) collective-permute-start(f32[64,256]{1,0:T(8,128)S(1)} %get-tuple-element.56), channel_id=1, source_target_pairs={{0,16},{1,0},{2,50},{3,34},{4,20},{5,4},{6,54},{7,38},{8,24},{9,8}... | collective-permute-start | bytes 196616 | tf_op jit(solution)/shard_map/ppermute | solution.py:142
  88.6 7.7 %collective-permute-start.8 = (f32[64,256]{1,0:T(8,128)S(1)}, f32[64,256]{1,0:T(8,128)S(1)}, u32[]{:S(2)}, u32[]{:S(2)}) collective-permute-start(f32[64,256]{1,0:T(8,128)S(1)} %get-tuple-element.58), channel_id=1, source_target_pairs={{0,1},{1,17},{2,35},{3,51},{4,5},{5,21},{6,39},{7,55},{8,9},{9,25}... | collective-permute-start | bytes 196616 | tf_op jit(solution)/shard_map/ppermute | solution.py:142
  92.1 9.4 %collective-permute-start.9 = (f32[64,256]{1,0:T(8,128)S(1)}, f32[64,256]{1,0:T(8,128)S(1)}, u32[]{:S(2)}, u32[]{:S(2)}) collective-permute-start(f32[64,256]{1,0:T(8,128)S(1)} %get-tuple-element.57), channel_id=1, source_target_pairs={{0,17},{1,1},{2,51},{3,35},{4,21},{5,5},{6,55},{7,39},{8,25},{9,9}... | collective-permute-start | bytes 196616 | tf_op jit(solution)/shard_map/ppermute | solution.py:142
  102.9 25.2 %all-to-all-start.3 = ((f32[8,64,256]{2,1,0:T(8,128)}), f32[8,64,256]{2,1,0:T(8,128)S(1)}, u32[]{:S(2)}, u32[]{:S(2)}) async-start(f32[8,64,256]{2,1,0:T(8,128)} %broadcast_in_dim.31), calls=%async_computation.3 | async-start | bytes 1048576 | tf_op jit(solution)/shard_map/all_to_all | solution.py:22
  110.8 110.2 %all-gather.8.cloned.1.call-start = ((), (), s32[]{:S(2)}) async-start(), calls=%async_computation.9 | async-start | bytes 1114112 | tf_op jit(solution)/shard_map/all_gather | solution.py:165
  117.2 27.8 %collective-permute-start.18 = (f32[256,512]{1,0:T(8,128)S(1)}, f32[256,512]{1,0:T(8,128)}, u32[]{:S(2)}, u32[]{:S(2)}) collective-permute-start(f32[256,512]{1,0:T(8,128)S(1)} %pad_maximum_fusion.4), channel_id=1, source_target_pairs={{0,33},{33,0},{1,32},{32,1},{2,35},{35,2},{3,34},{34,3},{4,37},{37... | collective-permute-start | bytes 1572872 | tf_op jit(solution)/shard_map/ppermute | solution.py:77
  128.1 5.7 %collective-permute-start.11 = (f32[8,64,256]{2,1,0:T(8,128)S(1)}, f32[8,64,256]{2,1,0:T(8,128)S(1)}, u32[]{:S(2)}, u32[]{:S(2)}) collective-permute-start(f32[8,64,256]{2,1,0:T(8,128)S(1)} %all-to-all-done.3), channel_id=1, source_target_pairs={{0,16},{16,0},{1,17},{17,1},{2,18},{18,2},{3,19},{19,3},{4,20},{20... | collective-permute-start | bytes 1572872 | tf_op jit(solution)/shard_map/ppermute | solution.py:26
  130.2 4.3 %collective-permute-start.10 = (f32[8,64,256]{2,1,0:T(8,128)S(1)}, f32[8,64,256]{2,1,0:T(8,128)S(1)}, u32[]{:S(2)}, u32[]{:S(2)}) collective-permute-start(f32[8,64,256]{2,1,0:T(8,128)S(1)} %all-to-all-done.2), channel_id=1, source_target_pairs={{0,16},{16,0},{1,17},{17,1},{2,18},{18,2},{3,19},{19,3},{4,20},{20... | collective-permute-start | bytes 1572872 | tf_op jit(solution)/shard_map/ppermute | solution.py:26
  135.2 13.9 %collective-permute-start.12 = (f32[128,128]{1,0:T(8,128)S(1)}, f32[128,128]{1,0:T(8,128)S(1)}, u32[]{:S(2)}, u32[]{:S(2)}) collective-permute-start(f32[128,128]{1,0:T(8,128)S(1)} %get-tuple-element.53), channel_id=1, source_target_pairs={{0,1},{1,0},{32,33},{33,32},{2,3},{3,2},{34,35},{35,34},{4,5},{5,4... | collective-permute-start | bytes 196616 | tf_op jit(solution)/shard_map/ppermute | solution.py:99
  137.1 11.9 %collective-permute-start.13 = (f32[128,128]{1,0:T(8,128)S(1)}, f32[128,128]{1,0:T(8,128)S(1)}, u32[]{:S(2)}, u32[]{:S(2)}) collective-permute-start(f32[128,128]{1,0:T(8,128)S(1)} %get-tuple-element.55), channel_id=1, source_target_pairs={{0,33},{1,32},{32,1},{33,0},{2,35},{3,34},{34,3},{35,2},{4,37},{5,... | collective-permute-start | bytes 196616 | tf_op jit(solution)/shard_map/ppermute | solution.py:99
  139.0 10.0 %collective-permute-start.14 = (f32[128,128]{1,0:T(8,128)S(1)}, f32[128,128]{1,0:T(8,128)S(1)}, u32[]{:S(2)}, u32[]{:S(2)}) collective-permute-start(f32[128,128]{1,0:T(8,128)S(1)} %get-tuple-element.54), channel_id=1, source_target_pairs={{0,32},{1,33},{32,0},{33,1},{2,34},{3,35},{34,2},{35,3},{4,36},{5,... | collective-permute-start | bytes 196616 | tf_op jit(solution)/shard_map/ppermute | solution.py:99
  147.1 35.0 %collective-permute-start.19 = (f32[512,512]{1,0:T(8,128)}, f32[512,512]{1,0:T(8,128)S(1)}, u32[]{:S(2)}, u32[]{:S(2)}) collective-permute-start(f32[512,512]{1,0:T(8,128)} %pad_maximum_fusion.1), channel_id=1, source_target_pairs={{0,16},{16,0},{1,17},{17,1},{2,18},{18,2},{3,19},{19,3},{4,20},{20... | collective-permute-start | bytes 3145736 | tf_op jit(solution)/shard_map/ppermute | solution.py:26
  152.0 22.1 %all-to-all-start.4 = ((f32[8,128,128]{2,1,0:T(8,128)}), f32[8,128,128]{2,1,0:T(8,128)S(1)}, u32[]{:S(2)}, u32[]{:S(2)}) async-start(f32[8,128,128]{2,1,0:T(8,128)} %broadcast_in_dim.32), calls=%async_computation.4 | async-start | bytes 1048576 | tf_op jit(solution)/shard_map/all_to_all | solution.py:22
  159.3 9.8 %collective-permute-start.15 = (f32[128,128]{1,0:T(8,128)S(1)}, f32[128,128]{1,0:T(8,128)S(1)}, u32[]{:S(2)}, u32[]{:S(2)}) collective-permute-start(f32[128,128]{1,0:T(8,128)S(1)} %get-tuple-element.50), channel_id=1, source_target_pairs={{0,1},{1,0},{32,33},{33,32},{2,3},{3,2},{34,35},{35,34},{4,5},{5,4... | collective-permute-start | bytes 196616 | tf_op jit(solution)/shard_map/ppermute | solution.py:99
  161.2 7.9 %collective-permute-start.16 = (f32[128,128]{1,0:T(8,128)S(1)}, f32[128,128]{1,0:T(8,128)S(1)}, u32[]{:S(2)}, u32[]{:S(2)}) collective-permute-start(f32[128,128]{1,0:T(8,128)S(1)} %get-tuple-element.52), channel_id=1, source_target_pairs={{0,33},{1,32},{32,1},{33,0},{2,35},{3,34},{34,3},{35,2},{4,37},{5,... | collective-permute-start | bytes 196616 | tf_op jit(solution)/shard_map/ppermute | solution.py:99
  165.4 8.0 %collective-permute-start.17 = (f32[128,128]{1,0:T(8,128)S(1)}, f32[128,128]{1,0:T(8,128)S(1)}, u32[]{:S(2)}, u32[]{:S(2)}) collective-permute-start(f32[128,128]{1,0:T(8,128)S(1)} %get-tuple-element.51), channel_id=1, source_target_pairs={{0,32},{1,33},{32,0},{33,1},{2,34},{3,35},{34,2},{35,3},{4,36},{5,... | collective-permute-start | bytes 196616 | tf_op jit(solution)/shard_map/ppermute | solution.py:99
  174.1 10.3 %copy-start.3 = (f32[128,128]{1,0:T(8,128)}, f32[128,128]{1,0:T(8,128)S(1)}, u32[]{:S(2)}) copy-start(f32[128,128]{1,0:T(8,128)S(1)} %add_multiply_fusion.2) | copy-start | bytes 196612
  174.9 24.2 %all-to-all-start.5 = ((f32[8,128,128]{2,1,0:T(8,128)}), f32[8,128,128]{2,1,0:T(8,128)S(1)}, u32[]{:S(2)}, u32[]{:S(2)}) async-start(f32[8,128,128]{2,1,0:T(8,128)} %broadcast_in_dim.34), calls=%async_computation.5 | async-start | bytes 1048576 | tf_op jit(solution)/shard_map/all_to_all | solution.py:22
  184.4 9.8 %collective-permute-start.20 = (f32[128,128]{1,0:T(8,128)S(1)}, f32[128,128]{1,0:T(8,128)S(1)}, u32[]{:S(2)}, u32[]{:S(2)}) collective-permute-start(f32[128,128]{1,0:T(8,128)S(1)} %get-tuple-element.47), channel_id=1, source_target_pairs={{0,1},{1,0},{32,33},{33,32},{2,3},{3,2},{34,35},{35,34},{4,5},{5,4... | collective-permute-start | bytes 196616 | tf_op jit(solution)/shard_map/ppermute | solution.py:99
  186.3 7.9 %collective-permute-start.21 = (f32[128,128]{1,0:T(8,128)S(1)}, f32[128,128]{1,0:T(8,128)S(1)}, u32[]{:S(2)}, u32[]{:S(2)}) collective-permute-start(f32[128,128]{1,0:T(8,128)S(1)} %get-tuple-element.49), channel_id=1, source_target_pairs={{0,33},{1,32},{32,1},{33,0},{2,35},{3,34},{34,3},{35,2},{4,37},{5,... | collective-permute-start | bytes 196616 | tf_op jit(solution)/shard_map/ppermute | solution.py:99
  190.6 7.9 %collective-permute-start.22 = (f32[128,128]{1,0:T(8,128)S(1)}, f32[128,128]{1,0:T(8,128)S(1)}, u32[]{:S(2)}, u32[]{:S(2)}) collective-permute-start(f32[128,128]{1,0:T(8,128)S(1)} %get-tuple-element.48), channel_id=1, source_target_pairs={{0,32},{1,33},{32,0},{33,1},{2,34},{3,35},{34,2},{35,3},{4,36},{5,... | collective-permute-start | bytes 196616 | tf_op jit(solution)/shard_map/ppermute | solution.py:99
  200.0 21.0 %all-to-all-start.6 = ((f32[8,128,128]{2,1,0:T(8,128)}), f32[8,128,128]{2,1,0:T(8,128)S(1)}, u32[]{:S(2)}, u32[]{:S(2)}) async-start(f32[8,128,128]{2,1,0:T(8,128)} %broadcast_in_dim.33), calls=%async_computation.6 | async-start | bytes 1048576 | tf_op jit(solution)/shard_map/all_to_all | solution.py:22
  203.5 90.6 %all-gather.10.cloned.1.call-start = ((), (), s32[]{:S(2)}) async-start(), calls=%async_computation.10 | async-start | bytes 1114112 | tf_op jit(solution)/shard_map/all_gather | solution.py:165
  206.5 9.8 %collective-permute-start.23 = (f32[128,128]{1,0:T(8,128)S(1)}, f32[128,128]{1,0:T(8,128)S(1)}, u32[]{:S(2)}, u32[]{:S(2)}) collective-permute-start(f32[128,128]{1,0:T(8,128)S(1)} %get-tuple-element.44), channel_id=1, source_target_pairs={{0,1},{1,0},{32,33},{33,32},{2,3},{3,2},{34,35},{35,34},{4,5},{5,4... | collective-permute-start | bytes 196616 | tf_op jit(solution)/shard_map/ppermute | solution.py:99
  209.3 8.1 %collective-permute-start.24 = (f32[128,128]{1,0:T(8,128)S(1)}, f32[128,128]{1,0:T(8,128)S(1)}, u32[]{:S(2)}, u32[]{:S(2)}) collective-permute-start(f32[128,128]{1,0:T(8,128)S(1)} %get-tuple-element.46), channel_id=1, source_target_pairs={{0,33},{1,32},{32,1},{33,0},{2,35},{3,34},{34,3},{35,2},{4,37},{5,... | collective-permute-start | bytes 196616 | tf_op jit(solution)/shard_map/ppermute | solution.py:99
  212.6 7.8 %collective-permute-start.25 = (f32[128,128]{1,0:T(8,128)S(1)}, f32[128,128]{1,0:T(8,128)S(1)}, u32[]{:S(2)}, u32[]{:S(2)}) collective-permute-start(f32[128,128]{1,0:T(8,128)S(1)} %get-tuple-element.45), channel_id=1, source_target_pairs={{0,32},{1,33},{32,0},{33,1},{2,34},{3,35},{34,2},{35,3},{4,36},{5,... | collective-permute-start | bytes 196616 | tf_op jit(solution)/shard_map/ppermute | solution.py:99
  221.0 73.1 %copy-start = (f32[2048,128]{1,0:T(8,128)S(1)}, f32[2048,128]{1,0:T(8,128)}, u32[]{:S(2)}) copy-start(f32[2048,128]{1,0:T(8,128)} %all-gather.8.cloned.1.call-done) | copy-start | bytes 3145732
  221.8 21.5 %all-to-all-start.7 = ((f32[8,128,128]{2,1,0:T(8,128)}), f32[8,128,128]{2,1,0:T(8,128)S(1)}, u32[]{:S(2)}, u32[]{:S(2)}) async-start(f32[8,128,128]{2,1,0:T(8,128)} %broadcast_in_dim.35), calls=%async_computation.7 | async-start | bytes 1048576 | tf_op jit(solution)/shard_map/all_to_all | solution.py:22
  228.9 68.1 %collective-permute-start.26 = (f32[8,128,128]{2,1,0:T(8,128)S(1)}, f32[8,128,128]{2,1,0:T(8,128)S(1)}, u32[]{:S(2)}, u32[]{:S(2)}) collective-permute-start(f32[8,128,128]{2,1,0:T(8,128)S(1)} %all-to-all-done.6.refs_0_), channel_id=1, source_target_pairs={{0,1},{1,0},{2,3},{3,2},{4,5},{5,4},{6,7},{7,6},{8,9},{9,8},{10,11... | collective-permute-start | bytes 1572872 | tf_op jit(solution)/shard_map/ppermute | solution.py:26
  243.4 53.6 %collective-permute-start.27 = (f32[8,128,128]{2,1,0:T(8,128)S(1)}, f32[8,128,128]{2,1,0:T(8,128)S(1)}, u32[]{:S(2)}, u32[]{:S(2)}) collective-permute-start(f32[8,128,128]{2,1,0:T(8,128)S(1)} %all-to-all-done.7.refs_1_), channel_id=1, source_target_pairs={{0,1},{1,0},{2,3},{3,2},{4,5},{5,4},{6,7},{7,6},{8,9},{9,8},{10,11... | collective-permute-start | bytes 1572872 | tf_op jit(solution)/shard_map/ppermute | solution.py:26
  294.1 1.2 copy-start.1
Sparse Core Ops, SparseCore 0:
  54.3 43.9 all-gather.5
  150.5 68.4 all-gather.7
  221.1 72.9 all-gather.9

commit v5 on v3

--- a/solution.py
+++ b/solution.py
@@ -20,29 +20,27 @@
     return lax.ppermute(array, axis, [(0, 1), (1, 0)])
 
 
-def place(own, other, blk):
-    layers = own[0].shape[0]
-    rows = own[0].shape[1]
-    n = len(own)
+def place(parts, blk):
+    layers = parts[0].shape[0]
+    half = blk // 2
 
     def kernel(*refs):
-        out = refs[2 * n]
+        out = refs[-1]
         xl = lax.axis_index("xl")
         core = lax.axis_index("core")
-        for k in range(2 * n):
-            mine = xl if k < n else 1 - xl
-            at = pl.multiple_of(mine * (n * rows) + (k % n) * rows, rows)
+        for share in range(2):
+            at = pl.multiple_of((xl ^ share) * half, half)
             for layer in range(layers):
                 to = pl.multiple_of((layer ^ core) * blk, blk)
-                out[pl.ds(at, rows), pl.ds(to, blk)] = refs[k][layer]
+                out[pl.ds(at, half), pl.ds(to, blk)] = refs[share][layer]
 
     return pl.pallas_call(
         kernel,
-        out_shape=jax.ShapeDtypeStruct((2 * n * rows, layers * blk), own[0].dtype),
-        in_specs=[pl.BlockSpec(memory_space=pltpu.VMEM)] * (2 * n),
+        out_shape=jax.ShapeDtypeStruct((blk, layers * blk), parts[0].dtype),
+        in_specs=[pl.BlockSpec(memory_space=pltpu.VMEM)] * len(parts),
         out_specs=pl.BlockSpec(memory_space=pltpu.VMEM),
         compiler_params=pltpu.CompilerParams(vmem_limit_bytes=24 * 1024 * 1024),
-    )(*own, *other)
+    )(*parts)
 
 
 def local(y_blocks, z_blocks, h_blocks, s_pattern, h_pattern, keep_mask):
@@ -92,10 +90,9 @@
         return sum_x(partial.reshape(4, half, blk)) * keep[row, column]
 
     y_copies = jnp.broadcast_to(piece(y_blocks)[None], (ny, half, blk))
-    y_copies, z_blocks, h_blocks = lax.optimization_barrier((y_copies, z_blocks, h_blocks))
+    y_copies, z_blocks = lax.optimization_barrier((y_copies, z_blocks))
     y_panel = lax.all_to_all(y_copies, "y", split_axis=0, concat_axis=0, tiled=True)
     y_panel = y_panel.reshape(ny * half, blk)
-    z_panel = lax.all_gather(piece(z_blocks), "y", axis=0)
     z_left = jnp.concatenate(left(z_blocks, fill), axis=0)
     t_part = multiply(z_left, swap(z_left, "core"), y_panel)
     at = (core ^ xh) * blk
@@ -111,8 +108,9 @@
     at_row = t_row * blk + lax.broadcasted_iota(jnp.int32, (blk, half), 0)
     at_col = t_col * blk + xl * half + lax.broadcasted_iota(jnp.int32, (blk, half), 1)
     q_share = jnp.where(at_row == at_col, 1.5, 0.0) - 0.5 * (keep[t_row, t_col] * t_share)
-    q_share, z_panel = lax.optimization_barrier((q_share, z_panel))
-    q_mine = spread(q_share, "z", nz)
+    q_mine = lax.all_gather(q_share, "z", axis=0)
+    z_piece, h_blocks, _ = lax.optimization_barrier((piece(z_blocks), h_blocks, q_share))
+    z_panel = spread(z_piece, "y", ny)
     q_theirs = swap(q_mine, "core")
     ordered = z_panel.reshape(2, ny // 2, half, blk).transpose(1, 0, 2, 3)
     ordered = jnp.where(xh == 0, ordered, ordered[:, ::-1]).reshape(ny * half, blk)
@@ -121,22 +119,31 @@
         q = q.transpose(1, 0, 2).reshape(blk, nz * half)
         return jnp.dot(q, ordered, precision=HIGH)
 
+    own, other = left(h_blocks, h_pattern.astype(jnp.float32))
+    own, other = jnp.where(xh == 0, own, other), jnp.where(xh == 0, other, own)
+    h_left = jnp.concatenate([own, other], axis=0)
+    h_theirs = swap(h_left, "core")
     z_mine, z_theirs = rows_of(q_mine), rows_of(q_theirs)
+    z_mine, h_left, h_theirs = lax.optimization_barrier((z_mine, h_left, h_theirs))
     first = core == 0
     z_share = finish(
         jnp.stack([jnp.where(first, z_mine, z_theirs), jnp.where(first, z_theirs, z_mine)])
     )
-    z_next_panel = spread(z_share, "y", ny).reshape(ny * half, blk)
+    z_copies = jnp.broadcast_to(z_share[None], (ny, half, blk))
+    z_next_panel = lax.all_to_all(z_copies, "y", split_axis=0, concat_axis=0, tiled=True)
+    z_next_panel = z_next_panel.reshape(ny * half, blk)
     z_own = lax.all_gather(z_share, "z", axis=0)
-    own, other = left(h_blocks, h_pattern.astype(jnp.float32))
-    own, other = jnp.where(xh == 0, own, other), jnp.where(xh == 0, other, own)
-    h_left = jnp.concatenate([own, other], axis=0)
-    h_partial = multiply(h_left, swap(h_left, "core"), z_next_panel)
+    h_partial = multiply(h_left, h_theirs, z_next_panel)
     h_share = finish(h_partial)
     h_share, z_own = lax.optimization_barrier((h_share, z_own))
-    z_next = place([z_own], [swap(z_own, "xl")], blk)
-    h_own = [spread(h_share[k * half // 2 : (k + 1) * half // 2], "z", nz) for k in range(2)]
-    h_times_z = place(h_own, [swap(part, "xl") for part in h_own], blk)
+    h_own = lax.all_gather(h_share, "z", axis=0)
+    h_swapped = swap(h_share, "xl")
+    h_copies, z_own = lax.optimization_barrier(
+        (jnp.broadcast_to(h_swapped[None], (nz, half, blk)), z_own)
+    )
+    h_other = lax.all_to_all(h_copies, "z", split_axis=0, concat_axis=0, tiled=True)
+    z_next = place([z_own, swap(z_own, "xl")], blk)
+    h_times_z = place([h_own, h_other], blk)
     return (z_next, h_times_z)
 
 

time: 271 us -> 246 us (0.908)
  blocking collectives: 59.8 us -> 24.5 us
  local copies, waits for them, and re-layouts: 6.01 us -> 9.82 us
  waiting for transfers between devices: 109 us -> 112 us
    all_to_all x2 -> x0, blocking collectives: 49.3 us -> none  [spread(): return lax.all_to_all(copies, axis, split_axis=0, concat_axis=0, tiled=True)]
    all_to_all x0 -> x2, waiting for transfers between devices: none -> 22.8 us  [the longest x1 22.8 us: local(): lax.all_to_all(z_copies, 'y', split_axis=0, concat_axis=0, tiled=True)]
    all_to_all x2 -> x1, waiting for transfers between devices: 20.9 us -> 0.01 us  [spread(): return lax.all_to_all(copies, axis, split_axis=0, concat_axis=0, tiled=True)]
    all_to_all x1 -> x2, blocking collectives: 10.5 us -> 24.5 us  [sum_x(): lax.all_to_all(parts, X, split_axis=0, concat_axis=0, tiled=True)]
    all_to_all x0 -> x2, starting transfers between devices: none -> 10.9 us  [the longest x1 6.99 us: local(): lax.all_to_all(z_copies, 'y', split_axis=0, concat_axis=0, tiled=True)]
    ppermute x2, waiting for transfers between devices: 15.8 us -> 23.8 us  [left(): lax.ppermute(pick(1 - xh, 1 - xl), X, [(0, 3), (3, 0), (1, 2), (2, 1)])]
    ppermute x7 -> x6, waiting for transfers between devices: 31 us -> 26.5 us  [swap(): return lax.ppermute(array, axis, [(0, 1), (1, 0)])]
    all_to_all x2 -> x1, starting transfers between devices: 8.25 us -> 4.03 us  [sum_x(): lax.all_to_all(parts, X, split_axis=0, concat_axis=0, tiled=True)]
  transfers between devices with their start and end apart: 16 -> 16, of which waited for: 14 -> 12; matrix products, arithmetic and copies ran while one was open for 8% -> 9% of each run, Pallas kernels for 1% -> 1%
where the time goes in v5:
time: 246 us; the launch traced here: 242 us
  waiting for transfers between devices  112 us (46%)
  starting transfers between devices  51.4 us (21%)
  blocking collectives  24.5 us (10%)
  other arithmetic  20 us (8%)
  between operations  14.2 us (6%)
  local copies, waits for them, and re-layouts  9.82 us (4%)
  matrix products  6.82 us (3%)
  Pallas kernels  2.95 us (1%)
    ppermute x6, waiting for transfers between devices, swap(): return lax.ppermute(array, axis, [(0, 1), (1, 0)])  26.5 us
    all_to_all x2, blocking collectives, sum_x(): lax.all_to_all(parts, X, split_axis=0, concat_axis=0, tiled=True)  24.5 us
    ppermute x2, waiting for transfers between devices, left(): lax.ppermute(pick(1 - xh, 1 - xl), X, [(0, 3), (3, 0), (1, 2), (2, 1)])  23.8 us
    all_to_all x1, waiting for transfers between devices, local(): lax.all_to_all(z_copies, 'y', split_axis=0, concat_axis=0, tiled=True)  22.8 us
    ppermute x6, starting transfers between devices, swap(): return lax.ppermute(array, axis, [(0, 1), (1, 0)])  14.6 us
    all_gather x1, waiting for transfers between devices, local(): h_own = lax.all_gather(h_share, 'z', axis=0)  13.8 us
    mul x2, other arithmetic, pick(): lax.dynamic_slice(values, (0, (2 * m + a) * blk + b * half), (blk, half))  11.6 us
    all_gather x1, waiting for transfers between devices, local(): q_mine = lax.all_gather(q_share, 'z', axis=0)  11 us
  transfers between devices with their start and end apart: 16, of which 12 were waited for; matrix products, arithmetic and copies ran while one was open for 9% of the time, Pallas kernels for 1%

profile of v5, /device:TPU:56, one launch (start us, length us, event | category | flops | bytes accessed | tf_op | source)
XLA Modules:
  0.0 241.9 jit_solution(5451206824748904043)
XLA Ops:
  7.2 0.8 convert_element_type.10
  8.1 0.7 fusion.16
  8.8 1.6 dynamic-slice_multiply_fusion.17
  10.4 1.1 broadcast_in_dim.18
  11.4 8.6 %all-to-all-start = ((f32[8,128,256]{2,1,0:T(8,128)}), f32[8,128,256]{2,1,0:T(8,128)S(1)}, u32[]{:S(2)}, u32[]{:S(2)}) async-start(f32[8,128,256]{2,1,0:T(8,128)} %broadcast_in_dim.18), calls=%async_computation | async-start | bytes 2097152 | tf_op jit(solution)/shard_map/all_to_all | solution.py:94
  20.1 5.2 %dynamic-slice_multiply_fusion.16 = (f32[256,128]{1,0:T(8,128)S(1)}, f32[256,128]{1,0:T(8,128)S(1)}, f32[256,128]{1,0:T(8,128)S(1)}, f32[256,128]{1,0:T(8,128)S(...) fusion(f32[256,2048]{1,0:T(8,128)S(1)} %copy-done.3, ...), kind=kLoop, calls=%fused_computation.43 | loop fusion | flops 262144 | bytes 2097216 | tf_op jit(solution)/shard_map/mul | solution.py:66
  25.3 2.9 %collective-permute-start = (f32[256,512]{1,0:T(8,128)S(1)}, f32[256,512]{1,0:T(8,128)S(1)}, u32[]{:S(2)}, u32[]{:S(2)}) collective-permute-start(f32[256,512]{1,0:T(8,128)S(1)} %pad_maximum_fusion.3), channel_id=1, source_target_pairs={{0,33},{33,0},{1,32},{32,1},{2,35},{35,2},{3,34},{34,3},{4,37},{37... | collective-permute-start | bytes 1572872 | tf_op jit(solution)/shard_map/ppermute | solution.py:74
  28.2 11.5 %collective-permute-done = f32[256,512]{1,0:T(8,128)S(1)} collective-permute-done((f32[256,512]{1,0:T(8,128)S(1)}, f32[256,512]{1,0:T(8,128)S(1)}, u32[]{:S(2)}, u32[]{:S(2)}) %collective-permute-start) | collective-permute-done | bytes 524320 | tf_op jit(solution)/shard_map/ppermute | solution.py:74
  39.7 0.1 pad_maximum_fusion
  39.8 0.7 copy-done.7
  40.5 1.9 collective-permute-start.1
  42.4 2.6 %collective-permute-done.1 = f32[512,512]{1,0:T(8,128)S(1)} collective-permute-done((f32[512,512]{1,0:T(8,128)S(1)}, f32[512,512]{1,0:T(8,128)S(1)}, u32[]{:S(2)}, u32[]{:S(2)}) %collective-permute-start.1) | collective-permute-done | bytes 1048608 | tf_op jit(solution)/shard_map/ppermute | solution.py:20
  45.1 0.6 fusion.4
  45.7 0.3 copy-done.5
  46.0 0.2 copy-done.8
  46.2 0.6 convolution_add_fusion.1
  46.8 2.0 collective-permute-start.2
  48.9 1.3 collective-permute-done.2
  50.3 0.8 fusion
  51.1 4.0 %all-to-all-start.1 = ((f32[4,256,128]{2,1,0:T(8,128)}), f32[4,256,128]{2,1,0:T(8,128)S(1)}, u32[]{:S(2)}, u32[]{:S(2)}) async-start(f32[4,256,128]{2,1,0:T(8,128)} %bitcast.13), calls=%async_computation.1 | async-start | bytes 1048576 | tf_op jit(solution)/shard_map/all_to_all | solution.py:87
  55.2 0.7 fusion.14
  55.9 9.0 %all-to-all-done.1 = f32[4,256,128]{2,1,0:T(8,128)S(1)} async-done(((f32[4,256,128]{2,1,0:T(8,128)}), f32[4,256,128]{2,1,0:T(8,128)S(1)}, u32[]{:S(2)}, u32[]{:S(2)}) %all-to-all-start.1) | async-done | bytes 524320 | tf_op jit(solution)/shard_map/all_to_all | solution.py:87
  65.0 1.4 bitcast_subtract_fusion
  66.4 0.0 all-gather.6.cloned.1.call-update
  66.4 1.6 dynamic-slice_multiply_fusion.8
  68.1 1.1 broadcast_in_dim.19
  69.1 7.2 %all-to-all-start.2 = ((f32[8,128,256]{2,1,0:T(8,128)}), f32[8,128,256]{2,1,0:T(8,128)S(1)}, u32[]{:S(2)}, u32[]{:S(2)}) async-start(f32[8,128,256]{2,1,0:T(8,128)} %broadcast_in_dim.19), calls=%async_computation.2 | async-start | bytes 2097152 | tf_op jit(solution)/shard_map/all_to_all | solution.py:16
  76.3 6.4 %dynamic-slice_multiply_fusion.7 = (f32[256,128]{1,0:T(8,128)S(1)}, f32[256,128]{1,0:T(8,128)S(1)}, f32[256,128]{1,0:T(8,128)S(1)}, f32[256,128]{1,0:T(8,128)S(1...) fusion(f32[256,2048]{1,0:T(8,128)} %param.8, ...), kind=kLoop, calls=%fused_computation.34 | loop fusion | flops 262144 | bytes 2097216 | tf_op jit(solution)/shard_map/mul | solution.py:66
  82.8 3.1 %collective-permute-start.3 = (f32[256,512]{1,0:T(8,128)S(1)}, f32[256,512]{1,0:T(8,128)S(1)}, u32[]{:S(2)}, u32[]{:S(2)}) collective-permute-start(f32[256,512]{1,0:T(8,128)S(1)} %pad_maximum_fusion.5), channel_id=1, source_target_pairs={{0,33},{33,0},{1,32},{32,1},{2,35},{35,2},{3,34},{34,3},{4,37},{37... | collective-permute-start | bytes 1572872 | tf_op jit(solution)/shard_map/ppermute | solution.py:74
  85.9 12.3 %collective-permute-done.3 = f32[256,512]{1,0:T(8,128)S(1)} collective-permute-done((f32[256,512]{1,0:T(8,128)S(1)}, f32[256,512]{1,0:T(8,128)S(1)}, u32[]{:S(2)}, u32[]{:S(2)}) %collective-permute-start.3) | collective-permute-done | bytes 524320 | tf_op jit(solution)/shard_map/ppermute | solution.py:74
  98.1 0.1 fusion.8
  98.3 0.1 pad_maximum_fusion.1
  98.4 1.9 collective-permute-start.4
  100.3 11.0 %all-gather.6.cloned.1.call-done = f32[8,256,128]{2,1,0:T(8,128)} async-done(((f32[1,256,128]{2,1,0:T(8,128)}), f32[8,256,128]{2,1,0:T(8,128)}) %all-gather.6.cloned.1.call-update) | async-done | bytes 1048592 | tf_op jit(solution)/shard_map/all_gather | solution.py:111
  111.3 1.6 copy.9
  112.8 1.9 collective-permute-start.5
  114.8 0.1 reverse_select_fusion
  114.9 0.1 copy.10
  115.0 1.0 fusion.17
  116.0 1.5 collective-permute-done.5
  117.5 2.2 fusion.18
  119.8 14.0 %all_to_all.35 = f32[4,128,256]{2,1,0:T(8,128)S(1)} all-to-all(f32[4,128,256]{2,1,0:T(8,128)S(1)} %bitcast.64), channel_id=1, replica_groups=mesh['y'=8,'xh'=2,'core'=2,'z'=8,'xl'=2] {'xh','xl'}, dimensions={0} | all-to-all | bytes 1048576 | tf_op jit(solution)/shard_map/all_to_all | solution.py:87
  133.8 0.7 broadcast_multiply_fusion.1
  134.6 1.1 broadcast_in_dim.36
  135.6 7.0 %all-to-all-start.4 = ((f32[8,128,256]{2,1,0:T(8,128)}), f32[8,128,256]{2,1,0:T(8,128)S(1)}, u32[]{:S(2)}, u32[]{:S(2)}) async-start(f32[8,128,256]{2,1,0:T(8,128)} %broadcast_in_dim.36), calls=%async_computation.4 | async-start | bytes 2097152 | tf_op jit(solution)/shard_map/all_to_all | solution.py:133
  142.6 0.7 all-gather.8.cloned.1.call-update
  143.4 0.0 all-gather.10.cloned.1.call-start
  143.4 22.8 %all-to-all-done.4 = f32[8,128,256]{2,1,0:T(8,128)S(1)} async-done(((f32[8,128,256]{2,1,0:T(8,128)}), f32[8,128,256]{2,1,0:T(8,128)S(1)}, u32[]{:S(2)}, u32[]{:S(2)}) %all-to-all-start.4) | async-done | bytes 1048608 | tf_op jit(solution)/shard_map/all_to_all | solution.py:133
  166.2 1.8 fusion.1
  168.0 0.6 convolution_add_fusion
  168.6 10.5 %all_to_all.36 = f32[4,128,256]{2,1,0:T(8,128)S(1)} all-to-all(f32[4,128,256]{2,1,0:T(8,128)S(1)} %bitcast.65), channel_id=1, replica_groups=mesh['y'=8,'xh'=2,'core'=2,'z'=8,'xl'=2] {'xh','xl'}, dimensions={0} | all-to-all | bytes 1048576 | tf_op jit(solution)/shard_map/all_to_all | solution.py:87
  179.2 0.7 broadcast_multiply_fusion
  179.9 4.6 %all-gather.8.cloned.1.call-done = f32[1024,256]{1,0:T(8,128)} async-done(((f32[128,256]{1,0:T(8,128)}), f32[1024,256]{1,0:T(8,128)}) %all-gather.8.cloned.1.call-update) | async-done | bytes 1048592 | tf_op jit(solution)/shard_map/all_gather | solution.py:135
  184.5 3.5 %collective-permute-start.6 = (f32[128,256]{1,0:T(8,128)S(1)}, f32[128,256]{1,0:T(8,128)S(1)}, u32[]{:S(2)}, u32[]{:S(2)}) collective-permute-start(f32[128,256]{1,0:T(8,128)S(1)} %broadcast_multiply_fusion), channel_id=1, source_target_pairs={{0,1},{1,0},{2,3},{3,2},{4,5},{5,4},{6,7},{7,6},{8,9},{9,8},{10,11... | collective-permute-start | bytes 393224 | tf_op jit(solution)/shard_map/ppermute | solution.py:20
  188.0 0.0 all-gather.10.cloned.1.call-update
  188.0 3.4 %collective-permute-done.6 = f32[128,256]{1,0:T(8,128)S(1)} collective-permute-done((f32[128,256]{1,0:T(8,128)S(1)}, f32[128,256]{1,0:T(8,128)S(1)}, u32[]{:S(2)}, u32[]{:S(2)}) %collective-permute-start.6) | collective-permute-done | bytes 131104 | tf_op jit(solution)/shard_map/ppermute | solution.py:20
  191.4 1.1 broadcast_in_dim.37
  192.5 3.9 %all-to-all-start.6 = ((f32[8,128,256]{2,1,0:T(8,128)}), f32[8,128,256]{2,1,0:T(8,128)S(1)}, u32[]{:S(2)}, u32[]{:S(2)}) async-start(f32[8,128,256]{2,1,0:T(8,128)} %broadcast_in_dim.37), calls=%async_computation.6 | async-start | bytes 2097152 | tf_op jit(solution)/shard_map/all_to_all | solution.py:144
  196.4 3.3 %collective-permute-start.7 = (f32[8,128,256]{2,1,0:T(8,128)S(1)}, f32[8,128,256]{2,1,0:T(8,128)S(1)}, u32[]{:S(2)}, u32[]{:S(2)}) collective-permute-start(f32[8,128,256]{2,1,0:T(8,128)S(1)} %bitcast.53), channel_id=1, source_target_pairs={{0,1},{1,0},{2,3},{3,2},{4,5},{5,4},{6,7},{7,6},{8,9},{9,8},{10,11... | collective-permute-start | bytes 3145736 | tf_op jit(solution)/shard_map/ppermute | solution.py:20
  199.7 17.6 %collective-permute-done.7.refs_1_ = f32[8,128,256]{2,1,0:T(8,128)S(1)} collective-permute-done((f32[8,128,256]{2,1,0:T(8,128)S(1)}, f32[8,128,256]{2,1,0:T(8,128)S(1)}, u32[]{:S(2)}, u32[]{:S(2)}) %collective-permute-start.7) | collective-permute-done | bytes 1048608 | tf_op jit(solution)/shard_map/ppermute | solution.py:20
  217.4 1.5 shard_map.77
  218.9 13.8 %all-gather.10.cloned.1.call-done = f32[1024,256]{1,0:T(8,128)} async-done(((f32[128,256]{1,0:T(8,128)}), f32[1024,256]{1,0:T(8,128)}) %all-gather.10.cloned.1.call-update) | async-done | bytes 1048592 | tf_op jit(solution)/shard_map/all_gather | solution.py:139
  232.7 1.2 copy-done.1
  233.9 1.5 shard_map.78
  (38 shorter events, 0.4 us)
Async XLA Ops:
  7.2 12.9 %copy-start.3 = (f32[256,2048]{1,0:T(8,128)S(1)}, f32[256,2048]{1,0:T(8,128)}, u32[]{:S(2)}) copy-start(f32[256,2048]{1,0:T(8,128)} %param.7) | copy-start | bytes 6291460
  11.4 33.6 %all-to-all-start = ((f32[8,128,256]{2,1,0:T(8,128)}), f32[8,128,256]{2,1,0:T(8,128)S(1)}, u32[]{:S(2)}, u32[]{:S(2)}) async-start(f32[8,128,256]{2,1,0:T(8,128)} %broadcast_in_dim.18), calls=%async_computation | async-start | bytes 2097152 | tf_op jit(solution)/shard_map/all_to_all | solution.py:94
  25.2 14.5 %copy-start.4 = (f32[256,128]{1,0:T(8,128)}, f32[256,128]{1,0:T(8,128)S(1)}, u32[]{:S(2)}) copy-start(f32[256,128]{1,0:T(8,128)S(1)} %get-tuple-element.39) | copy-start | bytes 393220
  25.3 14.4 %collective-permute-start = (f32[256,512]{1,0:T(8,128)S(1)}, f32[256,512]{1,0:T(8,128)S(1)}, u32[]{:S(2)}, u32[]{:S(2)}) collective-permute-start(f32[256,512]{1,0:T(8,128)S(1)} %pad_maximum_fusion.3), channel_id=1, source_target_pairs={{0,33},{33,0},{1,32},{32,1},{2,35},{35,2},{3,34},{34,3},{4,37},{37... | collective-permute-start | bytes 1572872 | tf_op jit(solution)/shard_map/ppermute | solution.py:74
  39.7 0.8 copy-start.7
  40.5 4.5 %collective-permute-start.1 = (f32[512,512]{1,0:T(8,128)S(1)}, f32[512,512]{1,0:T(8,128)S(1)}, u32[]{:S(2)}, u32[]{:S(2)}) collective-permute-start(f32[512,512]{1,0:T(8,128)S(1)} %pad_maximum_fusion), channel_id=1, source_target_pairs={{0,16},{16,0},{1,17},{17,1},{2,18},{18,2},{3,19},{19,3},{4,20},{20... | collective-permute-start | bytes 3145736 | tf_op jit(solution)/shard_map/ppermute | solution.py:20
  45.1 0.9 copy-start.5
  45.1 1.1 copy-start.8
  46.8 3.4 %collective-permute-start.2 = (f32[256,256]{1,0:T(8,128)S(1)}, f32[256,256]{1,0:T(8,128)S(1)}, u32[]{:S(2)}, u32[]{:S(2)}) collective-permute-start(f32[256,256]{1,0:T(8,128)S(1)} %constant_dynamic-slice_fusion), channel_id=1, source_target_pairs={{0,16},{16,0},{1,17},{17,1},{2,18},{18,2},{3,19},{19,3},{4,20},{20... | collective-permute-start | bytes 786440 | tf_op jit(solution)/shard_map/ppermute | solution.py:20
  48.9 6.3 %copy-start.9 = (s32[16,16]{1,0:T(8,128)S(1)}, s32[16,16]{1,0:T(8,128)}, u32[]{:S(2)}) copy-start(s32[16,16]{1,0:T(8,128)} %param.11) | copy-start | bytes 3076
  48.9 6.3 %copy-start.10 = (s32[16,16]{1,0:T(8,128)S(1)}, s32[16,16]{1,0:T(8,128)}, u32[]{:S(2)}) copy-start(s32[16,16]{1,0:T(8,128)} %param.10) | copy-start | bytes 3076
  51.1 13.8 %all-to-all-start.1 = ((f32[4,256,128]{2,1,0:T(8,128)}), f32[4,256,128]{2,1,0:T(8,128)S(1)}, u32[]{:S(2)}, u32[]{:S(2)}) async-start(f32[4,256,128]{2,1,0:T(8,128)} %bitcast.13), calls=%async_computation.1 | async-start | bytes 1048576 | tf_op jit(solution)/shard_map/all_to_all | solution.py:87
  55.2 56.1 %all-gather.6.cloned.1.call-start = ((), (), s32[]{:S(2)}) async-start(), calls=%async_computation.7 | async-start | bytes 1179648 | tf_op jit(solution)/shard_map/all_gather | solution.py:111
  69.1 45.6 %all-to-all-start.2 = ((f32[8,128,256]{2,1,0:T(8,128)}), f32[8,128,256]{2,1,0:T(8,128)S(1)}, u32[]{:S(2)}, u32[]{:S(2)}) async-start(f32[8,128,256]{2,1,0:T(8,128)} %broadcast_in_dim.19), calls=%async_computation.2 | async-start | bytes 2097152 | tf_op jit(solution)/shard_map/all_to_all | solution.py:16
  82.8 15.4 %collective-permute-start.3 = (f32[256,512]{1,0:T(8,128)S(1)}, f32[256,512]{1,0:T(8,128)S(1)}, u32[]{:S(2)}, u32[]{:S(2)}) collective-permute-start(f32[256,512]{1,0:T(8,128)S(1)} %pad_maximum_fusion.5), channel_id=1, source_target_pairs={{0,33},{33,0},{1,32},{32,1},{2,35},{35,2},{3,34},{34,3},{4,37},{37... | collective-permute-start | bytes 1572872 | tf_op jit(solution)/shard_map/ppermute | solution.py:74
  98.4 17.6 %collective-permute-start.4 = (f32[512,512]{1,0:T(8,128)S(1)}, f32[512,512]{1,0:T(8,128)}, u32[]{:S(2)}, u32[]{:S(2)}) collective-permute-start(f32[512,512]{1,0:T(8,128)S(1)} %pad_maximum_fusion.1), channel_id=1, source_target_pairs={{0,16},{16,0},{1,17},{17,1},{2,18},{18,2},{3,19},{19,3},{4,20},{20... | collective-permute-start | bytes 3145736 | tf_op jit(solution)/shard_map/ppermute | solution.py:20
  112.8 4.7 %collective-permute-start.5 = (f32[8,256,128]{1,2,0:T(8,128)S(1)}, f32[8,256,128]{1,2,0:T(8,128)}, u32[]{:S(2)}, u32[]{:S(2)}) collective-permute-start(f32[8,256,128]{1,2,0:T(8,128)S(1)} %copy.9), channel_id=1, source_target_pairs={{0,16},{16,0},{1,17},{17,1},{2,18},{18,2},{3,19},{19,3},{4,20},{20... | collective-permute-start | bytes 3145736 | tf_op jit(solution)/shard_map/ppermute | solution.py:20
  134.6 8.1 %copy-start.2 = (f32[128,256]{1,0:T(8,128)}, f32[128,256]{1,0:T(8,128)S(1)}, u32[]{:S(2)}) copy-start(f32[128,256]{1,0:T(8,128)S(1)} %broadcast_multiply_fusion.1) | copy-start | bytes 393220
  135.6 30.6 %all-to-all-start.4 = ((f32[8,128,256]{2,1,0:T(8,128)}), f32[8,128,256]{2,1,0:T(8,128)S(1)}, u32[]{:S(2)}, u32[]{:S(2)}) async-start(f32[8,128,256]{2,1,0:T(8,128)} %broadcast_in_dim.36), calls=%async_computation.4 | async-start | bytes 2097152 | tf_op jit(solution)/shard_map/all_to_all | solution.py:133
  142.6 41.8 %all-gather.8.cloned.1.call-start = ((), (), s32[]{:S(2)}) async-start(), calls=%async_computation.8 | async-start | bytes 1179648 | tf_op jit(solution)/shard_map/all_gather | solution.py:135
  143.4 89.3 %all-gather.10.cloned.1.call-start = ((), (), s32[]{:S(2)}) async-start(), calls=%async_computation.9 | async-start | bytes 1179648 | tf_op jit(solution)/shard_map/all_gather | solution.py:139
  179.9 8.1 %copy-start.6 = (f32[128,256]{1,0:T(8,128)}, f32[128,256]{1,0:T(8,128)S(1)}, u32[]{:S(2)}) copy-start(f32[128,256]{1,0:T(8,128)S(1)} %broadcast_multiply_fusion) | copy-start | bytes 393220
  184.5 12.0 %copy-start = (f32[1024,256]{1,0:T(8,128)S(1)}, f32[1024,256]{1,0:T(8,128)}, u32[]{:S(2)}) copy-start(f32[1024,256]{1,0:T(8,128)} %all-gather.8.cloned.1.call-done) | copy-start | bytes 3145732
  184.5 7.0 %collective-permute-start.6 = (f32[128,256]{1,0:T(8,128)S(1)}, f32[128,256]{1,0:T(8,128)S(1)}, u32[]{:S(2)}, u32[]{:S(2)}) collective-permute-start(f32[128,256]{1,0:T(8,128)S(1)} %broadcast_multiply_fusion), channel_id=1, source_target_pairs={{0,1},{1,0},{2,3},{3,2},{4,5},{5,4},{6,7},{7,6},{8,9},{9,8},{10,11... | collective-permute-start | bytes 393224 | tf_op jit(solution)/shard_map/ppermute | solution.py:20
  192.5 40.1 %all-to-all-start.6 = ((f32[8,128,256]{2,1,0:T(8,128)}), f32[8,128,256]{2,1,0:T(8,128)S(1)}, u32[]{:S(2)}, u32[]{:S(2)}) async-start(f32[8,128,256]{2,1,0:T(8,128)} %broadcast_in_dim.37), calls=%async_computation.6 | async-start | bytes 2097152 | tf_op jit(solution)/shard_map/all_to_all | solution.py:144
  196.4 21.0 %collective-permute-start.7 = (f32[8,128,256]{2,1,0:T(8,128)S(1)}, f32[8,128,256]{2,1,0:T(8,128)S(1)}, u32[]{:S(2)}, u32[]{:S(2)}) collective-permute-start(f32[8,128,256]{2,1,0:T(8,128)S(1)} %bitcast.53), channel_id=1, source_target_pairs={{0,1},{1,0},{2,3},{3,2},{4,5},{5,4},{6,7},{7,6},{8,9},{9,8},{10,11... | collective-permute-start | bytes 3145736 | tf_op jit(solution)/shard_map/ppermute | solution.py:20
  232.6 1.2 copy-start.1
Sparse Core Ops, SparseCore 0:
  66.6 44.6 all-gather.5
  146.1 38.3 all-gather.7
  188.1 44.4 all-gather.9

commit v6 on v5

--- a/solution.py
+++ b/solution.py
@@ -20,7 +20,7 @@
     return lax.ppermute(array, axis, [(0, 1), (1, 0)])
 
 
-def place(parts, blk):
+def place(parts, pieces, blk):
     layers = parts[0].shape[0]
     half = blk // 2
 
@@ -28,11 +28,11 @@
         out = refs[-1]
         xl = lax.axis_index("xl")
         core = lax.axis_index("core")
-        for share in range(2):
-            at = pl.multiple_of((xl ^ share) * half, half)
+        for part, first, share, offset, rows in pieces:
+            at = pl.multiple_of((xl ^ share) * half + offset, 8)
             for layer in range(layers):
                 to = pl.multiple_of((layer ^ core) * blk, blk)
-                out[pl.ds(at, half), pl.ds(to, blk)] = refs[share][layer]
+                out[pl.ds(at, rows), pl.ds(to, blk)] = refs[part][layer, first : first + rows]
 
     return pl.pallas_call(
         kernel,
@@ -90,7 +90,8 @@
         return sum_x(partial.reshape(4, half, blk)) * keep[row, column]
 
     y_copies = jnp.broadcast_to(piece(y_blocks)[None], (ny, half, blk))
-    y_copies, z_blocks = lax.optimization_barrier((y_copies, z_blocks))
+    z_piece = piece(z_blocks)
+    y_copies, z_piece, z_blocks = lax.optimization_barrier((y_copies, z_piece, z_blocks))
     y_panel = lax.all_to_all(y_copies, "y", split_axis=0, concat_axis=0, tiled=True)
     y_panel = y_panel.reshape(ny * half, blk)
     z_left = jnp.concatenate(left(z_blocks, fill), axis=0)
@@ -108,9 +109,10 @@
     at_row = t_row * blk + lax.broadcasted_iota(jnp.int32, (blk, half), 0)
     at_col = t_col * blk + xl * half + lax.broadcasted_iota(jnp.int32, (blk, half), 1)
     q_share = jnp.where(at_row == at_col, 1.5, 0.0) - 0.5 * (keep[t_row, t_col] * t_share)
-    q_mine = lax.all_gather(q_share, "z", axis=0)
-    z_piece, h_blocks, _ = lax.optimization_barrier((piece(z_blocks), h_blocks, q_share))
-    z_panel = spread(z_piece, "y", ny)
+    z_panel = lax.all_gather(z_piece, "y", axis=0)
+    q_share, h_blocks = lax.optimization_barrier((q_share, h_blocks))
+    q_mine = spread(q_share, "z", nz)
+    q_mine, z_panel = lax.optimization_barrier((q_mine, z_panel))
     q_theirs = swap(q_mine, "core")
     ordered = z_panel.reshape(2, ny // 2, half, blk).transpose(1, 0, 2, 3)
     ordered = jnp.where(xh == 0, ordered, ordered[:, ::-1]).reshape(ny * half, blk)
@@ -132,18 +134,30 @@
     z_copies = jnp.broadcast_to(z_share[None], (ny, half, blk))
     z_next_panel = lax.all_to_all(z_copies, "y", split_axis=0, concat_axis=0, tiled=True)
     z_next_panel = z_next_panel.reshape(ny * half, blk)
-    z_own = lax.all_gather(z_share, "z", axis=0)
+    z_shares = jnp.concatenate([z_share, swap(z_share, "xl")], axis=0)
+    z_all = lax.all_gather(z_shares, "z", axis=0)
     h_partial = multiply(h_left, h_theirs, z_next_panel)
     h_share = finish(h_partial)
-    h_share, z_own = lax.optimization_barrier((h_share, z_own))
-    h_own = lax.all_gather(h_share, "z", axis=0)
-    h_swapped = swap(h_share, "xl")
-    h_copies, z_own = lax.optimization_barrier(
-        (jnp.broadcast_to(h_swapped[None], (nz, half, blk)), z_own)
+    passed = half * 5 // 8
+    rest = half - passed
+    early = jnp.broadcast_to(h_share[:passed][None], (nz, passed, blk))
+    early, h_share = lax.optimization_barrier((early, h_share))
+    h_early = lax.all_to_all(early, "z", split_axis=0, concat_axis=0, tiled=True)
+    late = jnp.concatenate([h_share[passed:], swap(h_share[passed:], "xl")], axis=0)
+    late = jnp.broadcast_to(late[None], (nz, 2 * rest, blk))
+    late, z_all, h_early = lax.optimization_barrier((late, z_all, h_early))
+    h_late = lax.all_to_all(late, "z", split_axis=0, concat_axis=0, tiled=True)
+    z_next = place([z_all], [(0, 0, 0, 0, half), (0, half, 1, 0, half)], blk)
+    h_times_z = place(
+        [h_early, h_late, swap(h_early, "xl")],
+        [
+            (0, 0, 0, 0, passed),
+            (1, 0, 0, passed, rest),
+            (1, rest, 1, passed, rest),
+            (2, 0, 1, 0, passed),
+        ],
+        blk,
     )
-    h_other = lax.all_to_all(h_copies, "z", split_axis=0, concat_axis=0, tiled=True)
-    z_next = place([z_own, swap(z_own, "xl")], blk)
-    h_times_z = place([h_own, h_other], blk)
     return (z_next, h_times_z)
 
 

time: 246 us -> 241 us (0.980)
  the two profiles are of different devices: /device:TPU:56 before, /device:TPU:1 now
where the time goes in v6:
time: 241 us; the launch traced here: 239 us
  waiting for transfers between devices  97.5 us (40%)
  starting transfers between devices  64.9 us (27%)
  blocking collectives  23.2 us (10%)
  other arithmetic  20.9 us (9%)
  between operations  14.5 us (6%)
  local copies, waits for them, and re-layouts  9.8 us (4%)
  matrix products  5.59 us (2%)
  Pallas kernels  2.96 us (1%)
    all_to_all x2, blocking collectives, sum_x(): lax.all_to_all(parts, X, split_axis=0, concat_axis=0, tiled=True)  23.2 us
    ppermute x7, starting transfers between devices, swap(): return lax.ppermute(array, axis, [(0, 1), (1, 0)])  22.5 us
    all_to_all x1, waiting for transfers between devices, local(): lax.all_to_all(z_copies, 'y', split_axis=0, concat_axis=0, tiled=True)  22.4 us
    ppermute x2, waiting for transfers between devices, left(): lax.ppermute(pick(1 - xh, 1 - xl), X, [(0, 3), (3, 0), (1, 2), (2, 1)])  22.3 us
    ppermute x7, waiting for transfers between devices, swap(): return lax.ppermute(array, axis, [(0, 1), (1, 0)])  21.9 us
    all_to_all x1, waiting for transfers between devices, local(): lax.all_to_all(early, 'z', split_axis=0, concat_axis=0, tiled=True)  14.6 us
    mul x2, other arithmetic, pick(): lax.dynamic_slice(values, (0, (2 * m + a) * blk + b * half), (blk, half))  11.7 us
    all_to_all x1, starting transfers between devices, spread(): return lax.all_to_all(copies, axis, split_axis=0, concat_axis=0, tiled=True)  10 us
  transfers between devices with their start and end apart: 17, of which 12 were waited for; matrix products, arithmetic and copies ran while one was open for 9% of the time, Pallas kernels for 1%

profile of v6, /device:TPU:1, one launch (start us, length us, event | category | flops | bytes accessed | tf_op | source)
XLA Modules:
  0.0 239.3 jit_solution(127335780932682248)
XLA Ops:
  7.2 0.8 convert_element_type.10
  8.1 0.7 fusion.16
  8.7 2.3 dynamic-slice_multiply_fusion.16
  11.0 1.1 broadcast_in_dim.20
  12.1 7.7 %all-to-all-start = ((f32[8,128,256]{2,1,0:T(8,128)}), f32[8,128,256]{2,1,0:T(8,128)S(1)}, u32[]{:S(2)}, u32[]{:S(2)}) async-start(f32[8,128,256]{2,1,0:T(8,128)} %broadcast_in_dim.20), calls=%async_computation | async-start | bytes 2097152 | tf_op jit(solution)/shard_map/all_to_all | solution.py:95
  19.7 5.2 %dynamic-slice_multiply_fusion.15 = (f32[256,128]{1,0:T(8,128)S(1)}, f32[256,128]{1,0:T(8,128)S(1)}, f32[256,128]{1,0:T(8,128)S(1)}, f32[256,128]{1,0:T(8,128)S(...) fusion(f32[256,2048]{1,0:T(8,128)S(1)} %copy-done.3, ...), kind=kLoop, calls=%fused_computation.43 | loop fusion | flops 262144 | bytes 2097216 | tf_op jit(solution)/shard_map/mul | solution.py:66
  25.0 4.4 %collective-permute-start = (f32[256,512]{1,0:T(8,128)S(1)}, f32[256,512]{1,0:T(8,128)S(1)}, u32[]{:S(2)}, u32[]{:S(2)}) collective-permute-start(f32[256,512]{1,0:T(8,128)S(1)} %pad_maximum_fusion.3), channel_id=1, source_target_pairs={{0,33},{33,0},{1,32},{32,1},{2,35},{35,2},{3,34},{34,3},{4,37},{37... | collective-permute-start | bytes 1572872 | tf_op jit(solution)/shard_map/ppermute | solution.py:74
  29.3 10.3 %collective-permute-done = f32[256,512]{1,0:T(8,128)S(1)} collective-permute-done((f32[256,512]{1,0:T(8,128)S(1)}, f32[256,512]{1,0:T(8,128)S(1)}, u32[]{:S(2)}, u32[]{:S(2)}) %collective-permute-start) | collective-permute-done | bytes 524320 | tf_op jit(solution)/shard_map/ppermute | solution.py:74
  39.7 0.7 copy-done.6
  40.4 4.7 %collective-permute-start.1 = (f32[512,512]{1,0:T(8,128)S(1)}, f32[512,512]{1,0:T(8,128)S(1)}, u32[]{:S(2)}, u32[]{:S(2)}) collective-permute-start(f32[512,512]{1,0:T(8,128)S(1)} %pad_maximum_fusion), channel_id=1, source_target_pairs={{0,16},{16,0},{1,17},{17,1},{2,18},{18,2},{3,19},{19,3},{4,20},{20... | collective-permute-start | bytes 3145736 | tf_op jit(solution)/shard_map/ppermute | solution.py:20
  45.1 2.2 collective-permute-done.1
  47.4 0.6 fusion.4
  48.0 0.3 copy-done.5
  48.3 0.2 copy-done.7
  48.5 0.6 convolution_add_fusion.1
  49.1 3.9 %collective-permute-start.2 = (f32[256,256]{1,0:T(8,128)S(1)}, f32[256,256]{1,0:T(8,128)S(1)}, u32[]{:S(2)}, u32[]{:S(2)}) collective-permute-start(f32[256,256]{1,0:T(8,128)S(1)} %constant_dynamic-slice_fusion), channel_id=1, source_target_pairs={{0,16},{16,0},{1,17},{17,1},{2,18},{18,2},{3,19},{19,3},{4,20},{20... | collective-permute-start | bytes 786440 | tf_op jit(solution)/shard_map/ppermute | solution.py:20
  53.1 1.1 collective-permute-done.2
  54.2 0.8 fusion
  55.0 4.0 %all-to-all-start.1 = ((f32[4,256,128]{2,1,0:T(8,128)}), f32[4,256,128]{2,1,0:T(8,128)S(1)}, u32[]{:S(2)}, u32[]{:S(2)}) async-start(f32[4,256,128]{2,1,0:T(8,128)} %bitcast.13), calls=%async_computation.1 | async-start | bytes 1048576 | tf_op jit(solution)/shard_map/all_to_all | solution.py:87
  59.1 0.7 all-gather.5.cloned.1.call-update
  59.9 0.7 fusion.14
  60.6 7.4 %all-to-all-done.1 = f32[4,256,128]{2,1,0:T(8,128)S(1)} async-done(((f32[4,256,128]{2,1,0:T(8,128)}), f32[4,256,128]{2,1,0:T(8,128)S(1)}, u32[]{:S(2)}, u32[]{:S(2)}) %all-to-all-start.1) | async-done | bytes 524320 | tf_op jit(solution)/shard_map/all_to_all | solution.py:87
  68.0 0.7 multiply_subtract_fusion
  68.8 0.1 copy.9
  68.9 1.1 broadcast_in_dim.21
  69.9 10.0 %all-to-all-start.2 = ((f32[8,256,128]{1,2,0:T(8,128)}), f32[8,256,128]{1,2,0:T(8,128)S(1)}, u32[]{:S(2)}, u32[]{:S(2)}) async-start(f32[8,256,128]{1,2,0:T(8,128)} %broadcast_in_dim.21), calls=%async_computation.2 | async-start | bytes 2097152 | tf_op jit(solution)/shard_map/all_to_all | solution.py:16
  80.0 6.5 %dynamic-slice_multiply_fusion.7 = (f32[256,128]{1,0:T(8,128)S(1)}, f32[256,128]{1,0:T(8,128)S(1)}, f32[256,128]{1,0:T(8,128)S(1)}, f32[256,128]{1,0:T(8,128)S(1...) fusion(f32[256,2048]{1,0:T(8,128)} %param.8, ...), kind=kLoop, calls=%fused_computation.34 | loop fusion | flops 262144 | bytes 2097216 | tf_op jit(solution)/shard_map/mul | solution.py:66
  86.5 2.8 %collective-permute-start.3 = (f32[256,512]{1,0:T(8,128)S(1)}, f32[256,512]{1,0:T(8,128)S(1)}, u32[]{:S(2)}, u32[]{:S(2)}) collective-permute-start(f32[256,512]{1,0:T(8,128)S(1)} %pad_maximum_fusion.5), channel_id=1, source_target_pairs={{0,33},{33,0},{1,32},{32,1},{2,35},{35,2},{3,34},{34,3},{4,37},{37... | collective-permute-start | bytes 1572872 | tf_op jit(solution)/shard_map/ppermute | solution.py:74
  89.3 12.0 %collective-permute-done.3 = f32[256,512]{1,0:T(8,128)S(1)} collective-permute-done((f32[256,512]{1,0:T(8,128)S(1)}, f32[256,512]{1,0:T(8,128)S(1)}, u32[]{:S(2)}, u32[]{:S(2)}) %collective-permute-start.3) | collective-permute-done | bytes 524320 | tf_op jit(solution)/shard_map/ppermute | solution.py:74
  101.3 0.1 fusion.8
  101.5 0.1 pad_maximum_fusion.1
  101.5 4.5 %collective-permute-start.4 = (f32[512,512]{1,0:T(8,128)S(1)}, f32[512,512]{1,0:T(8,128)S(1)}, u32[]{:S(2)}, u32[]{:S(2)}) collective-permute-start(f32[512,512]{1,0:T(8,128)S(1)} %pad_maximum_fusion.1), channel_id=1, source_target_pairs={{0,16},{16,0},{1,17},{17,1},{2,18},{18,2},{3,19},{19,3},{4,20},{20... | collective-permute-start | bytes 3145736 | tf_op jit(solution)/shard_map/ppermute | solution.py:20
  106.1 3.0 %all-to-all-done.2 = f32[8,256,128]{1,2,0:T(8,128)S(1)} async-done(((f32[8,256,128]{1,2,0:T(8,128)}), f32[8,256,128]{1,2,0:T(8,128)S(1)}, u32[]{:S(2)}, u32[]{:S(2)}) %all-to-all-start.2) | async-done | bytes 1048608 | tf_op jit(solution)/shard_map/all_to_all | solution.py:16
  109.1 2.4 collective-permute-start.5
  111.6 1.8 reverse_select_fusion
  113.3 0.1 copy.10
  113.4 1.0 fusion.17
  114.4 2.2 fusion.18
  116.7 11.7 %all_to_all.40 = f32[4,128,256]{2,1,0:T(8,128)S(1)} all-to-all(f32[4,128,256]{2,1,0:T(8,128)S(1)} %bitcast.59), channel_id=1, replica_groups=mesh['y'=8,'xh'=2,'core'=2,'z'=8,'xl'=2] {'xh','xl'}, dimensions={0} | all-to-all | bytes 1048576 | tf_op jit(solution)/shard_map/all_to_all | solution.py:87
  128.5 0.7 broadcast_multiply_fusion.1
  129.2 1.1 broadcast_in_dim.22
  130.3 4.8 %all-to-all-start.4 = ((f32[8,128,256]{2,1,0:T(8,128)}), f32[8,128,256]{2,1,0:T(8,128)S(1)}, u32[]{:S(2)}, u32[]{:S(2)}) async-start(f32[8,128,256]{2,1,0:T(8,128)} %broadcast_in_dim.22), calls=%async_computation.4 | async-start | bytes 2097152 | tf_op jit(solution)/shard_map/all_to_all | solution.py:135
  135.1 2.2 collective-permute-start.7
  137.3 3.8 %collective-permute-done.7 = f32[128,256]{1,0:T(8,128)S(1)} collective-permute-done((f32[128,256]{1,0:T(8,128)S(1)}, f32[128,256]{1,0:T(8,128)S(1)}, u32[]{:S(2)}, u32[]{:S(2)}) %collective-permute-start.7) | collective-permute-done | bytes 131104 | tf_op jit(solution)/shard_map/ppermute | solution.py:20
  141.1 0.7 pad_maximum_fusion.7
  141.9 22.4 %all-to-all-done.4 = f32[8,128,256]{2,1,0:T(8,128)S(1)} async-done(((f32[8,128,256]{2,1,0:T(8,128)}), f32[8,128,256]{2,1,0:T(8,128)S(1)}, u32[]{:S(2)}, u32[]{:S(2)}) %all-to-all-start.4) | async-done | bytes 1048608 | tf_op jit(solution)/shard_map/all_to_all | solution.py:135
  164.3 0.6 fusion.1
  164.9 0.6 convolution_add_fusion
  165.5 11.5 %all_to_all.41 = f32[4,128,256]{2,1,0:T(8,128)S(1)} all-to-all(f32[4,128,256]{2,1,0:T(8,128)S(1)} %bitcast.60), channel_id=1, replica_groups=mesh['y'=8,'xh'=2,'core'=2,'z'=8,'xl'=2] {'xh','xl'}, dimensions={0} | all-to-all | bytes 1048576 | tf_op jit(solution)/shard_map/all_to_all | solution.py:87
  177.0 0.7 broadcast_multiply_fusion
  177.7 0.9 broadcast_in_dim.23
  178.6 5.1 %all-to-all-start.6 = ((f32[8,80,256]{2,1,0:T(8,128)}), f32[8,80,256]{2,1,0:T(8,128)S(1)}, u32[]{:S(2)}, u32[]{:S(2)}) async-start(f32[8,80,256]{2,1,0:T(8,128)} %broadcast_in_dim.23), calls=%async_computation.6 | async-start | bytes 1310720 | tf_op jit(solution)/shard_map/all_to_all | solution.py:145
  183.7 2.3 collective-permute-start.6
  186.0 2.5 %collective-permute-done.6 = f32[48,256]{1,0:T(8,128)S(1)} collective-permute-done((f32[48,256]{1,0:T(8,128)S(1)}, f32[48,256]{1,0:T(8,128)S(1)}, u32[]{:S(2)}, u32[]{:S(2)}) %collective-permute-start.6) | collective-permute-done | bytes 49184 | tf_op jit(solution)/shard_map/ppermute | solution.py:20
  188.5 14.6 %all-to-all-done.6.refs_0_ = f32[8,80,256]{2,1,0:T(8,128)S(1)} async-done(((f32[8,80,256]{2,1,0:T(8,128)}), f32[8,80,256]{2,1,0:T(8,128)S(1)}, u32[]{:S(2)}, u32[]{:S(2)}) %all-to-all-start.6) | async-done | bytes 655392 | tf_op jit(solution)/shard_map/all_to_all | solution.py:145
  203.1 0.9 broadcast_in_dim.44
  204.1 3.5 %all-to-all-start.7 = ((f32[8,96,256]{2,1,0:T(8,128)}), f32[8,96,256]{2,1,0:T(8,128)S(1)}, u32[]{:S(2)}, u32[]{:S(2)}) async-start(f32[8,96,256]{2,1,0:T(8,128)} %broadcast_in_dim.44), calls=%async_computation.7 | async-start | bytes 1572864 | tf_op jit(solution)/shard_map/all_to_all | solution.py:149
  207.6 2.5 %collective-permute-start.8 = (f32[8,80,256]{2,1,0:T(8,128)S(1)}, f32[8,80,256]{2,1,0:T(8,128)S(1)}, u32[]{:S(2)}, u32[]{:S(2)}) collective-permute-start(f32[8,80,256]{2,1,0:T(8,128)S(1)} %all-to-all-done.6.refs_0_), channel_id=1, source_target_pairs={{0,1},{1,0},{2,3},{3,2},{4,5},{5,4},{6,7},{7,6},{8,9},{9,8},{10,11... | collective-permute-start | bytes 1966088 | tf_op jit(solution)/shard_map/ppermute | solution.py:20
  210.2 1.5 shard_map.77
  211.7 12.3 %collective-permute-done.8.refs_2_ = f32[8,80,256]{2,1,0:T(8,128)S(1)} collective-permute-done((f32[8,80,256]{2,1,0:T(8,128)S(1)}, f32[8,80,256]{2,1,0:T(8,128)S(1)}, u32[]{:S(2)}, u32[]{:S(2)}) %collective-permute-start.8) | collective-permute-done | bytes 655392 | tf_op jit(solution)/shard_map/ppermute | solution.py:20
  224.0 0.8 copy-done.1
  224.8 5.1 %all-to-all-done.7.refs_1_ = f32[8,96,256]{2,1,0:T(8,128)S(1)} async-done(((f32[8,96,256]{2,1,0:T(8,128)}), f32[8,96,256]{2,1,0:T(8,128)S(1)}, u32[]{:S(2)}, u32[]{:S(2)}) %all-to-all-start.7) | async-done | bytes 786464 | tf_op jit(solution)/shard_map/all_to_all | solution.py:149
  229.9 1.1 copy-done.2
  231.0 1.5 shard_map.78
  (41 shorter events, 0.6 us)
Async XLA Ops:
  7.2 12.6 %copy-start.3 = (f32[256,2048]{1,0:T(8,128)S(1)}, f32[256,2048]{1,0:T(8,128)}, u32[]{:S(2)}) copy-start(f32[256,2048]{1,0:T(8,128)} %param.7) | copy-start | bytes 6291460
  12.1 35.3 %all-to-all-start = ((f32[8,128,256]{2,1,0:T(8,128)}), f32[8,128,256]{2,1,0:T(8,128)S(1)}, u32[]{:S(2)}, u32[]{:S(2)}) async-start(f32[8,128,256]{2,1,0:T(8,128)} %broadcast_in_dim.20), calls=%async_computation | async-start | bytes 2097152 | tf_op jit(solution)/shard_map/all_to_all | solution.py:95
  24.9 14.7 %copy-start.4 = (f32[256,128]{1,0:T(8,128)}, f32[256,128]{1,0:T(8,128)S(1)}, u32[]{:S(2)}) copy-start(f32[256,128]{1,0:T(8,128)S(1)} %get-tuple-element.47) | copy-start | bytes 393220
  25.0 14.6 %collective-permute-start = (f32[256,512]{1,0:T(8,128)S(1)}, f32[256,512]{1,0:T(8,128)S(1)}, u32[]{:S(2)}, u32[]{:S(2)}) collective-permute-start(f32[256,512]{1,0:T(8,128)S(1)} %pad_maximum_fusion.3), channel_id=1, source_target_pairs={{0,33},{33,0},{1,32},{32,1},{2,35},{35,2},{3,34},{34,3},{4,37},{37... | collective-permute-start | bytes 1572872 | tf_op jit(solution)/shard_map/ppermute | solution.py:74
  39.6 0.8 copy-start.6
  40.4 7.0 %collective-permute-start.1 = (f32[512,512]{1,0:T(8,128)S(1)}, f32[512,512]{1,0:T(8,128)S(1)}, u32[]{:S(2)}, u32[]{:S(2)}) collective-permute-start(f32[512,512]{1,0:T(8,128)S(1)} %pad_maximum_fusion), channel_id=1, source_target_pairs={{0,16},{16,0},{1,17},{17,1},{2,18},{18,2},{3,19},{19,3},{4,20},{20... | collective-permute-start | bytes 3145736 | tf_op jit(solution)/shard_map/ppermute | solution.py:20
  47.4 0.9 copy-start.5
  47.4 1.1 copy-start.7
  49.1 5.0 %collective-permute-start.2 = (f32[256,256]{1,0:T(8,128)S(1)}, f32[256,256]{1,0:T(8,128)S(1)}, u32[]{:S(2)}, u32[]{:S(2)}) collective-permute-start(f32[256,256]{1,0:T(8,128)S(1)} %constant_dynamic-slice_fusion), channel_id=1, source_target_pairs={{0,16},{16,0},{1,17},{17,1},{2,18},{18,2},{3,19},{19,3},{4,20},{20... | collective-permute-start | bytes 786440 | tf_op jit(solution)/shard_map/ppermute | solution.py:20
  53.0 6.8 %copy-start.8 = (s32[16,16]{1,0:T(8,128)S(1)}, s32[16,16]{1,0:T(8,128)}, u32[]{:S(2)}) copy-start(s32[16,16]{1,0:T(8,128)} %param.11) | copy-start | bytes 3076
  53.0 6.8 %copy-start.9 = (s32[16,16]{1,0:T(8,128)S(1)}, s32[16,16]{1,0:T(8,128)}, u32[]{:S(2)}) copy-start(s32[16,16]{1,0:T(8,128)} %param.10) | copy-start | bytes 3076
  55.0 12.9 %all-to-all-start.1 = ((f32[4,256,128]{2,1,0:T(8,128)}), f32[4,256,128]{2,1,0:T(8,128)S(1)}, u32[]{:S(2)}, u32[]{:S(2)}) async-start(f32[4,256,128]{2,1,0:T(8,128)} %bitcast.13), calls=%async_computation.1 | async-start | bytes 1048576 | tf_op jit(solution)/shard_map/all_to_all | solution.py:87
  59.1 47.0 %all-gather.5.cloned.1.call-start = ((), (), s32[]{:S(2)}) async-start(), calls=%async_computation.8 | async-start | bytes 1179648 | tf_op jit(solution)/shard_map/all_gather | solution.py:112
  69.9 39.2 %all-to-all-start.2 = ((f32[8,256,128]{1,2,0:T(8,128)}), f32[8,256,128]{1,2,0:T(8,128)S(1)}, u32[]{:S(2)}, u32[]{:S(2)}) async-start(f32[8,256,128]{1,2,0:T(8,128)} %broadcast_in_dim.21), calls=%async_computation.2 | async-start | bytes 2097152 | tf_op jit(solution)/shard_map/all_to_all | solution.py:16
  86.5 14.8 %collective-permute-start.3 = (f32[256,512]{1,0:T(8,128)S(1)}, f32[256,512]{1,0:T(8,128)S(1)}, u32[]{:S(2)}, u32[]{:S(2)}) collective-permute-start(f32[256,512]{1,0:T(8,128)S(1)} %pad_maximum_fusion.5), channel_id=1, source_target_pairs={{0,33},{33,0},{1,32},{32,1},{2,35},{35,2},{3,34},{34,3},{4,37},{37... | collective-permute-start | bytes 1572872 | tf_op jit(solution)/shard_map/ppermute | solution.py:74
  101.5 12.9 %collective-permute-start.4 = (f32[512,512]{1,0:T(8,128)S(1)}, f32[512,512]{1,0:T(8,128)S(1)}, u32[]{:S(2)}, u32[]{:S(2)}) collective-permute-start(f32[512,512]{1,0:T(8,128)S(1)} %pad_maximum_fusion.1), channel_id=1, source_target_pairs={{0,16},{16,0},{1,17},{17,1},{2,18},{18,2},{3,19},{19,3},{4,20},{20... | collective-permute-start | bytes 3145736 | tf_op jit(solution)/shard_map/ppermute | solution.py:20
  109.1 5.3 %collective-permute-start.5 = (f32[8,256,128]{1,2,0:T(8,128)S(1)}, f32[8,256,128]{1,2,0:T(8,128)}, u32[]{:S(2)}, u32[]{:S(2)}) collective-permute-start(f32[8,256,128]{1,2,0:T(8,128)S(1)} %all-to-all-done.2), channel_id=1, source_target_pairs={{0,16},{16,0},{1,17},{17,1},{2,18},{18,2},{3,19},{19,3},{4,20},{20... | collective-permute-start | bytes 3145736 | tf_op jit(solution)/shard_map/ppermute | solution.py:20
  130.3 34.0 %all-to-all-start.4 = ((f32[8,128,256]{2,1,0:T(8,128)}), f32[8,128,256]{2,1,0:T(8,128)S(1)}, u32[]{:S(2)}, u32[]{:S(2)}) async-start(f32[8,128,256]{2,1,0:T(8,128)} %broadcast_in_dim.22), calls=%async_computation.4 | async-start | bytes 2097152 | tf_op jit(solution)/shard_map/all_to_all | solution.py:135
  135.1 68.1 %all-gather.7.cloned.1.call-start = ((), (), s32[]{:S(2)}) async-start(), calls=%async_computation.9 | async-start | bytes 2359296 | tf_op jit(solution)/shard_map/all_gather | solution.py:138
  135.1 6.0 %collective-permute-start.7 = (f32[128,256]{1,0:T(8,128)S(1)}, f32[128,256]{1,0:T(8,128)S(1)}, u32[]{:S(2)}, u32[]{:S(2)}) collective-permute-start(f32[128,256]{1,0:T(8,128)S(1)} %broadcast_multiply_fusion.1), channel_id=1, source_target_pairs={{0,1},{1,0},{2,3},{3,2},{4,5},{5,4},{6,7},{7,6},{8,9},{9,8},{10,11... | collective-permute-start | bytes 393224 | tf_op jit(solution)/shard_map/ppermute | solution.py:20
  178.6 24.5 %all-to-all-start.6 = ((f32[8,80,256]{2,1,0:T(8,128)}), f32[8,80,256]{2,1,0:T(8,128)S(1)}, u32[]{:S(2)}, u32[]{:S(2)}) async-start(f32[8,80,256]{2,1,0:T(8,128)} %broadcast_in_dim.23), calls=%async_computation.6 | async-start | bytes 1310720 | tf_op jit(solution)/shard_map/all_to_all | solution.py:145
  183.7 4.8 %collective-permute-start.6 = (f32[48,256]{1,0:T(8,128)S(1)}, f32[48,256]{1,0:T(8,128)S(1)}, u32[]{:S(2)}, u32[]{:S(2)}) collective-permute-start(f32[48,256]{1,0:T(8,128)S(1)} %slice.16), channel_id=1, source_target_pairs={{0,1},{1,0},{2,3},{3,2},{4,5},{5,4},{6,7},{7,6},{8,9},{9,8},{10,11... | collective-permute-start | bytes 147464 | tf_op jit(solution)/shard_map/ppermute | solution.py:20
  203.1 7.1 %copy-start = (f32[2048,256]{1,0:T(8,128)S(1)}, f32[2048,256]{1,0:T(8,128)}, u32[]{:S(2)}) copy-start(f32[2048,256]{1,0:T(8,128)} %all-gather.7.cloned.1.call-done) | copy-start | bytes 6291460
  204.1 25.9 %all-to-all-start.7 = ((f32[8,96,256]{2,1,0:T(8,128)}), f32[8,96,256]{2,1,0:T(8,128)S(1)}, u32[]{:S(2)}, u32[]{:S(2)}) async-start(f32[8,96,256]{2,1,0:T(8,128)} %broadcast_in_dim.44), calls=%async_computation.7 | async-start | bytes 1572864 | tf_op jit(solution)/shard_map/all_to_all | solution.py:149
  207.6 16.3 %collective-permute-start.8 = (f32[8,80,256]{2,1,0:T(8,128)S(1)}, f32[8,80,256]{2,1,0:T(8,128)S(1)}, u32[]{:S(2)}, u32[]{:S(2)}) collective-permute-start(f32[8,80,256]{2,1,0:T(8,128)S(1)} %all-to-all-done.6.refs_0_), channel_id=1, source_target_pairs={{0,1},{1,0},{2,3},{3,2},{4,5},{5,4},{6,7},{7,6},{8,9},{9,8},{10,11... | collective-permute-start | bytes 1966088 | tf_op jit(solution)/shard_map/ppermute | solution.py:20
  224.0 0.9 copy-start.1
  229.9 1.1 copy-start.2
Sparse Core Ops, SparseCore 0:
  62.0 40.0 all-gather.4
  142.0 40.0 all-gather.6

commit v7 on v6

--- a/solution.py
+++ b/solution.py
@@ -59,7 +59,7 @@
     keep = keep_mask.astype(jnp.float32)
     fill = s_pattern.astype(jnp.float32)
 
-    def left(values, pattern):
+    def slices(values, pattern):
         def pick(a, b):
             return jnp.concatenate(
                 [
@@ -70,9 +70,13 @@
                 axis=1,
             )
 
-        own = pick(xh, xl)
-        other = lax.ppermute(pick(1 - xh, 1 - xl), X, [(0, 3), (3, 0), (1, 2), (2, 1)])
-        return own, other
+        part = pick(1 - xh, 1 - xl)
+        part, values = lax.optimization_barrier((part, values))
+        return part, pick(xh, xl)
+
+    def rows_with_partner(part, own):
+        other = lax.ppermute(part, X, [(0, 3), (3, 0), (1, 2), (2, 1)])
+        return [(rows, swap(rows, "core")) for rows in (own, other)]
 
     def multiply(mine, theirs, b):
         inner = mine.shape[1]
@@ -94,11 +98,12 @@
     y_copies, z_piece, z_blocks = lax.optimization_barrier((y_copies, z_piece, z_blocks))
     y_panel = lax.all_to_all(y_copies, "y", split_axis=0, concat_axis=0, tiled=True)
     y_panel = y_panel.reshape(ny * half, blk)
-    z_left = jnp.concatenate(left(z_blocks, fill), axis=0)
-    t_part = multiply(z_left, swap(z_left, "core"), y_panel)
-    at = (core ^ xh) * blk
-    mine = lax.dynamic_slice_in_dim(t_part, at, blk, 0)
-    theirs = swap(lax.dynamic_slice_in_dim(t_part, blk - at, blk, 0), "core")
+    t_own, t_other = [
+        multiply(*rows, y_panel) for rows in rows_with_partner(*slices(z_blocks, fill))
+    ]
+    same = core == xh
+    mine = jnp.where(same, t_own, t_other)
+    theirs = swap(jnp.where(same, t_other, t_own), "core")
     even = (panel % 2) == 0
     blocks = jnp.stack([jnp.where(even, mine, theirs), jnp.where(even, theirs, mine)])
     blocks = blocks.reshape(2, blk, 2, half).transpose(0, 2, 1, 3).reshape(4, blk, half)
@@ -112,7 +117,8 @@
     z_panel = lax.all_gather(z_piece, "y", axis=0)
     q_share, h_blocks = lax.optimization_barrier((q_share, h_blocks))
     q_mine = spread(q_share, "z", nz)
-    q_mine, z_panel = lax.optimization_barrier((q_mine, z_panel))
+    h_part, h_rows = slices(h_blocks, h_pattern.astype(jnp.float32))
+    q_mine, z_panel, h_part, h_rows = lax.optimization_barrier((q_mine, z_panel, h_part, h_rows))
     q_theirs = swap(q_mine, "core")
     ordered = z_panel.reshape(2, ny // 2, half, blk).transpose(1, 0, 2, 3)
     ordered = jnp.where(xh == 0, ordered, ordered[:, ::-1]).reshape(ny * half, blk)
@@ -121,22 +127,19 @@
         q = q.transpose(1, 0, 2).reshape(blk, nz * half)
         return jnp.dot(q, ordered, precision=HIGH)
 
-    own, other = left(h_blocks, h_pattern.astype(jnp.float32))
-    own, other = jnp.where(xh == 0, own, other), jnp.where(xh == 0, other, own)
-    h_left = jnp.concatenate([own, other], axis=0)
-    h_theirs = swap(h_left, "core")
     z_mine, z_theirs = rows_of(q_mine), rows_of(q_theirs)
-    z_mine, h_left, h_theirs = lax.optimization_barrier((z_mine, h_left, h_theirs))
     first = core == 0
     z_share = finish(
         jnp.stack([jnp.where(first, z_mine, z_theirs), jnp.where(first, z_theirs, z_mine)])
     )
     z_copies = jnp.broadcast_to(z_share[None], (ny, half, blk))
+    z_copies, h_part, h_rows = lax.optimization_barrier((z_copies, h_part, h_rows))
     z_next_panel = lax.all_to_all(z_copies, "y", split_axis=0, concat_axis=0, tiled=True)
     z_next_panel = z_next_panel.reshape(ny * half, blk)
     z_shares = jnp.concatenate([z_share, swap(z_share, "xl")], axis=0)
     z_all = lax.all_gather(z_shares, "z", axis=0)
-    h_partial = multiply(h_left, h_theirs, z_next_panel)
+    h_own, h_other = [multiply(*rows, z_next_panel) for rows in rows_with_partner(h_part, h_rows)]
+    h_partial = jnp.stack([jnp.where(xh == 0, h_own, h_other), jnp.where(xh == 0, h_other, h_own)])
     h_share = finish(h_partial)
     passed = half * 5 // 8
     rest = half - passed

time: 241 us -> 237 us (0.983)
  the two profiles are of different devices: /device:TPU:1 before, /device:TPU:56 now
where the time goes in v7:
time: 237 us; the launch traced here: 232 us
  waiting for transfers between devices  88.4 us (37%)
  starting transfers between devices  62.9 us (27%)
  blocking collectives  25.3 us (11%)
  other arithmetic  24.4 us (10%)
  between operations  14.6 us (6%)
  local copies, waits for them, and re-layouts  8.56 us (4%)
  matrix products  5.16 us (2%)
  Pallas kernels  2.96 us (1%)
    all_to_all x2, blocking collectives, sum_x(): lax.all_to_all(parts, X, split_axis=0, concat_axis=0, tiled=True)  25.3 us
    ppermute x9, waiting for transfers between devices, swap(): return lax.ppermute(array, axis, [(0, 1), (1, 0)])  23.6 us
    ppermute x9, starting transfers between devices, swap(): return lax.ppermute(array, axis, [(0, 1), (1, 0)])  19.2 us
    all_gather x1, waiting for transfers between devices, local(): z_panel = lax.all_gather(z_piece, 'y', axis=0)  17.4 us
    ppermute x2, waiting for transfers between devices, rows_with_partner(): other = lax.ppermute(part, X, [(0, 3), (3, 0), (1, 2), (2, 1)])  15.3 us
    mul x4, other arithmetic, pick(): lax.dynamic_slice(values, (0, (2 * m + a) * blk + b * half), (blk, half))  14.7 us
    all_to_all x1, waiting for transfers between devices, local(): lax.all_to_all(early, 'z', split_axis=0, concat_axis=0, tiled=True)  13 us
    all_to_all x1, starting transfers between devices, spread(): return lax.all_to_all(copies, axis, split_axis=0, concat_axis=0, tiled=True)  10.2 us
  transfers between devices with their start and end apart: 19, of which 13 were waited for; matrix products, arithmetic and copies ran while one was open for 11% of the time, Pallas kernels for 1%

profile of v7, /device:TPU:56, one launch (start us, length us, event | category | flops | bytes accessed | tf_op | source)
XLA Modules:
  0.0 232.2 jit_solution(14910429448121229544)
XLA Ops:
  7.2 0.7 convert_element_type.10
  7.9 0.7 fusion.24
  8.6 2.3 dynamic-slice_multiply_fusion.16
  10.9 1.1 broadcast_in_dim.20
  11.9 8.6 %all-to-all-start = ((f32[8,128,256]{2,1,0:T(8,128)}), f32[8,128,256]{2,1,0:T(8,128)S(1)}, u32[]{:S(2)}, u32[]{:S(2)}) async-start(f32[8,128,256]{2,1,0:T(8,128)} %broadcast_in_dim.20), calls=%async_computation | async-start | bytes 2097152 | tf_op jit(solution)/shard_map/all_to_all | solution.py:99
  20.6 3.6 %dynamic-slice_multiply_fusion.15 = (f32[256,128]{1,0:T(8,128)S(1)}, f32[256,128]{1,0:T(8,128)S(1)}, f32[256,128]{1,0:T(8,128)S(1)}, f32[256,128]{1,0:T(8,128)S(1)}) fusion(f32[256,2048]{1,0:T(8,128)} %param.7, s32[]{:T(128)S(6)} %select_n.191, f32[]{:T(128)} %bitcast.2, f32[]{:T(128)} %bitcast.5, s32[]{:T(128)S(6)} %select_n.197, f32[]{:T(128)} %bitcast.4, ...), kind=kLoop, calls=%fused_computation.51 | loop fusion | flops 131072 | bytes 1048608 | tf_op jit(solution)/shard_map/mul | solution.py:66
  24.2 2.9 %collective-permute-start.1 = (f32[256,512]{1,0:T(8,128)S(1)}, f32[256,512]{1,0:T(8,128)S(1)}, u32[]{:S(2)}, u32[]{:S(2)}) collective-permute-start(f32[256,512]{1,0:T(8,128)S(1)} %pad_maximum_fusion.1), channel_id=1, source_target_pairs={{0,33},{33,0},{1,32},{32,1},{2,35},{35,2},{3,34},{34,3},{4,37},{37... | collective-permute-start | bytes 1572872 | tf_op jit(solution)/shard_map/ppermute | solution.py:78
  27.1 3.7 %dynamic-slice_multiply_fusion.11 = (f32[256,128]{1,0:T(8,128)S(1)}, f32[256,128]{1,0:T(8,128)S(1)}, f32[256,128]{1,0:T(8,128)S(1)}, f32[256,128]{1,0:T(8,128)S(1)}) fusion(f32[256,2048]{1,0:T(8,128)} %param.7, s32[]{:T(128)S(6)} %select_n.199, f32[]{:T(128)} %bitcast.6, f32[]{:T(128)} %bitcast.9, s32[]{:T(128)S(6)} %select_n.205, f32[]{:T(128)} %bitcast.8, ...), kind=kLoop, calls=%fused_computation.47 | loop fusion | flops 131072 | bytes 1048608 | tf_op jit(solution)/shard_map/mul | solution.py:66
  30.8 0.8 pad_maximum_fusion.2
  31.7 1.9 collective-permute-start
  33.6 5.1 %collective-permute-done.1 = f32[256,512]{1,0:T(8,128)S(1)} collective-permute-done((f32[256,512]{1,0:T(8,128)S(1)}, f32[256,512]{1,0:T(8,128)S(1)}, u32[]{:S(2)}, u32[]{:S(2)}) %collective-permute-start.1) | collective-permute-done | bytes 524320 | tf_op jit(solution)/shard_map/ppermute | solution.py:78
  38.6 1.9 collective-permute-start.2
  40.6 2.9 %all-to-all-done = f32[8,128,256]{2,1,0:T(8,128)S(1)} async-done(((f32[8,128,256]{2,1,0:T(8,128)}), f32[8,128,256]{2,1,0:T(8,128)S(1)}, u32[]{:S(2)}, u32[]{:S(2)}) %all-to-all-start) | async-done | bytes 1048608 | tf_op jit(solution)/shard_map/all_to_all | solution.py:99
  43.9 0.4 fusion.9
  44.3 0.4 convolution_add_fusion.3
  44.7 0.4 broadcast_select_fusion
  45.1 1.9 collective-permute-start.3
  47.1 1.5 collective-permute-done.3
  48.6 0.8 fusion
  49.5 3.6 %all-to-all-start.1 = ((f32[4,256,128]{2,1,0:T(8,128)}), f32[4,256,128]{2,1,0:T(8,128)S(1)}, u32[]{:S(2)}, u32[]{:S(2)}) async-start(f32[4,256,128]{2,1,0:T(8,128)} %bitcast.13), calls=%async_computation.1 | async-start | bytes 1048576 | tf_op jit(solution)/shard_map/all_to_all | solution.py:91
  53.0 0.7 all-gather.5.cloned.1.call-update
  53.8 0.7 fusion.22
  54.5 8.4 %all-to-all-done.1 = f32[4,256,128]{2,1,0:T(8,128)S(1)} async-done(((f32[4,256,128]{2,1,0:T(8,128)}), f32[4,256,128]{2,1,0:T(8,128)S(1)}, u32[]{:S(2)}, u32[]{:S(2)}) %all-to-all-start.1) | async-done | bytes 524320 | tf_op jit(solution)/shard_map/all_to_all | solution.py:91
  63.0 0.7 multiply_subtract_fusion
  63.9 1.1 broadcast_in_dim.21
  64.9 10.2 %all-to-all-start.2 = ((f32[8,256,128]{1,2,0:T(8,128)}), f32[8,256,128]{1,2,0:T(8,128)S(1)}, u32[]{:S(2)}, u32[]{:S(2)}) async-start(f32[8,256,128]{1,2,0:T(8,128)} %broadcast_in_dim.21), calls=%async_computation.2 | async-start | bytes 2097152 | tf_op jit(solution)/shard_map/all_to_all | solution.py:16
  75.1 3.6 %dynamic-slice_multiply_fusion.7 = (f32[256,128]{1,0:T(8,128)S(1)}, f32[256,128]{1,0:T(8,128)S(1)}, f32[256,128]{1,0:T(8,128)S(1)}, f32[256,128]{1,0:T(8,128)S(1)}) fusion(f32[256,2048]{1,0:T(8,128)} %param.8, s32[]{:T(128)S(6)} %select_n.191, f32[]{:T(128)} %bitcast.15, f32[]{:T(128)} %bitcast.18, s32[]{:T(128)S(6)} %select_n.197, f32[]{:T(128)} %bitcast.17, ...), kind=kLoop, calls=%fused_computation.42 | loop fusion | flops 131072 | bytes 1048608 | tf_op jit(solution)/shard_map/mul | solution.py:66
  78.7 3.8 %dynamic-slice_multiply_fusion.3 = (f32[256,128]{1,0:T(8,128)S(1)}, f32[256,128]{1,0:T(8,128)S(1)}, f32[256,128]{1,0:T(8,128)S(1)}, f32[256,128]{1,0:T(8,128)S(1)}) fusion(f32[256,2048]{1,0:T(8,128)} %param.8, s32[]{:T(128)S(6)} %select_n.199, f32[]{:T(128)} %bitcast.19, f32[]{:T(128)} %bitcast.22, s32[]{:T(128)S(6)} %select_n.205, f32[]{:T(128)} %bitcast.21, ...), kind=kLoop, calls=%fused_computation.38 | loop fusion | flops 131072 | bytes 1048608 | tf_op jit(solution)/shard_map/mul | solution.py:66
  82.6 17.4 %all-gather.5.cloned.1.call-done = f32[1024,256]{1,0:T(8,128)} async-done(((f32[128,256]{1,0:T(8,128)}), f32[1024,256]{1,0:T(8,128)}) %all-gather.5.cloned.1.call-update) | async-done | bytes 1048592 | tf_op jit(solution)/shard_map/all_gather | solution.py:117
  100.0 3.0 %all-to-all-done.2 = f32[8,256,128]{1,2,0:T(8,128)S(1)} async-done(((f32[8,256,128]{1,2,0:T(8,128)}), f32[8,256,128]{1,2,0:T(8,128)S(1)}, u32[]{:S(2)}, u32[]{:S(2)}) %all-to-all-start.2) | async-done | bytes 1048608 | tf_op jit(solution)/shard_map/all_to_all | solution.py:16
  103.0 1.9 collective-permute-start.4
  104.9 1.8 reverse_select_fusion
  106.8 1.0 fusion.27
  107.8 1.0 select_bitcast_fusion.3
  108.8 12.8 %all_to_all.40 = f32[4,128,256]{2,1,0:T(8,128)S(1)} all-to-all(f32[4,128,256]{2,1,0:T(8,128)S(1)} %bitcast.71), channel_id=1, replica_groups=mesh['y'=8,'xh'=2,'core'=2,'z'=8,'xl'=2] {'xh','xl'}, dimensions={0} | all-to-all | bytes 1048576 | tf_op jit(solution)/shard_map/all_to_all | solution.py:91
  121.7 0.7 broadcast_multiply_fusion.1
  122.4 1.1 broadcast_in_dim.22
  123.5 8.3 %all-to-all-start.4 = ((f32[8,128,256]{2,1,0:T(8,128)}), f32[8,128,256]{2,1,0:T(8,128)S(1)}, u32[]{:S(2)}, u32[]{:S(2)}) async-start(f32[8,128,256]{2,1,0:T(8,128)} %broadcast_in_dim.22), calls=%async_computation.4 | async-start | bytes 2097152 | tf_op jit(solution)/shard_map/all_to_all | solution.py:137
  131.7 2.5 %collective-permute-start.9 = (f32[128,256]{1,0:T(8,128)S(1)}, f32[128,256]{1,0:T(8,128)S(1)}, u32[]{:S(2)}, u32[]{:S(2)}) collective-permute-start(f32[128,256]{1,0:T(8,128)S(1)} %broadcast_multiply_fusion.1), channel_id=1, source_target_pairs={{0,1},{1,0},{2,3},{3,2},{4,5},{5,4},{6,7},{7,6},{8,9},{9,8},{10,11... | collective-permute-start | bytes 393224 | tf_op jit(solution)/shard_map/ppermute | solution.py:20
  134.2 4.4 %collective-permute-done.9 = f32[128,256]{1,0:T(8,128)S(1)} collective-permute-done((f32[128,256]{1,0:T(8,128)S(1)}, f32[128,256]{1,0:T(8,128)S(1)}, u32[]{:S(2)}, u32[]{:S(2)}) %collective-permute-start.9) | collective-permute-done | bytes 131104 | tf_op jit(solution)/shard_map/ppermute | solution.py:20
  138.6 0.7 pad_maximum_fusion.7
  139.3 3.1 %collective-permute-start.6 = (f32[256,512]{1,0:T(8,128)S(1)}, f32[256,512]{1,0:T(8,128)S(1)}, u32[]{:S(2)}, u32[]{:S(2)}) collective-permute-start(f32[256,512]{1,0:T(8,128)S(1)} %pad_maximum_fusion.3), channel_id=1, source_target_pairs={{0,33},{33,0},{1,32},{32,1},{2,35},{35,2},{3,34},{34,3},{4,37},{37... | collective-permute-start | bytes 1572872 | tf_op jit(solution)/shard_map/ppermute | solution.py:78
  142.4 1.9 collective-permute-start.5
  144.3 10.2 %collective-permute-done.6 = f32[256,512]{1,0:T(8,128)S(1)} collective-permute-done((f32[256,512]{1,0:T(8,128)S(1)}, f32[256,512]{1,0:T(8,128)S(1)}, u32[]{:S(2)}, u32[]{:S(2)}) %collective-permute-start.6) | collective-permute-done | bytes 524320 | tf_op jit(solution)/shard_map/ppermute | solution.py:78
  154.5 1.9 collective-permute-start.7
  156.9 0.4 fusion.3
  157.3 0.4 convolution_add_fusion.1
  157.7 0.6 collective-permute-done.7
  158.8 12.5 %all_to_all.41 = f32[4,128,256]{2,1,0:T(8,128)S(1)} all-to-all(f32[4,128,256]{2,1,0:T(8,128)S(1)} %bitcast.72), channel_id=1, replica_groups=mesh['y'=8,'xh'=2,'core'=2,'z'=8,'xl'=2] {'xh','xl'}, dimensions={0} | all-to-all | bytes 1048576 | tf_op jit(solution)/shard_map/all_to_all | solution.py:91
  171.3 0.7 broadcast_multiply_fusion
  172.0 0.9 broadcast_in_dim.23
  172.9 3.5 %all-to-all-start.6 = ((f32[8,80,256]{2,1,0:T(8,128)}), f32[8,80,256]{2,1,0:T(8,128)S(1)}, u32[]{:S(2)}, u32[]{:S(2)}) async-start(f32[8,80,256]{2,1,0:T(8,128)} %broadcast_in_dim.23), calls=%async_computation.6 | async-start | bytes 1310720 | tf_op jit(solution)/shard_map/all_to_all | solution.py:148
  176.5 2.5 %collective-permute-start.8 = (f32[48,256]{1,0:T(8,128)S(1)}, f32[48,256]{1,0:T(8,128)S(1)}, u32[]{:S(2)}, u32[]{:S(2)}) collective-permute-start(f32[48,256]{1,0:T(8,128)S(1)} %slice.16), channel_id=1, source_target_pairs={{0,1},{1,0},{2,3},{3,2},{4,5},{5,4},{6,7},{7,6},{8,9},{9,8},{10,11... | collective-permute-start | bytes 147464 | tf_op jit(solution)/shard_map/ppermute | solution.py:20
  178.9 3.5 %collective-permute-done.8 = f32[48,256]{1,0:T(8,128)S(1)} collective-permute-done((f32[48,256]{1,0:T(8,128)S(1)}, f32[48,256]{1,0:T(8,128)S(1)}, u32[]{:S(2)}, u32[]{:S(2)}) %collective-permute-start.8) | collective-permute-done | bytes 49184 | tf_op jit(solution)/shard_map/ppermute | solution.py:20
  182.4 13.0 %all-to-all-done.6.refs_0_ = f32[8,80,256]{2,1,0:T(8,128)S(1)} async-done(((f32[8,80,256]{2,1,0:T(8,128)}), f32[8,80,256]{2,1,0:T(8,128)S(1)}, u32[]{:S(2)}, u32[]{:S(2)}) %all-to-all-start.6) | async-done | bytes 655392 | tf_op jit(solution)/shard_map/all_to_all | solution.py:148
  195.5 0.9 broadcast_in_dim.44
  196.4 3.5 %all-to-all-start.7 = ((f32[8,96,256]{2,1,0:T(8,128)}), f32[8,96,256]{2,1,0:T(8,128)S(1)}, u32[]{:S(2)}, u32[]{:S(2)}) async-start(f32[8,96,256]{2,1,0:T(8,128)} %broadcast_in_dim.44), calls=%async_computation.7 | async-start | bytes 1572864 | tf_op jit(solution)/shard_map/all_to_all | solution.py:152
  200.0 2.8 %collective-permute-start.10 = (f32[8,80,256]{2,1,0:T(8,128)S(1)}, f32[8,80,256]{2,1,0:T(8,128)S(1)}, u32[]{:S(2)}, u32[]{:S(2)}) collective-permute-start(f32[8,80,256]{2,1,0:T(8,128)S(1)} %all-to-all-done.6.refs_0_), channel_id=1, source_target_pairs={{0,1},{1,0},{2,3},{3,2},{4,5},{5,4},{6,7},{7,6},{8,9},{9,8},{10,11... | collective-permute-start | bytes 1966088 | tf_op jit(solution)/shard_map/ppermute | solution.py:20
  202.8 1.5 shard_map.77
  204.3 13.6 %collective-permute-done.10.refs_2_ = f32[8,80,256]{2,1,0:T(8,128)S(1)} collective-permute-done((f32[8,80,256]{2,1,0:T(8,128)S(1)}, f32[8,80,256]{2,1,0:T(8,128)S(1)}, u32[]{:S(2)}, u32[]{:S(2)}) %collective-permute-start.10) | collective-permute-done | bytes 655392 | tf_op jit(solution)/shard_map/ppermute | solution.py:20
  217.9 0.8 copy-done.1
  218.7 4.1 %all-to-all-done.7.refs_1_ = f32[8,96,256]{2,1,0:T(8,128)S(1)} async-done(((f32[8,96,256]{2,1,0:T(8,128)}), f32[8,96,256]{2,1,0:T(8,128)S(1)}, u32[]{:S(2)}, u32[]{:S(2)}) %all-to-all-start.7) | async-done | bytes 786464 | tf_op jit(solution)/shard_map/all_to_all | solution.py:152
  222.8 1.1 copy-done.2
  223.9 1.5 shard_map.78
  (39 shorter events, 1.8 us)
Async XLA Ops:
  11.9 31.6 %all-to-all-start = ((f32[8,128,256]{2,1,0:T(8,128)}), f32[8,128,256]{2,1,0:T(8,128)S(1)}, u32[]{:S(2)}, u32[]{:S(2)}) async-start(f32[8,128,256]{2,1,0:T(8,128)} %broadcast_in_dim.20), calls=%async_computation | async-start | bytes 2097152 | tf_op jit(solution)/shard_map/all_to_all | solution.py:99
  24.2 14.4 %collective-permute-start.1 = (f32[256,512]{1,0:T(8,128)S(1)}, f32[256,512]{1,0:T(8,128)S(1)}, u32[]{:S(2)}, u32[]{:S(2)}) collective-permute-start(f32[256,512]{1,0:T(8,128)S(1)} %pad_maximum_fusion.1), channel_id=1, source_target_pairs={{0,33},{33,0},{1,32},{32,1},{2,35},{35,2},{3,34},{34,3},{4,37},{37... | collective-permute-start | bytes 1572872 | tf_op jit(solution)/shard_map/ppermute | solution.py:78
  31.7 12.6 %collective-permute-start = (f32[256,512]{1,0:T(8,128)}, f32[256,512]{1,0:T(8,128)S(1)}, u32[]{:S(2)}, u32[]{:S(2)}) collective-permute-start(f32[256,512]{1,0:T(8,128)} %pad_maximum_fusion.2), channel_id=1, source_target_pairs={{0,16},{16,0},{1,17},{17,1},{2,18},{18,2},{3,19},{19,3},{4,20},{20... | collective-permute-start | bytes 1572872 | tf_op jit(solution)/shard_map/ppermute | solution.py:20
  38.6 6.1 %collective-permute-start.2 = (f32[256,512]{1,0:T(8,128)S(1)}, f32[256,512]{1,0:T(8,128)S(1)}, u32[]{:S(2)}, u32[]{:S(2)}) collective-permute-start(f32[256,512]{1,0:T(8,128)S(1)} %collective-permute-done.1), channel_id=1, source_target_pairs={{0,16},{16,0},{1,17},{17,1},{2,18},{18,2},{3,19},{19,3},{4,20},{20... | collective-permute-start | bytes 1572872 | tf_op jit(solution)/shard_map/ppermute | solution.py:20
  45.1 3.4 %collective-permute-start.3 = (f32[256,256]{1,0:T(8,128)S(1)}, f32[256,256]{1,0:T(8,128)S(1)}, u32[]{:S(2)}, u32[]{:S(2)}) collective-permute-start(f32[256,256]{1,0:T(8,128)S(1)} %get-tuple-element.85), channel_id=1, source_target_pairs={{0,16},{16,0},{1,17},{17,1},{2,18},{18,2},{3,19},{19,3},{4,20},{20... | collective-permute-start | bytes 786440 | tf_op jit(solution)/shard_map/ppermute | solution.py:20
  48.5 5.2 %copy-start.3 = (s32[16,16]{1,0:T(8,128)S(1)}, s32[16,16]{1,0:T(8,128)}, u32[]{:S(2)}) copy-start(s32[16,16]{1,0:T(8,128)} %param.10) | copy-start | bytes 3076
  48.6 5.2 %copy-start.4 = (s32[16,16]{1,0:T(8,128)S(1)}, s32[16,16]{1,0:T(8,128)}, u32[]{:S(2)}) copy-start(s32[16,16]{1,0:T(8,128)} %param.11) | copy-start | bytes 3076
  49.5 13.5 %all-to-all-start.1 = ((f32[4,256,128]{2,1,0:T(8,128)}), f32[4,256,128]{2,1,0:T(8,128)S(1)}, u32[]{:S(2)}, u32[]{:S(2)}) async-start(f32[4,256,128]{2,1,0:T(8,128)} %bitcast.13), calls=%async_computation.1 | async-start | bytes 1048576 | tf_op jit(solution)/shard_map/all_to_all | solution.py:91
  53.0 47.0 %all-gather.5.cloned.1.call-start = ((), (), s32[]{:S(2)}) async-start(), calls=%async_computation.8 | async-start | bytes 1179648 | tf_op jit(solution)/shard_map/all_gather | solution.py:117
  64.9 38.0 %all-to-all-start.2 = ((f32[8,256,128]{1,2,0:T(8,128)}), f32[8,256,128]{1,2,0:T(8,128)S(1)}, u32[]{:S(2)}, u32[]{:S(2)}) async-start(f32[8,256,128]{1,2,0:T(8,128)} %broadcast_in_dim.21), calls=%async_computation.2 | async-start | bytes 2097152 | tf_op jit(solution)/shard_map/all_to_all | solution.py:16
  103.0 4.8 %collective-permute-start.4 = (f32[8,256,128]{1,2,0:T(8,128)S(1)}, f32[8,256,128]{1,2,0:T(8,128)S(1)}, u32[]{:S(2)}, u32[]{:S(2)}) collective-permute-start(f32[8,256,128]{1,2,0:T(8,128)S(1)} %all-to-all-done.2), channel_id=1, source_target_pairs={{0,16},{16,0},{1,17},{17,1},{2,18},{18,2},{3,19},{19,3},{4,20},{20... | collective-permute-start | bytes 3145736 | tf_op jit(solution)/shard_map/ppermute | solution.py:20
  123.5 33.0 %all-to-all-start.4 = ((f32[8,128,256]{2,1,0:T(8,128)}), f32[8,128,256]{2,1,0:T(8,128)S(1)}, u32[]{:S(2)}, u32[]{:S(2)}) async-start(f32[8,128,256]{2,1,0:T(8,128)} %broadcast_in_dim.22), calls=%async_computation.4 | async-start | bytes 2097152 | tf_op jit(solution)/shard_map/all_to_all | solution.py:137
  131.7 63.7 %all-gather.7.cloned.1.call-start = ((), (), s32[]{:S(2)}) async-start(), calls=%async_computation.9 | async-start | bytes 2359296 | tf_op jit(solution)/shard_map/all_gather | solution.py:140
  131.7 6.8 %collective-permute-start.9 = (f32[128,256]{1,0:T(8,128)S(1)}, f32[128,256]{1,0:T(8,128)S(1)}, u32[]{:S(2)}, u32[]{:S(2)}) collective-permute-start(f32[128,256]{1,0:T(8,128)S(1)} %broadcast_multiply_fusion.1), channel_id=1, source_target_pairs={{0,1},{1,0},{2,3},{3,2},{4,5},{5,4},{6,7},{7,6},{8,9},{9,8},{10,11... | collective-permute-start | bytes 393224 | tf_op jit(solution)/shard_map/ppermute | solution.py:20
  139.3 15.2 %collective-permute-start.6 = (f32[256,512]{1,0:T(8,128)S(1)}, f32[256,512]{1,0:T(8,128)S(1)}, u32[]{:S(2)}, u32[]{:S(2)}) collective-permute-start(f32[256,512]{1,0:T(8,128)S(1)} %pad_maximum_fusion.3), channel_id=1, source_target_pairs={{0,33},{33,0},{1,32},{32,1},{2,35},{35,2},{3,34},{34,3},{4,37},{37... | collective-permute-start | bytes 1572872 | tf_op jit(solution)/shard_map/ppermute | solution.py:78
  142.4 14.9 %collective-permute-start.5 = (f32[256,512]{1,0:T(8,128)S(1)}, f32[256,512]{1,0:T(8,128)S(1)}, u32[]{:S(2)}, u32[]{:S(2)}) collective-permute-start(f32[256,512]{1,0:T(8,128)S(1)} %pad_maximum_fusion.4), channel_id=1, source_target_pairs={{0,16},{16,0},{1,17},{17,1},{2,18},{18,2},{3,19},{19,3},{4,20},{20... | collective-permute-start | bytes 1572872 | tf_op jit(solution)/shard_map/ppermute | solution.py:20
  154.5 3.8 %collective-permute-start.7 = (f32[256,512]{1,0:T(8,128)S(1)}, f32[256,512]{1,0:T(8,128)S(1)}, u32[]{:S(2)}, u32[]{:S(2)}) collective-permute-start(f32[256,512]{1,0:T(8,128)S(1)} %collective-permute-done.6), channel_id=1, source_target_pairs={{0,16},{16,0},{1,17},{17,1},{2,18},{18,2},{3,19},{19,3},{4,20},{20... | collective-permute-start | bytes 1572872 | tf_op jit(solution)/shard_map/ppermute | solution.py:20
  172.9 22.6 %all-to-all-start.6 = ((f32[8,80,256]{2,1,0:T(8,128)}), f32[8,80,256]{2,1,0:T(8,128)S(1)}, u32[]{:S(2)}, u32[]{:S(2)}) async-start(f32[8,80,256]{2,1,0:T(8,128)} %broadcast_in_dim.23), calls=%async_computation.6 | async-start | bytes 1310720 | tf_op jit(solution)/shard_map/all_to_all | solution.py:148
  176.5 6.0 %collective-permute-start.8 = (f32[48,256]{1,0:T(8,128)S(1)}, f32[48,256]{1,0:T(8,128)S(1)}, u32[]{:S(2)}, u32[]{:S(2)}) collective-permute-start(f32[48,256]{1,0:T(8,128)S(1)} %slice.16), channel_id=1, source_target_pairs={{0,1},{1,0},{2,3},{3,2},{4,5},{5,4},{6,7},{7,6},{8,9},{9,8},{10,11... | collective-permute-start | bytes 147464 | tf_op jit(solution)/shard_map/ppermute | solution.py:20
  195.5 7.3 %copy-start = (f32[2048,256]{1,0:T(8,128)S(1)}, f32[2048,256]{1,0:T(8,128)}, u32[]{:S(2)}) copy-start(f32[2048,256]{1,0:T(8,128)} %all-gather.7.cloned.1.call-done) | copy-start | bytes 6291460
  196.4 26.4 %all-to-all-start.7 = ((f32[8,96,256]{2,1,0:T(8,128)}), f32[8,96,256]{2,1,0:T(8,128)S(1)}, u32[]{:S(2)}, u32[]{:S(2)}) async-start(f32[8,96,256]{2,1,0:T(8,128)} %broadcast_in_dim.44), calls=%async_computation.7 | async-start | bytes 1572864 | tf_op jit(solution)/shard_map/all_to_all | solution.py:152
  200.0 17.9 %collective-permute-start.10 = (f32[8,80,256]{2,1,0:T(8,128)S(1)}, f32[8,80,256]{2,1,0:T(8,128)S(1)}, u32[]{:S(2)}, u32[]{:S(2)}) collective-permute-start(f32[8,80,256]{2,1,0:T(8,128)S(1)} %all-to-all-done.6.refs_0_), channel_id=1, source_target_pairs={{0,1},{1,0},{2,3},{3,2},{4,5},{5,4},{6,7},{7,6},{8,9},{9,8},{10,11... | collective-permute-start | bytes 1966088 | tf_op jit(solution)/shard_map/ppermute | solution.py:20
  217.9 0.9 copy-start.1
  222.8 1.1 copy-start.2
Sparse Core Ops, SparseCore 0:
  55.9 44.0 all-gather.4
  139.4 40.5 all-gather.6

commit v8 on v7

--- a/solution.py
+++ b/solution.py
@@ -59,24 +59,18 @@
     keep = keep_mask.astype(jnp.float32)
     fill = s_pattern.astype(jnp.float32)
 
-    def slices(values, pattern):
-        def pick(a, b):
-            return jnp.concatenate(
-                [
-                    lax.dynamic_slice(values, (0, (2 * m + a) * blk + b * half), (blk, half))
-                    * pattern[row, per_core * core + 2 * m + a]
-                    for m in range(per_core // 2)
-                ],
-                axis=1,
-            )
+    def slices(values, pattern, a, b):
+        return jnp.concatenate(
+            [
+                lax.dynamic_slice(values, (0, (2 * m + a) * blk + b * half), (blk, half))
+                * pattern[row, per_core * core + 2 * m + a]
+                for m in range(per_core // 2)
+            ],
+            axis=1,
+        )
 
-        part = pick(1 - xh, 1 - xl)
-        part, values = lax.optimization_barrier((part, values))
-        return part, pick(xh, xl)
-
-    def rows_with_partner(part, own):
-        other = lax.ppermute(part, X, [(0, 3), (3, 0), (1, 2), (2, 1)])
-        return [(rows, swap(rows, "core")) for rows in (own, other)]
+    def from_partner(part):
+        return lax.ppermute(part, X, [(0, 3), (3, 0), (1, 2), (2, 1)])
 
     def multiply(mine, theirs, b):
         inner = mine.shape[1]
@@ -98,8 +92,11 @@
     y_copies, z_piece, z_blocks = lax.optimization_barrier((y_copies, z_piece, z_blocks))
     y_panel = lax.all_to_all(y_copies, "y", split_axis=0, concat_axis=0, tiled=True)
     y_panel = y_panel.reshape(ny * half, blk)
+    z_part = slices(z_blocks, fill, 1 - xh, 1 - xl)
+    z_part, z_blocks = lax.optimization_barrier((z_part, z_blocks))
+    z_rows = slices(z_blocks, fill, xh, xl)
     t_own, t_other = [
-        multiply(*rows, y_panel) for rows in rows_with_partner(*slices(z_blocks, fill))
+        multiply(rows, swap(rows, "core"), y_panel) for rows in (z_rows, from_partner(z_part))
     ]
     same = core == xh
     mine = jnp.where(same, t_own, t_other)
@@ -117,8 +114,9 @@
     z_panel = lax.all_gather(z_piece, "y", axis=0)
     q_share, h_blocks = lax.optimization_barrier((q_share, h_blocks))
     q_mine = spread(q_share, "z", nz)
-    h_part, h_rows = slices(h_blocks, h_pattern.astype(jnp.float32))
-    q_mine, z_panel, h_part, h_rows = lax.optimization_barrier((q_mine, z_panel, h_part, h_rows))
+    h_fill = h_pattern.astype(jnp.float32)
+    h_others = from_partner(slices(h_blocks, h_fill, 1 - xh, 1 - xl))
+    q_mine, z_panel, h_others = lax.optimization_barrier((q_mine, z_panel, h_others))
     q_theirs = swap(q_mine, "core")
     ordered = z_panel.reshape(2, ny // 2, half, blk).transpose(1, 0, 2, 3)
     ordered = jnp.where(xh == 0, ordered, ordered[:, ::-1]).reshape(ny * half, blk)
@@ -133,12 +131,15 @@
         jnp.stack([jnp.where(first, z_mine, z_theirs), jnp.where(first, z_theirs, z_mine)])
     )
     z_copies = jnp.broadcast_to(z_share[None], (ny, half, blk))
-    z_copies, h_part, h_rows = lax.optimization_barrier((z_copies, h_part, h_rows))
+    z_copies, h_others, h_blocks = lax.optimization_barrier((z_copies, h_others, h_blocks))
+    h_rows = slices(h_blocks, h_fill, xh, xl)
     z_next_panel = lax.all_to_all(z_copies, "y", split_axis=0, concat_axis=0, tiled=True)
     z_next_panel = z_next_panel.reshape(ny * half, blk)
     z_shares = jnp.concatenate([z_share, swap(z_share, "xl")], axis=0)
     z_all = lax.all_gather(z_shares, "z", axis=0)
-    h_own, h_other = [multiply(*rows, z_next_panel) for rows in rows_with_partner(h_part, h_rows)]
+    h_own, h_other = [
+        multiply(rows, swap(rows, "core"), z_next_panel) for rows in (h_rows, h_others)
+    ]
     h_partial = jnp.stack([jnp.where(xh == 0, h_own, h_other), jnp.where(xh == 0, h_other, h_own)])
     h_share = finish(h_partial)
     passed = half * 5 // 8

time: 237 us -> 237 us (level)
  the two profiles are of different devices: /device:TPU:56 before, /device:TPU:1 now
where the time goes in v8:
time: 237 us; the launch traced here: 236 us
  waiting for transfers between devices  87.9 us (37%)
  starting transfers between devices  68.5 us (29%)
  other arithmetic  24.4 us (10%)
  blocking collectives  22.9 us (10%)
  between operations  14.6 us (6%)
  local copies, waits for them, and re-layouts  8.57 us (4%)
  matrix products  6.2 us (3%)
  Pallas kernels  2.96 us (1%)
    ppermute x9, starting transfers between devices, swap(): return lax.ppermute(array, axis, [(0, 1), (1, 0)])  27.5 us
    all_to_all x2, blocking collectives, sum_x(): lax.all_to_all(parts, X, split_axis=0, concat_axis=0, tiled=True)  22.9 us
    ppermute x9, waiting for transfers between devices, swap(): return lax.ppermute(array, axis, [(0, 1), (1, 0)])  20.2 us
    mul x4, other arithmetic, slices(): lax.dynamic_slice(values, (0, (2 * m + a) * blk + b * half), (blk, half))  14.8 us
    all_to_all x1, waiting for transfers between devices, local(): lax.all_to_all(early, 'z', split_axis=0, concat_axis=0, tiled=True)  14.6 us
    all_gather x1, waiting for transfers between devices, local(): z_panel = lax.all_gather(z_piece, 'y', axis=0)  12.4 us
    all_to_all x1, waiting for transfers between devices, local(): lax.all_to_all(z_copies, 'y', split_axis=0, concat_axis=0, tiled=True)  10.4 us
    all_to_all x1, waiting for transfers between devices, spread(): return lax.all_to_all(copies, axis, split_axis=0, concat_axis=0, tiled=True)  10.3 us
  transfers between devices with their start and end apart: 19, of which 13 were waited for; matrix products, arithmetic and copies ran while one was open for 11% of the time, Pallas kernels for 1%

profile of v8, /device:TPU:1, one launch (start us, length us, event | category | flops | bytes accessed | tf_op | source)
XLA Modules:
  0.0 235.9 jit_solution(4632624805035935968)
XLA Ops:
  7.2 0.7 convert_element_type.10
  7.9 0.7 fusion.24
  8.6 2.3 dynamic-slice_multiply_fusion.16
  10.9 1.1 broadcast_in_dim.20
  11.9 7.7 %all-to-all-start = ((f32[8,128,256]{2,1,0:T(8,128)}), f32[8,128,256]{2,1,0:T(8,128)S(1)}, u32[]{:S(2)}, u32[]{:S(2)}) async-start(f32[8,128,256]{2,1,0:T(8,128)} %broadcast_in_dim.20), calls=%async_computation | async-start | bytes 2097152 | tf_op jit(solution)/shard_map/all_to_all | solution.py:93
  19.6 3.6 %dynamic-slice_multiply_fusion.15 = (f32[256,128]{1,0:T(8,128)S(1)}, f32[256,128]{1,0:T(8,128)S(1)}, f32[256,128]{1,0:T(8,128)S(1)}, f32[256,128]{1,0:T(8,128)S(1)}) fusion(f32[256,2048]{1,0:T(8,128)} %param.7, s32[]{:T(128)S(6)} %select_n.191, f32[]{:T(128)} %bitcast.2, f32[]{:T(128)} %bitcast.5, s32[]{:T(128)S(6)} %select_n.197, f32[]{:T(128)} %bitcast.4, ...), kind=kLoop, calls=%fused_computation.51 | loop fusion | flops 131072 | bytes 1048608 | tf_op jit(solution)/shard_map/mul | solution.py:65
  23.2 4.4 %collective-permute-start.1 = (f32[256,512]{1,0:T(8,128)S(1)}, f32[256,512]{1,0:T(8,128)S(1)}, u32[]{:S(2)}, u32[]{:S(2)}) collective-permute-start(f32[256,512]{1,0:T(8,128)S(1)} %pad_maximum_fusion.1), channel_id=1, source_target_pairs={{0,33},{33,0},{1,32},{32,1},{2,35},{35,2},{3,34},{34,3},{4,37},{37... | collective-permute-start | bytes 1572872 | tf_op jit(solution)/shard_map/ppermute | solution.py:73
  27.6 3.7 %dynamic-slice_multiply_fusion.11 = (f32[256,128]{1,0:T(8,128)S(1)}, f32[256,128]{1,0:T(8,128)S(1)}, f32[256,128]{1,0:T(8,128)S(1)}, f32[256,128]{1,0:T(8,128)S(1)}) fusion(f32[256,2048]{1,0:T(8,128)} %param.7, s32[]{:T(128)S(6)} %select_n.199, f32[]{:T(128)} %bitcast.6, f32[]{:T(128)} %bitcast.9, s32[]{:T(128)S(6)} %select_n.205, f32[]{:T(128)} %bitcast.8, ...), kind=kLoop, calls=%fused_computation.47 | loop fusion | flops 131072 | bytes 1048608 | tf_op jit(solution)/shard_map/mul | solution.py:65
  31.3 0.8 pad_maximum_fusion.2
  32.2 3.1 %collective-permute-start = (f32[256,512]{1,0:T(8,128)}, f32[256,512]{1,0:T(8,128)S(1)}, u32[]{:S(2)}, u32[]{:S(2)}) collective-permute-start(f32[256,512]{1,0:T(8,128)} %pad_maximum_fusion.2), channel_id=1, source_target_pairs={{0,16},{16,0},{1,17},{17,1},{2,18},{18,2},{3,19},{19,3},{4,20},{20... | collective-permute-start | bytes 1572872 | tf_op jit(solution)/shard_map/ppermute | solution.py:20
  35.3 2.5 %collective-permute-done.1 = f32[256,512]{1,0:T(8,128)S(1)} collective-permute-done((f32[256,512]{1,0:T(8,128)S(1)}, f32[256,512]{1,0:T(8,128)S(1)}, u32[]{:S(2)}, u32[]{:S(2)}) %collective-permute-start.1) | collective-permute-done | bytes 524320 | tf_op jit(solution)/shard_map/ppermute | solution.py:73
  37.9 4.7 %collective-permute-start.2 = (f32[256,512]{1,0:T(8,128)S(1)}, f32[256,512]{1,0:T(8,128)S(1)}, u32[]{:S(2)}, u32[]{:S(2)}) collective-permute-start(f32[256,512]{1,0:T(8,128)S(1)} %collective-permute-done.1), channel_id=1, source_target_pairs={{0,16},{16,0},{1,17},{17,1},{2,18},{18,2},{3,19},{19,3},{4,20},{20... | collective-permute-start | bytes 1572872 | tf_op jit(solution)/shard_map/ppermute | solution.py:20
  42.6 4.2 %all-to-all-done = f32[8,128,256]{2,1,0:T(8,128)S(1)} async-done(((f32[8,128,256]{2,1,0:T(8,128)}), f32[8,128,256]{2,1,0:T(8,128)S(1)}, u32[]{:S(2)}, u32[]{:S(2)}) %all-to-all-start) | async-done | bytes 1048608 | tf_op jit(solution)/shard_map/all_to_all | solution.py:93
  47.6 0.4 convolution_add_fusion.3
  48.0 0.4 broadcast_select_fusion
  48.4 4.4 %collective-permute-start.3 = (f32[256,256]{1,0:T(8,128)S(1)}, f32[256,256]{1,0:T(8,128)S(1)}, u32[]{:S(2)}, u32[]{:S(2)}) collective-permute-start(f32[256,256]{1,0:T(8,128)S(1)} %get-tuple-element.79), channel_id=1, source_target_pairs={{0,16},{16,0},{1,17},{17,1},{2,18},{18,2},{3,19},{19,3},{4,20},{20... | collective-permute-start | bytes 786440 | tf_op jit(solution)/shard_map/ppermute | solution.py:20
  52.8 1.1 collective-permute-done.3
  54.0 0.8 fusion
  54.9 4.0 %all-to-all-start.1 = ((f32[4,256,128]{2,1,0:T(8,128)}), f32[4,256,128]{2,1,0:T(8,128)S(1)}, u32[]{:S(2)}, u32[]{:S(2)}) async-start(f32[4,256,128]{2,1,0:T(8,128)} %bitcast.13), calls=%async_computation.1 | async-start | bytes 1048576 | tf_op jit(solution)/shard_map/all_to_all | solution.py:85
  58.9 0.7 all-gather.5.cloned.1.call-update
  59.7 0.7 fusion.22
  60.4 7.4 %all-to-all-done.1 = f32[4,256,128]{2,1,0:T(8,128)S(1)} async-done(((f32[4,256,128]{2,1,0:T(8,128)}), f32[4,256,128]{2,1,0:T(8,128)S(1)}, u32[]{:S(2)}, u32[]{:S(2)}) %all-to-all-start.1) | async-done | bytes 524320 | tf_op jit(solution)/shard_map/all_to_all | solution.py:85
  67.8 0.7 multiply_subtract_fusion
  68.7 1.1 broadcast_in_dim.21
  69.7 10.0 %all-to-all-start.2 = ((f32[8,256,128]{1,2,0:T(8,128)}), f32[8,256,128]{1,2,0:T(8,128)S(1)}, u32[]{:S(2)}, u32[]{:S(2)}) async-start(f32[8,256,128]{1,2,0:T(8,128)} %broadcast_in_dim.21), calls=%async_computation.2 | async-start | bytes 2097152 | tf_op jit(solution)/shard_map/all_to_all | solution.py:16
  79.8 3.6 %dynamic-slice_multiply_fusion.7 = (f32[256,128]{1,0:T(8,128)S(1)}, f32[256,128]{1,0:T(8,128)S(1)}, f32[256,128]{1,0:T(8,128)S(1)}, f32[256,128]{1,0:T(8,128)S(1)}) fusion(f32[256,2048]{1,0:T(8,128)} %param.8, s32[]{:T(128)S(6)} %select_n.191, f32[]{:T(128)} %bitcast.15, f32[]{:T(128)} %bitcast.18, s32[]{:T(128)S(6)} %select_n.197, f32[]{:T(128)} %bitcast.17, ...), kind=kLoop, calls=%fused_computation.42 | loop fusion | flops 131072 | bytes 1048608 | tf_op jit(solution)/shard_map/mul | solution.py:65
  83.4 2.8 %collective-permute-start.4 = (f32[256,512]{1,0:T(8,128)S(1)}, f32[256,512]{1,0:T(8,128)S(1)}, u32[]{:S(2)}, u32[]{:S(2)}) collective-permute-start(f32[256,512]{1,0:T(8,128)S(1)} %pad_maximum_fusion.3), channel_id=1, source_target_pairs={{0,33},{33,0},{1,32},{32,1},{2,35},{35,2},{3,34},{34,3},{4,37},{37... | collective-permute-start | bytes 1572872 | tf_op jit(solution)/shard_map/ppermute | solution.py:73
  86.2 12.4 %all-gather.5.cloned.1.call-done = f32[1024,256]{1,0:T(8,128)} async-done(((f32[128,256]{1,0:T(8,128)}), f32[1024,256]{1,0:T(8,128)}) %all-gather.5.cloned.1.call-update) | async-done | bytes 1048592 | tf_op jit(solution)/shard_map/all_gather | solution.py:114
  98.7 10.3 %all-to-all-done.2 = f32[8,256,128]{1,2,0:T(8,128)S(1)} async-done(((f32[8,256,128]{1,2,0:T(8,128)}), f32[8,256,128]{1,2,0:T(8,128)S(1)}, u32[]{:S(2)}, u32[]{:S(2)}) %all-to-all-start.2) | async-done | bytes 1048608 | tf_op jit(solution)/shard_map/all_to_all | solution.py:16
  108.9 2.4 %collective-permute-start.5 = (f32[8,256,128]{1,2,0:T(8,128)S(1)}, f32[8,256,128]{1,2,0:T(8,128)S(1)}, u32[]{:S(2)}, u32[]{:S(2)}) collective-permute-start(f32[8,256,128]{1,2,0:T(8,128)S(1)} %all-to-all-done.2), channel_id=1, source_target_pairs={{0,16},{16,0},{1,17},{17,1},{2,18},{18,2},{3,19},{19,3},{4,20},{20... | collective-permute-start | bytes 3145736 | tf_op jit(solution)/shard_map/ppermute | solution.py:20
  111.4 1.8 reverse_select_fusion
  113.6 1.0 fusion.27
  114.6 1.0 select_bitcast_fusion.3
  115.7 11.6 %all_to_all.40 = f32[4,128,256]{2,1,0:T(8,128)S(1)} all-to-all(f32[4,128,256]{2,1,0:T(8,128)S(1)} %bitcast.70), channel_id=1, replica_groups=mesh['y'=8,'xh'=2,'core'=2,'z'=8,'xl'=2] {'xh','xl'}, dimensions={0} | all-to-all | bytes 1048576 | tf_op jit(solution)/shard_map/all_to_all | solution.py:85
  127.3 0.7 broadcast_multiply_fusion.1
  128.0 1.1 broadcast_in_dim.22
  129.1 3.6 %all-to-all-start.4 = ((f32[8,128,256]{2,1,0:T(8,128)}), f32[8,128,256]{2,1,0:T(8,128)S(1)}, u32[]{:S(2)}, u32[]{:S(2)}) async-start(f32[8,128,256]{2,1,0:T(8,128)} %broadcast_in_dim.22), calls=%async_computation.4 | async-start | bytes 2097152 | tf_op jit(solution)/shard_map/all_to_all | solution.py:136
  132.7 2.2 collective-permute-start.9
  134.9 3.8 %collective-permute-done.9 = f32[128,256]{1,0:T(8,128)S(1)} collective-permute-done((f32[128,256]{1,0:T(8,128)S(1)}, f32[128,256]{1,0:T(8,128)S(1)}, u32[]{:S(2)}, u32[]{:S(2)}) %collective-permute-start.9) | collective-permute-done | bytes 131104 | tf_op jit(solution)/shard_map/ppermute | solution.py:20
  138.7 0.7 pad_maximum_fusion.7
  139.4 4.0 %collective-permute-start.7 = (f32[256,512]{1,0:T(8,128)S(1)}, f32[256,512]{1,0:T(8,128)S(1)}, u32[]{:S(2)}, u32[]{:S(2)}) collective-permute-start(f32[256,512]{1,0:T(8,128)S(1)} %collective-permute-done.4), channel_id=1, source_target_pairs={{0,16},{16,0},{1,17},{17,1},{2,18},{18,2},{3,19},{19,3},{4,20},{20... | collective-permute-start | bytes 1572872 | tf_op jit(solution)/shard_map/ppermute | solution.py:20
  143.4 3.8 %dynamic-slice_multiply_fusion.3 = (f32[256,128]{1,0:T(8,128)S(1)}, f32[256,128]{1,0:T(8,128)S(1)}, f32[256,128]{1,0:T(8,128)S(1)}, f32[256,128]{1,0:T(8,128)S(1)}) fusion(f32[256,2048]{1,0:T(8,128)} %param.8, s32[]{:T(128)S(6)} %select_n.199, f32[]{:T(128)} %bitcast.31, f32[]{:T(128)} %bitcast.34, s32[]{:T(128)S(6)} %select_n.205, f32[]{:T(128)} %bitcast.33, ...), kind=kLoop, calls=%fused_computation.38 | loop fusion | flops 131072 | bytes 1048608 | tf_op jit(solution)/shard_map/mul | solution.py:65
  147.3 1.9 collective-permute-start.6
  149.2 10.4 %all-to-all-done.4 = f32[8,128,256]{2,1,0:T(8,128)S(1)} async-done(((f32[8,128,256]{2,1,0:T(8,128)}), f32[8,128,256]{2,1,0:T(8,128)S(1)}, u32[]{:S(2)}, u32[]{:S(2)}) %all-to-all-start.4) | async-done | bytes 1048608 | tf_op jit(solution)/shard_map/all_to_all | solution.py:136
  159.6 0.4 fusion.5
  160.0 0.4 fusion.3
  160.4 0.4 convolution_add_fusion
  160.8 1.4 select_bitcast_fusion.1
  162.3 11.3 %all_to_all.41 = f32[4,128,256]{2,1,0:T(8,128)S(1)} all-to-all(f32[4,128,256]{2,1,0:T(8,128)S(1)} %bitcast.71), channel_id=1, replica_groups=mesh['y'=8,'xh'=2,'core'=2,'z'=8,'xl'=2] {'xh','xl'}, dimensions={0} | all-to-all | bytes 1048576 | tf_op jit(solution)/shard_map/all_to_all | solution.py:85
  173.7 0.7 broadcast_multiply_fusion
  174.4 0.9 broadcast_in_dim.23
  175.3 4.9 %all-to-all-start.6 = ((f32[8,80,256]{2,1,0:T(8,128)}), f32[8,80,256]{2,1,0:T(8,128)S(1)}, u32[]{:S(2)}, u32[]{:S(2)}) async-start(f32[8,80,256]{2,1,0:T(8,128)} %broadcast_in_dim.23), calls=%async_computation.6 | async-start | bytes 1310720 | tf_op jit(solution)/shard_map/all_to_all | solution.py:149
  180.2 2.3 collective-permute-start.8
  182.5 2.5 %collective-permute-done.8 = f32[48,256]{1,0:T(8,128)S(1)} collective-permute-done((f32[48,256]{1,0:T(8,128)S(1)}, f32[48,256]{1,0:T(8,128)S(1)}, u32[]{:S(2)}, u32[]{:S(2)}) %collective-permute-start.8) | collective-permute-done | bytes 49184 | tf_op jit(solution)/shard_map/ppermute | solution.py:20
  185.0 14.6 %all-to-all-done.6.refs_0_ = f32[8,80,256]{2,1,0:T(8,128)S(1)} async-done(((f32[8,80,256]{2,1,0:T(8,128)}), f32[8,80,256]{2,1,0:T(8,128)S(1)}, u32[]{:S(2)}, u32[]{:S(2)}) %all-to-all-start.6) | async-done | bytes 655392 | tf_op jit(solution)/shard_map/all_to_all | solution.py:149
  199.7 0.9 broadcast_in_dim.44
  200.6 3.5 %all-to-all-start.7 = ((f32[8,96,256]{2,1,0:T(8,128)}), f32[8,96,256]{2,1,0:T(8,128)S(1)}, u32[]{:S(2)}, u32[]{:S(2)}) async-start(f32[8,96,256]{2,1,0:T(8,128)} %broadcast_in_dim.44), calls=%async_computation.7 | async-start | bytes 1572864 | tf_op jit(solution)/shard_map/all_to_all | solution.py:153
  204.2 2.5 %collective-permute-start.10 = (f32[8,80,256]{2,1,0:T(8,128)S(1)}, f32[8,80,256]{2,1,0:T(8,128)S(1)}, u32[]{:S(2)}, u32[]{:S(2)}) collective-permute-start(f32[8,80,256]{2,1,0:T(8,128)S(1)} %all-to-all-done.6.refs_0_), channel_id=1, source_target_pairs={{0,1},{1,0},{2,3},{3,2},{4,5},{5,4},{6,7},{7,6},{8,9},{9,8},{10,11... | collective-permute-start | bytes 1966088 | tf_op jit(solution)/shard_map/ppermute | solution.py:20
  206.7 1.5 shard_map.77
  208.2 12.4 %collective-permute-done.10.refs_2_ = f32[8,80,256]{2,1,0:T(8,128)S(1)} collective-permute-done((f32[8,80,256]{2,1,0:T(8,128)S(1)}, f32[8,80,256]{2,1,0:T(8,128)S(1)}, u32[]{:S(2)}, u32[]{:S(2)}) %collective-permute-start.10) | collective-permute-done | bytes 655392 | tf_op jit(solution)/shard_map/ppermute | solution.py:20
  220.6 0.8 copy-done.1
  221.4 5.1 %all-to-all-done.7.refs_1_ = f32[8,96,256]{2,1,0:T(8,128)S(1)} async-done(((f32[8,96,256]{2,1,0:T(8,128)}), f32[8,96,256]{2,1,0:T(8,128)S(1)}, u32[]{:S(2)}, u32[]{:S(2)}) %all-to-all-start.7) | async-done | bytes 786464 | tf_op jit(solution)/shard_map/all_to_all | solution.py:153
  226.5 1.1 copy-done.2
  227.6 1.5 shard_map.78
  (39 shorter events, 1.8 us)
Async XLA Ops:
  11.9 34.8 %all-to-all-start = ((f32[8,128,256]{2,1,0:T(8,128)}), f32[8,128,256]{2,1,0:T(8,128)S(1)}, u32[]{:S(2)}, u32[]{:S(2)}) async-start(f32[8,128,256]{2,1,0:T(8,128)} %broadcast_in_dim.20), calls=%async_computation | async-start | bytes 2097152 | tf_op jit(solution)/shard_map/all_to_all | solution.py:93
  23.2 14.6 %collective-permute-start.1 = (f32[256,512]{1,0:T(8,128)S(1)}, f32[256,512]{1,0:T(8,128)S(1)}, u32[]{:S(2)}, u32[]{:S(2)}) collective-permute-start(f32[256,512]{1,0:T(8,128)S(1)} %pad_maximum_fusion.1), channel_id=1, source_target_pairs={{0,33},{33,0},{1,32},{32,1},{2,35},{35,2},{3,34},{34,3},{4,37},{37... | collective-permute-start | bytes 1572872 | tf_op jit(solution)/shard_map/ppermute | solution.py:73
  32.2 15.4 %collective-permute-start = (f32[256,512]{1,0:T(8,128)}, f32[256,512]{1,0:T(8,128)S(1)}, u32[]{:S(2)}, u32[]{:S(2)}) collective-permute-start(f32[256,512]{1,0:T(8,128)} %pad_maximum_fusion.2), channel_id=1, source_target_pairs={{0,16},{16,0},{1,17},{17,1},{2,18},{18,2},{3,19},{19,3},{4,20},{20... | collective-permute-start | bytes 1572872 | tf_op jit(solution)/shard_map/ppermute | solution.py:20
  37.9 10.1 %collective-permute-start.2 = (f32[256,512]{1,0:T(8,128)S(1)}, f32[256,512]{1,0:T(8,128)S(1)}, u32[]{:S(2)}, u32[]{:S(2)}) collective-permute-start(f32[256,512]{1,0:T(8,128)S(1)} %collective-permute-done.1), channel_id=1, source_target_pairs={{0,16},{16,0},{1,17},{17,1},{2,18},{18,2},{3,19},{19,3},{4,20},{20... | collective-permute-start | bytes 1572872 | tf_op jit(solution)/shard_map/ppermute | solution.py:20
  48.4 5.6 %collective-permute-start.3 = (f32[256,256]{1,0:T(8,128)S(1)}, f32[256,256]{1,0:T(8,128)S(1)}, u32[]{:S(2)}, u32[]{:S(2)}) collective-permute-start(f32[256,256]{1,0:T(8,128)S(1)} %get-tuple-element.79), channel_id=1, source_target_pairs={{0,16},{16,0},{1,17},{17,1},{2,18},{18,2},{3,19},{19,3},{4,20},{20... | collective-permute-start | bytes 786440 | tf_op jit(solution)/shard_map/ppermute | solution.py:20
  54.0 5.7 %copy-start.3 = (s32[16,16]{1,0:T(8,128)S(1)}, s32[16,16]{1,0:T(8,128)}, u32[]{:S(2)}) copy-start(s32[16,16]{1,0:T(8,128)} %param.10) | copy-start | bytes 3076
  54.0 5.7 %copy-start.4 = (s32[16,16]{1,0:T(8,128)S(1)}, s32[16,16]{1,0:T(8,128)}, u32[]{:S(2)}) copy-start(s32[16,16]{1,0:T(8,128)} %param.11) | copy-start | bytes 3076
  54.9 12.9 %all-to-all-start.1 = ((f32[4,256,128]{2,1,0:T(8,128)}), f32[4,256,128]{2,1,0:T(8,128)S(1)}, u32[]{:S(2)}, u32[]{:S(2)}) async-start(f32[4,256,128]{2,1,0:T(8,128)} %bitcast.13), calls=%async_computation.1 | async-start | bytes 1048576 | tf_op jit(solution)/shard_map/all_to_all | solution.py:85
  58.9 39.8 %all-gather.5.cloned.1.call-start = ((), (), s32[]{:S(2)}) async-start(), calls=%async_computation.8 | async-start | bytes 1179648 | tf_op jit(solution)/shard_map/all_gather | solution.py:114
  69.7 39.2 %all-to-all-start.2 = ((f32[8,256,128]{1,2,0:T(8,128)}), f32[8,256,128]{1,2,0:T(8,128)S(1)}, u32[]{:S(2)}, u32[]{:S(2)}) async-start(f32[8,256,128]{1,2,0:T(8,128)} %broadcast_in_dim.21), calls=%async_computation.2 | async-start | bytes 2097152 | tf_op jit(solution)/shard_map/all_to_all | solution.py:16
  83.4 15.2 %collective-permute-start.4 = (f32[256,512]{1,0:T(8,128)S(1)}, f32[256,512]{1,0:T(8,128)S(1)}, u32[]{:S(2)}, u32[]{:S(2)}) collective-permute-start(f32[256,512]{1,0:T(8,128)S(1)} %pad_maximum_fusion.3), channel_id=1, source_target_pairs={{0,33},{33,0},{1,32},{32,1},{2,35},{35,2},{3,34},{34,3},{4,37},{37... | collective-permute-start | bytes 1572872 | tf_op jit(solution)/shard_map/ppermute | solution.py:73
  108.9 4.7 %collective-permute-start.5 = (f32[8,256,128]{1,2,0:T(8,128)S(1)}, f32[8,256,128]{1,2,0:T(8,128)S(1)}, u32[]{:S(2)}, u32[]{:S(2)}) collective-permute-start(f32[8,256,128]{1,2,0:T(8,128)S(1)} %all-to-all-done.2), channel_id=1, source_target_pairs={{0,16},{16,0},{1,17},{17,1},{2,18},{18,2},{3,19},{19,3},{4,20},{20... | collective-permute-start | bytes 3145736 | tf_op jit(solution)/shard_map/ppermute | solution.py:20
  129.1 30.5 %all-to-all-start.4 = ((f32[8,128,256]{2,1,0:T(8,128)}), f32[8,128,256]{2,1,0:T(8,128)S(1)}, u32[]{:S(2)}, u32[]{:S(2)}) async-start(f32[8,128,256]{2,1,0:T(8,128)} %broadcast_in_dim.22), calls=%async_computation.4 | async-start | bytes 2097152 | tf_op jit(solution)/shard_map/all_to_all | solution.py:136
  132.6 67.1 %all-gather.7.cloned.1.call-start = ((), (), s32[]{:S(2)}) async-start(), calls=%async_computation.9 | async-start | bytes 2359296 | tf_op jit(solution)/shard_map/all_gather | solution.py:139
  132.7 6.0 %collective-permute-start.9 = (f32[128,256]{1,0:T(8,128)S(1)}, f32[128,256]{1,0:T(8,128)S(1)}, u32[]{:S(2)}, u32[]{:S(2)}) collective-permute-start(f32[128,256]{1,0:T(8,128)S(1)} %broadcast_multiply_fusion.1), channel_id=1, source_target_pairs={{0,1},{1,0},{2,3},{3,2},{4,5},{5,4},{6,7},{7,6},{8,9},{9,8},{10,11... | collective-permute-start | bytes 393224 | tf_op jit(solution)/shard_map/ppermute | solution.py:20
  139.4 21.0 %collective-permute-start.7 = (f32[256,512]{1,0:T(8,128)S(1)}, f32[256,512]{1,0:T(8,128)S(1)}, u32[]{:S(2)}, u32[]{:S(2)}) collective-permute-start(f32[256,512]{1,0:T(8,128)S(1)} %collective-permute-done.4), channel_id=1, source_target_pairs={{0,16},{16,0},{1,17},{17,1},{2,18},{18,2},{3,19},{19,3},{4,20},{20... | collective-permute-start | bytes 1572872 | tf_op jit(solution)/shard_map/ppermute | solution.py:20
  147.3 13.5 %collective-permute-start.6 = (f32[256,512]{1,0:T(8,128)S(1)}, f32[256,512]{1,0:T(8,128)}, u32[]{:S(2)}, u32[]{:S(2)}) collective-permute-start(f32[256,512]{1,0:T(8,128)S(1)} %pad_maximum_fusion.5), channel_id=1, source_target_pairs={{0,16},{16,0},{1,17},{17,1},{2,18},{18,2},{3,19},{19,3},{4,20},{20... | collective-permute-start | bytes 1572872 | tf_op jit(solution)/shard_map/ppermute | solution.py:20
  175.3 24.4 %all-to-all-start.6 = ((f32[8,80,256]{2,1,0:T(8,128)}), f32[8,80,256]{2,1,0:T(8,128)S(1)}, u32[]{:S(2)}, u32[]{:S(2)}) async-start(f32[8,80,256]{2,1,0:T(8,128)} %broadcast_in_dim.23), calls=%async_computation.6 | async-start | bytes 1310720 | tf_op jit(solution)/shard_map/all_to_all | solution.py:149
  180.2 4.8 %collective-permute-start.8 = (f32[48,256]{1,0:T(8,128)S(1)}, f32[48,256]{1,0:T(8,128)S(1)}, u32[]{:S(2)}, u32[]{:S(2)}) collective-permute-start(f32[48,256]{1,0:T(8,128)S(1)} %slice.16), channel_id=1, source_target_pairs={{0,1},{1,0},{2,3},{3,2},{4,5},{5,4},{6,7},{7,6},{8,9},{9,8},{10,11... | collective-permute-start | bytes 147464 | tf_op jit(solution)/shard_map/ppermute | solution.py:20
  199.7 7.0 %copy-start = (f32[2048,256]{1,0:T(8,128)S(1)}, f32[2048,256]{1,0:T(8,128)}, u32[]{:S(2)}) copy-start(f32[2048,256]{1,0:T(8,128)} %all-gather.7.cloned.1.call-done) | copy-start | bytes 6291460
  200.6 25.9 %all-to-all-start.7 = ((f32[8,96,256]{2,1,0:T(8,128)}), f32[8,96,256]{2,1,0:T(8,128)S(1)}, u32[]{:S(2)}, u32[]{:S(2)}) async-start(f32[8,96,256]{2,1,0:T(8,128)} %broadcast_in_dim.44), calls=%async_computation.7 | async-start | bytes 1572864 | tf_op jit(solution)/shard_map/all_to_all | solution.py:153
  204.2 16.4 %collective-permute-start.10 = (f32[8,80,256]{2,1,0:T(8,128)S(1)}, f32[8,80,256]{2,1,0:T(8,128)S(1)}, u32[]{:S(2)}, u32[]{:S(2)}) collective-permute-start(f32[8,80,256]{2,1,0:T(8,128)S(1)} %all-to-all-done.6.refs_0_), channel_id=1, source_target_pairs={{0,1},{1,0},{2,3},{3,2},{4,5},{5,4},{6,7},{7,6},{8,9},{9,8},{10,11... | collective-permute-start | bytes 1966088 | tf_op jit(solution)/shard_map/ppermute | solution.py:20
  220.6 0.9 copy-start.1
  226.5 1.1 copy-start.2
Sparse Core Ops, SparseCore 0:
  61.8 36.8 all-gather.4
  139.6 38.2 all-gather.6

commit v9 on v8

--- a/solution.py
+++ b/solution.py
@@ -142,16 +142,16 @@
     ]
     h_partial = jnp.stack([jnp.where(xh == 0, h_own, h_other), jnp.where(xh == 0, h_other, h_own)])
     h_share = finish(h_partial)
-    passed = half * 5 // 8
+    passed = half * 9 // 16
     rest = half - passed
     early = jnp.broadcast_to(h_share[:passed][None], (nz, passed, blk))
     early, h_share = lax.optimization_barrier((early, h_share))
     h_early = lax.all_to_all(early, "z", split_axis=0, concat_axis=0, tiled=True)
     late = jnp.concatenate([h_share[passed:], swap(h_share[passed:], "xl")], axis=0)
-    late = jnp.broadcast_to(late[None], (nz, 2 * rest, blk))
-    late, z_all, h_early = lax.optimization_barrier((late, z_all, h_early))
-    h_late = lax.all_to_all(late, "z", split_axis=0, concat_axis=0, tiled=True)
     z_next = place([z_all], [(0, 0, 0, 0, half), (0, half, 1, 0, half)], blk)
+    h_early, z_next = lax.optimization_barrier((h_early, z_next))
+    late, h_early = lax.optimization_barrier((late, h_early))
+    h_late = lax.all_gather(late, "z", axis=0)
     h_times_z = place(
         [h_early, h_late, swap(h_early, "xl")],
         [

time: 237 us -> 237 us (level)
  the two profiles are of different devices: /device:TPU:1 before, /device:TPU:2 now
where the time goes in v9:
time: 237 us; the launch traced here: 235 us
  waiting for transfers between devices  73.3 us (31%)
  starting transfers between devices  57.1 us (24%)
  blocking collectives  49.9 us (21%)
  other arithmetic  24.2 us (10%)
  between operations  14.5 us (6%)
  local copies, waits for them, and re-layouts  7.22 us (3%)
  matrix products  6.2 us (3%)
  Pallas kernels  2.96 us (1%)
    all_gather x1, blocking collectives, local(): h_late = lax.all_gather(late, 'z', axis=0)  26.3 us
    all_to_all x2, blocking collectives, sum_x(): lax.all_to_all(parts, X, split_axis=0, concat_axis=0, tiled=True)  23.7 us
    ppermute x9, starting transfers between devices, swap(): return lax.ppermute(array, axis, [(0, 1), (1, 0)])  22 us
    all_gather x1, waiting for transfers between devices, local(): z_panel = lax.all_gather(z_piece, 'y', axis=0)  16.8 us
    mul x4, other arithmetic, slices(): lax.dynamic_slice(values, (0, (2 * m + a) * blk + b * half), (blk, half))  14.7 us
    all_to_all x1, waiting for transfers between devices, local(): lax.all_to_all(z_copies, 'y', split_axis=0, concat_axis=0, tiled=True)  12.7 us
    all_to_all x1, starting transfers between devices, spread(): return lax.all_to_all(copies, axis, split_axis=0, concat_axis=0, tiled=True)  10.3 us
    all_to_all x1, waiting for transfers between devices, local(): lax.all_to_all(early, 'z', split_axis=0, concat_axis=0, tiled=True)  9.15 us
  transfers between devices with their start and end apart: 18, of which 11 were waited for; matrix products, arithmetic and copies ran while one was open for 11% of the time, Pallas kernels for 1%

profile of v9, /device:TPU:2, one launch (start us, length us, event | category | flops | bytes accessed | tf_op | source)
XLA Modules:
  0.0 235.4 jit_solution(7068443799998245597)
XLA Ops:
  7.2 0.7 convert_element_type.10
  7.9 0.7 fusion.24
  8.6 2.3 dynamic-slice_multiply_fusion.16
  10.9 1.1 broadcast_in_dim.18
  11.9 7.1 %all-to-all-start = ((f32[8,128,256]{2,1,0:T(8,128)}), f32[8,128,256]{2,1,0:T(8,128)S(1)}, u32[]{:S(2)}, u32[]{:S(2)}) async-start(f32[8,128,256]{2,1,0:T(8,128)} %broadcast_in_dim.18), calls=%async_computation | async-start | bytes 2097152 | tf_op jit(solution)/shard_map/all_to_all | solution.py:93
  19.0 3.6 %dynamic-slice_multiply_fusion.15 = (f32[256,128]{1,0:T(8,128)S(1)}, f32[256,128]{1,0:T(8,128)S(1)}, f32[256,128]{1,0:T(8,128)S(1)}, f32[256,128]{1,0:T(8,128)S(1)}) fusion(f32[256,2048]{1,0:T(8,128)} %param.7, s32[]{:T(128)S(6)} %select_n.191, f32[]{:T(128)} %bitcast.2, f32[]{:T(128)} %bitcast.5, s32[]{:T(128)S(6)} %select_n.197, f32[]{:T(128)} %bitcast.4, ...), kind=kLoop, calls=%fused_computation.51 | loop fusion | flops 131072 | bytes 1048608 | tf_op jit(solution)/shard_map/mul | solution.py:65
  22.7 3.4 %collective-permute-start.1 = (f32[256,512]{1,0:T(8,128)S(1)}, f32[256,512]{1,0:T(8,128)S(1)}, u32[]{:S(2)}, u32[]{:S(2)}) collective-permute-start(f32[256,512]{1,0:T(8,128)S(1)} %pad_maximum_fusion.1), channel_id=1, source_target_pairs={{0,33},{33,0},{1,32},{32,1},{2,35},{35,2},{3,34},{34,3},{4,37},{37... | collective-permute-start | bytes 1572872 | tf_op jit(solution)/shard_map/ppermute | solution.py:73
  26.1 3.6 %dynamic-slice_multiply_fusion.11 = (f32[256,128]{1,0:T(8,128)S(1)}, f32[256,128]{1,0:T(8,128)S(1)}, f32[256,128]{1,0:T(8,128)S(1)}, f32[256,128]{1,0:T(8,128)S(1)}) fusion(f32[256,2048]{1,0:T(8,128)} %param.7, s32[]{:T(128)S(6)} %select_n.199, f32[]{:T(128)} %bitcast.6, f32[]{:T(128)} %bitcast.9, s32[]{:T(128)S(6)} %select_n.205, f32[]{:T(128)} %bitcast.8, ...), kind=kLoop, calls=%fused_computation.47 | loop fusion | flops 131072 | bytes 1048608 | tf_op jit(solution)/shard_map/mul | solution.py:65
  29.7 0.8 pad_maximum_fusion.2
  30.5 1.9 collective-permute-start
  32.5 5.5 %collective-permute-done.1 = f32[256,512]{1,0:T(8,128)S(1)} collective-permute-done((f32[256,512]{1,0:T(8,128)S(1)}, f32[256,512]{1,0:T(8,128)S(1)}, u32[]{:S(2)}, u32[]{:S(2)}) %collective-permute-start.1) | collective-permute-done | bytes 524320 | tf_op jit(solution)/shard_map/ppermute | solution.py:73
  38.0 1.9 collective-permute-start.2
  39.9 7.9 %all-to-all-done = f32[8,128,256]{2,1,0:T(8,128)S(1)} async-done(((f32[8,128,256]{2,1,0:T(8,128)}), f32[8,128,256]{2,1,0:T(8,128)S(1)}, u32[]{:S(2)}, u32[]{:S(2)}) %all-to-all-start) | async-done | bytes 1048608 | tf_op jit(solution)/shard_map/all_to_all | solution.py:93
  47.8 0.4 fusion.11
  48.2 0.4 fusion.9
  48.6 0.4 convolution_add_fusion.3
  49.0 0.4 broadcast_select_fusion
  49.4 1.9 collective-permute-start.3
  51.3 1.5 collective-permute-done.3
  52.9 0.8 fusion
  53.7 4.8 %all-to-all-start.1 = ((f32[4,256,128]{2,1,0:T(8,128)}), f32[4,256,128]{2,1,0:T(8,128)S(1)}, u32[]{:S(2)}, u32[]{:S(2)}) async-start(f32[4,256,128]{2,1,0:T(8,128)} %bitcast.13), calls=%async_computation.1 | async-start | bytes 1048576 | tf_op jit(solution)/shard_map/all_to_all | solution.py:85
  58.6 0.7 all-gather.6.cloned.1.call-update
  59.3 0.7 fusion.22
  60.1 6.8 %all-to-all-done.1 = f32[4,256,128]{2,1,0:T(8,128)S(1)} async-done(((f32[4,256,128]{2,1,0:T(8,128)}), f32[4,256,128]{2,1,0:T(8,128)S(1)}, u32[]{:S(2)}, u32[]{:S(2)}) %all-to-all-start.1) | async-done | bytes 524320 | tf_op jit(solution)/shard_map/all_to_all | solution.py:85
  66.9 0.8 multiply_subtract_fusion
  67.8 1.1 broadcast_in_dim.19
  68.9 10.3 %all-to-all-start.2 = ((f32[8,256,128]{1,2,0:T(8,128)}), f32[8,256,128]{1,2,0:T(8,128)S(1)}, u32[]{:S(2)}, u32[]{:S(2)}) async-start(f32[8,256,128]{1,2,0:T(8,128)} %broadcast_in_dim.19), calls=%async_computation.2 | async-start | bytes 2097152 | tf_op jit(solution)/shard_map/all_to_all | solution.py:16
  79.2 3.8 %dynamic-slice_multiply_fusion.7 = (f32[256,128]{1,0:T(8,128)S(1)}, f32[256,128]{1,0:T(8,128)S(1)}, f32[256,128]{1,0:T(8,128)S(1)}, f32[256,128]{1,0:T(8,128)S(1)}) fusion(f32[256,2048]{1,0:T(8,128)} %param.8, s32[]{:T(128)S(6)} %select_n.191, f32[]{:T(128)} %bitcast.15, f32[]{:T(128)} %bitcast.18, s32[]{:T(128)S(6)} %select_n.197, f32[]{:T(128)} %bitcast.17, ...), kind=kLoop, calls=%fused_computation.42 | loop fusion | flops 131072 | bytes 1048608 | tf_op jit(solution)/shard_map/mul | solution.py:65
  83.0 1.9 collective-permute-start.4
  85.0 16.8 %all-gather.6.cloned.1.call-done = f32[1024,256]{1,0:T(8,128)} async-done(((f32[128,256]{1,0:T(8,128)}), f32[1024,256]{1,0:T(8,128)}) %all-gather.6.cloned.1.call-update) | async-done | bytes 1048592 | tf_op jit(solution)/shard_map/all_gather | solution.py:114
  101.7 5.3 %all-to-all-done.2 = f32[8,256,128]{1,2,0:T(8,128)S(1)} async-done(((f32[8,256,128]{1,2,0:T(8,128)}), f32[8,256,128]{1,2,0:T(8,128)S(1)}, u32[]{:S(2)}, u32[]{:S(2)}) %all-to-all-start.2) | async-done | bytes 1048608 | tf_op jit(solution)/shard_map/all_to_all | solution.py:16
  107.1 1.9 collective-permute-start.5
  109.0 1.7 reverse_select_fusion
  110.7 0.1 copy.10
  110.8 0.8 collective-permute-done.5
  111.6 1.0 fusion.27
  112.6 1.0 select_bitcast_fusion.3
  113.6 12.5 %all_to_all.35 = f32[4,128,256]{2,1,0:T(8,128)S(1)} all-to-all(f32[4,128,256]{2,1,0:T(8,128)S(1)} %bitcast.72), channel_id=1, replica_groups=mesh['y'=8,'xh'=2,'core'=2,'z'=8,'xl'=2] {'xh','xl'}, dimensions={0} | all-to-all | bytes 1048576 | tf_op jit(solution)/shard_map/all_to_all | solution.py:85
  126.1 0.6 broadcast_multiply_fusion.1
  126.8 1.1 broadcast_in_dim.36
  127.8 3.6 %all-to-all-start.4 = ((f32[8,128,256]{2,1,0:T(8,128)}), f32[8,128,256]{2,1,0:T(8,128)S(1)}, u32[]{:S(2)}, u32[]{:S(2)}) async-start(f32[8,128,256]{2,1,0:T(8,128)} %broadcast_in_dim.36), calls=%async_computation.4 | async-start | bytes 2097152 | tf_op jit(solution)/shard_map/all_to_all | solution.py:136
  131.5 3.4 %collective-permute-start.8 = (f32[128,256]{1,0:T(8,128)S(1)}, f32[128,256]{1,0:T(8,128)S(1)}, u32[]{:S(2)}, u32[]{:S(2)}) collective-permute-start(f32[128,256]{1,0:T(8,128)S(1)} %broadcast_multiply_fusion.1), channel_id=1, source_target_pairs={{0,1},{1,0},{2,3},{3,2},{4,5},{5,4},{6,7},{7,6},{8,9},{9,8},{10,11... | collective-permute-start | bytes 393224 | tf_op jit(solution)/shard_map/ppermute | solution.py:20
  134.8 3.5 %collective-permute-done.8 = f32[128,256]{1,0:T(8,128)S(1)} collective-permute-done((f32[128,256]{1,0:T(8,128)S(1)}, f32[128,256]{1,0:T(8,128)S(1)}, u32[]{:S(2)}, u32[]{:S(2)}) %collective-permute-start.8) | collective-permute-done | bytes 131104 | tf_op jit(solution)/shard_map/ppermute | solution.py:20
  138.3 0.7 pad_maximum_fusion.7
  139.1 1.9 collective-permute-start.7
  141.0 3.7 %dynamic-slice_multiply_fusion.3 = (f32[256,128]{1,0:T(8,128)S(1)}, f32[256,128]{1,0:T(8,128)S(1)}, f32[256,128]{1,0:T(8,128)S(1)}, f32[256,128]{1,0:T(8,128)S(1)}) fusion(f32[256,2048]{1,0:T(8,128)} %param.8, s32[]{:T(128)S(6)} %select_n.199, f32[]{:T(128)} %bitcast.31, f32[]{:T(128)} %bitcast.34, s32[]{:T(128)S(6)} %select_n.205, f32[]{:T(128)} %bitcast.33, ...), kind=kLoop, calls=%fused_computation.38 | loop fusion | flops 131072 | bytes 1048608 | tf_op jit(solution)/shard_map/mul | solution.py:65
  144.7 2.4 %collective-permute-start.6 = (f32[256,512]{1,0:T(8,128)S(1)}, f32[256,512]{1,0:T(8,128)}, u32[]{:S(2)}, u32[]{:S(2)}) collective-permute-start(f32[256,512]{1,0:T(8,128)S(1)} %pad_maximum_fusion.5), channel_id=1, source_target_pairs={{0,16},{16,0},{1,17},{17,1},{2,18},{18,2},{3,19},{19,3},{4,20},{20... | collective-permute-start | bytes 1572872 | tf_op jit(solution)/shard_map/ppermute | solution.py:20
  147.2 12.7 %all-to-all-done.4 = f32[8,128,256]{2,1,0:T(8,128)S(1)} async-done(((f32[8,128,256]{2,1,0:T(8,128)}), f32[8,128,256]{2,1,0:T(8,128)S(1)}, u32[]{:S(2)}, u32[]{:S(2)}) %all-to-all-start.4) | async-done | bytes 1048608 | tf_op jit(solution)/shard_map/all_to_all | solution.py:136
  159.8 0.4 fusion.5
  160.2 0.4 fusion.3
  160.6 0.4 convolution_add_fusion
  161.0 1.4 select_bitcast_fusion.1
  162.5 11.2 %all_to_all.36 = f32[4,128,256]{2,1,0:T(8,128)S(1)} all-to-all(f32[4,128,256]{2,1,0:T(8,128)S(1)} %bitcast.73), channel_id=1, replica_groups=mesh['y'=8,'xh'=2,'core'=2,'z'=8,'xl'=2] {'xh','xl'}, dimensions={0} | all-to-all | bytes 1048576 | tf_op jit(solution)/shard_map/all_to_all | solution.py:85
  173.8 0.6 broadcast_multiply_fusion
  174.4 0.9 broadcast_in_dim.37
  175.3 4.0 %all-to-all-start.6 = ((f32[8,72,256]{2,1,0:T(8,128)}), f32[8,72,256]{2,1,0:T(8,128)S(1)}, u32[]{:S(2)}, u32[]{:S(2)}) async-start(f32[8,72,256]{2,1,0:T(8,128)} %broadcast_in_dim.37), calls=%async_computation.6 | async-start | bytes 1179648 | tf_op jit(solution)/shard_map/all_to_all | solution.py:149
  179.2 3.4 %collective-permute-start.9 = (f32[56,256]{1,0:T(8,128)S(1)}, f32[56,256]{1,0:T(8,128)S(1)}, u32[]{:S(2)}, u32[]{:S(2)}) collective-permute-start(f32[56,256]{1,0:T(8,128)S(1)} %slice.16), channel_id=1, source_target_pairs={{0,1},{1,0},{2,3},{3,2},{4,5},{5,4},{6,7},{7,6},{8,9},{9,8},{10,11... | collective-permute-start | bytes 172040 | tf_op jit(solution)/shard_map/ppermute | solution.py:20
  182.6 2.7 %collective-permute-done.9 = f32[56,256]{1,0:T(8,128)S(1)} collective-permute-done((f32[56,256]{1,0:T(8,128)S(1)}, f32[56,256]{1,0:T(8,128)S(1)}, u32[]{:S(2)}, u32[]{:S(2)}) %collective-permute-start.9) | collective-permute-done | bytes 57376 | tf_op jit(solution)/shard_map/ppermute | solution.py:20
  185.4 1.6 copy-done
  187.0 1.5 shard_map.77
  188.4 9.2 %all-to-all-done.6.refs_0_ = f32[8,72,256]{2,1,0:T(8,128)S(1)} async-done(((f32[8,72,256]{2,1,0:T(8,128)}), f32[8,72,256]{2,1,0:T(8,128)S(1)}, u32[]{:S(2)}, u32[]{:S(2)}) %all-to-all-start.6) | async-done | bytes 589856 | tf_op jit(solution)/shard_map/all_to_all | solution.py:149
  197.6 3.2 %collective-permute-start.10 = (f32[8,72,256]{2,1,0:T(8,128)S(1)}, f32[8,72,256]{2,1,0:T(8,128)S(1)}, u32[]{:S(2)}, u32[]{:S(2)}) collective-permute-start(f32[8,72,256]{2,1,0:T(8,128)S(1)} %all-to-all-done.6.refs_0_), channel_id=1, source_target_pairs={{0,1},{1,0},{2,3},{3,2},{4,5},{5,4},{6,7},{7,6},{8,9},{9,8},{10,11... | collective-permute-start | bytes 1769480 | tf_op jit(solution)/shard_map/ppermute | solution.py:20
  200.8 26.3 %all-gather.2 = f32[896,256]{1,0:T(8,128)S(1)} all-gather(f32[112,256]{1,0:T(8,128)S(1)} %pad_maximum_fusion.8), channel_id=4, replica_groups=mesh['y'=8,'xh'=2,'core'=2,'z'=8,'xl'=2] {'z'}, dimensions={0}, use_global_device_ids=true | all-gather | bytes 1032192 | tf_op jit(solution)/shard_map/all_gather | solution.py:154
  227.1 1.5 shard_map.78
  (33 shorter events, 0.6 us)
Async XLA Ops:
  11.9 35.8 %all-to-all-start = ((f32[8,128,256]{2,1,0:T(8,128)}), f32[8,128,256]{2,1,0:T(8,128)S(1)}, u32[]{:S(2)}, u32[]{:S(2)}) async-start(f32[8,128,256]{2,1,0:T(8,128)} %broadcast_in_dim.18), calls=%async_computation | async-start | bytes 2097152 | tf_op jit(solution)/shard_map/all_to_all | solution.py:93
  22.7 15.3 %collective-permute-start.1 = (f32[256,512]{1,0:T(8,128)S(1)}, f32[256,512]{1,0:T(8,128)S(1)}, u32[]{:S(2)}, u32[]{:S(2)}) collective-permute-start(f32[256,512]{1,0:T(8,128)S(1)} %pad_maximum_fusion.1), channel_id=1, source_target_pairs={{0,33},{33,0},{1,32},{32,1},{2,35},{35,2},{3,34},{34,3},{4,37},{37... | collective-permute-start | bytes 1572872 | tf_op jit(solution)/shard_map/ppermute | solution.py:73
  30.5 18.0 %collective-permute-start = (f32[256,512]{1,0:T(8,128)}, f32[256,512]{1,0:T(8,128)S(1)}, u32[]{:S(2)}, u32[]{:S(2)}) collective-permute-start(f32[256,512]{1,0:T(8,128)} %pad_maximum_fusion.2), channel_id=1, source_target_pairs={{0,16},{16,0},{1,17},{17,1},{2,18},{18,2},{3,19},{19,3},{4,20},{20... | collective-permute-start | bytes 1572872 | tf_op jit(solution)/shard_map/ppermute | solution.py:20
  38.0 11.0 %collective-permute-start.2 = (f32[256,512]{1,0:T(8,128)S(1)}, f32[256,512]{1,0:T(8,128)S(1)}, u32[]{:S(2)}, u32[]{:S(2)}) collective-permute-start(f32[256,512]{1,0:T(8,128)S(1)} %collective-permute-done.1), channel_id=1, source_target_pairs={{0,16},{16,0},{1,17},{17,1},{2,18},{18,2},{3,19},{19,3},{4,20},{20... | collective-permute-start | bytes 1572872 | tf_op jit(solution)/shard_map/ppermute | solution.py:20
  49.4 3.4 %collective-permute-start.3 = (f32[256,256]{1,0:T(8,128)S(1)}, f32[256,256]{1,0:T(8,128)S(1)}, u32[]{:S(2)}, u32[]{:S(2)}) collective-permute-start(f32[256,256]{1,0:T(8,128)S(1)} %get-tuple-element.81), channel_id=1, source_target_pairs={{0,16},{16,0},{1,17},{17,1},{2,18},{18,2},{3,19},{19,3},{4,20},{20... | collective-permute-start | bytes 786440 | tf_op jit(solution)/shard_map/ppermute | solution.py:20
  52.8 6.5 %copy-start.1 = (s32[16,16]{1,0:T(8,128)S(1)}, s32[16,16]{1,0:T(8,128)}, u32[]{:S(2)}) copy-start(s32[16,16]{1,0:T(8,128)} %param.10) | copy-start | bytes 3076
  52.8 6.5 %copy-start.2 = (s32[16,16]{1,0:T(8,128)S(1)}, s32[16,16]{1,0:T(8,128)}, u32[]{:S(2)}) copy-start(s32[16,16]{1,0:T(8,128)} %param.11) | copy-start | bytes 3076
  53.7 13.1 %all-to-all-start.1 = ((f32[4,256,128]{2,1,0:T(8,128)}), f32[4,256,128]{2,1,0:T(8,128)S(1)}, u32[]{:S(2)}, u32[]{:S(2)}) async-start(f32[4,256,128]{2,1,0:T(8,128)} %bitcast.13), calls=%async_computation.1 | async-start | bytes 1048576 | tf_op jit(solution)/shard_map/all_to_all | solution.py:85
  58.6 43.1 %all-gather.6.cloned.1.call-start = ((), (), s32[]{:S(2)}) async-start(), calls=%async_computation.7 | async-start | bytes 1179648 | tf_op jit(solution)/shard_map/all_gather | solution.py:114
  68.9 38.2 %all-to-all-start.2 = ((f32[8,256,128]{1,2,0:T(8,128)}), f32[8,256,128]{1,2,0:T(8,128)S(1)}, u32[]{:S(2)}, u32[]{:S(2)}) async-start(f32[8,256,128]{1,2,0:T(8,128)} %broadcast_in_dim.19), calls=%async_computation.2 | async-start | bytes 2097152 | tf_op jit(solution)/shard_map/all_to_all | solution.py:16
  83.0 18.7 %collective-permute-start.4 = (f32[256,512]{1,0:T(8,128)S(1)}, f32[256,512]{1,0:T(8,128)S(1)}, u32[]{:S(2)}, u32[]{:S(2)}) collective-permute-start(f32[256,512]{1,0:T(8,128)S(1)} %pad_maximum_fusion.3), channel_id=1, source_target_pairs={{0,33},{33,0},{1,32},{32,1},{2,35},{35,2},{3,34},{34,3},{4,37},{37... | collective-permute-start | bytes 1572872 | tf_op jit(solution)/shard_map/ppermute | solution.py:73
  107.1 4.5 %collective-permute-start.5 = (f32[8,256,128]{1,2,0:T(8,128)S(1)}, f32[8,256,128]{1,2,0:T(8,128)S(1)}, u32[]{:S(2)}, u32[]{:S(2)}) collective-permute-start(f32[8,256,128]{1,2,0:T(8,128)S(1)} %all-to-all-done.2), channel_id=1, source_target_pairs={{0,16},{16,0},{1,17},{17,1},{2,18},{18,2},{3,19},{19,3},{4,20},{20... | collective-permute-start | bytes 3145736 | tf_op jit(solution)/shard_map/ppermute | solution.py:20
  127.8 32.0 %all-to-all-start.4 = ((f32[8,128,256]{2,1,0:T(8,128)}), f32[8,128,256]{2,1,0:T(8,128)S(1)}, u32[]{:S(2)}, u32[]{:S(2)}) async-start(f32[8,128,256]{2,1,0:T(8,128)} %broadcast_in_dim.36), calls=%async_computation.4 | async-start | bytes 2097152 | tf_op jit(solution)/shard_map/all_to_all | solution.py:136
  131.4 53.9 %all-gather.8.cloned.1.call-start = ((), (), s32[]{:S(2)}) async-start(), calls=%async_computation.8 | async-start | bytes 2359296 | tf_op jit(solution)/shard_map/all_gather | solution.py:139
  131.5 6.9 %collective-permute-start.8 = (f32[128,256]{1,0:T(8,128)S(1)}, f32[128,256]{1,0:T(8,128)S(1)}, u32[]{:S(2)}, u32[]{:S(2)}) collective-permute-start(f32[128,256]{1,0:T(8,128)S(1)} %broadcast_multiply_fusion.1), channel_id=1, source_target_pairs={{0,1},{1,0},{2,3},{3,2},{4,5},{5,4},{6,7},{7,6},{8,9},{9,8},{10,11... | collective-permute-start | bytes 393224 | tf_op jit(solution)/shard_map/ppermute | solution.py:20
  139.1 21.5 %collective-permute-start.7 = (f32[256,512]{1,0:T(8,128)S(1)}, f32[256,512]{1,0:T(8,128)S(1)}, u32[]{:S(2)}, u32[]{:S(2)}) collective-permute-start(f32[256,512]{1,0:T(8,128)S(1)} %collective-permute-done.4), channel_id=1, source_target_pairs={{0,16},{16,0},{1,17},{17,1},{2,18},{18,2},{3,19},{19,3},{4,20},{20... | collective-permute-start | bytes 1572872 | tf_op jit(solution)/shard_map/ppermute | solution.py:20
  144.7 16.3 %collective-permute-start.6 = (f32[256,512]{1,0:T(8,128)S(1)}, f32[256,512]{1,0:T(8,128)}, u32[]{:S(2)}, u32[]{:S(2)}) collective-permute-start(f32[256,512]{1,0:T(8,128)S(1)} %pad_maximum_fusion.5), channel_id=1, source_target_pairs={{0,16},{16,0},{1,17},{17,1},{2,18},{18,2},{3,19},{19,3},{4,20},{20... | collective-permute-start | bytes 1572872 | tf_op jit(solution)/shard_map/ppermute | solution.py:20
  175.3 22.3 %all-to-all-start.6 = ((f32[8,72,256]{2,1,0:T(8,128)}), f32[8,72,256]{2,1,0:T(8,128)S(1)}, u32[]{:S(2)}, u32[]{:S(2)}) async-start(f32[8,72,256]{2,1,0:T(8,128)} %broadcast_in_dim.37), calls=%async_computation.6 | async-start | bytes 1179648 | tf_op jit(solution)/shard_map/all_to_all | solution.py:149
  179.2 6.1 %collective-permute-start.9 = (f32[56,256]{1,0:T(8,128)S(1)}, f32[56,256]{1,0:T(8,128)S(1)}, u32[]{:S(2)}, u32[]{:S(2)}) collective-permute-start(f32[56,256]{1,0:T(8,128)S(1)} %slice.16), channel_id=1, source_target_pairs={{0,1},{1,0},{2,3},{3,2},{4,5},{5,4},{6,7},{7,6},{8,9},{9,8},{10,11... | collective-permute-start | bytes 172040 | tf_op jit(solution)/shard_map/ppermute | solution.py:20
  185.4 1.6 copy-start
  197.6 29.5 %collective-permute-start.10 = (f32[8,72,256]{2,1,0:T(8,128)S(1)}, f32[8,72,256]{2,1,0:T(8,128)S(1)}, u32[]{:S(2)}, u32[]{:S(2)}) collective-permute-start(f32[8,72,256]{2,1,0:T(8,128)S(1)} %all-to-all-done.6.refs_0_), channel_id=1, source_target_pairs={{0,1},{1,0},{2,3},{3,2},{4,5},{5,4},{6,7},{7,6},{8,9},{9,8},{10,11... | collective-permute-start | bytes 1769480 | tf_op jit(solution)/shard_map/ppermute | solution.py:20
Sparse Core Ops, SparseCore 0:
  61.5 40.2 all-gather.5
  139.2 41.7 all-gather.7

commit v10 on v9

--- a/solution.py
+++ b/solution.py
@@ -142,15 +142,13 @@
     ]
     h_partial = jnp.stack([jnp.where(xh == 0, h_own, h_other), jnp.where(xh == 0, h_other, h_own)])
     h_share = finish(h_partial)
-    passed = half * 9 // 16
+    passed = half // 2
     rest = half - passed
     early = jnp.broadcast_to(h_share[:passed][None], (nz, passed, blk))
-    early, h_share = lax.optimization_barrier((early, h_share))
     h_early = lax.all_to_all(early, "z", split_axis=0, concat_axis=0, tiled=True)
     late = jnp.concatenate([h_share[passed:], swap(h_share[passed:], "xl")], axis=0)
     z_next = place([z_all], [(0, 0, 0, 0, half), (0, half, 1, 0, half)], blk)
     h_early, z_next = lax.optimization_barrier((h_early, z_next))
-    late, h_early = lax.optimization_barrier((late, h_early))
     h_late = lax.all_gather(late, "z", axis=0)
     h_times_z = place(
         [h_early, h_late, swap(h_early, "xl")],

time: 237 us -> 235 us (level)
  the two profiles are of different devices: /device:TPU:2 before, /device:TPU:56 now
where the time goes in v10:
time: 235 us; the launch traced here: 231 us
  waiting for transfers between devices  90.7 us (39%)
  starting transfers between devices  59.6 us (25%)
  other arithmetic  24.8 us (11%)
  blocking collectives  24.3 us (10%)
  between operations  14.2 us (6%)
  local copies, waits for them, and re-layouts  8.42 us (4%)
  matrix products  6.2 us (3%)
  Pallas kernels  2.96 us (1%)
    all_to_all x2, blocking collectives, sum_x(): lax.all_to_all(parts, X, split_axis=0, concat_axis=0, tiled=True)  24.3 us
    all_gather x1, waiting for transfers between devices, local(): h_late = lax.all_gather(late, 'z', axis=0)  21.6 us
    ppermute x9, starting transfers between devices, swap(): return lax.ppermute(array, axis, [(0, 1), (1, 0)])  19.5 us
    all_gather x1, waiting for transfers between devices, local(): z_panel = lax.all_gather(z_piece, 'y', axis=0)  18.2 us
    all_to_all x1, waiting for transfers between devices, local(): lax.all_to_all(z_copies, 'y', split_axis=0, concat_axis=0, tiled=True)  14.9 us
    mul x4, other arithmetic, slices(): lax.dynamic_slice(values, (0, (2 * m + a) * blk + b * half), (blk, half))  14.7 us
    all_to_all x1, starting transfers between devices, spread(): return lax.all_to_all(copies, axis, split_axis=0, concat_axis=0, tiled=True)  10.2 us
    all_to_all x1, waiting for transfers between devices, local(): lax.all_to_all(early, 'z', split_axis=0, concat_axis=0, tiled=True)  10.1 us
  transfers between devices with their start and end apart: 19, of which 11 were waited for; matrix products, arithmetic and copies ran while one was open for 12% of the time, Pallas kernels for 1%

profile of v10, /device:TPU:56, one launch (start us, length us, event | category | flops | bytes accessed | tf_op | source)
XLA Modules:
  0.0 231.3 jit_solution(13067997045025620252)
XLA Ops:
  7.2 0.7 convert_element_type.10
  7.9 0.7 fusion.25
  8.6 2.3 dynamic-slice_multiply_fusion.16
  10.9 1.1 broadcast_in_dim.18
  11.9 8.6 %all-to-all-start = ((f32[8,128,256]{2,1,0:T(8,128)}), f32[8,128,256]{2,1,0:T(8,128)S(1)}, u32[]{:S(2)}, u32[]{:S(2)}) async-start(f32[8,128,256]{2,1,0:T(8,128)} %broadcast_in_dim.18), calls=%async_computation | async-start | bytes 2097152 | tf_op jit(solution)/shard_map/all_to_all | solution.py:93
  20.6 3.6 %dynamic-slice_multiply_fusion.15 = (f32[256,128]{1,0:T(8,128)S(1)}, f32[256,128]{1,0:T(8,128)S(1)}, f32[256,128]{1,0:T(8,128)S(1)}, f32[256,128]{1,0:T(8,128)S(1)}) fusion(f32[256,2048]{1,0:T(8,128)} %param.7, s32[]{:T(128)S(6)} %select_n.191, f32[]{:T(128)} %bitcast.2, f32[]{:T(128)} %bitcast.5, s32[]{:T(128)S(6)} %select_n.197, f32[]{:T(128)} %bitcast.4, ...), kind=kLoop, calls=%fused_computation.52 | loop fusion | flops 131072 | bytes 1048608 | tf_op jit(solution)/shard_map/mul | solution.py:65
  24.2 2.9 %collective-permute-start.1 = (f32[256,512]{1,0:T(8,128)S(1)}, f32[256,512]{1,0:T(8,128)S(1)}, u32[]{:S(2)}, u32[]{:S(2)}) collective-permute-start(f32[256,512]{1,0:T(8,128)S(1)} %pad_maximum_fusion.1), channel_id=1, source_target_pairs={{0,33},{33,0},{1,32},{32,1},{2,35},{35,2},{3,34},{34,3},{4,37},{37... | collective-permute-start | bytes 1572872 | tf_op jit(solution)/shard_map/ppermute | solution.py:73
  27.1 3.7 %dynamic-slice_multiply_fusion.11 = (f32[256,128]{1,0:T(8,128)S(1)}, f32[256,128]{1,0:T(8,128)S(1)}, f32[256,128]{1,0:T(8,128)S(1)}, f32[256,128]{1,0:T(8,128)S(1)}) fusion(f32[256,2048]{1,0:T(8,128)} %param.7, s32[]{:T(128)S(6)} %select_n.199, f32[]{:T(128)} %bitcast.6, f32[]{:T(128)} %bitcast.9, s32[]{:T(128)S(6)} %select_n.205, f32[]{:T(128)} %bitcast.8, ...), kind=kLoop, calls=%fused_computation.48 | loop fusion | flops 131072 | bytes 1048608 | tf_op jit(solution)/shard_map/mul | solution.py:65
  30.8 0.8 pad_maximum_fusion.2
  31.6 1.9 collective-permute-start
  33.5 5.1 %collective-permute-done.1 = f32[256,512]{1,0:T(8,128)S(1)} collective-permute-done((f32[256,512]{1,0:T(8,128)S(1)}, f32[256,512]{1,0:T(8,128)S(1)}, u32[]{:S(2)}, u32[]{:S(2)}) %collective-permute-start.1) | collective-permute-done | bytes 524320 | tf_op jit(solution)/shard_map/ppermute | solution.py:73
  38.6 1.9 collective-permute-start.2
  40.6 2.9 %all-to-all-done = f32[8,128,256]{2,1,0:T(8,128)S(1)} async-done(((f32[8,128,256]{2,1,0:T(8,128)}), f32[8,128,256]{2,1,0:T(8,128)S(1)}, u32[]{:S(2)}, u32[]{:S(2)}) %all-to-all-start) | async-done | bytes 1048608 | tf_op jit(solution)/shard_map/all_to_all | solution.py:93
  43.5 0.4 fusion.11
  43.9 0.4 fusion.9
  44.3 0.4 convolution_add_fusion.3
  44.7 0.4 broadcast_select_fusion
  45.1 1.9 collective-permute-start.3
  47.1 1.5 collective-permute-done.3
  48.6 0.8 fusion
  49.5 3.6 %all-to-all-start.1 = ((f32[4,256,128]{2,1,0:T(8,128)}), f32[4,256,128]{2,1,0:T(8,128)S(1)}, u32[]{:S(2)}, u32[]{:S(2)}) async-start(f32[4,256,128]{2,1,0:T(8,128)} %bitcast.13), calls=%async_computation.1 | async-start | bytes 1048576 | tf_op jit(solution)/shard_map/all_to_all | solution.py:85
  53.0 0.7 all-gather.7.cloned.1.call-update
  53.8 0.7 fusion.23
  54.5 8.4 %all-to-all-done.1 = f32[4,256,128]{2,1,0:T(8,128)S(1)} async-done(((f32[4,256,128]{2,1,0:T(8,128)}), f32[4,256,128]{2,1,0:T(8,128)S(1)}, u32[]{:S(2)}, u32[]{:S(2)}) %all-to-all-start.1) | async-done | bytes 524320 | tf_op jit(solution)/shard_map/all_to_all | solution.py:85
  63.0 0.7 multiply_subtract_fusion
  63.8 1.1 broadcast_in_dim.19
  64.8 10.2 %all-to-all-start.2 = ((f32[8,256,128]{1,2,0:T(8,128)}), f32[8,256,128]{1,2,0:T(8,128)S(1)}, u32[]{:S(2)}, u32[]{:S(2)}) async-start(f32[8,256,128]{1,2,0:T(8,128)} %broadcast_in_dim.19), calls=%async_computation.2 | async-start | bytes 2097152 | tf_op jit(solution)/shard_map/all_to_all | solution.py:16
  75.0 3.7 %dynamic-slice_multiply_fusion.7 = (f32[256,128]{1,0:T(8,128)S(1)}, f32[256,128]{1,0:T(8,128)S(1)}, f32[256,128]{1,0:T(8,128)S(1)}, f32[256,128]{1,0:T(8,128)S(1)}) fusion(f32[256,2048]{1,0:T(8,128)} %param.8, s32[]{:T(128)S(6)} %select_n.191, f32[]{:T(128)} %bitcast.15, f32[]{:T(128)} %bitcast.18, s32[]{:T(128)S(6)} %select_n.197, f32[]{:T(128)} %bitcast.17, ...), kind=kLoop, calls=%fused_computation.43 | loop fusion | flops 131072 | bytes 1048608 | tf_op jit(solution)/shard_map/mul | solution.py:65
  78.7 3.1 %collective-permute-start.4 = (f32[256,512]{1,0:T(8,128)S(1)}, f32[256,512]{1,0:T(8,128)S(1)}, u32[]{:S(2)}, u32[]{:S(2)}) collective-permute-start(f32[256,512]{1,0:T(8,128)S(1)} %pad_maximum_fusion.3), channel_id=1, source_target_pairs={{0,33},{33,0},{1,32},{32,1},{2,35},{35,2},{3,34},{34,3},{4,37},{37... | collective-permute-start | bytes 1572872 | tf_op jit(solution)/shard_map/ppermute | solution.py:73
  81.8 18.2 %all-gather.7.cloned.1.call-done = f32[1024,256]{1,0:T(8,128)} async-done(((f32[128,256]{1,0:T(8,128)}), f32[1024,256]{1,0:T(8,128)}) %all-gather.7.cloned.1.call-update) | async-done | bytes 1048592 | tf_op jit(solution)/shard_map/all_gather | solution.py:114
  100.0 2.9 %all-to-all-done.2 = f32[8,256,128]{1,2,0:T(8,128)S(1)} async-done(((f32[8,256,128]{1,2,0:T(8,128)}), f32[8,256,128]{1,2,0:T(8,128)S(1)}, u32[]{:S(2)}, u32[]{:S(2)}) %all-to-all-start.2) | async-done | bytes 1048608 | tf_op jit(solution)/shard_map/all_to_all | solution.py:16
  102.9 1.9 collective-permute-start.5
  104.8 1.7 reverse_select_fusion
  106.6 0.8 collective-permute-done.5
  107.4 1.0 fusion.28
  108.4 1.0 select_bitcast_fusion.3
  109.5 12.5 %all_to_all.35 = f32[4,128,256]{2,1,0:T(8,128)S(1)} all-to-all(f32[4,128,256]{2,1,0:T(8,128)S(1)} %bitcast.72), channel_id=1, replica_groups=mesh['y'=8,'xh'=2,'core'=2,'z'=8,'xl'=2] {'xh','xl'}, dimensions={0} | all-to-all | bytes 1048576 | tf_op jit(solution)/shard_map/all_to_all | solution.py:85
  122.0 0.7 broadcast_multiply_fusion.1
  122.6 2.5 %collective-permute-start.8 = (f32[128,256]{1,0:T(8,128)S(1)}, f32[128,256]{1,0:T(8,128)S(1)}, u32[]{:S(2)}, u32[]{:S(2)}) collective-permute-start(f32[128,256]{1,0:T(8,128)S(1)} %broadcast_multiply_fusion.1), channel_id=1, source_target_pairs={{0,1},{1,0},{2,3},{3,2},{4,5},{5,4},{6,7},{7,6},{8,9},{9,8},{10,11... | collective-permute-start | bytes 393224 | tf_op jit(solution)/shard_map/ppermute | solution.py:20
  125.1 1.1 broadcast_in_dim.36
  126.2 8.3 %all-to-all-start.4 = ((f32[8,128,256]{2,1,0:T(8,128)}), f32[8,128,256]{2,1,0:T(8,128)S(1)}, u32[]{:S(2)}, u32[]{:S(2)}) async-start(f32[8,128,256]{2,1,0:T(8,128)} %broadcast_in_dim.36), calls=%async_computation.4 | async-start | bytes 2097152 | tf_op jit(solution)/shard_map/all_to_all | solution.py:136
  134.5 0.7 pad_maximum_fusion.7
  135.3 1.9 collective-permute-start.7
  137.2 3.7 %dynamic-slice_multiply_fusion.3 = (f32[256,128]{1,0:T(8,128)S(1)}, f32[256,128]{1,0:T(8,128)S(1)}, f32[256,128]{1,0:T(8,128)S(1)}, f32[256,128]{1,0:T(8,128)S(1)}) fusion(f32[256,2048]{1,0:T(8,128)} %param.8, s32[]{:T(128)S(6)} %select_n.199, f32[]{:T(128)} %bitcast.31, f32[]{:T(128)} %bitcast.34, s32[]{:T(128)S(6)} %select_n.205, f32[]{:T(128)} %bitcast.33, ...), kind=kLoop, calls=%fused_computation.39 | loop fusion | flops 131072 | bytes 1048608 | tf_op jit(solution)/shard_map/mul | solution.py:65
  140.9 2.4 %collective-permute-start.6 = (f32[256,512]{1,0:T(8,128)S(1)}, f32[256,512]{1,0:T(8,128)}, u32[]{:S(2)}, u32[]{:S(2)}) collective-permute-start(f32[256,512]{1,0:T(8,128)S(1)} %pad_maximum_fusion.5), channel_id=1, source_target_pairs={{0,16},{16,0},{1,17},{17,1},{2,18},{18,2},{3,19},{19,3},{4,20},{20... | collective-permute-start | bytes 1572872 | tf_op jit(solution)/shard_map/ppermute | solution.py:20
  143.4 14.9 %all-to-all-done.4 = f32[8,128,256]{2,1,0:T(8,128)S(1)} async-done(((f32[8,128,256]{2,1,0:T(8,128)}), f32[8,128,256]{2,1,0:T(8,128)S(1)}, u32[]{:S(2)}, u32[]{:S(2)}) %all-to-all-start.4) | async-done | bytes 1048608 | tf_op jit(solution)/shard_map/all_to_all | solution.py:136
  158.2 0.4 fusion.5
  158.6 0.4 fusion.3
  159.1 0.4 convolution_add_fusion
  159.5 1.4 select_bitcast_fusion.1
  161.0 11.8 %all_to_all.36 = f32[4,128,256]{2,1,0:T(8,128)S(1)} all-to-all(f32[4,128,256]{2,1,0:T(8,128)S(1)} %bitcast.73), channel_id=1, replica_groups=mesh['y'=8,'xh'=2,'core'=2,'z'=8,'xl'=2] {'xh','xl'}, dimensions={0} | all-to-all | bytes 1048576 | tf_op jit(solution)/shard_map/all_to_all | solution.py:85
  172.8 0.7 broadcast_multiply_fusion
  173.6 2.5 %collective-permute-start.9 = (f32[64,256]{1,0:T(8,128)S(1)}, f32[64,256]{1,0:T(8,128)S(1)}, u32[]{:S(2)}, u32[]{:S(2)}) collective-permute-start(f32[64,256]{1,0:T(8,128)S(1)} %get-tuple-element.54), channel_id=1, source_target_pairs={{0,1},{1,0},{2,3},{3,2},{4,5},{5,4},{6,7},{7,6},{8,9},{9,8},{10,11... | collective-permute-start | bytes 196616 | tf_op jit(solution)/shard_map/ppermute | solution.py:20
  176.1 3.6 %collective-permute-done.9 = f32[64,256]{1,0:T(8,128)S(1)} collective-permute-done((f32[64,256]{1,0:T(8,128)S(1)}, f32[64,256]{1,0:T(8,128)S(1)}, u32[]{:S(2)}, u32[]{:S(2)}) %collective-permute-start.9) | collective-permute-done | bytes 65568 | tf_op jit(solution)/shard_map/ppermute | solution.py:20
  179.7 0.7 pad_maximum_fusion.8
  180.4 0.8 broadcast_in_dim.37
  181.2 3.5 %all-to-all-start.6 = ((f32[8,64,256]{2,1,0:T(8,128)}), f32[8,64,256]{2,1,0:T(8,128)S(1)}, u32[]{:S(2)}, u32[]{:S(2)}) async-start(f32[8,64,256]{2,1,0:T(8,128)} %broadcast_in_dim.37), calls=%async_computation.6 | async-start | bytes 1048576 | tf_op jit(solution)/shard_map/all_to_all | solution.py:148
  184.8 1.6 copy-done
  186.4 1.5 shard_map.77
  187.8 10.1 %all-to-all-done.6.refs_0_ = f32[8,64,256]{2,1,0:T(8,128)S(1)} async-done(((f32[8,64,256]{2,1,0:T(8,128)}), f32[8,64,256]{2,1,0:T(8,128)S(1)}, u32[]{:S(2)}, u32[]{:S(2)}) %all-to-all-start.6) | async-done | bytes 524320 | tf_op jit(solution)/shard_map/all_to_all | solution.py:148
  197.9 2.5 %collective-permute-start.10 = (f32[8,64,256]{2,1,0:T(8,128)S(1)}, f32[8,64,256]{2,1,0:T(8,128)S(1)}, u32[]{:S(2)}, u32[]{:S(2)}) collective-permute-start(f32[8,64,256]{2,1,0:T(8,128)S(1)} %all-to-all-done.6.refs_0_), channel_id=1, source_target_pairs={{0,1},{1,0},{2,3},{3,2},{4,5},{5,4},{6,7},{7,6},{8,9},{9,8},{10,11... | collective-permute-start | bytes 1572872 | tf_op jit(solution)/shard_map/ppermute | solution.py:20
  200.5 21.6 %all-gather.11.cloned.1.call-done = f32[1024,256]{1,0:T(8,128)} async-done(((f32[128,256]{1,0:T(8,128)}), f32[1024,256]{1,0:T(8,128)}) %all-gather.11.cloned.1.call-update) | async-done | bytes 1048592 | tf_op jit(solution)/shard_map/all_gather | solution.py:152
  222.0 1.2 copy-done.1
  223.3 1.5 shard_map.78
  (36 shorter events, 0.7 us)
Async XLA Ops:
  11.9 31.6 %all-to-all-start = ((f32[8,128,256]{2,1,0:T(8,128)}), f32[8,128,256]{2,1,0:T(8,128)S(1)}, u32[]{:S(2)}, u32[]{:S(2)}) async-start(f32[8,128,256]{2,1,0:T(8,128)} %broadcast_in_dim.18), calls=%async_computation | async-start | bytes 2097152 | tf_op jit(solution)/shard_map/all_to_all | solution.py:93
  24.2 14.4 %collective-permute-start.1 = (f32[256,512]{1,0:T(8,128)S(1)}, f32[256,512]{1,0:T(8,128)S(1)}, u32[]{:S(2)}, u32[]{:S(2)}) collective-permute-start(f32[256,512]{1,0:T(8,128)S(1)} %pad_maximum_fusion.1), channel_id=1, source_target_pairs={{0,33},{33,0},{1,32},{32,1},{2,35},{35,2},{3,34},{34,3},{4,37},{37... | collective-permute-start | bytes 1572872 | tf_op jit(solution)/shard_map/ppermute | solution.py:73
  31.6 12.7 %collective-permute-start = (f32[256,512]{1,0:T(8,128)}, f32[256,512]{1,0:T(8,128)S(1)}, u32[]{:S(2)}, u32[]{:S(2)}) collective-permute-start(f32[256,512]{1,0:T(8,128)} %pad_maximum_fusion.2), channel_id=1, source_target_pairs={{0,16},{16,0},{1,17},{17,1},{2,18},{18,2},{3,19},{19,3},{4,20},{20... | collective-permute-start | bytes 1572872 | tf_op jit(solution)/shard_map/ppermute | solution.py:20
  38.6 6.1 %collective-permute-start.2 = (f32[256,512]{1,0:T(8,128)S(1)}, f32[256,512]{1,0:T(8,128)S(1)}, u32[]{:S(2)}, u32[]{:S(2)}) collective-permute-start(f32[256,512]{1,0:T(8,128)S(1)} %collective-permute-done.1), channel_id=1, source_target_pairs={{0,16},{16,0},{1,17},{17,1},{2,18},{18,2},{3,19},{19,3},{4,20},{20... | collective-permute-start | bytes 1572872 | tf_op jit(solution)/shard_map/ppermute | solution.py:20
  45.1 3.4 %collective-permute-start.3 = (f32[256,256]{1,0:T(8,128)S(1)}, f32[256,256]{1,0:T(8,128)S(1)}, u32[]{:S(2)}, u32[]{:S(2)}) collective-permute-start(f32[256,256]{1,0:T(8,128)S(1)} %get-tuple-element.75), channel_id=1, source_target_pairs={{0,16},{16,0},{1,17},{17,1},{2,18},{18,2},{3,19},{19,3},{4,20},{20... | collective-permute-start | bytes 786440 | tf_op jit(solution)/shard_map/ppermute | solution.py:20
  48.5 5.2 %copy-start.2 = (s32[16,16]{1,0:T(8,128)S(1)}, s32[16,16]{1,0:T(8,128)}, u32[]{:S(2)}) copy-start(s32[16,16]{1,0:T(8,128)} %param.10) | copy-start | bytes 3076
  48.5 5.2 %copy-start.3 = (s32[16,16]{1,0:T(8,128)S(1)}, s32[16,16]{1,0:T(8,128)}, u32[]{:S(2)}) copy-start(s32[16,16]{1,0:T(8,128)} %param.11) | copy-start | bytes 3076
  49.5 13.5 %all-to-all-start.1 = ((f32[4,256,128]{2,1,0:T(8,128)}), f32[4,256,128]{2,1,0:T(8,128)S(1)}, u32[]{:S(2)}, u32[]{:S(2)}) async-start(f32[4,256,128]{2,1,0:T(8,128)} %bitcast.13), calls=%async_computation.1 | async-start | bytes 1048576 | tf_op jit(solution)/shard_map/all_to_all | solution.py:85
  53.0 47.0 %all-gather.7.cloned.1.call-start = ((), (), s32[]{:S(2)}) async-start(), calls=%async_computation.7 | async-start | bytes 1179648 | tf_op jit(solution)/shard_map/all_gather | solution.py:114
  64.8 38.0 %all-to-all-start.2 = ((f32[8,256,128]{1,2,0:T(8,128)}), f32[8,256,128]{1,2,0:T(8,128)S(1)}, u32[]{:S(2)}, u32[]{:S(2)}) async-start(f32[8,256,128]{1,2,0:T(8,128)} %broadcast_in_dim.19), calls=%async_computation.2 | async-start | bytes 2097152 | tf_op jit(solution)/shard_map/all_to_all | solution.py:16
  78.7 21.3 %collective-permute-start.4 = (f32[256,512]{1,0:T(8,128)S(1)}, f32[256,512]{1,0:T(8,128)S(1)}, u32[]{:S(2)}, u32[]{:S(2)}) collective-permute-start(f32[256,512]{1,0:T(8,128)S(1)} %pad_maximum_fusion.3), channel_id=1, source_target_pairs={{0,33},{33,0},{1,32},{32,1},{2,35},{35,2},{3,34},{34,3},{4,37},{37... | collective-permute-start | bytes 1572872 | tf_op jit(solution)/shard_map/ppermute | solution.py:73
  102.9 4.5 %collective-permute-start.5 = (f32[8,256,128]{1,2,0:T(8,128)S(1)}, f32[8,256,128]{1,2,0:T(8,128)S(1)}, u32[]{:S(2)}, u32[]{:S(2)}) collective-permute-start(f32[8,256,128]{1,2,0:T(8,128)S(1)} %all-to-all-done.2), channel_id=1, source_target_pairs={{0,16},{16,0},{1,17},{17,1},{2,18},{18,2},{3,19},{19,3},{4,20},{20... | collective-permute-start | bytes 3145736 | tf_op jit(solution)/shard_map/ppermute | solution.py:20
  122.6 11.8 %collective-permute-start.8 = (f32[128,256]{1,0:T(8,128)S(1)}, f32[128,256]{1,0:T(8,128)S(1)}, u32[]{:S(2)}, u32[]{:S(2)}) collective-permute-start(f32[128,256]{1,0:T(8,128)S(1)} %broadcast_multiply_fusion.1), channel_id=1, source_target_pairs={{0,1},{1,0},{2,3},{3,2},{4,5},{5,4},{6,7},{7,6},{8,9},{9,8},{10,11... | collective-permute-start | bytes 393224 | tf_op jit(solution)/shard_map/ppermute | solution.py:20
  126.2 32.1 %all-to-all-start.4 = ((f32[8,128,256]{2,1,0:T(8,128)}), f32[8,128,256]{2,1,0:T(8,128)S(1)}, u32[]{:S(2)}, u32[]{:S(2)}) async-start(f32[8,128,256]{2,1,0:T(8,128)} %broadcast_in_dim.36), calls=%async_computation.4 | async-start | bytes 2097152 | tf_op jit(solution)/shard_map/all_to_all | solution.py:136
  134.4 50.3 %all-gather.9.cloned.1.call-start = ((), (), s32[]{:S(2)}) async-start(), calls=%async_computation.8 | async-start | bytes 2359296 | tf_op jit(solution)/shard_map/all_gather | solution.py:139
  135.2 86.8 %all-gather.11.cloned.1.call-start = ((), (), s32[]{:S(2)}) async-start(), calls=%async_computation.9 | async-start | bytes 1179648 | tf_op jit(solution)/shard_map/all_gather | solution.py:152
  135.3 23.8 %collective-permute-start.7 = (f32[256,512]{1,0:T(8,128)S(1)}, f32[256,512]{1,0:T(8,128)S(1)}, u32[]{:S(2)}, u32[]{:S(2)}) collective-permute-start(f32[256,512]{1,0:T(8,128)S(1)} %collective-permute-done.4), channel_id=1, source_target_pairs={{0,16},{16,0},{1,17},{17,1},{2,18},{18,2},{3,19},{19,3},{4,20},{20... | collective-permute-start | bytes 1572872 | tf_op jit(solution)/shard_map/ppermute | solution.py:20
  140.9 18.5 %collective-permute-start.6 = (f32[256,512]{1,0:T(8,128)S(1)}, f32[256,512]{1,0:T(8,128)}, u32[]{:S(2)}, u32[]{:S(2)}) collective-permute-start(f32[256,512]{1,0:T(8,128)S(1)} %pad_maximum_fusion.5), channel_id=1, source_target_pairs={{0,16},{16,0},{1,17},{17,1},{2,18},{18,2},{3,19},{19,3},{4,20},{20... | collective-permute-start | bytes 1572872 | tf_op jit(solution)/shard_map/ppermute | solution.py:20
  173.6 6.2 %collective-permute-start.9 = (f32[64,256]{1,0:T(8,128)S(1)}, f32[64,256]{1,0:T(8,128)S(1)}, u32[]{:S(2)}, u32[]{:S(2)}) collective-permute-start(f32[64,256]{1,0:T(8,128)S(1)} %get-tuple-element.54), channel_id=1, source_target_pairs={{0,1},{1,0},{2,3},{3,2},{4,5},{5,4},{6,7},{7,6},{8,9},{9,8},{10,11... | collective-permute-start | bytes 196616 | tf_op jit(solution)/shard_map/ppermute | solution.py:20
  181.2 16.7 %all-to-all-start.6 = ((f32[8,64,256]{2,1,0:T(8,128)}), f32[8,64,256]{2,1,0:T(8,128)S(1)}, u32[]{:S(2)}, u32[]{:S(2)}) async-start(f32[8,64,256]{2,1,0:T(8,128)} %broadcast_in_dim.37), calls=%async_computation.6 | async-start | bytes 1048576 | tf_op jit(solution)/shard_map/all_to_all | solution.py:148
  184.8 1.6 copy-start
  197.9 24.1 %collective-permute-start.10 = (f32[8,64,256]{2,1,0:T(8,128)S(1)}, f32[8,64,256]{2,1,0:T(8,128)S(1)}, u32[]{:S(2)}, u32[]{:S(2)}) collective-permute-start(f32[8,64,256]{2,1,0:T(8,128)S(1)} %all-to-all-done.6.refs_0_), channel_id=1, source_target_pairs={{0,1},{1,0},{2,3},{3,2},{4,5},{5,4},{6,7},{7,6},{8,9},{9,8},{10,11... | collective-permute-start | bytes 1572872 | tf_op jit(solution)/shard_map/ppermute | solution.py:20
  222.0 1.2 copy-start.1
Sparse Core Ops, SparseCore 0:
  55.9 44.0 all-gather.6
  137.9 41.5 all-gather.8
  181.6 40.3 all-gather.10

commit v11 on v10

--- a/solution.py
+++ b/solution.py
@@ -135,21 +135,22 @@
     h_rows = slices(h_blocks, h_fill, xh, xl)
     z_next_panel = lax.all_to_all(z_copies, "y", split_axis=0, concat_axis=0, tiled=True)
     z_next_panel = z_next_panel.reshape(ny * half, blk)
-    z_shares = jnp.concatenate([z_share, swap(z_share, "xl")], axis=0)
-    z_all = lax.all_gather(z_shares, "z", axis=0)
+    z_own = lax.all_gather(z_share, "z", axis=0)
     h_own, h_other = [
         multiply(rows, swap(rows, "core"), z_next_panel) for rows in (h_rows, h_others)
     ]
     h_partial = jnp.stack([jnp.where(xh == 0, h_own, h_other), jnp.where(xh == 0, h_other, h_own)])
     h_share = finish(h_partial)
-    passed = half // 2
+    h_share, z_own = lax.optimization_barrier((h_share, z_own))
+    passed = half * 3 // 8
     rest = half - passed
     early = jnp.broadcast_to(h_share[:passed][None], (nz, passed, blk))
+    late = jnp.concatenate([h_share[passed:], swap(h_share[passed:], "xl")], axis=0)
+    h_late = lax.all_gather(late, "z", axis=0)
     h_early = lax.all_to_all(early, "z", split_axis=0, concat_axis=0, tiled=True)
-    late = jnp.concatenate([h_share[passed:], swap(h_share[passed:], "xl")], axis=0)
-    z_next = place([z_all], [(0, 0, 0, 0, half), (0, half, 1, 0, half)], blk)
-    h_early, z_next = lax.optimization_barrier((h_early, z_next))
-    h_late = lax.all_gather(late, "z", axis=0)
+    z_other = swap(z_own, "xl")
+    h_early, z_other = lax.optimization_barrier((h_early, z_other))
+    z_next = place([z_own, z_other], [(0, 0, 0, 0, half), (1, 0, 1, 0, half)], blk)
     h_times_z = place(
         [h_early, h_late, swap(h_early, "xl")],
         [

time: 235 us -> 234 us (level)
  blocking collectives: 24.3 us -> 38.6 us
  waiting for transfers between devices: 90.7 us -> 80.9 us
    all_to_all x0 -> x1, blocking collectives: none -> 15.6 us  [local(): lax.all_to_all(early, 'z', split_axis=0, concat_axis=0, tiled=True)]
    all_gather x1, waiting for transfers between devices: 21.6 us -> 8.2 us  [local(): h_late = lax.all_gather(late, 'z', axis=0)]
    all_to_all x1 -> x0, waiting for transfers between devices: 10.1 us -> none  [local(): lax.all_to_all(early, 'z', split_axis=0, concat_axis=0, tiled=True)]
    ppermute x9, waiting for transfers between devices: 5.91 us -> 14.9 us  [swap(): return lax.ppermute(array, axis, [(0, 1), (1, 0)])]
    all_gather x1, waiting for transfers between devices: 0.02 us -> 3.77 us  [local(): z_own = lax.all_gather(z_share, 'z', axis=0)]
    all_to_all x1 -> x0, starting transfers between devices: 3.49 us -> none  [local(): lax.all_to_all(early, 'z', split_axis=0, concat_axis=0, tiled=True)]
    ppermute x9, starting transfers between devices: 19.5 us -> 22.2 us  [swap(): return lax.ppermute(array, axis, [(0, 1), (1, 0)])]
  transfers between devices with their start and end apart: 19 -> 18, of which waited for: 11 -> 13; matrix products, arithmetic and copies ran while one was open for 12% -> 11% of each run, Pallas kernels for 1% -> 1%
where the time goes in v11:
time: 234 us; the launch traced here: 232 us
  waiting for transfers between devices  80.9 us (35%)
  starting transfers between devices  58.9 us (25%)
  blocking collectives  38.6 us (16%)
  other arithmetic  24.2 us (10%)
  between operations  14.2 us (6%)
  matrix products  6.2 us (3%)
  local copies, waits for them, and re-layouts  6.13 us (3%)
  Pallas kernels  2.97 us (1%)
    all_to_all x2, blocking collectives, sum_x(): lax.all_to_all(parts, X, split_axis=0, concat_axis=0, tiled=True)  22.9 us
    ppermute x9, starting transfers between devices, swap(): return lax.ppermute(array, axis, [(0, 1), (1, 0)])  22.2 us
    all_gather x1, waiting for transfers between devices, local(): z_panel = lax.all_gather(z_piece, 'y', axis=0)  18 us
    all_to_all x1, blocking collectives, local(): lax.all_to_all(early, 'z', split_axis=0, concat_axis=0, tiled=True)  15.6 us
    all_to_all x1, waiting for transfers between devices, local(): lax.all_to_all(z_copies, 'y', split_axis=0, concat_axis=0, tiled=True)  15.1 us
    ppermute x9, waiting for transfers between devices, swap(): return lax.ppermute(array, axis, [(0, 1), (1, 0)])  14.9 us
    mul x4, other arithmetic, slices(): lax.dynamic_slice(values, (0, (2 * m + a) * blk + b * half), (blk, half))  14.7 us
    all_to_all x1, starting transfers between devices, spread(): return lax.all_to_all(copies, axis, split_axis=0, concat_axis=0, tiled=True)  10.2 us
  transfers between devices with their start and end apart: 18, of which 13 were waited for; matrix products, arithmetic and copies ran while one was open for 11% of the time, Pallas kernels for 1%

profile of v11, /device:TPU:56, one launch (start us, length us, event | category | flops | bytes accessed | tf_op | source)
XLA Modules:
  0.0 232.0 jit_solution(232763585073272118)
XLA Ops:
  7.2 0.7 convert_element_type.10
  7.9 0.7 fusion.24
  8.6 2.3 dynamic-slice_multiply_fusion.16
  10.9 1.1 broadcast_in_dim.18
  11.9 8.6 %all-to-all-start = ((f32[8,128,256]{2,1,0:T(8,128)}), f32[8,128,256]{2,1,0:T(8,128)S(1)}, u32[]{:S(2)}, u32[]{:S(2)}) async-start(f32[8,128,256]{2,1,0:T(8,128)} %broadcast_in_dim.18), calls=%async_computation | async-start | bytes 2097152 | tf_op jit(solution)/shard_map/all_to_all | solution.py:93
  20.6 3.6 %dynamic-slice_multiply_fusion.15 = (f32[256,128]{1,0:T(8,128)S(1)}, f32[256,128]{1,0:T(8,128)S(1)}, f32[256,128]{1,0:T(8,128)S(1)}, f32[256,128]{1,0:T(8,128)S(1)}) fusion(f32[256,2048]{1,0:T(8,128)} %param.7, s32[]{:T(128)S(6)} %select_n.191, f32[]{:T(128)} %bitcast.2, f32[]{:T(128)} %bitcast.5, s32[]{:T(128)S(6)} %select_n.197, f32[]{:T(128)} %bitcast.4, ...), kind=kLoop, calls=%fused_computation.51 | loop fusion | flops 131072 | bytes 1048608 | tf_op jit(solution)/shard_map/mul | solution.py:65
  24.2 2.9 %collective-permute-start.1 = (f32[256,512]{1,0:T(8,128)S(1)}, f32[256,512]{1,0:T(8,128)S(1)}, u32[]{:S(2)}, u32[]{:S(2)}) collective-permute-start(f32[256,512]{1,0:T(8,128)S(1)} %pad_maximum_fusion.1), channel_id=1, source_target_pairs={{0,33},{33,0},{1,32},{32,1},{2,35},{35,2},{3,34},{34,3},{4,37},{37... | collective-permute-start | bytes 1572872 | tf_op jit(solution)/shard_map/ppermute | solution.py:73
  27.1 3.7 %dynamic-slice_multiply_fusion.11 = (f32[256,128]{1,0:T(8,128)S(1)}, f32[256,128]{1,0:T(8,128)S(1)}, f32[256,128]{1,0:T(8,128)S(1)}, f32[256,128]{1,0:T(8,128)S(1)}) fusion(f32[256,2048]{1,0:T(8,128)} %param.7, s32[]{:T(128)S(6)} %select_n.199, f32[]{:T(128)} %bitcast.6, f32[]{:T(128)} %bitcast.9, s32[]{:T(128)S(6)} %select_n.205, f32[]{:T(128)} %bitcast.8, ...), kind=kLoop, calls=%fused_computation.47 | loop fusion | flops 131072 | bytes 1048608 | tf_op jit(solution)/shard_map/mul | solution.py:65
  30.8 0.8 pad_maximum_fusion.2
  31.6 1.9 collective-permute-start
  33.6 5.1 %collective-permute-done.1 = f32[256,512]{1,0:T(8,128)S(1)} collective-permute-done((f32[256,512]{1,0:T(8,128)S(1)}, f32[256,512]{1,0:T(8,128)S(1)}, u32[]{:S(2)}, u32[]{:S(2)}) %collective-permute-start.1) | collective-permute-done | bytes 524320 | tf_op jit(solution)/shard_map/ppermute | solution.py:73
  38.6 1.9 collective-permute-start.2
  40.5 2.9 %all-to-all-done = f32[8,128,256]{2,1,0:T(8,128)S(1)} async-done(((f32[8,128,256]{2,1,0:T(8,128)}), f32[8,128,256]{2,1,0:T(8,128)S(1)}, u32[]{:S(2)}, u32[]{:S(2)}) %all-to-all-start) | async-done | bytes 1048608 | tf_op jit(solution)/shard_map/all_to_all | solution.py:93
  43.5 0.4 fusion.11
  43.9 0.4 fusion.9
  44.3 0.4 convolution_add_fusion.3
  44.7 0.4 broadcast_select_fusion
  45.1 1.9 collective-permute-start.3
  47.1 1.5 collective-permute-done.3
  48.6 0.8 fusion
  49.5 3.6 %all-to-all-start.1 = ((f32[4,256,128]{2,1,0:T(8,128)}), f32[4,256,128]{2,1,0:T(8,128)S(1)}, u32[]{:S(2)}, u32[]{:S(2)}) async-start(f32[4,256,128]{2,1,0:T(8,128)} %bitcast.13), calls=%async_computation.1 | async-start | bytes 1048576 | tf_op jit(solution)/shard_map/all_to_all | solution.py:85
  53.0 0.7 all-gather.7.cloned.1.call-update
  53.8 0.7 fusion.22
  54.5 8.4 %all-to-all-done.1 = f32[4,256,128]{2,1,0:T(8,128)S(1)} async-done(((f32[4,256,128]{2,1,0:T(8,128)}), f32[4,256,128]{2,1,0:T(8,128)S(1)}, u32[]{:S(2)}, u32[]{:S(2)}) %all-to-all-start.1) | async-done | bytes 524320 | tf_op jit(solution)/shard_map/all_to_all | solution.py:85
  63.0 0.8 multiply_subtract_fusion
  63.9 1.1 broadcast_in_dim.19
  64.9 10.2 %all-to-all-start.2 = ((f32[8,256,128]{1,2,0:T(8,128)}), f32[8,256,128]{1,2,0:T(8,128)S(1)}, u32[]{:S(2)}, u32[]{:S(2)}) async-start(f32[8,256,128]{1,2,0:T(8,128)} %broadcast_in_dim.19), calls=%async_computation.2 | async-start | bytes 2097152 | tf_op jit(solution)/shard_map/all_to_all | solution.py:16
  75.1 3.8 %dynamic-slice_multiply_fusion.7 = (f32[256,128]{1,0:T(8,128)S(1)}, f32[256,128]{1,0:T(8,128)S(1)}, f32[256,128]{1,0:T(8,128)S(1)}, f32[256,128]{1,0:T(8,128)S(1)}) fusion(f32[256,2048]{1,0:T(8,128)} %param.8, s32[]{:T(128)S(6)} %select_n.191, f32[]{:T(128)} %bitcast.15, f32[]{:T(128)} %bitcast.18, s32[]{:T(128)S(6)} %select_n.197, f32[]{:T(128)} %bitcast.17, ...), kind=kLoop, calls=%fused_computation.42 | loop fusion | flops 131072 | bytes 1048608 | tf_op jit(solution)/shard_map/mul | solution.py:65
  78.9 3.1 %collective-permute-start.4 = (f32[256,512]{1,0:T(8,128)S(1)}, f32[256,512]{1,0:T(8,128)S(1)}, u32[]{:S(2)}, u32[]{:S(2)}) collective-permute-start(f32[256,512]{1,0:T(8,128)S(1)} %pad_maximum_fusion.3), channel_id=1, source_target_pairs={{0,33},{33,0},{1,32},{32,1},{2,35},{35,2},{3,34},{34,3},{4,37},{37... | collective-permute-start | bytes 1572872 | tf_op jit(solution)/shard_map/ppermute | solution.py:73
  82.0 18.0 %all-gather.7.cloned.1.call-done = f32[1024,256]{1,0:T(8,128)} async-done(((f32[128,256]{1,0:T(8,128)}), f32[1024,256]{1,0:T(8,128)}) %all-gather.7.cloned.1.call-update) | async-done | bytes 1048592 | tf_op jit(solution)/shard_map/all_gather | solution.py:114
  100.0 3.0 %all-to-all-done.2 = f32[8,256,128]{1,2,0:T(8,128)S(1)} async-done(((f32[8,256,128]{1,2,0:T(8,128)}), f32[8,256,128]{1,2,0:T(8,128)S(1)}, u32[]{:S(2)}, u32[]{:S(2)}) %all-to-all-start.2) | async-done | bytes 1048608 | tf_op jit(solution)/shard_map/all_to_all | solution.py:16
  103.0 1.9 collective-permute-start.5
  104.9 1.8 reverse_select_fusion
  106.8 0.7 collective-permute-done.5
  107.5 1.0 fusion.27
  108.5 1.0 select_bitcast_fusion.3
  109.6 12.5 %all_to_all.35 = f32[4,128,256]{2,1,0:T(8,128)S(1)} all-to-all(f32[4,128,256]{2,1,0:T(8,128)S(1)} %bitcast.73), channel_id=1, replica_groups=mesh['y'=8,'xh'=2,'core'=2,'z'=8,'xl'=2] {'xh','xl'}, dimensions={0} | all-to-all | bytes 1048576 | tf_op jit(solution)/shard_map/all_to_all | solution.py:85
  122.1 0.6 broadcast_multiply_fusion.1
  122.7 1.1 broadcast_in_dim.36
  123.8 8.3 %all-to-all-start.4 = ((f32[8,128,256]{2,1,0:T(8,128)}), f32[8,128,256]{2,1,0:T(8,128)S(1)}, u32[]{:S(2)}, u32[]{:S(2)}) async-start(f32[8,128,256]{2,1,0:T(8,128)} %broadcast_in_dim.36), calls=%async_computation.4 | async-start | bytes 2097152 | tf_op jit(solution)/shard_map/all_to_all | solution.py:136
  132.1 0.7 all-gather.9.cloned.1.call-update
  132.8 1.9 collective-permute-start.7
  134.8 3.6 %dynamic-slice_multiply_fusion.3 = (f32[256,128]{1,0:T(8,128)S(1)}, f32[256,128]{1,0:T(8,128)S(1)}, f32[256,128]{1,0:T(8,128)S(1)}, f32[256,128]{1,0:T(8,128)S(1)}) fusion(f32[256,2048]{1,0:T(8,128)} %param.8, s32[]{:T(128)S(6)} %select_n.199, f32[]{:T(128)} %bitcast.31, f32[]{:T(128)} %bitcast.34, s32[]{:T(128)S(6)} %select_n.205, f32[]{:T(128)} %bitcast.33, ...), kind=kLoop, calls=%fused_computation.38 | loop fusion | flops 131072 | bytes 1048608 | tf_op jit(solution)/shard_map/mul | solution.py:65
  138.4 2.4 %collective-permute-start.6 = (f32[256,512]{1,0:T(8,128)S(1)}, f32[256,512]{1,0:T(8,128)}, u32[]{:S(2)}, u32[]{:S(2)}) collective-permute-start(f32[256,512]{1,0:T(8,128)S(1)} %pad_maximum_fusion.5), channel_id=1, source_target_pairs={{0,16},{16,0},{1,17},{17,1},{2,18},{18,2},{3,19},{19,3},{4,20},{20... | collective-permute-start | bytes 1572872 | tf_op jit(solution)/shard_map/ppermute | solution.py:20
  140.8 15.1 %all-to-all-done.4 = f32[8,128,256]{2,1,0:T(8,128)S(1)} async-done(((f32[8,128,256]{2,1,0:T(8,128)}), f32[8,128,256]{2,1,0:T(8,128)S(1)}, u32[]{:S(2)}, u32[]{:S(2)}) %all-to-all-start.4) | async-done | bytes 1048608 | tf_op jit(solution)/shard_map/all_to_all | solution.py:136
  156.0 0.4 fusion.5
  156.4 0.4 fusion.3
  156.8 0.4 convolution_add_fusion
  157.2 1.4 select_bitcast_fusion.1
  158.7 10.5 %all_to_all.36 = f32[4,128,256]{2,1,0:T(8,128)S(1)} all-to-all(f32[4,128,256]{2,1,0:T(8,128)S(1)} %bitcast.74), channel_id=1, replica_groups=mesh['y'=8,'xh'=2,'core'=2,'z'=8,'xl'=2] {'xh','xl'}, dimensions={0} | all-to-all | bytes 1048576 | tf_op jit(solution)/shard_map/all_to_all | solution.py:85
  169.2 0.6 broadcast_multiply_fusion
  169.9 3.8 %all-gather.9.cloned.1.call-done = f32[1024,256]{1,0:T(8,128)} async-done(((f32[128,256]{1,0:T(8,128)}), f32[1024,256]{1,0:T(8,128)}) %all-gather.9.cloned.1.call-update) | async-done | bytes 1048592 | tf_op jit(solution)/shard_map/all_gather | solution.py:138
  173.6 3.5 %collective-permute-start.9 = (f32[80,256]{1,0:T(8,128)S(1)}, f32[80,256]{1,0:T(8,128)S(1)}, u32[]{:S(2)}, u32[]{:S(2)}) collective-permute-start(f32[80,256]{1,0:T(8,128)S(1)} %slice.16), channel_id=1, source_target_pairs={{0,1},{1,0},{2,3},{3,2},{4,5},{5,4},{6,7},{7,6},{8,9},{9,8},{10,11... | collective-permute-start | bytes 245768 | tf_op jit(solution)/shard_map/ppermute | solution.py:20
  177.2 3.4 %collective-permute-done.9 = f32[80,256]{1,0:T(8,128)S(1)} collective-permute-done((f32[80,256]{1,0:T(8,128)S(1)}, f32[80,256]{1,0:T(8,128)S(1)}, u32[]{:S(2)}, u32[]{:S(2)}) %collective-permute-start.9) | collective-permute-done | bytes 81952 | tf_op jit(solution)/shard_map/ppermute | solution.py:20
  180.6 0.7 pad_maximum_fusion.7
  181.3 3.4 %collective-permute-start.8 = (f32[8,128,256]{2,1,0:T(8,128)}, f32[8,128,256]{2,1,0:T(8,128)S(1)}, u32[]{:S(2)}, u32[]{:S(2)}) collective-permute-start(f32[8,128,256]{2,1,0:T(8,128)} %bitcast.60), channel_id=1, source_target_pairs={{0,1},{1,0},{2,3},{3,2},{4,5},{5,4},{6,7},{7,6},{8,9},{9,8},{10,11... | collective-permute-start | bytes 3145736 | tf_op jit(solution)/shard_map/ppermute | solution.py:20
  184.7 15.6 %all_to_all.37.refs_0_ = f32[8,48,256]{2,1,0:T(8,128)S(1)} all-to-all(f32[8,48,256]{2,1,0:T(8,128)S(1)} %broadcast_in_dim.37), channel_id=1, replica_groups=mesh['y'=8,'xh'=2,'core'=2,'z'=8,'xl'=2] {'z'}, dimensions={0} | all-to-all | bytes 786432 | tf_op jit(solution)/shard_map/all_to_all | solution.py:150
  200.4 4.5 %collective-permute-done.8.refs_1_ = f32[8,128,256]{2,1,0:T(8,128)S(1)} collective-permute-done((f32[8,128,256]{2,1,0:T(8,128)}, f32[8,128,256]{2,1,0:T(8,128)S(1)}, u32[]{:S(2)}, u32[]{:S(2)}) %collective-permute-start.8) | collective-permute-done | bytes 1048608 | tf_op jit(solution)/shard_map/ppermute | solution.py:20
  204.8 3.4 %collective-permute-start.10 = (f32[8,48,256]{2,1,0:T(8,128)S(1)}, f32[8,48,256]{2,1,0:T(8,128)S(1)}, u32[]{:S(2)}, u32[]{:S(2)}) collective-permute-start(f32[8,48,256]{2,1,0:T(8,128)S(1)} %all_to_all.37.refs_0_), channel_id=1, source_target_pairs={{0,1},{1,0},{2,3},{3,2},{4,5},{5,4},{6,7},{7,6},{8,9},{9,8},{10,11... | collective-permute-start | bytes 1179656 | tf_op jit(solution)/shard_map/ppermute | solution.py:20
  208.2 1.5 shard_map.77
  209.7 4.8 %collective-permute-done.10.refs_2_ = f32[8,48,256]{2,1,0:T(8,128)S(1)} collective-permute-done((f32[8,48,256]{2,1,0:T(8,128)S(1)}, f32[8,48,256]{2,1,0:T(8,128)S(1)}, u32[]{:S(2)}, u32[]{:S(2)}) %collective-permute-start.10) | collective-permute-done | bytes 393248 | tf_op jit(solution)/shard_map/ppermute | solution.py:20
  214.5 8.2 %all-gather.11.cloned.1.call-done = f32[1280,256]{1,0:T(8,128)} async-done(((f32[160,256]{1,0:T(8,128)}), f32[1280,256]{1,0:T(8,128)}) %all-gather.11.cloned.1.call-update) | async-done | bytes 1310736 | tf_op jit(solution)/shard_map/all_gather | solution.py:149
  222.7 1.3 copy-done
  224.0 1.5 shard_map.78
  (37 shorter events, 0.7 us)
Async XLA Ops:
  11.9 31.6 %all-to-all-start = ((f32[8,128,256]{2,1,0:T(8,128)}), f32[8,128,256]{2,1,0:T(8,128)S(1)}, u32[]{:S(2)}, u32[]{:S(2)}) async-start(f32[8,128,256]{2,1,0:T(8,128)} %broadcast_in_dim.18), calls=%async_computation | async-start | bytes 2097152 | tf_op jit(solution)/shard_map/all_to_all | solution.py:93
  24.2 14.4 %collective-permute-start.1 = (f32[256,512]{1,0:T(8,128)S(1)}, f32[256,512]{1,0:T(8,128)S(1)}, u32[]{:S(2)}, u32[]{:S(2)}) collective-permute-start(f32[256,512]{1,0:T(8,128)S(1)} %pad_maximum_fusion.1), channel_id=1, source_target_pairs={{0,33},{33,0},{1,32},{32,1},{2,35},{35,2},{3,34},{34,3},{4,37},{37... | collective-permute-start | bytes 1572872 | tf_op jit(solution)/shard_map/ppermute | solution.py:73
  31.6 12.6 %collective-permute-start = (f32[256,512]{1,0:T(8,128)}, f32[256,512]{1,0:T(8,128)S(1)}, u32[]{:S(2)}, u32[]{:S(2)}) collective-permute-start(f32[256,512]{1,0:T(8,128)} %pad_maximum_fusion.2), channel_id=1, source_target_pairs={{0,16},{16,0},{1,17},{17,1},{2,18},{18,2},{3,19},{19,3},{4,20},{20... | collective-permute-start | bytes 1572872 | tf_op jit(solution)/shard_map/ppermute | solution.py:20
  38.6 6.1 %collective-permute-start.2 = (f32[256,512]{1,0:T(8,128)S(1)}, f32[256,512]{1,0:T(8,128)S(1)}, u32[]{:S(2)}, u32[]{:S(2)}) collective-permute-start(f32[256,512]{1,0:T(8,128)S(1)} %collective-permute-done.1), channel_id=1, source_target_pairs={{0,16},{16,0},{1,17},{17,1},{2,18},{18,2},{3,19},{19,3},{4,20},{20... | collective-permute-start | bytes 1572872 | tf_op jit(solution)/shard_map/ppermute | solution.py:20
  45.1 3.4 %collective-permute-start.3 = (f32[256,256]{1,0:T(8,128)S(1)}, f32[256,256]{1,0:T(8,128)S(1)}, u32[]{:S(2)}, u32[]{:S(2)}) collective-permute-start(f32[256,256]{1,0:T(8,128)S(1)} %get-tuple-element.77), channel_id=1, source_target_pairs={{0,16},{16,0},{1,17},{17,1},{2,18},{18,2},{3,19},{19,3},{4,20},{20... | collective-permute-start | bytes 786440 | tf_op jit(solution)/shard_map/ppermute | solution.py:20
  48.5 5.2 %copy-start.3 = (s32[16,16]{1,0:T(8,128)S(1)}, s32[16,16]{1,0:T(8,128)}, u32[]{:S(2)}) copy-start(s32[16,16]{1,0:T(8,128)} %param.10) | copy-start | bytes 3076
  48.5 5.2 %copy-start.4 = (s32[16,16]{1,0:T(8,128)S(1)}, s32[16,16]{1,0:T(8,128)}, u32[]{:S(2)}) copy-start(s32[16,16]{1,0:T(8,128)} %param.11) | copy-start | bytes 3076
  49.5 13.5 %all-to-all-start.1 = ((f32[4,256,128]{2,1,0:T(8,128)}), f32[4,256,128]{2,1,0:T(8,128)S(1)}, u32[]{:S(2)}, u32[]{:S(2)}) async-start(f32[4,256,128]{2,1,0:T(8,128)} %bitcast.13), calls=%async_computation.1 | async-start | bytes 1048576 | tf_op jit(solution)/shard_map/all_to_all | solution.py:85
  53.0 47.0 %all-gather.7.cloned.1.call-start = ((), (), s32[]{:S(2)}) async-start(), calls=%async_computation.7 | async-start | bytes 1179648 | tf_op jit(solution)/shard_map/all_gather | solution.py:114
  64.9 38.0 %all-to-all-start.2 = ((f32[8,256,128]{1,2,0:T(8,128)}), f32[8,256,128]{1,2,0:T(8,128)S(1)}, u32[]{:S(2)}, u32[]{:S(2)}) async-start(f32[8,256,128]{1,2,0:T(8,128)} %broadcast_in_dim.19), calls=%async_computation.2 | async-start | bytes 2097152 | tf_op jit(solution)/shard_map/all_to_all | solution.py:16
  78.9 21.0 %collective-permute-start.4 = (f32[256,512]{1,0:T(8,128)S(1)}, f32[256,512]{1,0:T(8,128)S(1)}, u32[]{:S(2)}, u32[]{:S(2)}) collective-permute-start(f32[256,512]{1,0:T(8,128)S(1)} %pad_maximum_fusion.3), channel_id=1, source_target_pairs={{0,33},{33,0},{1,32},{32,1},{2,35},{35,2},{3,34},{34,3},{4,37},{37... | collective-permute-start | bytes 1572872 | tf_op jit(solution)/shard_map/ppermute | solution.py:73
  103.0 4.5 %collective-permute-start.5 = (f32[8,256,128]{1,2,0:T(8,128)S(1)}, f32[8,256,128]{1,2,0:T(8,128)S(1)}, u32[]{:S(2)}, u32[]{:S(2)}) collective-permute-start(f32[8,256,128]{1,2,0:T(8,128)S(1)} %all-to-all-done.2), channel_id=1, source_target_pairs={{0,16},{16,0},{1,17},{17,1},{2,18},{18,2},{3,19},{19,3},{4,20},{20... | collective-permute-start | bytes 3145736 | tf_op jit(solution)/shard_map/ppermute | solution.py:20
  122.7 9.4 %copy-start.2 = (f32[128,256]{1,0:T(8,128)}, f32[128,256]{1,0:T(8,128)S(1)}, u32[]{:S(2)}) copy-start(f32[128,256]{1,0:T(8,128)S(1)} %broadcast_multiply_fusion.1) | copy-start | bytes 393220
  123.8 32.2 %all-to-all-start.4 = ((f32[8,128,256]{2,1,0:T(8,128)}), f32[8,128,256]{2,1,0:T(8,128)S(1)}, u32[]{:S(2)}, u32[]{:S(2)}) async-start(f32[8,128,256]{2,1,0:T(8,128)} %broadcast_in_dim.36), calls=%async_computation.4 | async-start | bytes 2097152 | tf_op jit(solution)/shard_map/all_to_all | solution.py:136
  132.1 41.6 %all-gather.9.cloned.1.call-start = ((), (), s32[]{:S(2)}) async-start(), calls=%async_computation.8 | async-start | bytes 1179648 | tf_op jit(solution)/shard_map/all_gather | solution.py:138
  132.8 89.9 %all-gather.11.cloned.1.call-start = ((), (), s32[]{:S(2)}) async-start(), calls=%async_computation.9 | async-start | bytes 1474560 | tf_op jit(solution)/shard_map/all_gather | solution.py:149
  132.8 23.9 %collective-permute-start.7 = (f32[256,512]{1,0:T(8,128)S(1)}, f32[256,512]{1,0:T(8,128)S(1)}, u32[]{:S(2)}, u32[]{:S(2)}) collective-permute-start(f32[256,512]{1,0:T(8,128)S(1)} %collective-permute-done.4), channel_id=1, source_target_pairs={{0,16},{16,0},{1,17},{17,1},{2,18},{18,2},{3,19},{19,3},{4,20},{20... | collective-permute-start | bytes 1572872 | tf_op jit(solution)/shard_map/ppermute | solution.py:20
  138.4 18.8 %collective-permute-start.6 = (f32[256,512]{1,0:T(8,128)S(1)}, f32[256,512]{1,0:T(8,128)}, u32[]{:S(2)}, u32[]{:S(2)}) collective-permute-start(f32[256,512]{1,0:T(8,128)S(1)} %pad_maximum_fusion.5), channel_id=1, source_target_pairs={{0,16},{16,0},{1,17},{17,1},{2,18},{18,2},{3,19},{19,3},{4,20},{20... | collective-permute-start | bytes 1572872 | tf_op jit(solution)/shard_map/ppermute | solution.py:20
  173.6 34.6 %copy-start.1 = (f32[1024,256]{1,0:T(8,128)S(1)}, f32[1024,256]{1,0:T(8,128)}, u32[]{:S(2)}) copy-start(f32[1024,256]{1,0:T(8,128)} %all-gather.9.cloned.1.call-done) | copy-start | bytes 3145732
  173.6 6.9 %collective-permute-start.9 = (f32[80,256]{1,0:T(8,128)S(1)}, f32[80,256]{1,0:T(8,128)S(1)}, u32[]{:S(2)}, u32[]{:S(2)}) collective-permute-start(f32[80,256]{1,0:T(8,128)S(1)} %slice.16), channel_id=1, source_target_pairs={{0,1},{1,0},{2,3},{3,2},{4,5},{5,4},{6,7},{7,6},{8,9},{9,8},{10,11... | collective-permute-start | bytes 245768 | tf_op jit(solution)/shard_map/ppermute | solution.py:20
  181.3 23.6 %collective-permute-start.8 = (f32[8,128,256]{2,1,0:T(8,128)}, f32[8,128,256]{2,1,0:T(8,128)S(1)}, u32[]{:S(2)}, u32[]{:S(2)}) collective-permute-start(f32[8,128,256]{2,1,0:T(8,128)} %bitcast.60), channel_id=1, source_target_pairs={{0,1},{1,0},{2,3},{3,2},{4,5},{5,4},{6,7},{7,6},{8,9},{9,8},{10,11... | collective-permute-start | bytes 3145736 | tf_op jit(solution)/shard_map/ppermute | solution.py:20
  204.8 9.7 %collective-permute-start.10 = (f32[8,48,256]{2,1,0:T(8,128)S(1)}, f32[8,48,256]{2,1,0:T(8,128)S(1)}, u32[]{:S(2)}, u32[]{:S(2)}) collective-permute-start(f32[8,48,256]{2,1,0:T(8,128)S(1)} %all_to_all.37.refs_0_), channel_id=1, source_target_pairs={{0,1},{1,0},{2,3},{3,2},{4,5},{5,4},{6,7},{7,6},{8,9},{9,8},{10,11... | collective-permute-start | bytes 1179656 | tf_op jit(solution)/shard_map/ppermute | solution.py:20
  222.7 1.3 copy-start
Sparse Core Ops, SparseCore 0:
  55.9 44.0 all-gather.6
  135.5 38.0 all-gather.8
  181.4 41.2 all-gather.10

commit v12 on v11

--- a/solution.py
+++ b/solution.py
@@ -142,7 +142,7 @@
     h_partial = jnp.stack([jnp.where(xh == 0, h_own, h_other), jnp.where(xh == 0, h_other, h_own)])
     h_share = finish(h_partial)
     h_share, z_own = lax.optimization_barrier((h_share, z_own))
-    passed = half * 3 // 8
+    passed = half // 2
     rest = half - passed
     early = jnp.broadcast_to(h_share[:passed][None], (nz, passed, blk))
     late = jnp.concatenate([h_share[passed:], swap(h_share[passed:], "xl")], axis=0)

time: 234 us -> 234 us (level)
  waiting for transfers between devices: 80.9 us -> 78.2 us
where the time goes in v12:
time: 234 us; the launch traced here: 231 us
  waiting for transfers between devices  78.2 us (33%)
  starting transfers between devices  58.9 us (25%)
  blocking collectives  40.6 us (17%)
  other arithmetic  24.2 us (10%)
  between operations  14.2 us (6%)
  matrix products  6.19 us (3%)
  local copies, waits for them, and re-layouts  6.05 us (3%)
  Pallas kernels  2.96 us (1%)
    all_to_all x2, blocking collectives, sum_x(): lax.all_to_all(parts, X, split_axis=0, concat_axis=0, tiled=True)  22.9 us
    ppermute x9, starting transfers between devices, swap(): return lax.ppermute(array, axis, [(0, 1), (1, 0)])  22.3 us
    all_gather x1, waiting for transfers between devices, local(): z_panel = lax.all_gather(z_piece, 'y', axis=0)  18 us
    all_to_all x1, blocking collectives, local(): lax.all_to_all(early, 'z', split_axis=0, concat_axis=0, tiled=True)  17.6 us
    all_to_all x1, waiting for transfers between devices, local(): lax.all_to_all(z_copies, 'y', split_axis=0, concat_axis=0, tiled=True)  15.1 us
    mul x4, other arithmetic, slices(): lax.dynamic_slice(values, (0, (2 * m + a) * blk + b * half), (blk, half))  14.7 us
    ppermute x9, waiting for transfers between devices, swap(): return lax.ppermute(array, axis, [(0, 1), (1, 0)])  14.1 us
    all_to_all x1, starting transfers between devices, spread(): return lax.all_to_all(copies, axis, split_axis=0, concat_axis=0, tiled=True)  10.2 us
  transfers between devices with their start and end apart: 18, of which 13 were waited for; matrix products, arithmetic and copies ran while one was open for 11% of the time, Pallas kernels for 1%

profile of v12, /device:TPU:56, one launch (start us, length us, event | category | flops | bytes accessed | tf_op | source)
XLA Modules:
  0.0 231.2 jit_solution(18186636573940990241)
XLA Ops:
  7.2 0.7 convert_element_type.10
  7.9 0.7 fusion.25
  8.6 2.3 dynamic-slice_multiply_fusion.16
  10.9 1.1 broadcast_in_dim.18
  11.9 8.6 %all-to-all-start = ((f32[8,128,256]{2,1,0:T(8,128)}), f32[8,128,256]{2,1,0:T(8,128)S(1)}, u32[]{:S(2)}, u32[]{:S(2)}) async-start(f32[8,128,256]{2,1,0:T(8,128)} %broadcast_in_dim.18), calls=%async_computation | async-start | bytes 2097152 | tf_op jit(solution)/shard_map/all_to_all | solution.py:93
  20.6 3.6 %dynamic-slice_multiply_fusion.15 = (f32[256,128]{1,0:T(8,128)S(1)}, f32[256,128]{1,0:T(8,128)S(1)}, f32[256,128]{1,0:T(8,128)S(1)}, f32[256,128]{1,0:T(8,128)S(1)}) fusion(f32[256,2048]{1,0:T(8,128)} %param.7, s32[]{:T(128)S(6)} %select_n.191, f32[]{:T(128)} %bitcast.2, f32[]{:T(128)} %bitcast.5, s32[]{:T(128)S(6)} %select_n.197, f32[]{:T(128)} %bitcast.4, ...), kind=kLoop, calls=%fused_computation.51 | loop fusion | flops 131072 | bytes 1048608 | tf_op jit(solution)/shard_map/mul | solution.py:65
  24.2 2.9 %collective-permute-start.1 = (f32[256,512]{1,0:T(8,128)S(1)}, f32[256,512]{1,0:T(8,128)S(1)}, u32[]{:S(2)}, u32[]{:S(2)}) collective-permute-start(f32[256,512]{1,0:T(8,128)S(1)} %pad_maximum_fusion.1), channel_id=1, source_target_pairs={{0,33},{33,0},{1,32},{32,1},{2,35},{35,2},{3,34},{34,3},{4,37},{37... | collective-permute-start | bytes 1572872 | tf_op jit(solution)/shard_map/ppermute | solution.py:73
  27.1 3.7 %dynamic-slice_multiply_fusion.11 = (f32[256,128]{1,0:T(8,128)S(1)}, f32[256,128]{1,0:T(8,128)S(1)}, f32[256,128]{1,0:T(8,128)S(1)}, f32[256,128]{1,0:T(8,128)S(1)}) fusion(f32[256,2048]{1,0:T(8,128)} %param.7, s32[]{:T(128)S(6)} %select_n.199, f32[]{:T(128)} %bitcast.6, f32[]{:T(128)} %bitcast.9, s32[]{:T(128)S(6)} %select_n.205, f32[]{:T(128)} %bitcast.8, ...), kind=kLoop, calls=%fused_computation.47 | loop fusion | flops 131072 | bytes 1048608 | tf_op jit(solution)/shard_map/mul | solution.py:65
  30.8 0.8 pad_maximum_fusion.2
  31.7 1.9 collective-permute-start
  33.6 5.1 %collective-permute-done.1 = f32[256,512]{1,0:T(8,128)S(1)} collective-permute-done((f32[256,512]{1,0:T(8,128)S(1)}, f32[256,512]{1,0:T(8,128)S(1)}, u32[]{:S(2)}, u32[]{:S(2)}) %collective-permute-start.1) | collective-permute-done | bytes 524320 | tf_op jit(solution)/shard_map/ppermute | solution.py:73
  38.6 1.9 collective-permute-start.2
  40.6 2.9 %all-to-all-done = f32[8,128,256]{2,1,0:T(8,128)S(1)} async-done(((f32[8,128,256]{2,1,0:T(8,128)}), f32[8,128,256]{2,1,0:T(8,128)S(1)}, u32[]{:S(2)}, u32[]{:S(2)}) %all-to-all-start) | async-done | bytes 1048608 | tf_op jit(solution)/shard_map/all_to_all | solution.py:93
  43.5 0.4 fusion.11
  43.9 0.4 fusion.9
  44.3 0.4 convolution_add_fusion.3
  44.7 0.4 broadcast_select_fusion
  45.1 1.9 collective-permute-start.3
  47.1 1.5 collective-permute-done.3
  48.6 0.8 fusion
  49.5 3.6 %all-to-all-start.1 = ((f32[4,256,128]{2,1,0:T(8,128)}), f32[4,256,128]{2,1,0:T(8,128)S(1)}, u32[]{:S(2)}, u32[]{:S(2)}) async-start(f32[4,256,128]{2,1,0:T(8,128)} %bitcast.13), calls=%async_computation.1 | async-start | bytes 1048576 | tf_op jit(solution)/shard_map/all_to_all | solution.py:85
  53.0 0.7 all-gather.7.cloned.1.call-update
  53.8 0.7 fusion.23
  54.5 8.4 %all-to-all-done.1 = f32[4,256,128]{2,1,0:T(8,128)S(1)} async-done(((f32[4,256,128]{2,1,0:T(8,128)}), f32[4,256,128]{2,1,0:T(8,128)S(1)}, u32[]{:S(2)}, u32[]{:S(2)}) %all-to-all-start.1) | async-done | bytes 524320 | tf_op jit(solution)/shard_map/all_to_all | solution.py:85
  63.0 0.8 multiply_subtract_fusion
  63.9 1.1 broadcast_in_dim.19
  64.9 10.2 %all-to-all-start.2 = ((f32[8,256,128]{1,2,0:T(8,128)}), f32[8,256,128]{1,2,0:T(8,128)S(1)}, u32[]{:S(2)}, u32[]{:S(2)}) async-start(f32[8,256,128]{1,2,0:T(8,128)} %broadcast_in_dim.19), calls=%async_computation.2 | async-start | bytes 2097152 | tf_op jit(solution)/shard_map/all_to_all | solution.py:16
  75.1 3.8 %dynamic-slice_multiply_fusion.7 = (f32[256,128]{1,0:T(8,128)S(1)}, f32[256,128]{1,0:T(8,128)S(1)}, f32[256,128]{1,0:T(8,128)S(1)}, f32[256,128]{1,0:T(8,128)S(1)}) fusion(f32[256,2048]{1,0:T(8,128)} %param.8, s32[]{:T(128)S(6)} %select_n.191, f32[]{:T(128)} %bitcast.15, f32[]{:T(128)} %bitcast.18, s32[]{:T(128)S(6)} %select_n.197, f32[]{:T(128)} %bitcast.17, ...), kind=kLoop, calls=%fused_computation.42 | loop fusion | flops 131072 | bytes 1048608 | tf_op jit(solution)/shard_map/mul | solution.py:65
  79.0 3.1 %collective-permute-start.4 = (f32[256,512]{1,0:T(8,128)S(1)}, f32[256,512]{1,0:T(8,128)S(1)}, u32[]{:S(2)}, u32[]{:S(2)}) collective-permute-start(f32[256,512]{1,0:T(8,128)S(1)} %pad_maximum_fusion.3), channel_id=1, source_target_pairs={{0,33},{33,0},{1,32},{32,1},{2,35},{35,2},{3,34},{34,3},{4,37},{37... | collective-permute-start | bytes 1572872 | tf_op jit(solution)/shard_map/ppermute | solution.py:73
  82.0 18.0 %all-gather.7.cloned.1.call-done = f32[1024,256]{1,0:T(8,128)} async-done(((f32[128,256]{1,0:T(8,128)}), f32[1024,256]{1,0:T(8,128)}) %all-gather.7.cloned.1.call-update) | async-done | bytes 1048592 | tf_op jit(solution)/shard_map/all_gather | solution.py:114
  100.0 3.0 %all-to-all-done.2 = f32[8,256,128]{1,2,0:T(8,128)S(1)} async-done(((f32[8,256,128]{1,2,0:T(8,128)}), f32[8,256,128]{1,2,0:T(8,128)S(1)}, u32[]{:S(2)}, u32[]{:S(2)}) %all-to-all-start.2) | async-done | bytes 1048608 | tf_op jit(solution)/shard_map/all_to_all | solution.py:16
  103.0 1.9 collective-permute-start.5
  104.9 1.8 reverse_select_fusion
  106.8 0.7 collective-permute-done.5
  107.5 1.0 fusion.28
  108.5 1.0 select_bitcast_fusion.3
  109.6 12.5 %all_to_all.35 = f32[4,128,256]{2,1,0:T(8,128)S(1)} all-to-all(f32[4,128,256]{2,1,0:T(8,128)S(1)} %bitcast.73), channel_id=1, replica_groups=mesh['y'=8,'xh'=2,'core'=2,'z'=8,'xl'=2] {'xh','xl'}, dimensions={0} | all-to-all | bytes 1048576 | tf_op jit(solution)/shard_map/all_to_all | solution.py:85
  122.1 0.6 broadcast_multiply_fusion.1
  122.7 1.1 broadcast_in_dim.36
  123.8 8.3 %all-to-all-start.4 = ((f32[8,128,256]{2,1,0:T(8,128)}), f32[8,128,256]{2,1,0:T(8,128)S(1)}, u32[]{:S(2)}, u32[]{:S(2)}) async-start(f32[8,128,256]{2,1,0:T(8,128)} %broadcast_in_dim.36), calls=%async_computation.4 | async-start | bytes 2097152 | tf_op jit(solution)/shard_map/all_to_all | solution.py:136
  132.1 0.7 all-gather.9.cloned.1.call-update
  132.8 1.9 collective-permute-start.7
  134.8 3.6 %dynamic-slice_multiply_fusion.3 = (f32[256,128]{1,0:T(8,128)S(1)}, f32[256,128]{1,0:T(8,128)S(1)}, f32[256,128]{1,0:T(8,128)S(1)}, f32[256,128]{1,0:T(8,128)S(1)}) fusion(f32[256,2048]{1,0:T(8,128)} %param.8, s32[]{:T(128)S(6)} %select_n.199, f32[]{:T(128)} %bitcast.31, f32[]{:T(128)} %bitcast.34, s32[]{:T(128)S(6)} %select_n.205, f32[]{:T(128)} %bitcast.33, ...), kind=kLoop, calls=%fused_computation.38 | loop fusion | flops 131072 | bytes 1048608 | tf_op jit(solution)/shard_map/mul | solution.py:65
  138.4 2.4 %collective-permute-start.6 = (f32[256,512]{1,0:T(8,128)S(1)}, f32[256,512]{1,0:T(8,128)}, u32[]{:S(2)}, u32[]{:S(2)}) collective-permute-start(f32[256,512]{1,0:T(8,128)S(1)} %pad_maximum_fusion.5), channel_id=1, source_target_pairs={{0,16},{16,0},{1,17},{17,1},{2,18},{18,2},{3,19},{19,3},{4,20},{20... | collective-permute-start | bytes 1572872 | tf_op jit(solution)/shard_map/ppermute | solution.py:20
  140.8 15.1 %all-to-all-done.4 = f32[8,128,256]{2,1,0:T(8,128)S(1)} async-done(((f32[8,128,256]{2,1,0:T(8,128)}), f32[8,128,256]{2,1,0:T(8,128)S(1)}, u32[]{:S(2)}, u32[]{:S(2)}) %all-to-all-start.4) | async-done | bytes 1048608 | tf_op jit(solution)/shard_map/all_to_all | solution.py:136
  155.9 0.4 fusion.5
  156.3 0.4 fusion.3
  156.8 0.4 convolution_add_fusion
  157.2 1.4 select_bitcast_fusion.1
  158.7 10.5 %all_to_all.36 = f32[4,128,256]{2,1,0:T(8,128)S(1)} all-to-all(f32[4,128,256]{2,1,0:T(8,128)S(1)} %bitcast.74), channel_id=1, replica_groups=mesh['y'=8,'xh'=2,'core'=2,'z'=8,'xl'=2] {'xh','xl'}, dimensions={0} | all-to-all | bytes 1048576 | tf_op jit(solution)/shard_map/all_to_all | solution.py:85
  169.2 0.6 broadcast_multiply_fusion
  169.8 3.8 %all-gather.9.cloned.1.call-done = f32[1024,256]{1,0:T(8,128)} async-done(((f32[128,256]{1,0:T(8,128)}), f32[1024,256]{1,0:T(8,128)}) %all-gather.9.cloned.1.call-update) | async-done | bytes 1048592 | tf_op jit(solution)/shard_map/all_gather | solution.py:138
  173.6 3.5 %collective-permute-start.9 = (f32[64,256]{1,0:T(8,128)S(1)}, f32[64,256]{1,0:T(8,128)S(1)}, u32[]{:S(2)}, u32[]{:S(2)}) collective-permute-start(f32[64,256]{1,0:T(8,128)S(1)} %get-tuple-element.58), channel_id=1, source_target_pairs={{0,1},{1,0},{2,3},{3,2},{4,5},{5,4},{6,7},{7,6},{8,9},{9,8},{10,11... | collective-permute-start | bytes 196616 | tf_op jit(solution)/shard_map/ppermute | solution.py:20
  177.1 3.2 %collective-permute-done.9 = f32[64,256]{1,0:T(8,128)S(1)} collective-permute-done((f32[64,256]{1,0:T(8,128)S(1)}, f32[64,256]{1,0:T(8,128)S(1)}, u32[]{:S(2)}, u32[]{:S(2)}) %collective-permute-start.9) | collective-permute-done | bytes 65568 | tf_op jit(solution)/shard_map/ppermute | solution.py:20
  180.3 0.7 pad_maximum_fusion.7
  181.0 3.4 %collective-permute-start.8 = (f32[8,128,256]{2,1,0:T(8,128)}, f32[8,128,256]{2,1,0:T(8,128)S(1)}, u32[]{:S(2)}, u32[]{:S(2)}) collective-permute-start(f32[8,128,256]{2,1,0:T(8,128)} %bitcast.59), channel_id=1, source_target_pairs={{0,1},{1,0},{2,3},{3,2},{4,5},{5,4},{6,7},{7,6},{8,9},{9,8},{10,11... | collective-permute-start | bytes 3145736 | tf_op jit(solution)/shard_map/ppermute | solution.py:20
  184.5 17.6 %all_to_all.37.refs_0_ = f32[8,64,256]{2,1,0:T(8,128)S(1)} all-to-all(f32[8,64,256]{2,1,0:T(8,128)S(1)} %broadcast_in_dim.37), channel_id=1, replica_groups=mesh['y'=8,'xh'=2,'core'=2,'z'=8,'xl'=2] {'z'}, dimensions={0} | all-to-all | bytes 1048576 | tf_op jit(solution)/shard_map/all_to_all | solution.py:150
  202.1 2.5 %collective-permute-done.8.refs_1_ = f32[8,128,256]{2,1,0:T(8,128)S(1)} collective-permute-done((f32[8,128,256]{2,1,0:T(8,128)}, f32[8,128,256]{2,1,0:T(8,128)S(1)}, u32[]{:S(2)}, u32[]{:S(2)}) %collective-permute-start.8) | collective-permute-done | bytes 1048608 | tf_op jit(solution)/shard_map/ppermute | solution.py:20
  204.6 3.4 %collective-permute-start.10 = (f32[8,64,256]{2,1,0:T(8,128)S(1)}, f32[8,64,256]{2,1,0:T(8,128)S(1)}, u32[]{:S(2)}, u32[]{:S(2)}) collective-permute-start(f32[8,64,256]{2,1,0:T(8,128)S(1)} %all_to_all.37.refs_0_), channel_id=1, source_target_pairs={{0,1},{1,0},{2,3},{3,2},{4,5},{5,4},{6,7},{7,6},{8,9},{9,8},{10,11... | collective-permute-start | bytes 1572872 | tf_op jit(solution)/shard_map/ppermute | solution.py:20
  208.0 1.5 shard_map.77
  209.4 6.2 %collective-permute-done.10.refs_2_ = f32[8,64,256]{2,1,0:T(8,128)S(1)} collective-permute-done((f32[8,64,256]{2,1,0:T(8,128)S(1)}, f32[8,64,256]{2,1,0:T(8,128)S(1)}, u32[]{:S(2)}, u32[]{:S(2)}) %collective-permute-start.10) | collective-permute-done | bytes 524320 | tf_op jit(solution)/shard_map/ppermute | solution.py:20
  215.6 6.4 %all-gather.11.cloned.1.call-done = f32[1024,256]{1,0:T(8,128)} async-done(((f32[128,256]{1,0:T(8,128)}), f32[1024,256]{1,0:T(8,128)}) %all-gather.11.cloned.1.call-update) | async-done | bytes 1048592 | tf_op jit(solution)/shard_map/all_gather | solution.py:149
  222.0 1.2 copy-done.1
  223.2 1.5 shard_map.78
  (36 shorter events, 0.7 us)
Async XLA Ops:
  11.9 31.6 %all-to-all-start = ((f32[8,128,256]{2,1,0:T(8,128)}), f32[8,128,256]{2,1,0:T(8,128)S(1)}, u32[]{:S(2)}, u32[]{:S(2)}) async-start(f32[8,128,256]{2,1,0:T(8,128)} %broadcast_in_dim.18), calls=%async_computation | async-start | bytes 2097152 | tf_op jit(solution)/shard_map/all_to_all | solution.py:93
  24.2 14.4 %collective-permute-start.1 = (f32[256,512]{1,0:T(8,128)S(1)}, f32[256,512]{1,0:T(8,128)S(1)}, u32[]{:S(2)}, u32[]{:S(2)}) collective-permute-start(f32[256,512]{1,0:T(8,128)S(1)} %pad_maximum_fusion.1), channel_id=1, source_target_pairs={{0,33},{33,0},{1,32},{32,1},{2,35},{35,2},{3,34},{34,3},{4,37},{37... | collective-permute-start | bytes 1572872 | tf_op jit(solution)/shard_map/ppermute | solution.py:73
  31.7 12.6 %collective-permute-start = (f32[256,512]{1,0:T(8,128)}, f32[256,512]{1,0:T(8,128)S(1)}, u32[]{:S(2)}, u32[]{:S(2)}) collective-permute-start(f32[256,512]{1,0:T(8,128)} %pad_maximum_fusion.2), channel_id=1, source_target_pairs={{0,16},{16,0},{1,17},{17,1},{2,18},{18,2},{3,19},{19,3},{4,20},{20... | collective-permute-start | bytes 1572872 | tf_op jit(solution)/shard_map/ppermute | solution.py:20
  38.6 6.1 %collective-permute-start.2 = (f32[256,512]{1,0:T(8,128)S(1)}, f32[256,512]{1,0:T(8,128)S(1)}, u32[]{:S(2)}, u32[]{:S(2)}) collective-permute-start(f32[256,512]{1,0:T(8,128)S(1)} %collective-permute-done.1), channel_id=1, source_target_pairs={{0,16},{16,0},{1,17},{17,1},{2,18},{18,2},{3,19},{19,3},{4,20},{20... | collective-permute-start | bytes 1572872 | tf_op jit(solution)/shard_map/ppermute | solution.py:20
  45.1 3.4 %collective-permute-start.3 = (f32[256,256]{1,0:T(8,128)S(1)}, f32[256,256]{1,0:T(8,128)S(1)}, u32[]{:S(2)}, u32[]{:S(2)}) collective-permute-start(f32[256,256]{1,0:T(8,128)S(1)} %get-tuple-element.79), channel_id=1, source_target_pairs={{0,16},{16,0},{1,17},{17,1},{2,18},{18,2},{3,19},{19,3},{4,20},{20... | collective-permute-start | bytes 786440 | tf_op jit(solution)/shard_map/ppermute | solution.py:20
  48.5 5.2 %copy-start.3 = (s32[16,16]{1,0:T(8,128)S(1)}, s32[16,16]{1,0:T(8,128)}, u32[]{:S(2)}) copy-start(s32[16,16]{1,0:T(8,128)} %param.10) | copy-start | bytes 3076
  48.6 5.2 %copy-start.4 = (s32[16,16]{1,0:T(8,128)S(1)}, s32[16,16]{1,0:T(8,128)}, u32[]{:S(2)}) copy-start(s32[16,16]{1,0:T(8,128)} %param.11) | copy-start | bytes 3076
  49.5 13.5 %all-to-all-start.1 = ((f32[4,256,128]{2,1,0:T(8,128)}), f32[4,256,128]{2,1,0:T(8,128)S(1)}, u32[]{:S(2)}, u32[]{:S(2)}) async-start(f32[4,256,128]{2,1,0:T(8,128)} %bitcast.13), calls=%async_computation.1 | async-start | bytes 1048576 | tf_op jit(solution)/shard_map/all_to_all | solution.py:85
  53.0 47.0 %all-gather.7.cloned.1.call-start = ((), (), s32[]{:S(2)}) async-start(), calls=%async_computation.7 | async-start | bytes 1179648 | tf_op jit(solution)/shard_map/all_gather | solution.py:114
  64.9 38.0 %all-to-all-start.2 = ((f32[8,256,128]{1,2,0:T(8,128)}), f32[8,256,128]{1,2,0:T(8,128)S(1)}, u32[]{:S(2)}, u32[]{:S(2)}) async-start(f32[8,256,128]{1,2,0:T(8,128)} %broadcast_in_dim.19), calls=%async_computation.2 | async-start | bytes 2097152 | tf_op jit(solution)/shard_map/all_to_all | solution.py:16
  79.0 21.0 %collective-permute-start.4 = (f32[256,512]{1,0:T(8,128)S(1)}, f32[256,512]{1,0:T(8,128)S(1)}, u32[]{:S(2)}, u32[]{:S(2)}) collective-permute-start(f32[256,512]{1,0:T(8,128)S(1)} %pad_maximum_fusion.3), channel_id=1, source_target_pairs={{0,33},{33,0},{1,32},{32,1},{2,35},{35,2},{3,34},{34,3},{4,37},{37... | collective-permute-start | bytes 1572872 | tf_op jit(solution)/shard_map/ppermute | solution.py:73
  103.0 4.5 %collective-permute-start.5 = (f32[8,256,128]{1,2,0:T(8,128)S(1)}, f32[8,256,128]{1,2,0:T(8,128)S(1)}, u32[]{:S(2)}, u32[]{:S(2)}) collective-permute-start(f32[8,256,128]{1,2,0:T(8,128)S(1)} %all-to-all-done.2), channel_id=1, source_target_pairs={{0,16},{16,0},{1,17},{17,1},{2,18},{18,2},{3,19},{19,3},{4,20},{20... | collective-permute-start | bytes 3145736 | tf_op jit(solution)/shard_map/ppermute | solution.py:20
  122.7 9.3 %copy-start.2 = (f32[128,256]{1,0:T(8,128)}, f32[128,256]{1,0:T(8,128)S(1)}, u32[]{:S(2)}) copy-start(f32[128,256]{1,0:T(8,128)S(1)} %broadcast_multiply_fusion.1) | copy-start | bytes 393220
  123.8 32.2 %all-to-all-start.4 = ((f32[8,128,256]{2,1,0:T(8,128)}), f32[8,128,256]{2,1,0:T(8,128)S(1)}, u32[]{:S(2)}, u32[]{:S(2)}) async-start(f32[8,128,256]{2,1,0:T(8,128)} %broadcast_in_dim.36), calls=%async_computation.4 | async-start | bytes 2097152 | tf_op jit(solution)/shard_map/all_to_all | solution.py:136
  132.1 41.6 %all-gather.9.cloned.1.call-start = ((), (), s32[]{:S(2)}) async-start(), calls=%async_computation.8 | async-start | bytes 1179648 | tf_op jit(solution)/shard_map/all_gather | solution.py:138
  132.8 89.2 %all-gather.11.cloned.1.call-start = ((), (), s32[]{:S(2)}) async-start(), calls=%async_computation.9 | async-start | bytes 1179648 | tf_op jit(solution)/shard_map/all_gather | solution.py:149
  132.8 23.9 %collective-permute-start.7 = (f32[256,512]{1,0:T(8,128)S(1)}, f32[256,512]{1,0:T(8,128)S(1)}, u32[]{:S(2)}, u32[]{:S(2)}) collective-permute-start(f32[256,512]{1,0:T(8,128)S(1)} %collective-permute-done.4), channel_id=1, source_target_pairs={{0,16},{16,0},{1,17},{17,1},{2,18},{18,2},{3,19},{19,3},{4,20},{20... | collective-permute-start | bytes 1572872 | tf_op jit(solution)/shard_map/ppermute | solution.py:20
  138.4 18.8 %collective-permute-start.6 = (f32[256,512]{1,0:T(8,128)S(1)}, f32[256,512]{1,0:T(8,128)}, u32[]{:S(2)}, u32[]{:S(2)}) collective-permute-start(f32[256,512]{1,0:T(8,128)S(1)} %pad_maximum_fusion.5), channel_id=1, source_target_pairs={{0,16},{16,0},{1,17},{17,1},{2,18},{18,2},{3,19},{19,3},{4,20},{20... | collective-permute-start | bytes 1572872 | tf_op jit(solution)/shard_map/ppermute | solution.py:20
  173.6 34.3 %copy-start = (f32[1024,256]{1,0:T(8,128)S(1)}, f32[1024,256]{1,0:T(8,128)}, u32[]{:S(2)}) copy-start(f32[1024,256]{1,0:T(8,128)} %all-gather.9.cloned.1.call-done) | copy-start | bytes 3145732
  173.6 6.7 %collective-permute-start.9 = (f32[64,256]{1,0:T(8,128)S(1)}, f32[64,256]{1,0:T(8,128)S(1)}, u32[]{:S(2)}, u32[]{:S(2)}) collective-permute-start(f32[64,256]{1,0:T(8,128)S(1)} %get-tuple-element.58), channel_id=1, source_target_pairs={{0,1},{1,0},{2,3},{3,2},{4,5},{5,4},{6,7},{7,6},{8,9},{9,8},{10,11... | collective-permute-start | bytes 196616 | tf_op jit(solution)/shard_map/ppermute | solution.py:20
  181.0 23.5 %collective-permute-start.8 = (f32[8,128,256]{2,1,0:T(8,128)}, f32[8,128,256]{2,1,0:T(8,128)S(1)}, u32[]{:S(2)}, u32[]{:S(2)}) collective-permute-start(f32[8,128,256]{2,1,0:T(8,128)} %bitcast.59), channel_id=1, source_target_pairs={{0,1},{1,0},{2,3},{3,2},{4,5},{5,4},{6,7},{7,6},{8,9},{9,8},{10,11... | collective-permute-start | bytes 3145736 | tf_op jit(solution)/shard_map/ppermute | solution.py:20
  204.6 11.1 %collective-permute-start.10 = (f32[8,64,256]{2,1,0:T(8,128)S(1)}, f32[8,64,256]{2,1,0:T(8,128)S(1)}, u32[]{:S(2)}, u32[]{:S(2)}) collective-permute-start(f32[8,64,256]{2,1,0:T(8,128)S(1)} %all_to_all.37.refs_0_), channel_id=1, source_target_pairs={{0,1},{1,0},{2,3},{3,2},{4,5},{5,4},{6,7},{7,6},{8,9},{9,8},{10,11... | collective-permute-start | bytes 1572872 | tf_op jit(solution)/shard_map/ppermute | solution.py:20
  222.0 1.2 copy-start.1
Sparse Core Ops, SparseCore 0:
  55.9 44.0 all-gather.6
  135.5 38.0 all-gather.8
  181.1 40.8 all-gather.10

commit v13 on v10

--- a/solution.py
+++ b/solution.py
@@ -56,14 +56,15 @@
     row = 2 * y + xh
     panel = z ^ core
     column = per_core * core + panel
-    keep = keep_mask.astype(jnp.float32)
-    fill = s_pattern.astype(jnp.float32)
+
+    def entry(pattern, a, b):
+        return lax.dynamic_slice(pattern, (a, b), (1, 1)).astype(jnp.float32)
 
     def slices(values, pattern, a, b):
         return jnp.concatenate(
             [
                 lax.dynamic_slice(values, (0, (2 * m + a) * blk + b * half), (blk, half))
-                * pattern[row, per_core * core + 2 * m + a]
+                * entry(pattern, row, per_core * core + 2 * m + a)
                 for m in range(per_core // 2)
             ],
             axis=1,
@@ -79,22 +80,22 @@
         return jnp.dot(mine, b_mine, precision=HIGH) + jnp.dot(theirs, b_theirs, precision=HIGH)
 
     def piece(values):
-        return lax.dynamic_slice(values, (xl * half, panel * blk), (half, blk)) * fill[row, column]
+        return lax.dynamic_slice(values, (xl * half, panel * blk), (half, blk)) * entry(s_pattern, row, column)
 
     def sum_x(parts):
         return jnp.sum(lax.all_to_all(parts, X, split_axis=0, concat_axis=0, tiled=True), axis=0)
 
     def finish(partial):
-        return sum_x(partial.reshape(4, half, blk)) * keep[row, column]
+        return sum_x(partial.reshape(4, half, blk)) * entry(keep_mask, row, column)
 
     y_copies = jnp.broadcast_to(piece(y_blocks)[None], (ny, half, blk))
-    z_piece = piece(z_blocks)
-    y_copies, z_piece, z_blocks = lax.optimization_barrier((y_copies, z_piece, z_blocks))
+    y_copies, z_blocks = lax.optimization_barrier((y_copies, z_blocks))
     y_panel = lax.all_to_all(y_copies, "y", split_axis=0, concat_axis=0, tiled=True)
     y_panel = y_panel.reshape(ny * half, blk)
-    z_part = slices(z_blocks, fill, 1 - xh, 1 - xl)
-    z_part, z_blocks = lax.optimization_barrier((z_part, z_blocks))
-    z_rows = slices(z_blocks, fill, xh, xl)
+    z_part, z_piece = slices(z_blocks, s_pattern, 1 - xh, 1 - xl), piece(z_blocks)
+    z_part, z_piece, z_blocks = lax.optimization_barrier((z_part, z_piece, z_blocks))
+    z_panel = lax.all_gather(z_piece, "y", axis=0)
+    z_rows = slices(z_blocks, s_pattern, xh, xl)
     t_own, t_other = [
         multiply(rows, swap(rows, "core"), y_panel) for rows in (z_rows, from_partner(z_part))
     ]
@@ -110,12 +111,10 @@
     t_col = per_core * source + (z ^ source)
     at_row = t_row * blk + lax.broadcasted_iota(jnp.int32, (blk, half), 0)
     at_col = t_col * blk + xl * half + lax.broadcasted_iota(jnp.int32, (blk, half), 1)
-    q_share = jnp.where(at_row == at_col, 1.5, 0.0) - 0.5 * (keep[t_row, t_col] * t_share)
-    z_panel = lax.all_gather(z_piece, "y", axis=0)
+    q_share = jnp.where(at_row == at_col, 1.5, 0.0) - 0.5 * (entry(keep_mask, t_row, t_col) * t_share)
     q_share, h_blocks = lax.optimization_barrier((q_share, h_blocks))
     q_mine = spread(q_share, "z", nz)
-    h_fill = h_pattern.astype(jnp.float32)
-    h_others = from_partner(slices(h_blocks, h_fill, 1 - xh, 1 - xl))
+    h_others = from_partner(slices(h_blocks, h_pattern, 1 - xh, 1 - xl))
     q_mine, z_panel, h_others = lax.optimization_barrier((q_mine, z_panel, h_others))
     q_theirs = swap(q_mine, "core")
     ordered = z_panel.reshape(2, ny // 2, half, blk).transpose(1, 0, 2, 3)
@@ -132,7 +131,7 @@
     )
     z_copies = jnp.broadcast_to(z_share[None], (ny, half, blk))
     z_copies, h_others, h_blocks = lax.optimization_barrier((z_copies, h_others, h_blocks))
-    h_rows = slices(h_blocks, h_fill, xh, xl)
+    h_rows = slices(h_blocks, h_pattern, xh, xl)
     z_next_panel = lax.all_to_all(z_copies, "y", split_axis=0, concat_axis=0, tiled=True)
     z_next_panel = z_next_panel.reshape(ny * half, blk)
     z_shares = jnp.concatenate([z_share, swap(z_share, "xl")], axis=0)

time: 235 us -> 234 us (level)
  blocking collectives: 24.3 us -> 11.9 us
  between operations: 14.2 us -> 26.3 us
  other arithmetic: 24.8 us -> 13.1 us
  waiting for transfers between devices: 90.7 us -> 97.5 us
  starting transfers between devices: 59.6 us -> 63 us
    all_to_all x2 -> x1, blocking collectives: 24.3 us -> 11.9 us  [sum_x(): lax.all_to_all(parts, X, split_axis=0, concat_axis=0, tiled=True)]
    mul x4, other arithmetic: 14.7 us -> 4.59 us  [slices(): lax.dynamic_slice(values, (0, (2 * m + a) * blk + b * half), (blk, half))]
    all_to_all x1 -> x2, waiting for transfers between devices: 8.43 us -> 16.3 us  [sum_x(): lax.all_to_all(parts, X, split_axis=0, concat_axis=0, tiled=True)]
    all_to_all x1 -> x2, starting transfers between devices: 3.56 us -> 7.04 us  [sum_x(): lax.all_to_all(parts, X, split_axis=0, concat_axis=0, tiled=True)]
  transfers between devices with their start and end apart: 19 -> 20, of which waited for: 11 -> 12; matrix products, arithmetic and copies ran while one was open for 12% -> 8% of each run, Pallas kernels for 1% -> 1%
where the time goes in v13:
time: 234 us; the launch traced here: 231 us
  waiting for transfers between devices  97.5 us (42%)
  starting transfers between devices  63 us (27%)
  between operations  26.3 us (11%)
  other arithmetic  13.1 us (6%)
  blocking collectives  11.9 us (5%)
  local copies, waits for them, and re-layouts  10.2 us (4%)
  matrix products  6.19 us (3%)
  Pallas kernels  2.96 us (1%)
    all_gather x1, waiting for transfers between devices, local(): h_late = lax.all_gather(late, 'z', axis=0)  22 us
    ppermute x9, starting transfers between devices, swap(): return lax.ppermute(array, axis, [(0, 1), (1, 0)])  19.4 us
    all_gather x1, waiting for transfers between devices, local(): z_panel = lax.all_gather(z_piece, 'y', axis=0)  19.2 us
    all_to_all x2, waiting for transfers between devices, sum_x(): lax.all_to_all(parts, X, split_axis=0, concat_axis=0, tiled=True)  16.3 us
    all_to_all x1, waiting for transfers between devices, local(): lax.all_to_all(z_copies, 'y', split_axis=0, concat_axis=0, tiled=True)  14.9 us
    all_to_all x1, blocking collectives, sum_x(): lax.all_to_all(parts, X, split_axis=0, concat_axis=0, tiled=True)  11.9 us
    all_to_all x1, starting transfers between devices, spread(): return lax.all_to_all(copies, axis, split_axis=0, concat_axis=0, tiled=True)  10.2 us
    all_to_all x1, waiting for transfers between devices, local(): lax.all_to_all(early, 'z', split_axis=0, concat_axis=0, tiled=True)  10.1 us
  transfers between devices with their start and end apart: 20, of which 12 were waited for; matrix products, arithmetic and copies ran while one was open for 8% of the time, Pallas kernels for 1%

profile of v13, /device:TPU:56, one launch (start us, length us, event | category | flops | bytes accessed | tf_op | source)
XLA Modules:
  0.0 231.3 jit_solution(7078502357113790257)
XLA Ops:
  7.2 1.7 fusion.25
  9.6 0.9 dynamic-slice_multiply_fusion.17
  10.5 1.1 broadcast_in_dim.18
  11.5 8.6 %all-to-all-start = ((f32[8,128,256]{2,1,0:T(8,128)}), f32[8,128,256]{2,1,0:T(8,128)S(1)}, u32[]{:S(2)}, u32[]{:S(2)}) async-start(f32[8,128,256]{2,1,0:T(8,128)} %broadcast_in_dim.18), calls=%async_computation | async-start | bytes 2097152 | tf_op jit(solution)/shard_map/all_to_all | solution.py:93
  22.7 1.6 dynamic-slice_multiply_fusion.12
  24.3 1.1 dynamic-slice_multiply_fusion.16
  25.5 2.9 %collective-permute-start.1 = (f32[256,512]{1,0:T(8,128)S(1)}, f32[256,512]{1,0:T(8,128)S(1)}, u32[]{:S(2)}, u32[]{:S(2)}) collective-permute-start(f32[256,512]{1,0:T(8,128)S(1)} %pad_maximum_fusion.1), channel_id=1, source_target_pairs={{0,33},{33,0},{1,32},{32,1},{2,35},{35,2},{3,34},{34,3},{4,37},{37... | collective-permute-start | bytes 1572872 | tf_op jit(solution)/shard_map/ppermute | solution.py:74
  30.9 1.2 dynamic-slice_multiply_fusion.11
  32.0 0.8 pad_maximum_fusion.2
  32.9 1.9 collective-permute-start
  34.8 5.1 %collective-permute-done.1 = f32[256,512]{1,0:T(8,128)S(1)} collective-permute-done((f32[256,512]{1,0:T(8,128)S(1)}, f32[256,512]{1,0:T(8,128)S(1)}, u32[]{:S(2)}, u32[]{:S(2)}) %collective-permute-start.1) | collective-permute-done | bytes 524320 | tf_op jit(solution)/shard_map/ppermute | solution.py:74
  39.9 1.9 collective-permute-start.2
  41.8 1.3 all-to-all-done
  43.1 0.4 fusion.11
  43.5 0.4 fusion.9
  43.9 0.4 convolution_add_fusion.3
  44.3 0.4 broadcast_select_fusion
  44.7 1.9 collective-permute-start.3
  46.7 1.5 collective-permute-done.3
  48.3 0.8 fusion
  49.1 3.6 %all-to-all-start.1 = ((f32[4,256,128]{2,1,0:T(8,128)}), f32[4,256,128]{2,1,0:T(8,128)S(1)}, u32[]{:S(2)}, u32[]{:S(2)}) async-start(f32[4,256,128]{2,1,0:T(8,128)} %bitcast.13), calls=%async_computation.1 | async-start | bytes 1048576 | tf_op jit(solution)/shard_map/all_to_all | solution.py:86
  52.6 0.7 all-gather.7.cloned.1.call-update
  53.4 1.5 fusion.23
  55.6 7.0 %all-to-all-done.1 = f32[4,256,128]{2,1,0:T(8,128)S(1)} async-done(((f32[4,256,128]{2,1,0:T(8,128)}), f32[4,256,128]{2,1,0:T(8,128)S(1)}, u32[]{:S(2)}, u32[]{:S(2)}) %all-to-all-start.1) | async-done | bytes 524320 | tf_op jit(solution)/shard_map/all_to_all | solution.py:86
  62.6 0.1 multiply_subtract_fusion
  62.8 1.1 broadcast_in_dim.19
  63.9 10.2 %all-to-all-start.2 = ((f32[8,256,128]{1,2,0:T(8,128)}), f32[8,256,128]{1,2,0:T(8,128)S(1)}, u32[]{:S(2)}, u32[]{:S(2)}) async-start(f32[8,256,128]{1,2,0:T(8,128)} %broadcast_in_dim.19), calls=%async_computation.2 | async-start | bytes 2097152 | tf_op jit(solution)/shard_map/all_to_all | solution.py:16
  76.5 1.2 dynamic-slice_multiply_fusion.7
  77.7 3.1 %collective-permute-start.4 = (f32[256,512]{1,0:T(8,128)S(1)}, f32[256,512]{1,0:T(8,128)S(1)}, u32[]{:S(2)}, u32[]{:S(2)}) collective-permute-start(f32[256,512]{1,0:T(8,128)S(1)} %pad_maximum_fusion.3), channel_id=1, source_target_pairs={{0,33},{33,0},{1,32},{32,1},{2,35},{35,2},{3,34},{34,3},{4,37},{37... | collective-permute-start | bytes 1572872 | tf_op jit(solution)/shard_map/ppermute | solution.py:74
  80.8 19.2 %all-gather.7.cloned.1.call-done = f32[1024,256]{1,0:T(8,128)} async-done(((f32[128,256]{1,0:T(8,128)}), f32[1024,256]{1,0:T(8,128)}) %all-gather.7.cloned.1.call-update) | async-done | bytes 1048592 | tf_op jit(solution)/shard_map/all_gather | solution.py:97
  100.0 1.9 all-to-all-done.2
  101.9 1.9 collective-permute-start.5
  103.9 1.7 reverse_select_fusion
  105.7 0.8 collective-permute-done.5
  106.5 1.0 fusion.28
  107.5 1.0 select_bitcast_fusion.3
  108.5 0.8 pad_maximum_fusion.4
  109.3 3.5 %all-to-all-start.3 = ((f32[4,128,256]{2,1,0:T(8,128)}), f32[4,128,256]{2,1,0:T(8,128)S(1)}, u32[]{:S(2)}, u32[]{:S(2)}) async-start(f32[4,128,256]{2,1,0:T(8,128)} %bitcast.29), calls=%async_computation.3 | async-start | bytes 1048576 | tf_op jit(solution)/shard_map/all_to_all | solution.py:86
  113.5 9.3 %all-to-all-done.3 = f32[4,128,256]{2,1,0:T(8,128)S(1)} async-done(((f32[4,128,256]{2,1,0:T(8,128)}), f32[4,128,256]{2,1,0:T(8,128)S(1)}, u32[]{:S(2)}, u32[]{:S(2)}) %all-to-all-start.3) | async-done | bytes 524320 | tf_op jit(solution)/shard_map/all_to_all | solution.py:86
  122.9 2.5 %collective-permute-start.8 = (f32[128,256]{1,0:T(8,128)S(1)}, f32[128,256]{1,0:T(8,128)S(1)}, u32[]{:S(2)}, u32[]{:S(2)}) collective-permute-start(f32[128,256]{1,0:T(8,128)S(1)} %broadcast_multiply_fusion.1), channel_id=1, source_target_pairs={{0,1},{1,0},{2,3},{3,2},{4,5},{5,4},{6,7},{7,6},{8,9},{9,8},{10,11... | collective-permute-start | bytes 393224 | tf_op jit(solution)/shard_map/ppermute | solution.py:20
  125.3 1.1 broadcast_in_dim.36
  126.4 8.3 %all-to-all-start.4 = ((f32[8,128,256]{2,1,0:T(8,128)}), f32[8,128,256]{2,1,0:T(8,128)S(1)}, u32[]{:S(2)}, u32[]{:S(2)}) async-start(f32[8,128,256]{2,1,0:T(8,128)} %broadcast_in_dim.36), calls=%async_computation.4 | async-start | bytes 2097152 | tf_op jit(solution)/shard_map/all_to_all | solution.py:135
  134.7 0.7 pad_maximum_fusion.7
  138.1 1.9 collective-permute-start.7
  140.0 1.2 dynamic-slice_multiply_fusion.3
  141.2 2.4 %collective-permute-start.6 = (f32[256,512]{1,0:T(8,128)S(1)}, f32[256,512]{1,0:T(8,128)}, u32[]{:S(2)}, u32[]{:S(2)}) collective-permute-start(f32[256,512]{1,0:T(8,128)S(1)} %pad_maximum_fusion.5), channel_id=1, source_target_pairs={{0,16},{16,0},{1,17},{17,1},{2,18},{18,2},{3,19},{19,3},{4,20},{20... | collective-permute-start | bytes 1572872 | tf_op jit(solution)/shard_map/ppermute | solution.py:20
  143.6 14.9 %all-to-all-done.4 = f32[8,128,256]{2,1,0:T(8,128)S(1)} async-done(((f32[8,128,256]{2,1,0:T(8,128)}), f32[8,128,256]{2,1,0:T(8,128)S(1)}, u32[]{:S(2)}, u32[]{:S(2)}) %all-to-all-start.4) | async-done | bytes 1048608 | tf_op jit(solution)/shard_map/all_to_all | solution.py:135
  158.5 0.4 fusion.5
  158.9 0.4 fusion.3
  159.3 0.4 convolution_add_fusion
  159.7 1.4 select_bitcast_fusion.1
  161.2 11.9 %all_to_all.35 = f32[4,128,256]{2,1,0:T(8,128)S(1)} all-to-all(f32[4,128,256]{2,1,0:T(8,128)S(1)} %bitcast.72), channel_id=1, replica_groups=mesh['y'=8,'xh'=2,'core'=2,'z'=8,'xl'=2] {'xh','xl'}, dimensions={0} | all-to-all | bytes 1048576 | tf_op jit(solution)/shard_map/all_to_all | solution.py:86
  173.2 2.5 %collective-permute-start.9 = (f32[64,256]{1,0:T(8,128)S(1)}, f32[64,256]{1,0:T(8,128)S(1)}, u32[]{:S(2)}, u32[]{:S(2)}) collective-permute-start(f32[64,256]{1,0:T(8,128)S(1)} %get-tuple-element.54), channel_id=1, source_target_pairs={{0,1},{1,0},{2,3},{3,2},{4,5},{5,4},{6,7},{7,6},{8,9},{9,8},{10,11... | collective-permute-start | bytes 196616 | tf_op jit(solution)/shard_map/ppermute | solution.py:20
  175.7 3.7 %collective-permute-done.9 = f32[64,256]{1,0:T(8,128)S(1)} collective-permute-done((f32[64,256]{1,0:T(8,128)S(1)}, f32[64,256]{1,0:T(8,128)S(1)}, u32[]{:S(2)}, u32[]{:S(2)}) %collective-permute-start.9) | collective-permute-done | bytes 65568 | tf_op jit(solution)/shard_map/ppermute | solution.py:20
  179.3 0.7 pad_maximum_fusion.8
  180.0 0.8 broadcast_in_dim.37
  180.9 3.5 %all-to-all-start.6 = ((f32[8,64,256]{2,1,0:T(8,128)}), f32[8,64,256]{2,1,0:T(8,128)S(1)}, u32[]{:S(2)}, u32[]{:S(2)}) async-start(f32[8,64,256]{2,1,0:T(8,128)} %broadcast_in_dim.37), calls=%async_computation.6 | async-start | bytes 1048576 | tf_op jit(solution)/shard_map/all_to_all | solution.py:147
  184.4 1.6 copy-done
  186.0 1.5 shard_map.77
  187.5 10.1 %all-to-all-done.6.refs_0_ = f32[8,64,256]{2,1,0:T(8,128)S(1)} async-done(((f32[8,64,256]{2,1,0:T(8,128)}), f32[8,64,256]{2,1,0:T(8,128)S(1)}, u32[]{:S(2)}, u32[]{:S(2)}) %all-to-all-start.6) | async-done | bytes 524320 | tf_op jit(solution)/shard_map/all_to_all | solution.py:147
  197.6 2.5 %collective-permute-start.10 = (f32[8,64,256]{2,1,0:T(8,128)S(1)}, f32[8,64,256]{2,1,0:T(8,128)S(1)}, u32[]{:S(2)}, u32[]{:S(2)}) collective-permute-start(f32[8,64,256]{2,1,0:T(8,128)S(1)} %all-to-all-done.6.refs_0_), channel_id=1, source_target_pairs={{0,1},{1,0},{2,3},{3,2},{4,5},{5,4},{6,7},{7,6},{8,9},{9,8},{10,11... | collective-permute-start | bytes 1572872 | tf_op jit(solution)/shard_map/ppermute | solution.py:20
  200.0 22.0 %all-gather.11.cloned.1.call-done = f32[1024,256]{1,0:T(8,128)} async-done(((f32[128,256]{1,0:T(8,128)}), f32[1024,256]{1,0:T(8,128)}) %all-gather.11.cloned.1.call-update) | async-done | bytes 1048592 | tf_op jit(solution)/shard_map/all_gather | solution.py:151
  222.0 1.2 copy-done.1
  223.3 1.5 shard_map.78
  (33 shorter events, 0.7 us)
Async XLA Ops:
  11.5 31.6 %all-to-all-start = ((f32[8,128,256]{2,1,0:T(8,128)}), f32[8,128,256]{2,1,0:T(8,128)S(1)}, u32[]{:S(2)}, u32[]{:S(2)}) async-start(f32[8,128,256]{2,1,0:T(8,128)} %broadcast_in_dim.18), calls=%async_computation | async-start | bytes 2097152 | tf_op jit(solution)/shard_map/all_to_all | solution.py:93
  25.5 14.4 %collective-permute-start.1 = (f32[256,512]{1,0:T(8,128)S(1)}, f32[256,512]{1,0:T(8,128)S(1)}, u32[]{:S(2)}, u32[]{:S(2)}) collective-permute-start(f32[256,512]{1,0:T(8,128)S(1)} %pad_maximum_fusion.1), channel_id=1, source_target_pairs={{0,33},{33,0},{1,32},{32,1},{2,35},{35,2},{3,34},{34,3},{4,37},{37... | collective-permute-start | bytes 1572872 | tf_op jit(solution)/shard_map/ppermute | solution.py:74
  32.9 11.0 %collective-permute-start = (f32[256,512]{1,0:T(8,128)}, f32[256,512]{1,0:T(8,128)S(1)}, u32[]{:S(2)}, u32[]{:S(2)}) collective-permute-start(f32[256,512]{1,0:T(8,128)} %pad_maximum_fusion.2), channel_id=1, source_target_pairs={{0,16},{16,0},{1,17},{17,1},{2,18},{18,2},{3,19},{19,3},{4,20},{20... | collective-permute-start | bytes 1572872 | tf_op jit(solution)/shard_map/ppermute | solution.py:20
  39.9 4.4 %collective-permute-start.2 = (f32[256,512]{1,0:T(8,128)S(1)}, f32[256,512]{1,0:T(8,128)S(1)}, u32[]{:S(2)}, u32[]{:S(2)}) collective-permute-start(f32[256,512]{1,0:T(8,128)S(1)} %collective-permute-done.1), channel_id=1, source_target_pairs={{0,16},{16,0},{1,17},{17,1},{2,18},{18,2},{3,19},{19,3},{4,20},{20... | collective-permute-start | bytes 1572872 | tf_op jit(solution)/shard_map/ppermute | solution.py:20
  44.7 3.4 %collective-permute-start.3 = (f32[256,256]{1,0:T(8,128)S(1)}, f32[256,256]{1,0:T(8,128)S(1)}, u32[]{:S(2)}, u32[]{:S(2)}) collective-permute-start(f32[256,256]{1,0:T(8,128)S(1)} %get-tuple-element.75), channel_id=1, source_target_pairs={{0,16},{16,0},{1,17},{17,1},{2,18},{18,2},{3,19},{19,3},{4,20},{20... | collective-permute-start | bytes 786440 | tf_op jit(solution)/shard_map/ppermute | solution.py:20
  48.2 5.2 %copy-start.2 = (s32[16,16]{1,0:T(8,128)S(1)}, s32[16,16]{1,0:T(8,128)}, u32[]{:S(2)}) copy-start(s32[16,16]{1,0:T(8,128)} %param.10) | copy-start | bytes 3076
  49.1 13.5 %all-to-all-start.1 = ((f32[4,256,128]{2,1,0:T(8,128)}), f32[4,256,128]{2,1,0:T(8,128)S(1)}, u32[]{:S(2)}, u32[]{:S(2)}) async-start(f32[4,256,128]{2,1,0:T(8,128)} %bitcast.13), calls=%async_computation.1 | async-start | bytes 1048576 | tf_op jit(solution)/shard_map/all_to_all | solution.py:86
  52.6 47.4 %all-gather.7.cloned.1.call-start = ((), (), s32[]{:S(2)}) async-start(), calls=%async_computation.7 | async-start | bytes 1179648 | tf_op jit(solution)/shard_map/all_gather | solution.py:97
  63.9 38.0 %all-to-all-start.2 = ((f32[8,256,128]{1,2,0:T(8,128)}), f32[8,256,128]{1,2,0:T(8,128)S(1)}, u32[]{:S(2)}, u32[]{:S(2)}) async-start(f32[8,256,128]{1,2,0:T(8,128)} %broadcast_in_dim.19), calls=%async_computation.2 | async-start | bytes 2097152 | tf_op jit(solution)/shard_map/all_to_all | solution.py:16
  77.7 22.3 %collective-permute-start.4 = (f32[256,512]{1,0:T(8,128)S(1)}, f32[256,512]{1,0:T(8,128)S(1)}, u32[]{:S(2)}, u32[]{:S(2)}) collective-permute-start(f32[256,512]{1,0:T(8,128)S(1)} %pad_maximum_fusion.3), channel_id=1, source_target_pairs={{0,33},{33,0},{1,32},{32,1},{2,35},{35,2},{3,34},{34,3},{4,37},{37... | collective-permute-start | bytes 1572872 | tf_op jit(solution)/shard_map/ppermute | solution.py:74
  101.9 4.5 %collective-permute-start.5 = (f32[8,256,128]{1,2,0:T(8,128)S(1)}, f32[8,256,128]{1,2,0:T(8,128)S(1)}, u32[]{:S(2)}, u32[]{:S(2)}) collective-permute-start(f32[8,256,128]{1,2,0:T(8,128)S(1)} %all-to-all-done.2), channel_id=1, source_target_pairs={{0,16},{16,0},{1,17},{17,1},{2,18},{18,2},{3,19},{19,3},{4,20},{20... | collective-permute-start | bytes 3145736 | tf_op jit(solution)/shard_map/ppermute | solution.py:20
  109.3 13.5 %all-to-all-start.3 = ((f32[4,128,256]{2,1,0:T(8,128)}), f32[4,128,256]{2,1,0:T(8,128)S(1)}, u32[]{:S(2)}, u32[]{:S(2)}) async-start(f32[4,128,256]{2,1,0:T(8,128)} %bitcast.29), calls=%async_computation.3 | async-start | bytes 1048576 | tf_op jit(solution)/shard_map/all_to_all | solution.py:86
  122.9 11.8 %collective-permute-start.8 = (f32[128,256]{1,0:T(8,128)S(1)}, f32[128,256]{1,0:T(8,128)S(1)}, u32[]{:S(2)}, u32[]{:S(2)}) collective-permute-start(f32[128,256]{1,0:T(8,128)S(1)} %broadcast_multiply_fusion.1), channel_id=1, source_target_pairs={{0,1},{1,0},{2,3},{3,2},{4,5},{5,4},{6,7},{7,6},{8,9},{9,8},{10,11... | collective-permute-start | bytes 393224 | tf_op jit(solution)/shard_map/ppermute | solution.py:20
  126.4 32.1 %all-to-all-start.4 = ((f32[8,128,256]{2,1,0:T(8,128)}), f32[8,128,256]{2,1,0:T(8,128)S(1)}, u32[]{:S(2)}, u32[]{:S(2)}) async-start(f32[8,128,256]{2,1,0:T(8,128)} %broadcast_in_dim.36), calls=%async_computation.4 | async-start | bytes 2097152 | tf_op jit(solution)/shard_map/all_to_all | solution.py:135
  134.7 49.7 %all-gather.9.cloned.1.call-start = ((), (), s32[]{:S(2)}) async-start(), calls=%async_computation.8 | async-start | bytes 2359296 | tf_op jit(solution)/shard_map/all_gather | solution.py:138
  135.4 86.6 %all-gather.11.cloned.1.call-start = ((), (), s32[]{:S(2)}) async-start(), calls=%async_computation.9 | async-start | bytes 1179648 | tf_op jit(solution)/shard_map/all_gather | solution.py:151
  138.1 21.2 %collective-permute-start.7 = (f32[256,512]{1,0:T(8,128)S(1)}, f32[256,512]{1,0:T(8,128)S(1)}, u32[]{:S(2)}, u32[]{:S(2)}) collective-permute-start(f32[256,512]{1,0:T(8,128)S(1)} %collective-permute-done.4), channel_id=1, source_target_pairs={{0,16},{16,0},{1,17},{17,1},{2,18},{18,2},{3,19},{19,3},{4,20},{20... | collective-permute-start | bytes 1572872 | tf_op jit(solution)/shard_map/ppermute | solution.py:20
  141.2 18.5 %collective-permute-start.6 = (f32[256,512]{1,0:T(8,128)S(1)}, f32[256,512]{1,0:T(8,128)}, u32[]{:S(2)}, u32[]{:S(2)}) collective-permute-start(f32[256,512]{1,0:T(8,128)S(1)} %pad_maximum_fusion.5), channel_id=1, source_target_pairs={{0,16},{16,0},{1,17},{17,1},{2,18},{18,2},{3,19},{19,3},{4,20},{20... | collective-permute-start | bytes 1572872 | tf_op jit(solution)/shard_map/ppermute | solution.py:20
  173.2 6.2 %collective-permute-start.9 = (f32[64,256]{1,0:T(8,128)S(1)}, f32[64,256]{1,0:T(8,128)S(1)}, u32[]{:S(2)}, u32[]{:S(2)}) collective-permute-start(f32[64,256]{1,0:T(8,128)S(1)} %get-tuple-element.54), channel_id=1, source_target_pairs={{0,1},{1,0},{2,3},{3,2},{4,5},{5,4},{6,7},{7,6},{8,9},{9,8},{10,11... | collective-permute-start | bytes 196616 | tf_op jit(solution)/shard_map/ppermute | solution.py:20
  180.9 16.7 %all-to-all-start.6 = ((f32[8,64,256]{2,1,0:T(8,128)}), f32[8,64,256]{2,1,0:T(8,128)S(1)}, u32[]{:S(2)}, u32[]{:S(2)}) async-start(f32[8,64,256]{2,1,0:T(8,128)} %broadcast_in_dim.37), calls=%async_computation.6 | async-start | bytes 1048576 | tf_op jit(solution)/shard_map/all_to_all | solution.py:147
  184.4 1.6 copy-start
  197.6 24.5 %collective-permute-start.10 = (f32[8,64,256]{2,1,0:T(8,128)S(1)}, f32[8,64,256]{2,1,0:T(8,128)S(1)}, u32[]{:S(2)}, u32[]{:S(2)}) collective-permute-start(f32[8,64,256]{2,1,0:T(8,128)S(1)} %all-to-all-done.6.refs_0_), channel_id=1, source_target_pairs={{0,1},{1,0},{2,3},{3,2},{4,5},{5,4},{6,7},{7,6},{8,9},{9,8},{10,11... | collective-permute-start | bytes 1572872 | tf_op jit(solution)/shard_map/ppermute | solution.py:20
  222.0 1.2 copy-start.1
Sparse Core Ops, SparseCore 0:
  55.5 44.4 all-gather.6
  138.2 41.6 all-gather.8
  182.0 40.0 all-gather.10
